TPU v7x, 32 devices: a whole 2x2x4 slice. The times are simulated.
32 devices in a mesh: parts: 2 (over y), walk: 4 (over z), slab: 2 (over x), row: 2 (over core).
Axes of the slice: x: 2, y: 2, z: 4, core: 2. Of those that a mesh axis runs over, the one named last changes fastest.
Arguments:
- walkers: bfloat16 [64, 1024, 256], P(('parts', 'walk'), ('slab', 'row')), parts along dimension 0
- trial_orbitals: bfloat16 [2048, 256], P(('parts', 'slab', 'row')), parts along dimension 0
- cholesky: bfloat16 [16, 256, 1024], P(('parts', 'slab', 'row')), parts along dimension 0, may hold values from -0.359375 to 0.359375
- branches: int32 [64], P('parts'), parts along dimension 0, may hold values from 0 to 31, as said below
- counts: int32 [8], P(('parts', 'walk')), parts along dimension 0, may hold values from 4 to 8, as said below
- field: float32 [64, 1024], P(('parts', 'walk'), ('slab', 'row')), parts along dimension 0, may hold values from 0.7 to 1.3
Outputs:
- force_bias: float32 [64, 8], P(('parts', 'walk'), ('slab', 'row')), parts along dimension 0
- exchange_energy: float32 [64, 8], P(('parts', 'walk'), ('slab', 'row')), parts along dimension 0
There are 2 independent parts, one for each index of `parts`. A program takes and returns all parts, laid end to end along the dimension named above; each array names one. Nothing has to cross between parts.
Inputs may be any that keep to these rules, and one draw needn't show every extreme that they name: `branches`: the new walkers of one walk index copy at most 2 walkers from any one walk index, and some walk index gives exactly 2 to some walk index. `counts`: at least one walk index has all 8 alive; the alive ones are the first of its walkers.
All inputs are finite; a program needn't handle non-finite values. Where the computation divides by a largest or mean magnitude, that divisor is 1e-20 or more.
Results may differ from a plain program's by a relative error of at most 0.0068.
Values may be sent and summed in bfloat16 or wider, within the bound.
No kernel may reach another device: no remote copies, remote signals or barrier semaphores. Data moves between devices by JAX's collectives and lax.ppermute only.
A program may use at most 64 MiB of HBM per device.

v0:
```python
import jax
import jax.numpy as jnp
from jax import lax
from jax.sharding import PartitionSpec as P

ITERS = 10


HIGHEST = lax.Precision.HIGHEST


def newton_schulz(intersection):
    column_max = jnp.max(jnp.sum(jnp.abs(intersection), axis=0))
    row_max = jnp.max(jnp.sum(jnp.abs(intersection), axis=1))
    inverse = intersection.T / (column_max * row_max)
    twice_identity = 2.0 * jnp.eye(intersection.shape[0], dtype=intersection.dtype)
    for iteration in range(ITERS):
        inverse = jnp.dot(
            inverse,
            twice_identity - jnp.dot(intersection, inverse, precision=HIGHEST),
            precision=HIGHEST,
        )
    return inverse


def on_device(walkers, trial_orbitals, cholesky, branches, counts, field):
    walk_size = lax.axis_size("walk")
    position = lax.axis_index("walk")
    per_device = walkers.shape[0]
    row_count = walkers.shape[1]
    electrons = walkers.shape[2]
    capacity = (per_device + walk_size - 1) // walk_size
    sender = branches.reshape(walk_size, per_device) // per_device
    local_index = branches.reshape(walk_size, per_device) % per_device
    same_sender = sender[:, :, None] == sender[:, None, :]
    earlier = jnp.arange(per_device)[None, :] < jnp.arange(per_device)[:, None]
    arrival_rank = jnp.sum(same_sender & earlier[None], axis=2)
    wanted = (sender[:, None, :] == position) & (
        arrival_rank[:, None, :] == jnp.arange(capacity, dtype=jnp.int32)[None, :, None]
    )
    chosen = jnp.sum(jnp.where(wanted, local_index[:, None, :], 0), axis=2).reshape(-1)
    present = jnp.any(wanted, axis=2).reshape(-1)
    outgoing = jnp.take(walkers, chosen, axis=0)
    outgoing = jnp.where(present[:, None, None], outgoing, jnp.zeros_like(outgoing))
    outgoing = outgoing.reshape(walk_size, capacity, row_count, electrons)
    arrived = lax.all_to_all(outgoing, "walk", split_axis=0, concat_axis=0, tiled=True)
    my_sender = lax.dynamic_index_in_dim(sender, position, 0, keepdims=False)
    my_rank = lax.dynamic_index_in_dim(arrival_rank, position, 0, keepdims=False)
    arrived_flat = arrived.reshape(walk_size * capacity, row_count, electrons)
    migrated = jnp.take(arrived_flat, my_sender * capacity + my_rank, axis=0)
    propagated = (migrated.astype(jnp.float32) * field[:, :, None]).astype(jnp.bfloat16)
    everything = lax.all_gather(propagated, ("slab", "row"), axis=1, tiled=True)
    shard_count = lax.axis_size(("slab", "row"))
    shard_index = lax.axis_index(("slab", "row"))
    share = per_device // shard_count
    trial_whole = lax.all_gather(trial_orbitals, ("slab", "row"), axis=0, tiled=True)
    own_walkers = lax.dynamic_slice_in_dim(everything, shard_index * share, share, 0)
    intersection = jnp.einsum(
        "mn,wmk->wnk", trial_whole, own_walkers, preferred_element_type=jnp.float32
    )
    inverse = jax.vmap(newton_schulz)(intersection).astype(jnp.bfloat16)
    inverses = lax.all_gather(inverse, ("slab", "row"), axis=0, tiled=True)
    green_full = jnp.einsum(
        "wmn,wnk->wmk", everything, inverses, preferred_element_type=jnp.float32
    ).astype(jnp.bfloat16)
    contracted = jnp.einsum(
        "gnm,wmk->wgnk", cholesky, green_full, preferred_element_type=jnp.float32
    )
    living = (jnp.arange(per_device, dtype=jnp.int32) < counts[0]).astype(jnp.float32)[:, None]
    force_bias = jnp.trace(contracted, axis1=2, axis2=3) * living
    exchange_energy = -0.5 * jnp.einsum("wgnk,wgkn->wg", contracted, contracted) * living
    return (force_bias, exchange_energy)


def solution(mesh):
    return jax.shard_map(
        on_device,
        mesh=mesh,
        in_specs=(
            P(("parts", "walk"), ("slab", "row"), None),
            P(("parts", "slab", "row"), None),
            P(("parts", "slab", "row"), None, None),
            P("parts"),
            P(("parts", "walk")),
            P(("parts", "walk"), ("slab", "row")),
        ),
        out_specs=(P(("parts", "walk"), ("slab", "row")), P(("parts", "walk"), ("slab", "row"))),
        check_vma=False,
    )
```

profile of v0, /device:TPU:0, one launch (start us, length us, event | category | flops | bytes accessed | tf_op | source)
XLA Modules:
  0.0 143.9 jit_solution(5911564659753167839)
XLA Ops:
  7.2 0.0 copy-start
  7.2 0.8 reshape.146
  8.0 0.2 convert_reduce_fusion
  8.3 0.2 select_reduce_fusion
  8.4 0.1 copy.28
  8.5 0.1 reshape.147
  8.6 0.1 fusion.17
  8.8 0.1 copy.27
  8.9 0.1 broadcast_in_dim.41
  9.0 1.8 %gather_fusion = bf16[8,256,256]{2,1,0:T(8,128)(2,1)S(1)} fusion(bf16[8,256,256]{2,1,0:T(8,128)(2,1)} %param.8, s32[1024]{0:T(1024)S(1)} %pad_clamp_fusion.1), kind=kCustom, calls=%fused_computation.clone | custom fusion | bytes 2097184 | tf_op jit(solution)/shard_map/jit(_take)/gather | solution.py:43
  10.8 0.0 copy-start.2
  10.8 1.2 select_select_fusion
  12.0 6.3 %all-to-all-start = ((bf16[4,2,256,256]{3,2,1,0:T(8,128)(2,1)}), bf16[4,2,256,256]{3,2,1,0:T(8,128)(2,1)S(1)}, u32[]{:S(2)}, u32[]{:S(2)}) async-start(bf16[4,2,256,256]{3,2,1,0:T(8,128)(2,1)} %bitcast.2), calls=%async_computation | async-start | bytes 2097152 | tf_op jit(solution)/shard_map/all_to_all | solution.py:46
  18.3 0.0 copy-start.1
  18.3 0.0 all-gather.3.cloned.1.call-start
  18.4 25.7 %all-to-all-done = bf16[4,2,256,256]{3,2,1,0:T(8,128)(2,1)S(1)} async-done(((bf16[4,2,256,256]{3,2,1,0:T(8,128)(2,1)}), bf16[4,2,256,256]{3,2,1,0:T(8,128)(2,1)S(1)}, u32[]{:S(2)}, u32[]{:S(2)}) %all-to-all-start) | async-done | bytes 1048608 | tf_op jit(solution)/shard_map/all_to_all | solution.py:46
  44.1 0.6 gather_fusion.1
  44.7 0.5 copy.29
  45.2 0.0 copy-done.2
  45.2 1.3 multiply_convert_fusion
  46.5 0.0 all-gather.3.cloned.1.call-update
  46.5 0.0 all-gather.5.cloned.1.call-start
  46.6 0.0 copy-done.1
  46.6 7.2 %all_gather.10 = bf16[1024,256]{1,0:T(8,128)(2,1)S(1)} all-gather(bf16[256,256]{1,0:T(8,128)(2,1)S(1)} %copy-done.1), channel_id=1, replica_groups=mesh['parts'=2,'walk'=4,'slab'=2,'row'=2] {'slab','row'}, dimensions={0}, use_global_device_ids=true | all-gather | bytes 655360 | tf_op jit(solution)/shard_map/all_gather | solution.py:56
  53.8 27.0 %all-gather.3.cloned.1.call-done = bf16[8,1024,256]{1,2,0:T(8,128)(2,1)} async-done(((bf16[8,256,256]{1,2,0:T(8,128)(2,1)}), bf16[8,1024,256]{1,2,0:T(8,128)(2,1)}) %all-gather.3.cloned.1.call-update) | async-done | bytes 4194320 | tf_op jit(solution)/shard_map/all_gather | solution.py:52
  80.8 1.7 %abs_reduce_fusion = (f32[2,256]{1,0:T(2,128)S(1)}, f32[2,256]{1,0:T(2,128)S(1)}, f32[2,256,256]{2,1,0:T(8,128)S(1)}) fusion(bf16[1024,256]{1,0:T(8,128)(2,1)S(1)} %all_gather.10, bf16[8,1024,256]{1,2,0:T(8,128)(2,1)} %all-gather.3.cloned.1.call-done, s32[]{:T(128)S(6)} %select_n.60), kind=kOutput, calls=%fused_computation.27 | convolution fusion | flops 268827648 | bytes 2101252 | tf_op jit(solution)/shard_map/mn,wmk->wnk/dot_general | solution.py:58
  82.6 0.1 reduce_max.18
  82.7 0.1 reduce_max.19
  82.8 1.1 convolution_subtract_fusion.9
  83.9 0.7 fusion.11
  84.6 1.0 convolution_subtract_fusion.8
  85.6 0.7 fusion.22
  86.3 1.0 convolution_subtract_fusion.7
  87.4 0.7 fusion.23
  88.0 1.0 convolution_subtract_fusion.6
  89.1 0.7 fusion.24
  89.7 1.0 convolution_subtract_fusion.5
  90.8 0.7 fusion.25
  91.4 1.0 convolution_subtract_fusion.4
  92.5 0.7 fusion.26
  93.2 1.0 convolution_subtract_fusion.3
  94.2 0.7 fusion.27
  94.9 1.2 convolution_subtract_fusion.2
  96.1 0.7 fusion.28
  96.8 1.0 convolution_subtract_fusion.1
  97.8 0.7 fusion.29
  98.5 1.0 convolution_subtract_fusion
  99.5 1.3 convolution_convert_fusion
  100.9 0.0 all-gather.5.cloned.1.call-update
  101.0 0.2 copy.26
  101.8 16.0 %all-gather.5.cloned.1.call-done = bf16[8,256,256]{2,1,0:T(8,128)(2,1)} async-done(((bf16[2,256,256]{2,1,0:T(8,128)(2,1)}), bf16[8,256,256]{2,1,0:T(8,128)(2,1)}) %all-gather.5.cloned.1.call-update) | async-done | bytes 1048592 | tf_op jit(solution)/shard_map/all_gather | solution.py:62
  117.8 0.0 copy-done
  117.8 8.1 %fusion = f32[8,256,2,256]{3,1,2,0:T(8,128)} fusion(bf16[8,1024,256]{1,2,0:T(8,128)(2,1)} %all-gather.3.cloned.1.call-done, bf16[8,256,256]{2,1,0:T(8,128)(2,1)} %all-gather.5.cloned.1.call-done, bf16[2,256,1024]{2,1,0:T(8,128)(2,1)S(1)} %copy-done), kind=kOutput, calls=%fused_computation.2 | convolution fusion | flops 3223322624 | bytes 10485760 | tf_op jit(solution)/shard_map/gnm,wmk->wgnk/dot_general | solution.py:66
  125.9 5.3 %copy.59 = f32[8,2,256,256]{2,3,1,0:T(8,128)} copy(f32[8,2,256,256]{3,2,1,0:T(8,128)} %bitcast.70) | data formatting | bytes 8388608
  131.3 4.4 %fusion.3 = (f32[8,2]{1,0:T(8,128)S(1)}, f32[8,2]{1,0:T(8,128)S(1)}) fusion(f32[8,2,256,256]{2,3,1,0:T(8,128)} %copy.59, f32[8,256,2,256]{3,1,2,0:T(8,128)} %fusion, pred[256,256]{0,1:T(8,128)(4,1)S(1)} %copy.26), kind=kLoop, calls=%fused_computation.7 | loop fusion | flops 4194272 | bytes 8454272
  135.7 0.1 broadcast_multiply_fusion
  135.8 0.6 copy.42
  136.4 0.1 copy.60
  136.5 0.6 broadcast_multiply_fusion.1
  (13 shorter events, 0.1 us)
Async XLA Ops:
  7.2 110.7 %copy-start = (bf16[2,256,1024]{2,1,0:T(8,128)(2,1)S(1)}, bf16[2,256,1024]{2,1,0:T(8,128)(2,1)}, u32[]{:S(2)}) copy-start(bf16[2,256,1024]{2,1,0:T(8,128)(2,1)} %param.10) | copy-start | bytes 3145732
  10.8 34.4 %copy-start.2 = (f32[8,256]{1,0:T(8,128)S(1)}, f32[8,256]{1,0:T(8,128)}, u32[]{:S(2)}) copy-start(f32[8,256]{1,0:T(8,128)} %param.13) | copy-start | bytes 24580
  12.0 32.0 %all-to-all-start = ((bf16[4,2,256,256]{3,2,1,0:T(8,128)(2,1)}), bf16[4,2,256,256]{3,2,1,0:T(8,128)(2,1)S(1)}, u32[]{:S(2)}, u32[]{:S(2)}) async-start(bf16[4,2,256,256]{3,2,1,0:T(8,128)(2,1)} %bitcast.2), calls=%async_computation | async-start | bytes 2097152 | tf_op jit(solution)/shard_map/all_to_all | solution.py:46
  18.3 28.3 %copy-start.1 = (bf16[256,256]{1,0:T(8,128)(2,1)S(1)}, bf16[256,256]{1,0:T(8,128)(2,1)}, u32[]{:S(2)}) copy-start(bf16[256,256]{1,0:T(8,128)(2,1)} %param.9) | copy-start | bytes 393220
  18.3 62.5 %all-gather.3.cloned.1.call-start = ((), (), s32[]{:S(2)}) async-start(), calls=%async_computation.1 | async-start | bytes 5242880 | tf_op jit(solution)/shard_map/all_gather | solution.py:52
  46.5 71.3 %all-gather.5.cloned.1.call-start = ((), (), s32[]{:S(2)}) async-start(), calls=%async_computation.2 | async-start | bytes 1310720 | tf_op jit(solution)/shard_map/all_gather | solution.py:62
Sparse Core Ops, SparseCore 0:
  46.7 34.1 all-gather.2
  101.0 16.7 all-gather.4
where the time goes:
time: 144 us
  waiting for transfers between devices  68.8 us (48%)
  matrix products  27.8 us (19%)
  between operations  15 us (10%)
  local copies, waits for them, and re-layouts  10.4 us (7%)
  other arithmetic  8.38 us (6%)
  blocking collectives  7.17 us (5%)
  starting transfers between devices  6.36 us (4%)
    all_gather x1, waiting for transfers between devices, on_device(): everything = lax.all_gather(propagated, ('slab', 'row'), axis=1, tiled=True)  27 us
    all_to_all x1, waiting for transfers between devices, on_device(): lax.all_to_all(outgoing, 'walk', split_axis=0, concat_axis=0, tiled=True)  25.7 us
    all_gather x1, waiting for transfers between devices, on_device(): inverses = lax.all_gather(inverse, ('slab', 'row'), axis=0, tiled=True)  16 us
    dot_general x10, matrix products, newton_schulz(): jnp.dot(intersection, inverse, precision=HIGHEST)  10.7 us
    dot_general x1, matrix products, on_device(): jnp.einsum('gnm,wmk->wgnk', cholesky, green_full, preferred_element_type=...  8.12 us
    dot_general x10, matrix products, newton_schulz(): jnp.dot(inverse, twice_identity - jnp.dot(intersection, inverse, precisio...  7.25 us
    all_gather x1, blocking collectives, on_device(): lax.all_gather(trial_orbitals, ('slab', 'row'), axis=0, tiled=True)  7.17 us
    all_to_all x1, starting transfers between devices, on_device(): lax.all_to_all(outgoing, 'walk', split_axis=0, concat_axis=0, tiled=True)  6.32 us
  transfers between devices with their start and end apart: 3, of which 3 were waited for; matrix products, arithmetic and copies ran while one was open for 0% of the time, Pallas kernels for 0%

commit v1 on v0

v1 whole, which is shorter than its diff:
```python
import functools

import jax
import jax.numpy as jnp
from jax import lax
from jax.experimental import pallas as pl
from jax.experimental.pallas import tpu as pltpu
from jax.sharding import PartitionSpec as P

ITERS = 10
SR = ("slab", "row")
ALL = ("walk", "slab", "row")
F32 = jnp.float32
BF16 = jnp.bfloat16
VMEM_LIMIT = 24 * 2**20
SMALL_LIMIT = 2**20
HIGHEST = lax.Precision.HIGHEST


def dot(a, b, dims=((1,), (0,))):
    return lax.dot_general(a, b, (dims, ((), ())), preferred_element_type=F32)


def split(x):
    high = x.astype(BF16)
    return high, (x - high.astype(F32)).astype(BF16)


def place():
    return lax.axis_index("walk"), lax.axis_index("slab") * lax.axis_size("row") + lax.axis_index("row")


def whole(memory=pltpu.VMEM):
    return pl.BlockSpec(memory_space=memory)


def select_kernel(n, per, share, branches, walkers, field, *refs):
    sends, fields, sems = refs[:n], refs[n : 2 * n], refs[2 * n]
    walk, q = place()
    for k in range(n):
        other = q ^ k
        rank = jnp.int32(0)
        for i in range(per):
            branch = branches[other * per + i]
            hit = lax.div(branch, per) == walk

            @pl.when(hit)
            def _(branch=branch, rank=rank):
                pltpu.make_async_copy(
                    walkers.at[lax.rem(branch, per)], sends[k].at[rank], sems.at[k, rank]
                ).start()

            rank = rank + hit.astype(jnp.int32)
    for k in range(n):
        other = q ^ k
        rank = jnp.int32(0)
        for i in range(per):
            hit = lax.div(branches[walk * per + i], per) == other

            @pl.when(hit)
            def _(i=i, rank=rank):
                fields[k][pl.ds(rank, 1), :] = field[i : i + 1, :]

            rank = rank + hit.astype(jnp.int32)
    for k in range(n):
        for rank in range(share):
            pltpu.make_async_copy(walkers.at[0], sends[k].at[rank], sems.at[k, rank]).wait()


def select(n, per, share, branches, walkers, field):
    rows, electrons = walkers.shape[1:]
    return pl.pallas_call(
        functools.partial(select_kernel, n, per, share),
        out_shape=[jax.ShapeDtypeStruct((share, rows, electrons), walkers.dtype)] * n
        + [jax.ShapeDtypeStruct((share, rows), field.dtype)] * n,
        in_specs=[whole(pltpu.SMEM), whole(pl.ANY), whole()],
        out_specs=[whole(pl.ANY)] * n + [whole()] * n,
        scratch_shapes=[pltpu.SemaphoreType.DMA((n, share))],
        compiler_params=pltpu.CompilerParams(vmem_limit_bytes=VMEM_LIMIT),
        cost_estimate=pl.CostEstimate(flops=0, bytes_accessed=4 * walkers.size, transcendentals=0),
        name="select",
    )(branches, walkers, field)


def green_kernel(n, share, *refs):
    blocks, fields, trials = refs[:n], refs[n : 2 * n], refs[2 * n : 3 * n]
    green, by_block, moved, state = refs[3 * n :]
    walk, q = place()
    rows, electrons = blocks[0].shape[1:]
    for k in range(n):
        by_block[pl.ds(walk ^ k, 1), :share, :] = fields[k][...][None]
    columns = [by_block[pl.ds(q ^ k, 1), :, :].reshape(by_block.shape[1:]).T for k in range(n)]
    for i in range(share):
        transposed = jnp.zeros((electrons, electrons), F32)
        for k in range(n):
            part = (blocks[k][i].astype(F32) * columns[k][:, i : i + 1]).astype(BF16)
            moved[i, k * rows : (k + 1) * rows, :] = part
            transposed = transposed + dot(part, trials[k][...], ((0,), (0,)))
        size = jnp.abs(transposed)
        scale = jnp.max(jnp.sum(size, axis=0)) * jnp.max(jnp.sum(size, axis=1))
        start = transposed / scale
        high, low = split(transposed)
        start_high, start_low = split(start)
        across = ((0,), (0,))
        state[i, :electrons, :] = start
        state[i, electrons:, :] = dot(high, start_high, across) + (
            dot(high, start_low, across) + dot(low, start_high, across)
        )

    def advance(step, carry):
        for i in range(share):
            now = state[i]
            high, low = split(now)
            right_high, right_low = high[electrons:], low[electrons:]
            product = dot(high, right_high) + (dot(high, right_low) + dot(low, right_high))
            state[i] = 2.0 * now - product
        return carry

    lax.fori_loop(0, ITERS - 1, advance, 0)
    for i in range(share):
        now = state[i]
        high, low = split(now)
        left_high, left_low = high[:electrons], low[:electrons]
        right_high, right_low = high[electrons:], low[electrons:]
        product = dot(left_high, right_high) + (dot(left_high, right_low) + dot(left_low, right_high))
        inverse = (2.0 * now[:electrons] - product).astype(BF16)
        for k in range(n):
            at = pl.multiple_of((q ^ k) * rows, rows)
            green[pl.ds(at, rows), i * electrons : (i + 1) * electrons] = dot(
                moved[i, k * rows : (k + 1) * rows, :], inverse
            ).astype(BF16)


def make_green(n, share, blocks, fields, trials):
    rows, electrons = blocks[0].shape[1:]
    padded = -(-share // 8) * 8
    flops = share * (8 * rows * n * electrons**2 + 2 * 6 * ITERS * electrons**3)
    return pl.pallas_call(
        functools.partial(green_kernel, n, share),
        out_shape=jax.ShapeDtypeStruct((n * rows, share * electrons), BF16),
        in_specs=[whole()] * (3 * n),
        out_specs=whole(),
        scratch_shapes=[
            pltpu.VMEM((n, padded, rows), F32),
            pltpu.VMEM((share, n * rows, electrons), BF16),
            pltpu.VMEM((share, 2 * electrons, electrons), F32),
        ],
        compiler_params=pltpu.CompilerParams(vmem_limit_bytes=VMEM_LIMIT),
        cost_estimate=pl.CostEstimate(flops=flops, bytes_accessed=3 * 2**20, transcendentals=0),
        name="green",
    )(*blocks, *fields, *trials)


def contract_kernel(share, count, *refs):
    vectors, green, outs = refs[:count], refs[count], refs[count + 1 :]
    electrons = vectors[0].shape[1]
    half = electrons // 2
    row = lax.broadcasted_iota(jnp.int32, (electrons, electrons), 0)
    column = lax.broadcasted_iota(jnp.int32, (electrons, electrons), 1)
    out_row = lax.broadcasted_iota(jnp.int32, (8, 128), 0)
    lane = lax.broadcasted_iota(jnp.int32, (8, 128), 1)
    for v in range(count):
        held = jnp.zeros((8, 128), F32)
        for g in range(vectors[v].shape[0]):
            both = dot(vectors[v][g], green[...])
            for i in range(share):
                one = both[:, i * electrons : (i + 1) * electrons]
                trace = jnp.sum(jnp.where(row == column, one, 0.0))
                a, b = one[:half, :half], one[:half, half:]
                c, d = one[half:, :half], one[half:, half:]
                exchange = -0.5 * jnp.sum(a * a.T + d * d.T + 2.0 * (b * c.T))
                here = out_row == g * share + i
                held = jnp.where(here & (lane == 0), trace, held)
                held = jnp.where(here & (lane == 1), exchange, held)
        outs[v][...] = held


def contract(share, vectors, green):
    flops = sum(2 * v.size * green.shape[1] for v in vectors)
    return pl.pallas_call(
        functools.partial(contract_kernel, share, len(vectors)),
        out_shape=[jax.ShapeDtypeStruct((8, 128), F32)] * len(vectors),
        in_specs=[whole()] * (len(vectors) + 1),
        out_specs=[whole()] * len(vectors),
        compiler_params=pltpu.CompilerParams(vmem_limit_bytes=VMEM_LIMIT),
        cost_estimate=pl.CostEstimate(
            flops=flops, bytes_accessed=sum(2 * v.size for v in vectors) + 2 * green.size, transcendentals=0
        ),
        name="contract",
    )(*vectors, green)


def unpack_kernel(n, per, share, branches, counts, *refs):
    arrived, force, exchange = refs[:n], refs[n], refs[n + 1]
    walk, q = place()
    vectors = force.shape[0]
    row = lax.broadcasted_iota(jnp.int32, force.shape, 1)
    column = lax.broadcasted_iota(jnp.int32, force.shape, 0)
    force_all = jnp.zeros(force.shape, F32)
    exchange_all = jnp.zeros(force.shape, F32)
    senders = [lax.div(branches[walk * per + i], per) for i in range(per)]
    for i in range(per):
        rank = jnp.int32(0)
        for j in range(i):
            rank = rank + (senders[j] == senders[i]).astype(jnp.int32)
        living = (i < counts[0]).astype(F32)
        for g in range(vectors):
            at = g * share + rank
            values = [jnp.float32(0.0), jnp.float32(0.0)]
            for k in range(n):
                mine = (senders[i] ^ q) == k
                values = [jnp.where(mine, arrived[k][at, c], values[c]) for c in range(2)]
            here = (row == i) & (column == g)
            force_all = jnp.where(here, values[0] * living, force_all)
            exchange_all = jnp.where(here, values[1] * living, exchange_all)
    force[...] = force_all
    exchange[...] = exchange_all


def unpack(n, per, share, vectors, branches, counts, arrived):
    return pl.pallas_call(
        functools.partial(unpack_kernel, n, per, share),
        out_shape=[jax.ShapeDtypeStruct((vectors, per), F32)] * 2,
        in_specs=[whole(pltpu.SMEM)] * (2 + n),
        out_specs=[whole()] * 2,
        compiler_params=pltpu.CompilerParams(vmem_limit_bytes=SMALL_LIMIT),
        name="unpack",
    )(branches, counts, *arrived)


def at_the_source(walkers, trial_orbitals, cholesky, branches, counts, field):
    n = lax.axis_size("walk")
    per = walkers.shape[0]
    share = per // n
    row_size = lax.axis_size("row")
    partner = lambda k: [(i, i ^ k) for i in range(n)]
    move = lambda x, k: lax.ppermute(x, SR, partner(k)) if k else x
    pairs = [(w, q) for w in range(n) for q in range(n)]
    ask = lambda x, k: lax.ppermute(x, ALL, [(w * n + q, (q ^ k) * n + w) for w, q in pairs])
    answer = lambda x, k: lax.ppermute(x, ALL, [(w * n + q, q * n + (w ^ k)) for w, q in pairs])

    def gathered(x):
        blocks = [x]
        for k in range(1, n):
            low = k & (row_size - 1)
            blocks.append(move(x, k) if low == 0 or low == k else move(blocks[k ^ low], low))
        return blocks

    trials = gathered(trial_orbitals)
    chosen = select(n, per, share, branches, walkers, field)
    blocks = [move(x, k) for k, x in enumerate(chosen[:n])]
    fields = [ask(x, k) for k, x in enumerate(chosen[n:])]
    chunks = cholesky.shape[0]
    parts = [cholesky[c : c + 1] for c in range(chunks)]
    near = [k for k in range(n) if k < row_size]
    far = [k for k in range(n) if k >= row_size]
    whole_near = [cholesky] + [move(cholesky, k) for k in near[1:]]
    far_parts = [gathered_far(parts[c], move, far, row_size) for c in range(chunks)]
    green = make_green(n, share, blocks, fields, trials)
    results = dict()
    for k, held in zip(near, contract(share, whole_near, green)):
        results[k] = held
    late = [contract(share, [far_parts[c][k] for k in far], green) for c in range(chunks)]
    merged = merge(n, near, far, chunks, share, results, late)
    arrived = [answer(x, k) for k, x in enumerate(merged)]
    return tuple(x.T for x in unpack(n, per, share, cholesky.shape[0], branches, counts, arrived))


def gathered_far(x, move, far, row_size):
    held = {}
    for k in far:
        low = k & (row_size - 1)
        held[k] = move(x, k) if low == 0 else move(held[k ^ low], low)
    return held


def merge_kernel(n, near, far, chunks, share, *refs):
    close, late, outs = refs[: len(near)], refs[len(near) : -n], refs[-n:]
    walk, q = place()
    rows = lax.broadcasted_iota(jnp.int32, (8, 128), 0)
    groups = {}
    for at, k in enumerate(near):
        groups[k] = close[at][...]
    for at, k in enumerate(far):
        held = late[at][...]
        for c in range(1, chunks):
            moved = pltpu.roll(late[c * len(far) + at][...], c * share, 0)
            held = jnp.where(rows >= c * share, moved, held)
        groups[k] = held
    for k in range(n):
        group = q ^ walk ^ k
        value = groups[0]
        for j in range(1, n):
            value = jnp.where(group == j, groups[j], value)
        outs[k][...] = value


def merge(n, near, far, chunks, share, results, late):
    operands = [results[k] for k in near] + [x for held in late for x in held]
    return pl.pallas_call(
        functools.partial(merge_kernel, n, near, far, chunks, share),
        out_shape=[jax.ShapeDtypeStruct((8, 128), F32)] * n,
        in_specs=[whole()] * len(operands),
        out_specs=[whole()] * n,
        compiler_params=pltpu.CompilerParams(vmem_limit_bytes=SMALL_LIMIT),
        name="merge",
    )(*operands)


def newton_schulz(intersection):
    column_max = jnp.max(jnp.sum(jnp.abs(intersection), axis=0))
    row_max = jnp.max(jnp.sum(jnp.abs(intersection), axis=1))
    inverse = intersection.T / (column_max * row_max)
    twice_identity = 2.0 * jnp.eye(intersection.shape[0], dtype=intersection.dtype)
    for iteration in range(ITERS):
        inverse = jnp.dot(
            inverse,
            twice_identity - jnp.dot(intersection, inverse, precision=HIGHEST),
            precision=HIGHEST,
        )
    return inverse


def pick(array, indices):
    return jnp.concatenate(
        [lax.dynamic_slice_in_dim(array, indices[i], 1, 0) for i in range(indices.shape[0])], axis=0
    )


def at_the_target(walkers, trial_orbitals, cholesky, branches, counts, field):
    walk_size = lax.axis_size("walk")
    position = lax.axis_index("walk")
    per_device, row_count, electrons = walkers.shape
    capacity = (per_device + walk_size - 1) // walk_size
    sender = branches.reshape(walk_size, per_device) // per_device
    local_index = branches.reshape(walk_size, per_device) % per_device
    same_sender = sender[:, :, None] == sender[:, None, :]
    earlier = jnp.arange(per_device)[None, :] < jnp.arange(per_device)[:, None]
    arrival_rank = jnp.sum(same_sender & earlier[None], axis=2)
    wanted = (sender[:, None, :] == position) & (
        arrival_rank[:, None, :] == jnp.arange(capacity, dtype=jnp.int32)[None, :, None]
    )
    chosen = jnp.sum(jnp.where(wanted, local_index[:, None, :], 0), axis=2).reshape(-1)
    outgoing = pick(walkers, chosen).reshape(walk_size, capacity, row_count, electrons)
    arrived = lax.all_to_all(outgoing, "walk", split_axis=0, concat_axis=0, tiled=True)
    my_sender = lax.dynamic_index_in_dim(sender, position, 0, keepdims=False)
    my_rank = lax.dynamic_index_in_dim(arrival_rank, position, 0, keepdims=False)
    arrived_flat = arrived.reshape(walk_size * capacity, row_count, electrons)
    migrated = pick(arrived_flat, my_sender * capacity + my_rank)
    propagated = (migrated.astype(F32) * field[:, :, None]).astype(BF16)
    everything = lax.all_gather(propagated, SR, axis=1, tiled=True)
    shard_count = lax.axis_size(SR)
    share = per_device // shard_count
    trial_whole = lax.all_gather(trial_orbitals, SR, axis=0, tiled=True)
    own_walkers = lax.dynamic_slice_in_dim(everything, lax.axis_index(SR) * share, share, 0)
    intersection = jnp.einsum("mn,wmk->wnk", trial_whole, own_walkers, preferred_element_type=F32)
    inverse = jax.vmap(newton_schulz)(intersection).astype(BF16)
    inverses = lax.all_gather(inverse, SR, axis=0, tiled=True)
    green = jnp.einsum("wmn,wnk->wmk", everything, inverses, preferred_element_type=F32).astype(BF16)
    contracted = jnp.einsum("gnm,wmk->wgnk", cholesky, green, preferred_element_type=F32)
    living = (jnp.arange(per_device, dtype=jnp.int32) < counts[0]).astype(F32)[:, None]
    force_bias = jnp.trace(contracted, axis1=2, axis2=3) * living
    exchange_energy = -0.5 * jnp.einsum("wgnk,wgkn->wg", contracted, contracted) * living
    return (force_bias, exchange_energy)


def on_device(walkers, trial_orbitals, cholesky, branches, counts, field):
    walk_size, shard_count = lax.axis_size("walk"), lax.axis_size(SR)
    per = walkers.shape[0]
    if walk_size == shard_count and per % walk_size == 0 and not walk_size & (walk_size - 1):
        if cholesky.shape[0] * (per // walk_size) <= 8:
            return at_the_source(walkers, trial_orbitals, cholesky, branches, counts, field)
    return at_the_target(walkers, trial_orbitals, cholesky, branches, counts, field)


def solution(mesh):
    return jax.shard_map(
        on_device,
        mesh=mesh,
        in_specs=(
            P(("parts", "walk"), SR, None),
            P(("parts",) + SR, None),
            P(("parts",) + SR, None, None),
            P("parts"),
            P(("parts", "walk")),
            P(("parts", "walk"), SR),
        ),
        out_specs=(P(("parts", "walk"), SR), P(("parts", "walk"), SR)),
        check_vma=False,
    )
```

time: 144 us -> 69.4 us (0.48)
  waiting for transfers between devices: 68.8 us -> 25.7 us
  matrix products: 27.8 us -> 0 us
  starting transfers between devices: 6.36 us -> 23.9 us
  Pallas kernels: 0 us -> 16.9 us
  between operations: 15 us -> 1.44 us
  local copies, waits for them, and re-layouts: 10.4 us -> 1.33 us
  other arithmetic: 8.38 us -> 0 us
  blocking collectives: 7.17 us -> 0 us
    all_gather x2 -> x0, waiting for transfers between devices: 43 us -> none  [the longest x1 27 us: on_device(): everything = lax.all_gather(propagated, ('slab', 'row'), axis=1, tiled=True)]
    dot_general x22 -> x0, matrix products: 27.8 us -> none  [the longest x10 10.7 us: newton_schulz(): jnp.dot(intersection, inverse, precision=HIGHEST)]
    all_to_all x1 -> x0, waiting for transfers between devices: 25.7 us -> none  [on_device(): lax.all_to_all(outgoing, 'walk', split_axis=0, concat_axis=0, tiled=True)]
    ppermute x0 -> x19, waiting for transfers between devices: none -> 25.7 us  [the longest x11 21.2 us: at_the_source(): move = lambda x, k: lax.ppermute(x, SR, partner(k)) if k else x]
    ppermute x0 -> x19, starting transfers between devices: none -> 23.9 us  [the longest x4 11.7 us: at_the_source(): lax.ppermute(x, ALL, [(w * n + q, (q ^ k) * n + w) for w, q in pairs])]
    pallas_call x0 -> x7, Pallas kernels: none -> 16.9 us  [the longest x1 9.11 us: make_green(): pl.pallas_call(functools.partial(green_kernel, n, share), out_shape=jax.S...]
    all_gather x1 -> x0, blocking collectives: 7.17 us -> none  [on_device(): lax.all_gather(trial_orbitals, ('slab', 'row'), axis=0, tiled=True)]
    all_to_all x1 -> x0, starting transfers between devices: 6.32 us -> none  [on_device(): lax.all_to_all(outgoing, 'walk', split_axis=0, concat_axis=0, tiled=True)]
  transfers between devices with their start and end apart: 3 -> 19, of which waited for: 3 -> 6; matrix products, arithmetic and copies ran while one was open for 0% -> 2% of each run, Pallas kernels for 0% -> 20%
where the time goes in v1:
time: 69.4 us; the launch traced here: 69.2 us
  waiting for transfers between devices  25.7 us (37%)
  starting transfers between devices  23.9 us (34%)
  Pallas kernels  16.9 us (24%)
  between operations  1.44 us (2%)
  local copies, waits for them, and re-layouts  1.33 us (2%)
    ppermute x11, waiting for transfers between devices, at_the_source(): move = lambda x, k: lax.ppermute(x, SR, partner(k)) if k else x  21.2 us
    ppermute x4, starting transfers between devices, at_the_source(): lax.ppermute(x, ALL, [(w * n + q, (q ^ k) * n + w) for w, q in pairs])  11.7 us
    pallas_call x1, Pallas kernels, make_green(): pl.pallas_call(functools.partial(green_kernel, n, share), out_shape=jax.S...  9.11 us
    ppermute x11, starting transfers between devices, at_the_source(): move = lambda x, k: lax.ppermute(x, SR, partner(k)) if k else x  6.8 us
    ppermute x4, starting transfers between devices, at_the_source(): lax.ppermute(x, ALL, [(w * n + q, q * n + (w ^ k)) for w, q in pairs])  5.42 us
    ppermute x4, waiting for transfers between devices, at_the_source(): lax.ppermute(x, ALL, [(w * n + q, q * n + (w ^ k)) for w, q in pairs])  4.22 us
    pallas_call x3, Pallas kernels, contract(): pl.pallas_call(functools.partial(contract_kernel, share, len(vectors)), o...  3.51 us
    pallas_call x1, Pallas kernels, select(): pl.pallas_call(functools.partial(select_kernel, n, per, share), out_shape...  2.73 us
  transfers between devices with their start and end apart: 19, of which 6 were waited for; matrix products, arithmetic and copies ran while one was open for 2% of the time, Pallas kernels for 20%

profile of v1, /device:TPU:0, one launch (start us, length us, event | category | flops | bytes accessed | tf_op | source)
XLA Modules:
  0.0 69.2 jit_solution(10254078755215482608)
XLA Ops:
  0.6 0.0 copy-start.2
  0.6 0.0 copy-start
  0.7 3.0 %collective-permute-start.9 = (bf16[256,256]{1,0:T(8,128)(2,1)}, bf16[256,256]{1,0:T(8,128)(2,1)S(1)}, u32[]{:S(2)}, u32[]{:S(2)}) collective-permute-start(bf16[256,256]{1,0:T(8,128)(2,1)} %refs_8_.1), channel_id=1, source_target_pairs={{0,2},{1,3},{2,0},{3,1},{4,6},{5,7},{6,4},{7,5},{8,10},{9,11},{10,... | collective-permute-start | bytes 393224 | tf_op jit(solution)/shard_map/ppermute | solution.py:237
  3.7 0.0 copy-start.3
  3.7 0.0 copy-start.4
  3.7 1.3 %fusion = (bf16[1,256,1024]{2,1,0:T(8,128)(2,1)S(1)}, bf16[1,256,1024]{2,1,0:T(8,128)(2,1)S(1)}) fusion(bf16[2,256,1024]{2,1,0:T(8,128)(2,1)} %refs_0_.1), kind=kLoop, calls=%fused_computation | loop fusion | bytes 2097152 | tf_op jit(solution)/shard_map/slice | solution.py:254
  5.0 0.0 copy-start.1
  5.0 0.1 collective-permute-start.13
  5.1 0.0 copy-done.2
  5.1 0.0 copy-done
  5.1 0.0 copy-done.3
  5.1 2.7 %select.1 = (bf16[2,256,256]{2,1,0:T(8,128)(2,1)S(1)}, bf16[2,256,256]{2,1,0:T(8,128)(2,1)S(1)}, bf16[2,256,256]{2,1,0:T(8,128)(2,1)S(1)}, bf16[2,256,256]{2,1,0...) custom-call(s32[32]{0:T(128)S(1)} %copy-done.3, ...), custom_call_target="tpu_custom_call" | custom-call | bytes 2097152 | tf_op jit(solution)/shard_map/select/pallas_call | solution.py:72
  7.9 0.7 collective-permute-start.4
  8.5 3.4 %collective-permute-start.5 = (f32[2,256]{1,0:T(2,128)S(1)}, f32[2,256]{1,0:T(2,128)S(1)}, u32[]{:S(2)}, u32[]{:S(2)}) collective-permute-start(f32[2,256]{1,0:T(2,128)S(1)} %get-tuple-element.27), channel_id=1, source_target_pairs={{0,4},{1,0},{2,12},{3,8},{4,5},{5,1},{6,13},{7,9},{8,6},{9,2},{10,... | collective-permute-start | bytes 6152 | tf_op jit(solution)/shard_map/ppermute | solution.py:239
  11.9 2.8 %collective-permute-start.6 = (f32[2,256]{1,0:T(2,128)S(1)}, f32[2,256]{1,0:T(2,128)S(1)}, u32[]{:S(2)}, u32[]{:S(2)}) collective-permute-start(f32[2,256]{1,0:T(2,128)S(1)} %get-tuple-element.28), channel_id=1, source_target_pairs={{0,8},{1,12},{2,0},{3,4},{4,9},{5,13},{6,1},{7,5},{8,10},{9,14},{1... | collective-permute-start | bytes 6152 | tf_op jit(solution)/shard_map/ppermute | solution.py:239
  14.7 0.0 collective-permute-done.4.refs_4_
  14.7 4.8 %collective-permute-start.7 = (f32[2,256]{1,0:T(2,128)S(1)}, f32[2,256]{1,0:T(2,128)S(1)}, u32[]{:S(2)}, u32[]{:S(2)}) collective-permute-start(f32[2,256]{1,0:T(2,128)S(1)} %get-tuple-element.29), channel_id=1, source_target_pairs={{0,12},{1,8},{2,4},{3,0},{4,13},{5,9},{6,5},{7,1},{8,14},{9,10},{1... | collective-permute-start | bytes 6152 | tf_op jit(solution)/shard_map/ppermute | solution.py:239
  19.5 0.0 collective-permute-done.5.refs_5_
  19.5 0.0 collective-permute-start.1
  19.5 0.0 collective-permute-done.6.refs_6_
  19.5 1.1 %collective-permute-start.11 = (bf16[1,256,1024]{2,1,0:T(8,128)(2,1)S(1)}, bf16[1,256,1024]{2,1,0:T(8,128)(2,1)S(1)}, u32[]{:S(2)}, u32[]{:S(2)}) collective-permute-start(bf16[1,256,1024]{2,1,0:T(8,128)(2,1)S(1)} %get-tuple-element.43), channel_id=1, source_target_pairs={{0,2},{1,3},{2,0},{3,1},{4,6},{5,7},{6,4},{7,5},{8,10},{9,11},{10,... | collective-permute-start | bytes 1572872 | tf_op jit(solution)/shard_map/ppermute | solution.py:237
  20.6 0.2 collective-permute-done.7.refs_7_
  20.8 0.0 copy-done.4
  20.8 0.0 collective-permute-start.8
  20.9 0.0 collective-permute-done.9.refs_10_
  20.9 0.0 copy-done.1
  20.9 0.5 collective-permute-start
  21.4 0.8 %collective-permute-done.8.refs_9_ = bf16[256,256]{1,0:T(8,128)(2,1)S(1)} collective-permute-done((bf16[256,256]{1,0:T(8,128)(2,1)S(1)}, bf16[256,256]{1,0:T(8,128)(2,1)S(1)}, u32[]{:S(2)}, u32[]{:S(2)}) %collective-permute-start.8) | collective-permute-done | bytes 131104 | tf_op jit(solution)/shard_map/ppermute | solution.py:237
  22.2 0.8 %collective-permute-start.2 = (bf16[2,256,256]{2,1,0:T(8,128)(2,1)S(1)}, bf16[2,256,256]{2,1,0:T(8,128)(2,1)S(1)}, u32[]{:S(2)}, u32[]{:S(2)}) collective-permute-start(bf16[2,256,256]{2,1,0:T(8,128)(2,1)S(1)} %get-tuple-element.24), channel_id=1, source_target_pairs={{0,2},{1,3},{2,0},{3,1},{4,6},{5,7},{6,4},{7,5},{8,10},{9,11},{10,... | collective-permute-start | bytes 786440 | tf_op jit(solution)/shard_map/ppermute | solution.py:237
  23.0 0.0 collective-permute-done.1.refs_1_
  23.0 0.7 %collective-permute-start.3 = (bf16[2,256,256]{2,1,0:T(8,128)(2,1)S(1)}, bf16[2,256,256]{2,1,0:T(8,128)(2,1)S(1)}, u32[]{:S(2)}, u32[]{:S(2)}) collective-permute-start(bf16[2,256,256]{2,1,0:T(8,128)(2,1)S(1)} %get-tuple-element.25), channel_id=1, source_target_pairs={{0,3},{1,2},{2,1},{3,0},{4,7},{5,6},{6,5},{7,4},{8,11},{9,10},{10,... | collective-permute-start | bytes 786440 | tf_op jit(solution)/shard_map/ppermute | solution.py:237
  23.7 16.3 %collective-permute-done.2.refs_2_ = bf16[2,256,256]{2,1,0:T(8,128)(2,1)S(1)} collective-permute-done((bf16[2,256,256]{2,1,0:T(8,128)(2,1)S(1)}, bf16[2,256,256]{2,1,0:T(8,128)(2,1)S(1)}, u32[]{:S(2)}, u32[]{:S(2)}) %collective-permute-start.2) | collective-permute-done | bytes 262176 | tf_op jit(solution)/shard_map/ppermute | solution.py:237
  40.0 0.0 collective-permute-start.10
  40.0 0.0 collective-permute-done.13.refs_0_
  40.0 0.5 collective-permute-start.14
  40.5 0.0 collective-permute-done.11.refs_0_
  40.5 0.1 collective-permute-start.12
  40.5 4.1 %collective-permute-done.3.refs_3_ = bf16[2,256,256]{2,1,0:T(8,128)(2,1)S(1)} collective-permute-done((bf16[2,256,256]{2,1,0:T(8,128)(2,1)S(1)}, bf16[2,256,256]{2,1,0:T(8,128)(2,1)S(1)}, u32[]{:S(2)}, u32[]{:S(2)}) %collective-permute-start.3) | collective-permute-done | bytes 262176 | tf_op jit(solution)/shard_map/ppermute | solution.py:237
  44.7 0.0 collective-permute-done.10.refs_11_
  44.7 9.1 %green.1.refs_2_ = bf16[1024,512]{1,0:T(8,128)(2,1)S(1)} custom-call(bf16[2,256,256]{2,1,0:T(8,128)(2,1)S(1)} %get-tuple-element.22.refs_0_, bf16[2,256,256]{2,1,0:T(8,128)(2,1)S(1)} %collective-permute-done.1.refs_1_, bf16[2,256,256]{2,1,0:T(8,128)(2,1)S(1)} %collective-permute-done.2.refs_2_, bf16[2,256,256]{2,1,0:T(8,128)(2,1)S(1)} %collective-permute-done.3.refs_3_, ...), custom_call_target="tpu_custom_call" | custom-call | flops 5100273664 | bytes 3145728 | tf_op jit(solution)/shard_map/green/pallas_call | solution.py:138
  53.8 0.0 collective-permute-done.14.refs_1_
  53.8 1.0 %contract.5 = (f32[8,128]{1,0:T(8,128)S(1)}, f32[8,128]{1,0:T(8,128)S(1)}) custom-call(bf16[1,256,1024]{2,1,0:T(8,128)(2,1)S(1)} %collective-permute-done.13.refs_0_, bf16[1,256,1024]{2,1,0:T(8,128)(2,1)S(1)} %collective-permute-done.14.refs_1_, bf16[1024,512]{1,0:T(8,128)(2,1)S(1)} %green.1.refs_2_), custom_call_target="tpu_custom_call" | custom-call | flops 536870912 | bytes 2097152 | tf_op jit(solution)/shard_map/contract/pallas_call | solution.py:180
  54.8 0.0 collective-permute-done.12.refs_1_
  54.8 1.0 %contract.4 = (f32[8,128]{1,0:T(8,128)S(1)}, f32[8,128]{1,0:T(8,128)S(1)}) custom-call(bf16[1,256,1024]{2,1,0:T(8,128)(2,1)S(1)} %collective-permute-done.11.refs_0_, bf16[1,256,1024]{2,1,0:T(8,128)(2,1)S(1)} %collective-permute-done.12.refs_1_, bf16[1024,512]{1,0:T(8,128)(2,1)S(1)} %green.1.refs_2_), custom_call_target="tpu_custom_call" | custom-call | flops 536870912 | bytes 2097152 | tf_op jit(solution)/shard_map/contract/pallas_call | solution.py:180
  55.8 0.0 collective-permute-done.refs_1_
  55.8 1.5 %contract.3 = (f32[8,128]{1,0:T(8,128)S(1)}, f32[8,128]{1,0:T(8,128)S(1)}) custom-call(bf16[2,256,1024]{2,1,0:T(8,128)(2,1)S(1)} %copy-done.1, bf16[2,256,1024]{2,1,0:T(8,128)(2,1)S(1)} %collective-permute-done.refs_1_, bf16[1024,512]{1,0:T(8,128)(2,1)S(1)} %green.1.refs_2_), custom_call_target="tpu_custom_call" | custom-call | flops 1073741824 | bytes 3145728 | tf_op jit(solution)/shard_map/contract/pallas_call | solution.py:180
  57.4 0.7 collective-permute-start.15
  58.0 1.6 %collective-permute-start.16 = (f32[8,128]{1,0:T(8,128)S(1)}, f32[8,128]{1,0:T(8,128)S(1)}, u32[]{:S(2)}, u32[]{:S(2)}) collective-permute-start(f32[8,128]{1,0:T(8,128)S(1)} %get-tuple-element.37), channel_id=1, source_target_pairs={{0,1},{1,5},{2,9},{3,13},{4,0},{5,4},{6,8},{7,12},{8,3},{9,7},{10,... | collective-permute-start | bytes 12296 | tf_op jit(solution)/shard_map/ppermute | solution.py:240
  59.6 2.6 %collective-permute-start.17 = (f32[8,128]{1,0:T(8,128)S(1)}, f32[8,128]{1,0:T(8,128)S(1)}, u32[]{:S(2)}, u32[]{:S(2)}) collective-permute-start(f32[8,128]{1,0:T(8,128)S(1)} %get-tuple-element.38), channel_id=1, source_target_pairs={{0,2},{1,6},{2,10},{3,14},{4,3},{5,7},{6,11},{7,15},{8,0},{9,4},{1... | collective-permute-start | bytes 12296 | tf_op jit(solution)/shard_map/ppermute | solution.py:240
  62.3 0.5 collective-permute-start.18
  63.4 0.0 collective-permute-done.15.refs_0_
  63.5 0.0 collective-permute-done.16.refs_1_
  63.5 3.0 %collective-permute-done.17.refs_2_ = f32[8,128]{1,0:T(8,128)S(1)} collective-permute-done((f32[8,128]{1,0:T(8,128)S(1)}, f32[8,128]{1,0:T(8,128)S(1)}, u32[]{:S(2)}, u32[]{:S(2)}) %collective-permute-start.17) | collective-permute-done | bytes 4128 | tf_op jit(solution)/shard_map/ppermute | solution.py:240
  66.4 1.3 %collective-permute-done.18.refs_3_ = f32[8,128]{1,0:T(8,128)S(1)} collective-permute-done((f32[8,128]{1,0:T(8,128)S(1)}, f32[8,128]{1,0:T(8,128)S(1)}, u32[]{:S(2)}, u32[]{:S(2)}) %collective-permute-start.18) | collective-permute-done | bytes 4128 | tf_op jit(solution)/shard_map/ppermute | solution.py:240
  67.7 1.6 %unpack.1 = (f32[2,8]{1,0:T(2,128)}, f32[2,8]{1,0:T(2,128)}) custom-call(s32[32]{0:T(128)S(1)} %copy-done.3, s32[1]{0:T(128)S(6)} %copy.8.counts, f32[8,128]{1,0:T(8,128)S(1)} %collective-permute-done.15.refs_0_, f32[8,128]{1,0:T(8,128)S(1)} %collective-permute-done.16.refs_1_, f32[8,128]{1,0:T(8,128)S(1)} %collective-permute-done.17.refs_2_, ...), custom_call_target="tpu_custom_call" | custom-call | tf_op jit(solution)/shard_map/unpack/pallas_call | solution.py:221
  (1 shorter events, 0.0 us)
Async XLA Ops:
  0.6 4.5 %copy-start.2 = (f32[8,256]{1,0:T(8,128)S(1)}, f32[8,256]{1,0:T(8,128)}, u32[]{:S(2)}) copy-start(f32[8,256]{1,0:T(8,128)} %field.1) | copy-start | bytes 24580
  0.6 4.5 %copy-start = (bf16[8,256,256]{2,1,0:T(8,128)(2,1)S(1)}, bf16[8,256,256]{2,1,0:T(8,128)(2,1)}, u32[]{:S(2)}) copy-start(bf16[8,256,256]{2,1,0:T(8,128)(2,1)} %walkers.1) | copy-start | bytes 3145732
  0.7 20.2 %collective-permute-start.9 = (bf16[256,256]{1,0:T(8,128)(2,1)}, bf16[256,256]{1,0:T(8,128)(2,1)S(1)}, u32[]{:S(2)}, u32[]{:S(2)}) collective-permute-start(bf16[256,256]{1,0:T(8,128)(2,1)} %refs_8_.1), channel_id=1, source_target_pairs={{0,2},{1,3},{2,0},{3,1},{4,6},{5,7},{6,4},{7,5},{8,10},{9,11},{10,... | collective-permute-start | bytes 393224 | tf_op jit(solution)/shard_map/ppermute | solution.py:237
  3.7 1.5 %copy-start.3 = (s32[32]{0:T(128)S(1)}, s32[32]{0:T(128)}, u32[]{:S(2)}) copy-start(s32[32]{0:T(128)} %branches.3) | copy-start | bytes 388
  3.7 17.2 %copy-start.4 = (bf16[256,256]{1,0:T(8,128)(2,1)S(1)}, bf16[256,256]{1,0:T(8,128)(2,1)}, u32[]{:S(2)}) copy-start(bf16[256,256]{1,0:T(8,128)(2,1)} %refs_8_.1) | copy-start | bytes 393220
  5.0 15.9 %copy-start.1 = (bf16[2,256,1024]{2,1,0:T(8,128)(2,1)S(1)}, bf16[2,256,1024]{2,1,0:T(8,128)(2,1)}, u32[]{:S(2)}) copy-start(bf16[2,256,1024]{2,1,0:T(8,128)(2,1)} %refs_0_.1) | copy-start | bytes 3145732
  5.0 35.0 %collective-permute-start.13 = (bf16[1,256,1024]{2,1,0:T(8,128)(2,1)S(1)}, bf16[1,256,1024]{2,1,0:T(8,128)(2,1)S(1)}, u32[]{:S(2)}, u32[]{:S(2)}) collective-permute-start(bf16[1,256,1024]{2,1,0:T(8,128)(2,1)S(1)} %get-tuple-element.42), channel_id=1, source_target_pairs={{0,2},{1,3},{2,0},{3,1},{4,6},{5,7},{6,4},{7,5},{8,10},{9,11},{10,... | collective-permute-start | bytes 1572872 | tf_op jit(solution)/shard_map/ppermute | solution.py:237
  7.9 6.8 %collective-permute-start.4 = (f32[2,256]{1,0:T(2,128)S(1)}, f32[2,256]{1,0:T(2,128)S(1)}, u32[]{:S(2)}, u32[]{:S(2)}) collective-permute-start(f32[2,256]{1,0:T(2,128)S(1)} %get-tuple-element.26), channel_id=1, source_target_pairs={{0,0},{1,4},{2,8},{3,12},{4,1},{5,5},{6,9},{7,13},{8,2},{9,6},{10,... | collective-permute-start | bytes 6152 | tf_op jit(solution)/shard_map/ppermute | solution.py:239
  8.5 11.0 %collective-permute-start.5 = (f32[2,256]{1,0:T(2,128)S(1)}, f32[2,256]{1,0:T(2,128)S(1)}, u32[]{:S(2)}, u32[]{:S(2)}) collective-permute-start(f32[2,256]{1,0:T(2,128)S(1)} %get-tuple-element.27), channel_id=1, source_target_pairs={{0,4},{1,0},{2,12},{3,8},{4,5},{5,1},{6,13},{7,9},{8,6},{9,2},{10,... | collective-permute-start | bytes 6152 | tf_op jit(solution)/shard_map/ppermute | solution.py:239
  11.9 7.6 %collective-permute-start.6 = (f32[2,256]{1,0:T(2,128)S(1)}, f32[2,256]{1,0:T(2,128)S(1)}, u32[]{:S(2)}, u32[]{:S(2)}) collective-permute-start(f32[2,256]{1,0:T(2,128)S(1)} %get-tuple-element.28), channel_id=1, source_target_pairs={{0,8},{1,12},{2,0},{3,4},{4,9},{5,13},{6,1},{7,5},{8,10},{9,14},{1... | collective-permute-start | bytes 6152 | tf_op jit(solution)/shard_map/ppermute | solution.py:239
  14.7 6.1 %collective-permute-start.7 = (f32[2,256]{1,0:T(2,128)S(1)}, f32[2,256]{1,0:T(2,128)S(1)}, u32[]{:S(2)}, u32[]{:S(2)}) collective-permute-start(f32[2,256]{1,0:T(2,128)S(1)} %get-tuple-element.29), channel_id=1, source_target_pairs={{0,12},{1,8},{2,4},{3,0},{4,13},{5,9},{6,5},{7,1},{8,14},{9,10},{1... | collective-permute-start | bytes 6152 | tf_op jit(solution)/shard_map/ppermute | solution.py:239
  19.5 3.5 %collective-permute-start.1 = (bf16[2,256,256]{2,1,0:T(8,128)(2,1)S(1)}, bf16[2,256,256]{2,1,0:T(8,128)(2,1)S(1)}, u32[]{:S(2)}, u32[]{:S(2)}) collective-permute-start(bf16[2,256,256]{2,1,0:T(8,128)(2,1)S(1)} %get-tuple-element.23), channel_id=1, source_target_pairs={{0,1},{1,0},{2,3},{3,2},{4,5},{5,4},{6,7},{7,6},{8,9},{9,8},{10,11... | collective-permute-start | bytes 786440 | tf_op jit(solution)/shard_map/ppermute | solution.py:237
  19.5 20.9 %collective-permute-start.11 = (bf16[1,256,1024]{2,1,0:T(8,128)(2,1)S(1)}, bf16[1,256,1024]{2,1,0:T(8,128)(2,1)S(1)}, u32[]{:S(2)}, u32[]{:S(2)}) collective-permute-start(bf16[1,256,1024]{2,1,0:T(8,128)(2,1)S(1)} %get-tuple-element.43), channel_id=1, source_target_pairs={{0,2},{1,3},{2,0},{3,1},{4,6},{5,7},{6,4},{7,5},{8,10},{9,11},{10,... | collective-permute-start | bytes 1572872 | tf_op jit(solution)/shard_map/ppermute | solution.py:237
  20.8 1.3 %collective-permute-start.8 = (bf16[256,256]{1,0:T(8,128)(2,1)S(1)}, bf16[256,256]{1,0:T(8,128)(2,1)S(1)}, u32[]{:S(2)}, u32[]{:S(2)}) collective-permute-start(bf16[256,256]{1,0:T(8,128)(2,1)S(1)} %copy-done.4), channel_id=1, source_target_pairs={{0,1},{1,0},{2,3},{3,2},{4,5},{5,4},{6,7},{7,6},{8,9},{9,8},{10,11... | collective-permute-start | bytes 393224 | tf_op jit(solution)/shard_map/ppermute | solution.py:237
  20.9 34.9 %collective-permute-start = (bf16[2,256,1024]{2,1,0:T(8,128)(2,1)S(1)}, bf16[2,256,1024]{2,1,0:T(8,128)(2,1)S(1)}, u32[]{:S(2)}, u32[]{:S(2)}) collective-permute-start(bf16[2,256,1024]{2,1,0:T(8,128)(2,1)S(1)} %copy-done.1), channel_id=1, source_target_pairs={{0,1},{1,0},{2,3},{3,2},{4,5},{5,4},{6,7},{7,6},{8,9},{9,8},{10,11... | collective-permute-start | bytes 3145736 | tf_op jit(solution)/shard_map/ppermute | solution.py:237
  22.2 17.8 %collective-permute-start.2 = (bf16[2,256,256]{2,1,0:T(8,128)(2,1)S(1)}, bf16[2,256,256]{2,1,0:T(8,128)(2,1)S(1)}, u32[]{:S(2)}, u32[]{:S(2)}) collective-permute-start(bf16[2,256,256]{2,1,0:T(8,128)(2,1)S(1)} %get-tuple-element.24), channel_id=1, source_target_pairs={{0,2},{1,3},{2,0},{3,1},{4,6},{5,7},{6,4},{7,5},{8,10},{9,11},{10,... | collective-permute-start | bytes 786440 | tf_op jit(solution)/shard_map/ppermute | solution.py:237
  23.0 21.7 %collective-permute-start.3 = (bf16[2,256,256]{2,1,0:T(8,128)(2,1)S(1)}, bf16[2,256,256]{2,1,0:T(8,128)(2,1)S(1)}, u32[]{:S(2)}, u32[]{:S(2)}) collective-permute-start(bf16[2,256,256]{2,1,0:T(8,128)(2,1)S(1)} %get-tuple-element.25), channel_id=1, source_target_pairs={{0,3},{1,2},{2,1},{3,0},{4,7},{5,6},{6,5},{7,4},{8,11},{9,10},{10,... | collective-permute-start | bytes 786440 | tf_op jit(solution)/shard_map/ppermute | solution.py:237
  40.0 4.7 %collective-permute-start.10 = (bf16[256,256]{1,0:T(8,128)(2,1)S(1)}, bf16[256,256]{1,0:T(8,128)(2,1)S(1)}, u32[]{:S(2)}, u32[]{:S(2)}) collective-permute-start(bf16[256,256]{1,0:T(8,128)(2,1)S(1)} %collective-permute-done.9.refs_10_), channel_id=1, source_target_pairs={{0,1},{1,0},{2,3},{3,2},{4,5},{5,4},{6,7},{7,6},{8,9},{9,8},{10,11... | collective-permute-start | bytes 393224 | tf_op jit(solution)/shard_map/ppermute | solution.py:237
  40.0 13.8 %collective-permute-start.14 = (bf16[1,256,1024]{2,1,0:T(8,128)(2,1)S(1)}, bf16[1,256,1024]{2,1,0:T(8,128)(2,1)S(1)}, u32[]{:S(2)}, u32[]{:S(2)}) collective-permute-start(bf16[1,256,1024]{2,1,0:T(8,128)(2,1)S(1)} %collective-permute-done.13.refs_0_), channel_id=1, source_target_pairs={{0,1},{1,0},{2,3},{3,2},{4,5},{5,4},{6,7},{7,6},{8,9},{9,8},{10,11... | collective-permute-start | bytes 1572872 | tf_op jit(solution)/shard_map/ppermute | solution.py:237
  40.5 14.3 %collective-permute-start.12 = (bf16[1,256,1024]{2,1,0:T(8,128)(2,1)S(1)}, bf16[1,256,1024]{2,1,0:T(8,128)(2,1)S(1)}, u32[]{:S(2)}, u32[]{:S(2)}) collective-permute-start(bf16[1,256,1024]{2,1,0:T(8,128)(2,1)S(1)} %collective-permute-done.11.refs_0_), channel_id=1, source_target_pairs={{0,1},{1,0},{2,3},{3,2},{4,5},{5,4},{6,7},{7,6},{8,9},{9,8},{10,11... | collective-permute-start | bytes 1572872 | tf_op jit(solution)/shard_map/ppermute | solution.py:237
  57.4 6.1 %collective-permute-start.15 = (f32[8,128]{1,0:T(8,128)S(1)}, f32[8,128]{1,0:T(8,128)S(1)}, u32[]{:S(2)}, u32[]{:S(2)}) collective-permute-start(f32[8,128]{1,0:T(8,128)S(1)} %get-tuple-element.36), channel_id=1, source_target_pairs={{0,0},{1,4},{2,8},{3,12},{4,1},{5,5},{6,9},{7,13},{8,2},{9,6},{10,... | collective-permute-start | bytes 12296 | tf_op jit(solution)/shard_map/ppermute | solution.py:240
  58.0 5.4 %collective-permute-start.16 = (f32[8,128]{1,0:T(8,128)S(1)}, f32[8,128]{1,0:T(8,128)S(1)}, u32[]{:S(2)}, u32[]{:S(2)}) collective-permute-start(f32[8,128]{1,0:T(8,128)S(1)} %get-tuple-element.37), channel_id=1, source_target_pairs={{0,1},{1,5},{2,9},{3,13},{4,0},{5,4},{6,8},{7,12},{8,3},{9,7},{10,... | collective-permute-start | bytes 12296 | tf_op jit(solution)/shard_map/ppermute | solution.py:240
  59.6 6.8 %collective-permute-start.17 = (f32[8,128]{1,0:T(8,128)S(1)}, f32[8,128]{1,0:T(8,128)S(1)}, u32[]{:S(2)}, u32[]{:S(2)}) collective-permute-start(f32[8,128]{1,0:T(8,128)S(1)} %get-tuple-element.38), channel_id=1, source_target_pairs={{0,2},{1,6},{2,10},{3,14},{4,3},{5,7},{6,11},{7,15},{8,0},{9,4},{1... | collective-permute-start | bytes 12296 | tf_op jit(solution)/shard_map/ppermute | solution.py:240
  62.3 5.4 %collective-permute-start.18 = (f32[8,128]{1,0:T(8,128)S(1)}, f32[8,128]{1,0:T(8,128)S(1)}, u32[]{:S(2)}, u32[]{:S(2)}) collective-permute-start(f32[8,128]{1,0:T(8,128)S(1)} %get-tuple-element.39), channel_id=1, source_target_pairs={{0,3},{1,7},{2,11},{3,15},{4,2},{5,6},{6,10},{7,14},{8,1},{9,5},{1... | collective-permute-start | bytes 12296 | tf_op jit(solution)/shard_map/ppermute | solution.py:240

commit v2 on v1

v2 whole, which is shorter than its diff:
```python
import functools

import jax
import jax.numpy as jnp
from jax import lax
from jax.experimental import pallas as pl
from jax.experimental.pallas import tpu as pltpu
from jax.sharding import PartitionSpec as P

ITERS = 10
SR = ("slab", "row")
ALL = ("walk", "slab", "row")
F32 = jnp.float32
BF16 = jnp.bfloat16
VMEM_LIMIT = 24 * 2**20
SMALL_LIMIT = 2**20
HIGHEST = lax.Precision.HIGHEST


def dot(a, b, dims=((1,), (0,))):
    return lax.dot_general(a, b, (dims, ((), ())), preferred_element_type=F32)


def split(x):
    high = x.astype(BF16)
    return high, (x - high.astype(F32)).astype(BF16)


def place():
    return lax.axis_index("walk"), lax.axis_index("slab") * lax.axis_size("row") + lax.axis_index("row")


def whole(memory=pltpu.VMEM):
    return pl.BlockSpec(memory_space=memory)


def picks(branches, start, per, sender, share):
    places, olds = [jnp.int32(0)] * share, [jnp.int32(0)] * share
    rank = jnp.int32(0)
    for i in range(per):
        branch = branches[start + i]
        hit = lax.div(branch, per) == sender
        old = lax.rem(branch, per)
        for r in range(share):
            here = hit & (rank == r)
            places[r] = jnp.where(here, i, places[r])
            olds[r] = jnp.where(here, old, olds[r])
        rank = rank + hit.astype(jnp.int32)
    return places, olds


def select_kernel(n, per, share, branches, walkers, cholesky, *refs):
    sends, direct, shared, sems, more = refs[:n], refs[n], refs[n + 1], refs[n + 2], refs[n + 3]
    walk, q = place()
    split_at, half = direct.shape[0], shared.shape[1]
    rows = pl.ds(pl.multiple_of((walk & 1) * half, half), half)
    copies = []
    for k in range(1, n):
        olds = picks(branches, (q ^ k ^ walk) * per, per, walk, share)[1]
        for r in range(share):
            copies.append(pltpu.make_async_copy(walkers.at[olds[r]], sends[k].at[r], sems.at[k, r]))
            copies[-1].start()
    copies.append(pltpu.make_async_copy(cholesky.at[pl.ds(split_at, shared.shape[0]), rows, :], shared, more.at[0]))
    copies[-1].start()
    copies.append(pltpu.make_async_copy(cholesky.at[pl.ds(0, split_at)], direct, more.at[1]))
    copies[-1].start()
    olds = picks(branches, (q ^ walk) * per, per, walk, share)[1]
    for r in range(share):
        copies.append(pltpu.make_async_copy(walkers.at[olds[r]], sends[0].at[r], sems.at[0, r]))
        copies[-1].start()
    for copy in copies:
        copy.wait()


def select(n, per, share, branches, walkers, cholesky):
    rows, electrons = walkers.shape[1:]
    vectors, height, width = cholesky.shape
    later = vectors // 2
    return pl.pallas_call(
        functools.partial(select_kernel, n, per, share),
        out_shape=[jax.ShapeDtypeStruct((share, rows, electrons), walkers.dtype)] * n
        + [
            jax.ShapeDtypeStruct((vectors - later, height, width), cholesky.dtype),
            jax.ShapeDtypeStruct((later, height // 2, width), cholesky.dtype),
        ],
        in_specs=[whole(pltpu.SMEM), whole(pl.ANY), whole(pl.ANY)],
        out_specs=[whole(pl.ANY)] * (n + 2),
        scratch_shapes=[pltpu.SemaphoreType.DMA((n, share)), pltpu.SemaphoreType.DMA((2,))],
        compiler_params=pltpu.CompilerParams(vmem_limit_bytes=SMALL_LIMIT),
        cost_estimate=pl.CostEstimate(flops=0, bytes_accessed=4 * walkers.size, transcendentals=0),
        name="select",
    )(branches, walkers, cholesky)


def message_kernel(trial, field, out):
    rows = trial.shape[0]
    out[:rows, :] = trial[...]
    rest, terms = field[...], []
    for _ in range(3):
        terms.append(rest.astype(BF16).astype(F32))
        rest = rest - terms[-1]
    spare = out.shape[0] - rows - 3 * field.shape[0]
    if spare:
        terms.append(jnp.zeros((spare, field.shape[1]), F32))
    out[rows:, :] = jnp.concatenate(terms, axis=0).astype(BF16)


def message(trial, field):
    height = trial.shape[0] + -(-3 * field.shape[0] // 16) * 16
    return pl.pallas_call(
        message_kernel,
        out_shape=jax.ShapeDtypeStruct((height, trial.shape[1]), trial.dtype),
        in_specs=[whole()] * 2,
        out_specs=whole(),
        compiler_params=pltpu.CompilerParams(vmem_limit_bytes=SMALL_LIMIT),
        name="message",
    )(trial, field)


def fields_kernel(n, per, share, branches, *refs):
    messages, fields = refs[:n], refs[n]
    walk, q = place()
    rows = fields.shape[2]
    places = picks(branches, walk * per, per, q, share)[0]
    walker = lax.broadcasted_iota(jnp.int32, (per, rows), 0)
    for k in range(n):
        terms = messages[k][rows:, :].astype(F32)
        value = terms[:per] + terms[per : 2 * per] + terms[2 * per : 3 * per]
        chosen = [jnp.sum(jnp.where(walker == p, value, 0.0), axis=0, keepdims=True) for p in places]
        fields[pl.ds(q ^ k, 1), :, :] = jnp.concatenate(chosen, axis=0)[None]


def pick_fields(n, per, share, branches, messages):
    return pl.pallas_call(
        functools.partial(fields_kernel, n, per, share),
        out_shape=jax.ShapeDtypeStruct((n, share, messages[0].shape[1]), F32),
        in_specs=[whole(pltpu.SMEM)] + [whole()] * n,
        out_specs=whole(),
        compiler_params=pltpu.CompilerParams(vmem_limit_bytes=SMALL_LIMIT),
        name="fields",
    )(branches, *messages)


def green_kernel(n, share, *refs):
    blocks, messages, fields = refs[:n], refs[n : 2 * n], refs[2 * n]
    green, moved, state = refs[2 * n + 1 :]
    walk, q = place()
    rows, electrons = blocks[0].shape[1:]
    spare = jnp.zeros((-share % 8, rows), F32)
    columns = []
    for k in range(n):
        lines = fields[pl.ds(q ^ k, 1), :, :].reshape(share, rows)
        columns.append((jnp.concatenate([lines, spare], axis=0) if share % 8 else lines).T)
    for i in range(share):
        transposed = jnp.zeros((electrons, electrons), F32)
        for k in range(n):
            part = (blocks[k][i].astype(F32) * columns[k][:, i : i + 1]).astype(BF16)
            moved[i, k * rows : (k + 1) * rows, :] = part
            transposed = transposed + dot(part, messages[k][:rows, :], ((0,), (0,)))
        size = jnp.abs(transposed)
        scale = jnp.max(jnp.sum(size, axis=0)) * jnp.max(jnp.sum(size, axis=1))
        start = transposed / scale
        high, low = split(transposed)
        start_high, start_low = split(start)
        across = ((0,), (0,))
        state[i, :electrons, :] = start
        state[i, electrons:, :] = dot(high, start_high, across) + (
            dot(high, start_low, across) + dot(low, start_high, across)
        )

    def advance(step, carry):
        for i in range(share):
            now = state[i]
            high, low = split(now)
            right_high, right_low = high[electrons:], low[electrons:]
            product = dot(high, right_high) + (dot(high, right_low) + dot(low, right_high))
            state[i] = 2.0 * now - product
        return carry

    lax.fori_loop(0, ITERS - 1, advance, 0)
    for i in range(share):
        now = state[i]
        high, low = split(now)
        left_high, left_low = high[:electrons], low[:electrons]
        right_high, right_low = high[electrons:], low[electrons:]
        product = dot(left_high, right_high) + (dot(left_high, right_low) + dot(left_low, right_high))
        inverse = (2.0 * now[:electrons] - product).astype(BF16)
        for k in range(n):
            at = pl.multiple_of((q ^ k) * rows, rows)
            green[pl.ds(at, rows), i * electrons : (i + 1) * electrons] = dot(
                moved[i, k * rows : (k + 1) * rows, :], inverse
            ).astype(BF16)


def make_green(n, share, blocks, messages, fields):
    rows, electrons = blocks[0].shape[1:]
    flops = share * (8 * rows * n * electrons**2 + 2 * 6 * ITERS * electrons**3)
    return pl.pallas_call(
        functools.partial(green_kernel, n, share),
        out_shape=jax.ShapeDtypeStruct((n * rows, share * electrons), BF16),
        in_specs=[whole()] * (2 * n + 1),
        out_specs=whole(),
        scratch_shapes=[
            pltpu.VMEM((share, n * rows, electrons), BF16),
            pltpu.VMEM((share, 2 * electrons, electrons), F32),
        ],
        compiler_params=pltpu.CompilerParams(vmem_limit_bytes=VMEM_LIMIT),
        cost_estimate=pl.CostEstimate(flops=flops, bytes_accessed=3 * 2**20, transcendentals=0),
        name="green",
    )(*blocks, *messages, fields)


def contract_kernel(share, first, pieces, count, going_on, *refs):
    vectors, green = refs[: pieces * count], refs[pieces * count]
    before = refs[pieces * count + 1 :][: count if going_on else 0]
    outs, both = refs[-1 - count : -1], refs[-1]
    electrons = both.shape[0]
    half = electrons // 2
    parity = lax.axis_index("walk") & 1
    row = lax.broadcasted_iota(jnp.int32, (half, half), 0)
    column = lax.broadcasted_iota(jnp.int32, (half, half), 1)
    out_row = lax.broadcasted_iota(jnp.int32, (8, 128), 0)
    lane = lax.broadcasted_iota(jnp.int32, (8, 128), 1)
    for v in range(count):
        held = before[v][...] if going_on else jnp.zeros((8, 128), F32)
        mine = vectors[v * pieces : (v + 1) * pieces]
        for g in range(mine[0].shape[0]):
            if pieces == 1:
                full = dot(mine[0][g], green[...])
                upper, lower = full[:half], full[half:]
            else:
                for at, piece in zip((parity, 1 - parity), mine):
                    both[pl.ds(pl.multiple_of(at * half, half), half), :] = dot(piece[g], green[...])
                upper, lower = both[:half], both[half:]
            for i in range(share):
                left, middle, right = i * electrons, i * electrons + half, (i + 1) * electrons
                a, b = upper[:, left:middle], upper[:, middle:right]
                c, d = lower[:, left:middle], lower[:, middle:right]
                trace = jnp.sum(jnp.where(row == column, a + d, 0.0))
                exchange = -0.5 * jnp.sum(a * a.T + d * d.T + 2.0 * (b * c.T))
                here = out_row == (first + g) * share + i
                held = jnp.where(here & (lane == 0), trace, held)
                held = jnp.where(here & (lane == 1), exchange, held)
        outs[v][...] = held


def contract(share, first, groups, green, before=(), after=()):
    vectors = [v for group in groups for v in group]
    electrons = green.shape[1] // share
    return pl.pallas_call(
        functools.partial(contract_kernel, share, first, len(groups[0]), len(groups), bool(before)),
        out_shape=[jax.ShapeDtypeStruct((8, 128), F32)] * len(groups),
        in_specs=[whole()] * (len(vectors) + 1 + len(before)) + [whole(pl.ANY)] * len(after),
        out_specs=[whole()] * len(groups),
        scratch_shapes=[pltpu.VMEM((electrons, green.shape[1]), F32)],
        compiler_params=pltpu.CompilerParams(vmem_limit_bytes=VMEM_LIMIT),
        cost_estimate=pl.CostEstimate(
            flops=sum(2 * v.size * green.shape[1] for v in vectors),
            bytes_accessed=sum(2 * v.size for v in vectors) + 2 * green.size,
            transcendentals=0,
        ),
        name="contract",
    )(*vectors, green, *before, *after)


def unpack_kernel(n, per, share, branches, counts, *refs):
    arrived, force, exchange = refs[:n], refs[n], refs[n + 1]
    walk, q = place()
    vectors = force.shape[0]
    walker = lax.broadcasted_iota(jnp.int32, force.shape, 1)
    vector = lax.broadcasted_iota(jnp.int32, force.shape, 0)
    force_all = jnp.zeros(force.shape, F32)
    exchange_all = jnp.zeros(force.shape, F32)
    for k in range(n):
        places = picks(branches, walk * per, per, walk ^ q ^ k, share)[0]
        for r in range(share):
            for g in range(vectors):
                here = (walker == places[r]) & (vector == g)
                force_all = jnp.where(here, arrived[k][g * share + r, 0], force_all)
                exchange_all = jnp.where(here, arrived[k][g * share + r, 1], exchange_all)
    living = (walker < counts[0]).astype(F32)
    force[...] = force_all * living
    exchange[...] = exchange_all * living


def unpack(n, per, share, vectors, branches, counts, arrived):
    return pl.pallas_call(
        functools.partial(unpack_kernel, n, per, share),
        out_shape=[jax.ShapeDtypeStruct((vectors, per), F32)] * 2,
        in_specs=[whole(pltpu.SMEM)] * (2 + n),
        out_specs=[whole()] * 2,
        compiler_params=pltpu.CompilerParams(vmem_limit_bytes=SMALL_LIMIT),
        name="unpack",
    )(branches, counts, *arrived)


def at_the_source(walkers, trial_orbitals, cholesky, branches, counts, field):
    n = lax.axis_size("walk")
    per = walkers.shape[0]
    share = per // n
    row_size = lax.axis_size("row")
    vectors = cholesky.shape[0]
    pairs = [(w, q) for w in range(n) for q in range(n)]
    move = lambda x, k: lax.ppermute(x, SR, [(i, i ^ k) for i in range(n)])
    swap = lambda x: lax.ppermute(x, "walk", [(w, w ^ 1) for w in range(n)])
    ask = lambda x: lax.ppermute(x, ALL, [(w * n + q, q * n + (w ^ q)) for w, q in pairs])
    answer = lambda x, k: lax.ppermute(x, ALL, [(w * n + q, (w ^ q) * n + (q ^ k)) for w, q in pairs])
    near = [k for k in range(n) if k < row_size]
    far = [k for k in range(n) if k >= row_size]

    def spread(x):
        held = {}
        for k in far:
            low = k & (row_size - 1)
            held[k] = move(held[k ^ low], low) if low else move(x, k)
        return held

    def along(held):
        return {k: move(held[k & ~(row_size - 1)], k & (row_size - 1)) if k & (row_size - 1) else held[k] for k in far}

    ordered = lambda x, *first: lax.optimization_barrier((x,) + first)[0]
    heads = [k for k in far if not k & (row_size - 1)]
    own = message(trial_orbitals, field)
    messages = {0: own, **spread(own)}
    messages.update({k: move(own, k) for k in near[1:]})
    messages = [messages[k] for k in range(n)]
    *sends, direct, shared = select(n, per, share, ordered(branches, own), walkers, cholesky)
    blocks = [sends[0]] + [move(sends[k], k) for k in range(1, n)]
    asked = ask(pick_fields(n, per, share, branches, messages))
    shared = ordered(shared, *messages[1 : far[0] + 1])
    crossed = {k: move(shared, k) for k in heads}
    direct = ordered(direct, *messages)
    direct = {k: move(direct, k) for k in heads}
    other = along({k: swap(x) for k, x in crossed.items()})
    crossed = along(crossed)
    close = [cholesky] + [move(ordered(cholesky, asked, *blocks), k) for k in near[1:]]
    green = make_green(n, share, blocks, messages, asked)
    direct = along({k: ordered(x, green) for k, x in direct.items()})
    results = contract(share, 0, [[x] for x in close], green)
    late = contract(share, vectors - vectors // 2, [[crossed[k], other[k]] for k in far], green, after=results[:1])
    late = contract(share, 0, [[direct[k]] for k in far], green, late)
    arrived = [answer(x, k) for k, x in enumerate(list(results) + list(late))]
    return tuple(x.T for x in unpack(n, per, share, vectors, branches, counts, arrived))


def newton_schulz(intersection):
    column_max = jnp.max(jnp.sum(jnp.abs(intersection), axis=0))
    row_max = jnp.max(jnp.sum(jnp.abs(intersection), axis=1))
    inverse = intersection.T / (column_max * row_max)
    twice_identity = 2.0 * jnp.eye(intersection.shape[0], dtype=intersection.dtype)
    for iteration in range(ITERS):
        inverse = jnp.dot(
            inverse,
            twice_identity - jnp.dot(intersection, inverse, precision=HIGHEST),
            precision=HIGHEST,
        )
    return inverse


def pick(array, indices):
    return jnp.concatenate(
        [lax.dynamic_slice_in_dim(array, indices[i], 1, 0) for i in range(indices.shape[0])], axis=0
    )


def at_the_target(walkers, trial_orbitals, cholesky, branches, counts, field):
    walk_size = lax.axis_size("walk")
    position = lax.axis_index("walk")
    per_device, row_count, electrons = walkers.shape
    capacity = (per_device + walk_size - 1) // walk_size
    sender = branches.reshape(walk_size, per_device) // per_device
    local_index = branches.reshape(walk_size, per_device) % per_device
    same_sender = sender[:, :, None] == sender[:, None, :]
    earlier = jnp.arange(per_device)[None, :] < jnp.arange(per_device)[:, None]
    arrival_rank = jnp.sum(same_sender & earlier[None], axis=2)
    wanted = (sender[:, None, :] == position) & (
        arrival_rank[:, None, :] == jnp.arange(capacity, dtype=jnp.int32)[None, :, None]
    )
    chosen = jnp.sum(jnp.where(wanted, local_index[:, None, :], 0), axis=2).reshape(-1)
    outgoing = pick(walkers, chosen).reshape(walk_size, capacity, row_count, electrons)
    arrived = lax.all_to_all(outgoing, "walk", split_axis=0, concat_axis=0, tiled=True)
    my_sender = lax.dynamic_index_in_dim(sender, position, 0, keepdims=False)
    my_rank = lax.dynamic_index_in_dim(arrival_rank, position, 0, keepdims=False)
    arrived_flat = arrived.reshape(walk_size * capacity, row_count, electrons)
    migrated = pick(arrived_flat, my_sender * capacity + my_rank)
    propagated = (migrated.astype(F32) * field[:, :, None]).astype(BF16)
    everything = lax.all_gather(propagated, SR, axis=1, tiled=True)
    shard_count = lax.axis_size(SR)
    share = per_device // shard_count
    trial_whole = lax.all_gather(trial_orbitals, SR, axis=0, tiled=True)
    own_walkers = lax.dynamic_slice_in_dim(everything, lax.axis_index(SR) * share, share, 0)
    intersection = jnp.einsum("mn,wmk->wnk", trial_whole, own_walkers, preferred_element_type=F32)
    inverse = jax.vmap(newton_schulz)(intersection).astype(BF16)
    inverses = lax.all_gather(inverse, SR, axis=0, tiled=True)
    green = jnp.einsum("wmn,wnk->wmk", everything, inverses, preferred_element_type=F32).astype(BF16)
    contracted = jnp.einsum("gnm,wmk->wgnk", cholesky, green, preferred_element_type=F32)
    living = (jnp.arange(per_device, dtype=jnp.int32) < counts[0]).astype(F32)[:, None]
    force_bias = jnp.trace(contracted, axis1=2, axis2=3) * living
    exchange_energy = -0.5 * jnp.einsum("wgnk,wgkn->wg", contracted, contracted) * living
    return (force_bias, exchange_energy)


def on_device(walkers, trial_orbitals, cholesky, branches, counts, field):
    walk_size, shard_count = lax.axis_size("walk"), lax.axis_size(SR)
    per = walkers.shape[0]
    if walk_size == shard_count and per % walk_size == 0 and not walk_size & (walk_size - 1):
        if 2 <= cholesky.shape[0] <= 8 // (per // walk_size):
            return at_the_source(walkers, trial_orbitals, cholesky, branches, counts, field)
    return at_the_target(walkers, trial_orbitals, cholesky, branches, counts, field)


def solution(mesh):
    return jax.shard_map(
        on_device,
        mesh=mesh,
        in_specs=(
            P(("parts", "walk"), SR, None),
            P(("parts",) + SR, None),
            P(("parts",) + SR, None, None),
            P("parts"),
            P(("parts", "walk")),
            P(("parts", "walk"), SR),
        ),
        out_specs=(P(("parts", "walk"), SR), P(("parts", "walk"), SR)),
        check_vma=False,
    )
```

time: 69.4 us -> 61.7 us (0.89)
  waiting for transfers between devices: 25.7 us -> 17.7 us
  starting transfers between devices: 23.9 us -> 20.5 us
  Pallas kernels: 16.9 us -> 19 us
  local copies, waits for them, and re-layouts: 1.33 us -> 2.82 us
    ppermute x19 -> x18, waiting for transfers between devices: 25.7 us -> 17.7 us  [the longest x12 14.8 us: at_the_source(): move = lambda x, k: lax.ppermute(x, SR, [(i, i ^ k) for i in range(n)])]
    ppermute x19 -> x18, starting transfers between devices: 23.9 us -> 20.5 us  [the longest x4 10.3 us: at_the_source(): lax.ppermute(x, ALL, [(w * n + q, (w ^ q) * n + (q ^ k)) for w, q in pairs])]
    unnamed x10 -> x8, local copies, waits for them, and re-layouts: 0.02 us -> 2.82 us
    pallas_call x4 -> x5, Pallas kernels: 3.54 us -> 5.44 us  [the longest x3 4.81 us: contract(): pl.pallas_call(functools.partial(contract_kernel, share, first, len(group...]
    slice x1 -> x0, local copies, waits for them, and re-layouts: 1.3 us -> none  [at_the_source(): parts = [cholesky[c:c + 1] for c in range(chunks)]]
  transfers between devices with their start and end apart: 19 -> 18, of which waited for: 6 -> 6; matrix products, arithmetic and copies ran while one was open for 2% -> 0% of each run, Pallas kernels for 20% -> 28%
where the time goes in v2:
time: 61.7 us; the launch traced here: 61.4 us
  starting transfers between devices  20.5 us (33%)
  Pallas kernels  19 us (31%)
  waiting for transfers between devices  17.7 us (29%)
  local copies, waits for them, and re-layouts  2.82 us (5%)
  between operations  1.42 us (2%)
    ppermute x12, waiting for transfers between devices, at_the_source(): move = lambda x, k: lax.ppermute(x, SR, [(i, i ^ k) for i in range(n)])  14.8 us
    ppermute x4, starting transfers between devices, at_the_source(): lax.ppermute(x, ALL, [(w * n + q, (w ^ q) * n + (q ^ k)) for w, q in pairs])  10.3 us
    pallas_call x1, Pallas kernels, make_green(): pl.pallas_call(functools.partial(green_kernel, n, share), out_shape=jax.S...  9.1 us
    ppermute x12, starting transfers between devices, at_the_source(): move = lambda x, k: lax.ppermute(x, SR, [(i, i ^ k) for i in range(n)])  8.04 us
    pallas_call x3, Pallas kernels, contract(): pl.pallas_call(functools.partial(contract_kernel, share, first, len(group...  4.81 us
    pallas_call x1, Pallas kernels, select(): pl.pallas_call(functools.partial(select_kernel, n, per, share), out_shape...  2.92 us
    ppermute x4, waiting for transfers between devices, at_the_source(): lax.ppermute(x, ALL, [(w * n + q, (w ^ q) * n + (q ^ k)) for w, q in pairs])  2.88 us
    unnamed x8, local copies, waits for them, and re-layouts  2.82 us
  transfers between devices with their start and end apart: 18, of which 6 were waited for; matrix products, arithmetic and copies ran while one was open for 0% of the time, Pallas kernels for 28%

profile of v2, /device:TPU:0, one launch (start us, length us, event | category | flops | bytes accessed | tf_op | source)
XLA Modules:
  0.0 61.4 jit_solution(12211382976758212372)
XLA Ops:
  0.6 0.0 copy-start.1
  0.6 0.9 %copy-done.1 = bf16[256,256]{1,0:T(8,128)(2,1)S(1)} copy-done((bf16[256,256]{1,0:T(8,128)(2,1)S(1)}, bf16[256,256]{1,0:T(8,128)(2,1)}, u32[]{:S(2)}) %copy-start.1) | copy-done | bytes 131096
  1.5 0.0 copy-start.2
  1.5 0.7 %copy-done.2 = f32[8,256]{1,0:T(8,128)S(1)} copy-done((f32[8,256]{1,0:T(8,128)S(1)}, f32[8,256]{1,0:T(8,128)}, u32[]{:S(2)}) %copy-start.2) | copy-done | bytes 8216
  2.2 0.0 copy-start.3
  2.3 3.0 %collective-permute-start.1 = (bf16[288,256]{1,0:T(8,128)(2,1)S(1)}, bf16[288,256]{1,0:T(8,128)(2,1)S(1)}, u32[]{:S(2)}, u32[]{:S(2)}) collective-permute-start(bf16[288,256]{1,0:T(8,128)(2,1)S(1)} %message.1.refs_0_.refs_4_), channel_id=1, source_target_pairs={{0,2},{1,3},{2,0},{3,1},{4,6},{5,7},{6,4},{7,5},{8,10},{9,11},{10,... | collective-permute-start | bytes 442376 | tf_op jit(solution)/shard_map/ppermute | solution.py:304
  5.3 0.0 copy-done.3
  5.3 0.0 copy-start
  5.3 1.2 %copy-done = bf16[8,256,256]{2,1,0:T(8,128)(2,1)S(1)} copy-done((bf16[8,256,256]{2,1,0:T(8,128)(2,1)S(1)}, bf16[8,256,256]{2,1,0:T(8,128)(2,1)}, u32[]{:S(2)}) %copy-start) | copy-done | bytes 1048600
  6.5 2.9 %select.1 = (bf16[2,256,256]{2,1,0:T(8,128)(2,1)S(1)}, bf16[2,256,256]{2,1,0:T(8,128)(2,1)S(1)}, bf16[2,256,256]{2,1,0:T(8,128)(2,1)S(1)}, bf16[2,256,256]{2,1,0...) custom-call(s32[32]{0:T(128)S(1)} %copy-done.3, ...), custom_call_target="tpu_custom_call" | custom-call | bytes 2097152 | tf_op jit(solution)/shard_map/select/pallas_call | solution.py:79
  9.4 0.1 collective-permute-start.4
  9.5 0.6 %collective-permute-start.5 = (bf16[2,256,256]{2,1,0:T(8,128)(2,1)S(1)}, bf16[2,256,256]{2,1,0:T(8,128)(2,1)S(1)}, u32[]{:S(2)}, u32[]{:S(2)}) collective-permute-start(bf16[2,256,256]{2,1,0:T(8,128)(2,1)S(1)} %get-tuple-element.24), channel_id=1, source_target_pairs={{0,2},{1,3},{2,0},{3,1},{4,6},{5,7},{6,4},{7,5},{8,10},{9,11},{10,... | collective-permute-start | bytes 786440 | tf_op jit(solution)/shard_map/ppermute | solution.py:304
  10.1 1.2 %collective-permute-start.6 = (bf16[2,256,256]{2,1,0:T(8,128)(2,1)S(1)}, bf16[2,256,256]{2,1,0:T(8,128)(2,1)S(1)}, u32[]{:S(2)}, u32[]{:S(2)}) collective-permute-start(bf16[2,256,256]{2,1,0:T(8,128)(2,1)S(1)} %get-tuple-element.25), channel_id=1, source_target_pairs={{0,3},{1,2},{2,1},{3,0},{4,7},{5,6},{6,5},{7,4},{8,11},{9,10},{10,... | collective-permute-start | bytes 786440 | tf_op jit(solution)/shard_map/ppermute | solution.py:304
  11.4 0.3 collective-permute-start
  11.7 0.0 collective-permute-done.1.refs_2_.refs_6_
  11.7 0.2 collective-permute-start.2
  11.9 0.9 %collective-permute-done.refs_1_.refs_5_ = bf16[288,256]{1,0:T(8,128)(2,1)S(1)} collective-permute-done((bf16[288,256]{1,0:T(8,128)(2,1)S(1)}, bf16[288,256]{1,0:T(8,128)(2,1)S(1)}, u32[]{:S(2)}, u32[]{:S(2)}) %collective-permute-start) | collective-permute-done | bytes 147488 | tf_op jit(solution)/shard_map/ppermute | solution.py:304
  12.7 0.6 collective-permute-start.12
  13.3 0.0 collective-permute-done.2.refs_3_.refs_7_
  13.3 0.6 fields.1
  13.9 0.7 %collective-permute-start.3 = (f32[4,2,256]{2,1,0:T(2,128)S(1)}, f32[4,2,256]{2,1,0:T(2,128)S(1)}, u32[]{:S(2)}, u32[]{:S(2)}) collective-permute-start(f32[4,2,256]{2,1,0:T(2,128)S(1)} %fields.1), channel_id=1, source_target_pairs={{0,0},{1,5},{2,10},{3,15},{4,1},{5,4},{6,11},{7,14},{8,2},{9,7},{1... | collective-permute-start | bytes 24584 | tf_op jit(solution)/shard_map/ppermute | solution.py:306
  14.6 0.0 collective-permute-done.4.refs_1_
  14.6 4.1 %collective-permute-done.5.refs_2_ = bf16[2,256,256]{2,1,0:T(8,128)(2,1)S(1)} collective-permute-done((bf16[2,256,256]{2,1,0:T(8,128)(2,1)S(1)}, bf16[2,256,256]{2,1,0:T(8,128)(2,1)S(1)}, u32[]{:S(2)}, u32[]{:S(2)}) %collective-permute-start.5) | collective-permute-done | bytes 262176 | tf_op jit(solution)/shard_map/ppermute | solution.py:304
  18.7 4.7 %collective-permute-done.6.refs_3_ = bf16[2,256,256]{2,1,0:T(8,128)(2,1)S(1)} collective-permute-done((bf16[2,256,256]{2,1,0:T(8,128)(2,1)S(1)}, bf16[2,256,256]{2,1,0:T(8,128)(2,1)S(1)}, u32[]{:S(2)}, u32[]{:S(2)}) %collective-permute-start.6) | collective-permute-done | bytes 262176 | tf_op jit(solution)/shard_map/ppermute | solution.py:304
  23.4 0.0 collective-permute-done.3.refs_8_
  23.4 0.7 %collective-permute-start.7 = (bf16[2,256,1024]{2,1,0:T(8,128)(2,1)}, bf16[2,256,1024]{2,1,0:T(8,128)(2,1)S(1)}, u32[]{:S(2)}, u32[]{:S(2)}) collective-permute-start(bf16[2,256,1024]{2,1,0:T(8,128)(2,1)} %refs_0_.1), channel_id=1, source_target_pairs={{0,1},{1,0},{2,3},{3,2},{4,5},{5,4},{6,7},{7,6},{8,9},{9,8},{10,11... | collective-permute-start | bytes 3145736 | tf_op jit(solution)/shard_map/ppermute | solution.py:304
  24.1 0.7 %collective-permute-start.10 = (bf16[1,256,1024]{2,1,0:T(8,128)(2,1)S(1)}, bf16[1,256,1024]{2,1,0:T(8,128)(2,1)S(1)}, u32[]{:S(2)}, u32[]{:S(2)}) collective-permute-start(bf16[1,256,1024]{2,1,0:T(8,128)(2,1)S(1)} %get-tuple-element.30), channel_id=1, source_target_pairs={{0,2},{1,3},{2,0},{3,1},{4,6},{5,7},{6,4},{7,5},{8,10},{9,11},{10,... | collective-permute-start | bytes 1572872 | tf_op jit(solution)/shard_map/ppermute | solution.py:304
  24.8 5.1 %collective-permute-done.12.refs_0_ = bf16[1,128,1024]{2,1,0:T(8,128)(2,1)S(1)} collective-permute-done((bf16[1,128,1024]{2,1,0:T(8,128)(2,1)S(1)}, bf16[1,128,1024]{2,1,0:T(8,128)(2,1)S(1)}, u32[]{:S(2)}, u32[]{:S(2)}) %collective-permute-start.12) | collective-permute-done | bytes 262176 | tf_op jit(solution)/shard_map/ppermute | solution.py:304
  29.9 1.6 %collective-permute-start.13 = (bf16[1,128,1024]{2,1,0:T(8,128)(2,1)S(1)}, bf16[1,128,1024]{2,1,0:T(8,128)(2,1)S(1)}, u32[]{:S(2)}, u32[]{:S(2)}) collective-permute-start(bf16[1,128,1024]{2,1,0:T(8,128)(2,1)S(1)} %collective-permute-done.12.refs_0_), channel_id=1, source_target_pairs={{0,4},{4,0},{8,12},{12,8},{1,5},{5,1},{9,13},{13,9},{2,6},{6,2},{1... | collective-permute-start | bytes 786440 | tf_op jit(solution)/shard_map/ppermute | solution.py:305
  31.5 9.1 %green.1.refs_2_.refs_4_ = bf16[1024,512]{1,0:T(8,128)(2,1)S(1)} custom-call(bf16[2,256,256]{2,1,0:T(8,128)(2,1)S(1)} %get-tuple-element.22.refs_0_, bf16[2,256,256]{2,1,0:T(8,128)(2,1)S(1)} %collective-permute-done.4.refs_1_, bf16[2,256,256]{2,1,0:T(8,128)(2,1)S(1)} %collective-permute-done.5.refs_2_, ...), custom_call_target="tpu_custom_call" | custom-call | flops 5100273664 | bytes 3145728 | tf_op jit(solution)/shard_map/green/pallas_call | solution.py:198
  40.6 0.1 collective-permute-done.10.refs_0_
  40.7 0.0 collective-permute-start.11
  40.7 0.5 collective-permute-start.14
  41.2 0.0 collective-permute-done.13.refs_1_
  41.2 0.1 collective-permute-start.15
  41.3 0.0 collective-permute-done.7.refs_1_
  41.3 2.7 %contract.3 = (f32[8,128]{1,0:T(8,128)S(1)}, f32[8,128]{1,0:T(8,128)S(1)}) custom-call(bf16[2,256,1024]{2,1,0:T(8,128)(2,1)} %refs_0_.1, bf16[2,256,1024]{2,1,0:T(8,128)(2,1)S(1)} %collective-permute-done.7.refs_1_, bf16[1024,512]{1,0:T(8,128)(2,1)S(1)} %green.1.refs_2_.refs_4_), custom_call_target="tpu_custom_call" | custom-call | flops 1073741824 | bytes 3145728 | tf_op jit(solution)/shard_map/contract/pallas_call | solution.py:250
  44.0 0.7 %collective-permute-start.8 = (f32[8,128]{1,0:T(8,128)S(1)}, f32[8,128]{1,0:T(8,128)S(1)}, u32[]{:S(2)}, u32[]{:S(2)}) collective-permute-start(f32[8,128]{1,0:T(8,128)S(1)} %get-tuple-element.27.refs_5_), channel_id=1, source_target_pairs={{0,0},{1,5},{2,10},{3,15},{4,4},{5,1},{6,14},{7,11},{8,8},{9,13},{... | collective-permute-start | bytes 12296 | tf_op jit(solution)/shard_map/ppermute | solution.py:307
  44.7 0.0 collective-permute-done.14.refs_2_
  44.7 0.0 collective-permute-done.15.refs_3_
  44.7 1.1 %contract.4 = (f32[8,128]{1,0:T(8,128)S(1)}, f32[8,128]{1,0:T(8,128)S(1)}) custom-call(bf16[1,128,1024]{2,1,0:T(8,128)(2,1)S(1)} %collective-permute-done.12.refs_0_, bf16[1,128,1024]{2,1,0:T(8,128)(2,1)S(1)} %collective-permute-done.13.refs_1_, bf16[1,128,1024]{2,1,0:T(8,128)(2,1)S(1)} %collective-permute-done.14.refs_2_, ...), custom_call_target="tpu_custom_call" | custom-call | flops 536870912 | bytes 2097152 | tf_op jit(solution)/shard_map/contract/pallas_call | solution.py:250
  45.8 0.0 collective-permute-done.11.refs_1_
  45.8 1.0 %contract.5 = (f32[8,128]{1,0:T(8,128)S(1)}, f32[8,128]{1,0:T(8,128)S(1)}) custom-call(bf16[1,256,1024]{2,1,0:T(8,128)(2,1)S(1)} %collective-permute-done.10.refs_0_, bf16[1,256,1024]{2,1,0:T(8,128)(2,1)S(1)} %collective-permute-done.11.refs_1_, bf16[1024,512]{1,0:T(8,128)(2,1)S(1)} %green.1.refs_2_.refs_4_, f32[8,128]{1,0:T(8,128)S(1)} %get-tuple-element.34.refs_3_, ...), custom_call_target="tpu_custom_call" | custom-call | flops 536870912 | bytes 2097152 | tf_op jit(solution)/shard_map/contract/pallas_call | solution.py:250
  46.8 7.4 %collective-permute-start.16 = (f32[8,128]{1,0:T(8,128)S(1)}, f32[8,128]{1,0:T(8,128)S(1)}, u32[]{:S(2)}, u32[]{:S(2)}) collective-permute-start(f32[8,128]{1,0:T(8,128)S(1)} %get-tuple-element.36), channel_id=1, source_target_pairs={{0,2},{1,7},{2,8},{3,13},{4,6},{5,3},{6,12},{7,9},{8,10},{9,15},{1... | collective-permute-start | bytes 12296 | tf_op jit(solution)/shard_map/ppermute | solution.py:307
  54.2 2.2 %collective-permute-start.17 = (f32[8,128]{1,0:T(8,128)S(1)}, f32[8,128]{1,0:T(8,128)S(1)}, u32[]{:S(2)}, u32[]{:S(2)}) collective-permute-start(f32[8,128]{1,0:T(8,128)S(1)} %get-tuple-element.37), channel_id=1, source_target_pairs={{0,3},{1,6},{2,9},{3,12},{4,7},{5,2},{6,13},{7,8},{8,11},{9,14},{1... | collective-permute-start | bytes 12296 | tf_op jit(solution)/shard_map/ppermute | solution.py:307
  56.4 0.0 collective-permute-start.9
  57.0 0.0 collective-permute-done.16.refs_2_
  57.1 2.9 %collective-permute-done.17.refs_3_ = f32[8,128]{1,0:T(8,128)S(1)} collective-permute-done((f32[8,128]{1,0:T(8,128)S(1)}, f32[8,128]{1,0:T(8,128)S(1)}, u32[]{:S(2)}, u32[]{:S(2)}) %collective-permute-start.17) | collective-permute-done | bytes 4128 | tf_op jit(solution)/shard_map/ppermute | solution.py:307
  59.9 0.0 collective-permute-done.8.refs_0_
  59.9 0.0 collective-permute-done.9.refs_1_
  59.9 1.5 %unpack.1 = (f32[2,8]{1,0:T(2,128)}, f32[2,8]{1,0:T(2,128)}) custom-call(s32[32]{0:T(128)S(1)} %copy-done.3, s32[1]{0:T(128)S(6)} %copy.8.counts, f32[8,128]{1,0:T(8,128)S(1)} %collective-permute-done.8.refs_0_, f32[8,128]{1,0:T(8,128)S(1)} %collective-permute-done.9.refs_1_, f32[8,128]{1,0:T(8,128)S(1)} %collective-permute-done.16.refs_2_, ...), custom_call_target="tpu_custom_call" | custom-call | tf_op jit(solution)/shard_map/unpack/pallas_call | solution.py:287
  (1 shorter events, 0.0 us)
Async XLA Ops:
  0.6 0.9 %copy-start.1 = (bf16[256,256]{1,0:T(8,128)(2,1)S(1)}, bf16[256,256]{1,0:T(8,128)(2,1)}, u32[]{:S(2)}) copy-start(bf16[256,256]{1,0:T(8,128)(2,1)} %trial.1) | copy-start | bytes 393220
  1.5 0.7 %copy-start.2 = (f32[8,256]{1,0:T(8,128)S(1)}, f32[8,256]{1,0:T(8,128)}, u32[]{:S(2)}) copy-start(f32[8,256]{1,0:T(8,128)} %field.1) | copy-start | bytes 24580
  2.2 3.0 %copy-start.3 = (s32[32]{0:T(128)S(1)}, s32[32]{0:T(128)}, u32[]{:S(2)}) copy-start(s32[32]{0:T(128)} %branches.4) | copy-start | bytes 388
  2.3 9.4 %collective-permute-start.1 = (bf16[288,256]{1,0:T(8,128)(2,1)S(1)}, bf16[288,256]{1,0:T(8,128)(2,1)S(1)}, u32[]{:S(2)}, u32[]{:S(2)}) collective-permute-start(bf16[288,256]{1,0:T(8,128)(2,1)S(1)} %message.1.refs_0_.refs_4_), channel_id=1, source_target_pairs={{0,2},{1,3},{2,0},{3,1},{4,6},{5,7},{6,4},{7,5},{8,10},{9,11},{10,... | collective-permute-start | bytes 442376 | tf_op jit(solution)/shard_map/ppermute | solution.py:304
  5.3 1.2 %copy-start = (bf16[8,256,256]{2,1,0:T(8,128)(2,1)S(1)}, bf16[8,256,256]{2,1,0:T(8,128)(2,1)}, u32[]{:S(2)}) copy-start(bf16[8,256,256]{2,1,0:T(8,128)(2,1)} %walkers.1) | copy-start | bytes 3145732
  9.4 5.2 %collective-permute-start.4 = (bf16[2,256,256]{2,1,0:T(8,128)(2,1)S(1)}, bf16[2,256,256]{2,1,0:T(8,128)(2,1)S(1)}, u32[]{:S(2)}, u32[]{:S(2)}) collective-permute-start(bf16[2,256,256]{2,1,0:T(8,128)(2,1)S(1)} %get-tuple-element.23), channel_id=1, source_target_pairs={{0,1},{1,0},{2,3},{3,2},{4,5},{5,4},{6,7},{7,6},{8,9},{9,8},{10,11... | collective-permute-start | bytes 786440 | tf_op jit(solution)/shard_map/ppermute | solution.py:304
  9.5 9.2 %collective-permute-start.5 = (bf16[2,256,256]{2,1,0:T(8,128)(2,1)S(1)}, bf16[2,256,256]{2,1,0:T(8,128)(2,1)S(1)}, u32[]{:S(2)}, u32[]{:S(2)}) collective-permute-start(bf16[2,256,256]{2,1,0:T(8,128)(2,1)S(1)} %get-tuple-element.24), channel_id=1, source_target_pairs={{0,2},{1,3},{2,0},{3,1},{4,6},{5,7},{6,4},{7,5},{8,10},{9,11},{10,... | collective-permute-start | bytes 786440 | tf_op jit(solution)/shard_map/ppermute | solution.py:304
  10.1 13.3 %collective-permute-start.6 = (bf16[2,256,256]{2,1,0:T(8,128)(2,1)S(1)}, bf16[2,256,256]{2,1,0:T(8,128)(2,1)S(1)}, u32[]{:S(2)}, u32[]{:S(2)}) collective-permute-start(bf16[2,256,256]{2,1,0:T(8,128)(2,1)S(1)} %get-tuple-element.25), channel_id=1, source_target_pairs={{0,3},{1,2},{2,1},{3,0},{4,7},{5,6},{6,5},{7,4},{8,11},{9,10},{10,... | collective-permute-start | bytes 786440 | tf_op jit(solution)/shard_map/ppermute | solution.py:304
  11.4 1.4 %collective-permute-start = (bf16[288,256]{1,0:T(8,128)(2,1)S(1)}, bf16[288,256]{1,0:T(8,128)(2,1)S(1)}, u32[]{:S(2)}, u32[]{:S(2)}) collective-permute-start(bf16[288,256]{1,0:T(8,128)(2,1)S(1)} %message.1.refs_0_.refs_4_), channel_id=1, source_target_pairs={{0,1},{1,0},{2,3},{3,2},{4,5},{5,4},{6,7},{7,6},{8,9},{9,8},{10,11... | collective-permute-start | bytes 442376 | tf_op jit(solution)/shard_map/ppermute | solution.py:304
  11.7 1.6 %collective-permute-start.2 = (bf16[288,256]{1,0:T(8,128)(2,1)S(1)}, bf16[288,256]{1,0:T(8,128)(2,1)S(1)}, u32[]{:S(2)}, u32[]{:S(2)}) collective-permute-start(bf16[288,256]{1,0:T(8,128)(2,1)S(1)} %collective-permute-done.1.refs_2_.refs_6_), channel_id=1, source_target_pairs={{0,1},{1,0},{2,3},{3,2},{4,5},{5,4},{6,7},{7,6},{8,9},{9,8},{10,11... | collective-permute-start | bytes 442376 | tf_op jit(solution)/shard_map/ppermute | solution.py:304
  12.7 17.2 %collective-permute-start.12 = (bf16[1,128,1024]{2,1,0:T(8,128)(2,1)S(1)}, bf16[1,128,1024]{2,1,0:T(8,128)(2,1)S(1)}, u32[]{:S(2)}, u32[]{:S(2)}) collective-permute-start(bf16[1,128,1024]{2,1,0:T(8,128)(2,1)S(1)} %get-tuple-element.33), channel_id=1, source_target_pairs={{0,2},{1,3},{2,0},{3,1},{4,6},{5,7},{6,4},{7,5},{8,10},{9,11},{10,... | collective-permute-start | bytes 786440 | tf_op jit(solution)/shard_map/ppermute | solution.py:304
  13.9 9.5 %collective-permute-start.3 = (f32[4,2,256]{2,1,0:T(2,128)S(1)}, f32[4,2,256]{2,1,0:T(2,128)S(1)}, u32[]{:S(2)}, u32[]{:S(2)}) collective-permute-start(f32[4,2,256]{2,1,0:T(2,128)S(1)} %fields.1), channel_id=1, source_target_pairs={{0,0},{1,5},{2,10},{3,15},{4,1},{5,4},{6,11},{7,14},{8,2},{9,7},{1... | collective-permute-start | bytes 24584 | tf_op jit(solution)/shard_map/ppermute | solution.py:306
  23.4 17.9 %collective-permute-start.7 = (bf16[2,256,1024]{2,1,0:T(8,128)(2,1)}, bf16[2,256,1024]{2,1,0:T(8,128)(2,1)S(1)}, u32[]{:S(2)}, u32[]{:S(2)}) collective-permute-start(bf16[2,256,1024]{2,1,0:T(8,128)(2,1)} %refs_0_.1), channel_id=1, source_target_pairs={{0,1},{1,0},{2,3},{3,2},{4,5},{5,4},{6,7},{7,6},{8,9},{9,8},{10,11... | collective-permute-start | bytes 3145736 | tf_op jit(solution)/shard_map/ppermute | solution.py:304
  24.1 16.6 %collective-permute-start.10 = (bf16[1,256,1024]{2,1,0:T(8,128)(2,1)S(1)}, bf16[1,256,1024]{2,1,0:T(8,128)(2,1)S(1)}, u32[]{:S(2)}, u32[]{:S(2)}) collective-permute-start(bf16[1,256,1024]{2,1,0:T(8,128)(2,1)S(1)} %get-tuple-element.30), channel_id=1, source_target_pairs={{0,2},{1,3},{2,0},{3,1},{4,6},{5,7},{6,4},{7,5},{8,10},{9,11},{10,... | collective-permute-start | bytes 1572872 | tf_op jit(solution)/shard_map/ppermute | solution.py:304
  29.9 11.3 %collective-permute-start.13 = (bf16[1,128,1024]{2,1,0:T(8,128)(2,1)S(1)}, bf16[1,128,1024]{2,1,0:T(8,128)(2,1)S(1)}, u32[]{:S(2)}, u32[]{:S(2)}) collective-permute-start(bf16[1,128,1024]{2,1,0:T(8,128)(2,1)S(1)} %collective-permute-done.12.refs_0_), channel_id=1, source_target_pairs={{0,4},{4,0},{8,12},{12,8},{1,5},{5,1},{9,13},{13,9},{2,6},{6,2},{1... | collective-permute-start | bytes 786440 | tf_op jit(solution)/shard_map/ppermute | solution.py:305
  40.7 5.1 %collective-permute-start.11 = (bf16[1,256,1024]{2,1,0:T(8,128)(2,1)S(1)}, bf16[1,256,1024]{2,1,0:T(8,128)(2,1)S(1)}, u32[]{:S(2)}, u32[]{:S(2)}) collective-permute-start(bf16[1,256,1024]{2,1,0:T(8,128)(2,1)S(1)} %collective-permute-done.10.refs_0_), channel_id=1, source_target_pairs={{0,1},{1,0},{2,3},{3,2},{4,5},{5,4},{6,7},{7,6},{8,9},{9,8},{10,11... | collective-permute-start | bytes 1572872 | tf_op jit(solution)/shard_map/ppermute | solution.py:304
  40.7 4.0 %collective-permute-start.14 = (bf16[1,128,1024]{2,1,0:T(8,128)(2,1)S(1)}, bf16[1,128,1024]{2,1,0:T(8,128)(2,1)S(1)}, u32[]{:S(2)}, u32[]{:S(2)}) collective-permute-start(bf16[1,128,1024]{2,1,0:T(8,128)(2,1)S(1)} %collective-permute-done.12.refs_0_), channel_id=1, source_target_pairs={{0,1},{1,0},{2,3},{3,2},{4,5},{5,4},{6,7},{7,6},{8,9},{9,8},{10,11... | collective-permute-start | bytes 786440 | tf_op jit(solution)/shard_map/ppermute | solution.py:304
  41.2 3.5 %collective-permute-start.15 = (bf16[1,128,1024]{2,1,0:T(8,128)(2,1)S(1)}, bf16[1,128,1024]{2,1,0:T(8,128)(2,1)S(1)}, u32[]{:S(2)}, u32[]{:S(2)}) collective-permute-start(bf16[1,128,1024]{2,1,0:T(8,128)(2,1)S(1)} %collective-permute-done.13.refs_1_), channel_id=1, source_target_pairs={{0,1},{1,0},{2,3},{3,2},{4,5},{5,4},{6,7},{7,6},{8,9},{9,8},{10,11... | collective-permute-start | bytes 786440 | tf_op jit(solution)/shard_map/ppermute | solution.py:304
  44.0 15.9 %collective-permute-start.8 = (f32[8,128]{1,0:T(8,128)S(1)}, f32[8,128]{1,0:T(8,128)S(1)}, u32[]{:S(2)}, u32[]{:S(2)}) collective-permute-start(f32[8,128]{1,0:T(8,128)S(1)} %get-tuple-element.27.refs_5_), channel_id=1, source_target_pairs={{0,0},{1,5},{2,10},{3,15},{4,4},{5,1},{6,14},{7,11},{8,8},{9,13},{... | collective-permute-start | bytes 12296 | tf_op jit(solution)/shard_map/ppermute | solution.py:307
  46.8 10.3 %collective-permute-start.16 = (f32[8,128]{1,0:T(8,128)S(1)}, f32[8,128]{1,0:T(8,128)S(1)}, u32[]{:S(2)}, u32[]{:S(2)}) collective-permute-start(f32[8,128]{1,0:T(8,128)S(1)} %get-tuple-element.36), channel_id=1, source_target_pairs={{0,2},{1,7},{2,8},{3,13},{4,6},{5,3},{6,12},{7,9},{8,10},{9,15},{1... | collective-permute-start | bytes 12296 | tf_op jit(solution)/shard_map/ppermute | solution.py:307
  54.2 5.7 %collective-permute-start.17 = (f32[8,128]{1,0:T(8,128)S(1)}, f32[8,128]{1,0:T(8,128)S(1)}, u32[]{:S(2)}, u32[]{:S(2)}) collective-permute-start(f32[8,128]{1,0:T(8,128)S(1)} %get-tuple-element.37), channel_id=1, source_target_pairs={{0,3},{1,6},{2,9},{3,12},{4,7},{5,2},{6,13},{7,8},{8,11},{9,14},{1... | collective-permute-start | bytes 12296 | tf_op jit(solution)/shard_map/ppermute | solution.py:307
  56.4 3.5 %collective-permute-start.9 = (f32[8,128]{1,0:T(8,128)S(1)}, f32[8,128]{1,0:T(8,128)S(1)}, u32[]{:S(2)}, u32[]{:S(2)}) collective-permute-start(f32[8,128]{1,0:T(8,128)S(1)} %get-tuple-element.28), channel_id=1, source_target_pairs={{0,1},{1,4},{2,11},{3,14},{4,5},{5,0},{6,15},{7,10},{8,9},{9,12},{... | collective-permute-start | bytes 12296 | tf_op jit(solution)/shard_map/ppermute | solution.py:307

commit v3 on v2

--- a/solution.py
+++ b/solution.py
@@ -49,79 +49,77 @@
     return places, olds
 
 
-def select_kernel(n, per, share, branches, walkers, cholesky, *refs):
-    sends, direct, shared, sems, more = refs[:n], refs[n], refs[n + 1], refs[n + 2], refs[n + 3]
+def select_kernel(n, per, share, branches, walkers, *refs):
+    sends, sems = refs[:n], refs[n]
     walk, q = place()
-    split_at, half = direct.shape[0], shared.shape[1]
-    rows = pl.ds(pl.multiple_of((walk & 1) * half, half), half)
     copies = []
-    for k in range(1, n):
+    for k in list(range(1, n)) + [0]:
         olds = picks(branches, (q ^ k ^ walk) * per, per, walk, share)[1]
         for r in range(share):
             copies.append(pltpu.make_async_copy(walkers.at[olds[r]], sends[k].at[r], sems.at[k, r]))
             copies[-1].start()
-    copies.append(pltpu.make_async_copy(cholesky.at[pl.ds(split_at, shared.shape[0]), rows, :], shared, more.at[0]))
-    copies[-1].start()
-    copies.append(pltpu.make_async_copy(cholesky.at[pl.ds(0, split_at)], direct, more.at[1]))
-    copies[-1].start()
-    olds = picks(branches, (q ^ walk) * per, per, walk, share)[1]
-    for r in range(share):
-        copies.append(pltpu.make_async_copy(walkers.at[olds[r]], sends[0].at[r], sems.at[0, r]))
-        copies[-1].start()
     for copy in copies:
         copy.wait()
 
 
-def select(n, per, share, branches, walkers, cholesky):
+def select(n, per, share, branches, walkers):
     rows, electrons = walkers.shape[1:]
-    vectors, height, width = cholesky.shape
-    later = vectors // 2
     return pl.pallas_call(
         functools.partial(select_kernel, n, per, share),
-        out_shape=[jax.ShapeDtypeStruct((share, rows, electrons), walkers.dtype)] * n
-        + [
-            jax.ShapeDtypeStruct((vectors - later, height, width), cholesky.dtype),
-            jax.ShapeDtypeStruct((later, height // 2, width), cholesky.dtype),
+        out_shape=[jax.ShapeDtypeStruct((share, rows, electrons), walkers.dtype)] * n,
+        in_specs=[whole(pltpu.SMEM), whole(pl.ANY)],
+        out_specs=[whole(pl.ANY)] * n,
+        scratch_shapes=[pltpu.SemaphoreType.DMA((n, share))],
+        compiler_params=pltpu.CompilerParams(vmem_limit_bytes=SMALL_LIMIT),
+        name="select",
+    )(branches, walkers)
+
+
+def message_kernel(trial, field, cholesky, out, shared, terms, sems):
+    walk, _ = place()
+    rows, height, count = trial.shape[0], cholesky.shape[0], shared.shape[0]
+    start = height - 2 * count + (walk & 1) * count
+    copies = [
+        pltpu.make_async_copy(cholesky.at[pl.ds(pl.multiple_of(start, 16), count)], shared, sems.at[0]),
+        pltpu.make_async_copy(trial, out.at[pl.ds(0, rows)], sems.at[1]),
+        pltpu.make_async_copy(terms, out.at[pl.ds(rows, terms.shape[0])], sems.at[2]),
+    ]
+    copies[0].start()
+    copies[1].start()
+    rest, parts = field[...], []
+    for _ in range(3):
+        parts.append(rest.astype(BF16).astype(F32))
+        rest = rest - parts[-1]
+    spare = terms.shape[0] - 3 * field.shape[0]
+    if spare:
+        parts.append(jnp.zeros((spare, field.shape[1]), F32))
+    terms[...] = jnp.concatenate(parts, axis=0).astype(BF16)
+    copies[2].start()
+    for copy in copies:
+        copy.wait()
+
+
+def message(trial, field, cholesky, shared_rows):
+    extra = -(-3 * field.shape[0] // 16) * 16
+    return pl.pallas_call(
+        message_kernel,
+        out_shape=[
+            jax.ShapeDtypeStruct((trial.shape[0] + extra, trial.shape[1]), trial.dtype),
+            jax.ShapeDtypeStruct((shared_rows, cholesky.shape[1]), cholesky.dtype),
         ],
-        in_specs=[whole(pltpu.SMEM), whole(pl.ANY), whole(pl.ANY)],
-        out_specs=[whole(pl.ANY)] * (n + 2),
-        scratch_shapes=[pltpu.SemaphoreType.DMA((n, share)), pltpu.SemaphoreType.DMA((2,))],
-        compiler_params=pltpu.CompilerParams(vmem_limit_bytes=SMALL_LIMIT),
-        cost_estimate=pl.CostEstimate(flops=0, bytes_accessed=4 * walkers.size, transcendentals=0),
-        name="select",
-    )(branches, walkers, cholesky)
-
-
-def message_kernel(trial, field, out):
-    rows = trial.shape[0]
-    out[:rows, :] = trial[...]
-    rest, terms = field[...], []
-    for _ in range(3):
-        terms.append(rest.astype(BF16).astype(F32))
-        rest = rest - terms[-1]
-    spare = out.shape[0] - rows - 3 * field.shape[0]
-    if spare:
-        terms.append(jnp.zeros((spare, field.shape[1]), F32))
-    out[rows:, :] = jnp.concatenate(terms, axis=0).astype(BF16)
-
-
-def message(trial, field):
-    height = trial.shape[0] + -(-3 * field.shape[0] // 16) * 16
-    return pl.pallas_call(
-        message_kernel,
-        out_shape=jax.ShapeDtypeStruct((height, trial.shape[1]), trial.dtype),
-        in_specs=[whole()] * 2,
-        out_specs=whole(),
+        in_specs=[whole(pl.ANY), whole(), whole(pl.ANY)],
+        out_specs=[whole(pl.ANY)] * 2,
+        scratch_shapes=[pltpu.VMEM((extra, trial.shape[1]), BF16), pltpu.SemaphoreType.DMA((3,))],
         compiler_params=pltpu.CompilerParams(vmem_limit_bytes=SMALL_LIMIT),
         name="message",
-    )(trial, field)
+    )(trial, field, cholesky)
 
 
 def fields_kernel(n, per, share, branches, *refs):
     messages, fields = refs[:n], refs[n]
     walk, q = place()
     rows = fields.shape[2]
-    places = picks(branches, walk * per, per, q, share)[0]
+    places = picks(branches, walk * per, per, walk ^ q, share)[0]
     walker = lax.broadcasted_iota(jnp.int32, (per, rows), 0)
     for k in range(n):
         terms = messages[k][rows:, :].astype(F32)
@@ -210,57 +208,75 @@
     )(*blocks, *messages, fields)
 
 
-def contract_kernel(share, first, pieces, count, going_on, *refs):
-    vectors, green = refs[: pieces * count], refs[pieces * count]
-    before = refs[pieces * count + 1 :][: count if going_on else 0]
-    outs, both = refs[-1 - count : -1], refs[-1]
-    electrons = both.shape[0]
-    half = electrons // 2
-    parity = lax.axis_index("walk") & 1
+def report(share, held, index, upper, lower):
+    half = upper.shape[0]
     row = lax.broadcasted_iota(jnp.int32, (half, half), 0)
     column = lax.broadcasted_iota(jnp.int32, (half, half), 1)
-    out_row = lax.broadcasted_iota(jnp.int32, (8, 128), 0)
-    lane = lax.broadcasted_iota(jnp.int32, (8, 128), 1)
+    out_row = lax.broadcasted_iota(jnp.int32, held.shape, 0)
+    lane = lax.broadcasted_iota(jnp.int32, held.shape, 1)
+    for i in range(share):
+        left, middle, right = 2 * i * half, (2 * i + 1) * half, 2 * (i + 1) * half
+        a, b = upper[:, left:middle], upper[:, middle:right]
+        c, d = lower[:, left:middle], lower[:, middle:right]
+        trace = jnp.sum(jnp.where(row == column, a + d, 0.0))
+        exchange = -0.5 * jnp.sum(a * a.T + d * d.T + 2.0 * (b * c.T))
+        here = out_row == index * share + i
+        held = jnp.where(here & (lane == 0), trace, held)
+        held = jnp.where(here & (lane == 1), exchange, held)
+    return held
+
+
+def near_kernel(share, count, height, *refs):
+    vectors, green, outs = refs[:count], refs[count], refs[-count:]
     for v in range(count):
-        held = before[v][...] if going_on else jnp.zeros((8, 128), F32)
-        mine = vectors[v * pieces : (v + 1) * pieces]
-        for g in range(mine[0].shape[0]):
-            if pieces == 1:
-                full = dot(mine[0][g], green[...])
-                upper, lower = full[:half], full[half:]
-            else:
-                for at, piece in zip((parity, 1 - parity), mine):
-                    both[pl.ds(pl.multiple_of(at * half, half), half), :] = dot(piece[g], green[...])
-                upper, lower = both[:half], both[half:]
-            for i in range(share):
-                left, middle, right = i * electrons, i * electrons + half, (i + 1) * electrons
-                a, b = upper[:, left:middle], upper[:, middle:right]
-                c, d = lower[:, left:middle], lower[:, middle:right]
-                trace = jnp.sum(jnp.where(row == column, a + d, 0.0))
-                exchange = -0.5 * jnp.sum(a * a.T + d * d.T + 2.0 * (b * c.T))
-                here = out_row == (first + g) * share + i
-                held = jnp.where(here & (lane == 0), trace, held)
-                held = jnp.where(here & (lane == 1), exchange, held)
+        held = jnp.zeros(outs[v].shape, F32)
+        for g in range(vectors[v].shape[0] // height):
+            full = dot(vectors[v][g * height : (g + 1) * height, :], green[...])
+            held = report(share, held, g, full[: height // 2], full[height // 2 :])
         outs[v][...] = held
 
 
-def contract(share, first, groups, green, before=(), after=()):
-    vectors = [v for group in groups for v in group]
-    electrons = green.shape[1] // share
-    return pl.pallas_call(
-        functools.partial(contract_kernel, share, first, len(groups[0]), len(groups), bool(before)),
-        out_shape=[jax.ShapeDtypeStruct((8, 128), F32)] * len(groups),
-        in_specs=[whole()] * (len(vectors) + 1 + len(before)) + [whole(pl.ANY)] * len(after),
-        out_specs=[whole()] * len(groups),
-        scratch_shapes=[pltpu.VMEM((electrons, green.shape[1]), F32)],
+def shared_kernel(share, count, height, *refs):
+    firsts, seconds, green = refs[:count], refs[count : 2 * count], refs[2 * count]
+    outs, kept, both = refs[-2 * count - 1 : -count - 1], refs[-count - 1 : -1], refs[-1]
+    parity = lax.axis_index("walk") & 1
+    half = height // 2
+    for v in range(count):
+        rows = firsts[v].shape[0]
+        for at, piece in ((parity, firsts[v]), (1 - parity, seconds[v])):
+            both[pl.ds(pl.multiple_of(at * rows, 16), rows), :] = dot(piece[...], green[...])
+        kept[v][...] = both[:half, :]
+        held = jnp.zeros(outs[v].shape, F32)
+        for g in range(1, (2 * rows + half) // height):
+            start = g * height - half
+            held = report(share, held, g, both[start : start + half, :], both[start + half : start + height, :])
+        outs[v][...] = held
+
+
+def direct_kernel(share, count, *refs):
+    uppers, green, kept, before = refs[:count], refs[count], refs[count + 1 : 2 * count + 1], refs[2 * count + 1 : -count]
+    outs = refs[-count:]
+    for v in range(count):
+        outs[v][...] = report(share, before[v][...], 0, dot(uppers[v][...], green[...]), kept[v][...])
+
+
+def contract(kernel, count, vectors, green, *more, kept_rows=0, scratch_rows=0):
+    wide = green.shape[1]
+    kept = [jax.ShapeDtypeStruct((kept_rows, wide), F32)] * count if kept_rows else []
+    return pl.pallas_call(
+        kernel,
+        out_shape=[jax.ShapeDtypeStruct((8, 128), F32)] * count + kept,
+        in_specs=[whole()] * (len(vectors) + 1 + len(more)),
+        out_specs=[whole()] * (count + len(kept)),
+        scratch_shapes=[pltpu.VMEM((scratch_rows, wide), F32)] if scratch_rows else [],
         compiler_params=pltpu.CompilerParams(vmem_limit_bytes=VMEM_LIMIT),
         cost_estimate=pl.CostEstimate(
-            flops=sum(2 * v.size * green.shape[1] for v in vectors),
+            flops=sum(2 * v.size * wide for v in vectors),
             bytes_accessed=sum(2 * v.size for v in vectors) + 2 * green.size,
             transcendentals=0,
         ),
         name="contract",
-    )(*vectors, green, *before, *after)
+    )(*vectors, green, *more)
 
 
 def unpack_kernel(n, per, share, branches, counts, *refs):
@@ -303,7 +319,7 @@
     pairs = [(w, q) for w in range(n) for q in range(n)]
     move = lambda x, k: lax.ppermute(x, SR, [(i, i ^ k) for i in range(n)])
     swap = lambda x: lax.ppermute(x, "walk", [(w, w ^ 1) for w in range(n)])
-    ask = lambda x: lax.ppermute(x, ALL, [(w * n + q, q * n + (w ^ q)) for w, q in pairs])
+    ask = lambda x: lax.ppermute(x, ALL, [(w * n + q, (w ^ q) * n + q) for w, q in pairs])
     answer = lambda x, k: lax.ppermute(x, ALL, [(w * n + q, (w ^ q) * n + (q ^ k)) for w, q in pairs])
     near = [k for k in range(n) if k < row_size]
     far = [k for k in range(n) if k >= row_size]
@@ -320,25 +336,39 @@
 
     ordered = lambda x, *first: lax.optimization_barrier((x,) + first)[0]
     heads = [k for k in far if not k & (row_size - 1)]
-    own = message(trial_orbitals, field)
+    height = cholesky.shape[1]
+    rows = cholesky.reshape(vectors * height, cholesky.shape[2])
+    direct_rows = height // 2
+    shared_rows = (rows.shape[0] - direct_rows) // 2
+    own, shared = message(trial_orbitals, field, rows, shared_rows)
     messages = {0: own, **spread(own)}
     messages.update({k: move(own, k) for k in near[1:]})
     messages = [messages[k] for k in range(n)]
-    *sends, direct, shared = select(n, per, share, ordered(branches, own), walkers, cholesky)
-    blocks = [sends[0]] + [move(sends[k], k) for k in range(1, n)]
+    sends = select(n, per, share, ordered(branches, own), walkers)
+    crossed = {k: move(shared, k) for k in heads}
+    close = [rows] + [move(rows, k) for k in near[1:]]
+    early = [messages[far[0]], *close[1:]]
+    blocks = [sends[0]] + [
+        move(ordered(sends[k], *(crossed.values() if k == n - 1 else early)), k) for k in range(1, n)
+    ]
     asked = ask(pick_fields(n, per, share, branches, messages))
-    shared = ordered(shared, *messages[1 : far[0] + 1])
-    crossed = {k: move(shared, k) for k in heads}
-    direct = ordered(direct, *messages)
-    direct = {k: move(direct, k) for k in heads}
-    other = along({k: swap(x) for k, x in crossed.items()})
-    crossed = along(crossed)
-    close = [cholesky] + [move(ordered(cholesky, asked, *blocks), k) for k in near[1:]]
+    direct = {k: move(ordered(rows[:direct_rows], asked), k) for k in heads}
+    other = {k: swap(x) for k, x in crossed.items()}
     green = make_green(n, share, blocks, messages, asked)
-    direct = along({k: ordered(x, green) for k, x in direct.items()})
-    results = contract(share, 0, [[x] for x in close], green)
-    late = contract(share, vectors - vectors // 2, [[crossed[k], other[k]] for k in far], green, after=results[:1])
-    late = contract(share, 0, [[direct[k]] for k in far], green, late)
+    crossed, other, direct = (along({k: ordered(x, green) for k, x in held.items()}) for held in (crossed, other, direct))
+    results = contract(functools.partial(near_kernel, share, len(near), height), len(near), close, green)
+    late = contract(
+        functools.partial(shared_kernel, share, len(far), height),
+        len(far),
+        [crossed[k] for k in far] + [other[k] for k in far],
+        ordered(green, results[0]),
+        kept_rows=direct_rows,
+        scratch_rows=2 * shared_rows,
+    )
+    late = contract(
+        functools.partial(direct_kernel, share, len(far)), len(far), [direct[k] for k in far], green,
+        *late[len(far) :], *late[: len(far)],
+    )
     arrived = [answer(x, k) for k, x in enumerate(list(results) + list(late))]
     return tuple(x.T for x in unpack(n, per, share, vectors, branches, counts, arrived))
 
@@ -404,7 +434,7 @@
     walk_size, shard_count = lax.axis_size("walk"), lax.axis_size(SR)
     per = walkers.shape[0]
     if walk_size == shard_count and per % walk_size == 0 and not walk_size & (walk_size - 1):
-        if 2 <= cholesky.shape[0] <= 8 // (per // walk_size):
+        if cholesky.shape[0] * (per // walk_size) <= 8 and cholesky.shape[1] % 64 == 0:
             return at_the_source(walkers, trial_orbitals, cholesky, branches, counts, field)
     return at_the_target(walkers, trial_orbitals, cholesky, branches, counts, field)
 

time: 61.7 us -> 58.4 us (0.947)
  waiting for transfers between devices: 17.7 us -> 13.9 us
  starting transfers between devices: 20.5 us -> 22.5 us
  Pallas kernels: 19 us -> 17.4 us
    ppermute x12, starting transfers between devices: 8.04 us -> 13 us  [at_the_source(): move = lambda x, k: lax.ppermute(x, SR, [(i, i ^ k) for i in range(n)])]
    ppermute x12, waiting for transfers between devices: 14.8 us -> 11.2 us  [at_the_source(): move = lambda x, k: lax.ppermute(x, SR, [(i, i ^ k) for i in range(n)])]
    ppermute x4, starting transfers between devices: 10.3 us -> 7.05 us  [at_the_source(): lax.ppermute(x, ALL, [(w * n + q, (w ^ q) * n + (q ^ k)) for w, q in pairs])]
    pallas_call x4, Pallas kernels: 4.83 us -> 4.01 us  [the longest x3 3.61 us: contract(): pl.pallas_call(kernel, out_shape=[jax.ShapeDtypeStruct((8, 128), F32)] *...]
    pallas_call x1, Pallas kernels: 2.92 us -> 2.17 us  [select(): pl.pallas_call(functools.partial(select_kernel, n, per, share), out_shape...]
    unnamed x8 -> x12, local copies, waits for them, and re-layouts: 2.82 us -> 2.84 us
  transfers between devices with their start and end apart: 18 -> 18, of which waited for: 6 -> 6; matrix products, arithmetic and copies ran while one was open for 0% -> 0% of each run, Pallas kernels for 28% -> 27%
where the time goes in v3:
time: 58.4 us; the launch traced here: 58.1 us
  starting transfers between devices  22.5 us (39%)
  Pallas kernels  17.4 us (30%)
  waiting for transfers between devices  13.9 us (24%)
  local copies, waits for them, and re-layouts  2.86 us (5%)
  between operations  1.45 us (2%)
    ppermute x12, starting transfers between devices, at_the_source(): move = lambda x, k: lax.ppermute(x, SR, [(i, i ^ k) for i in range(n)])  13 us
    ppermute x12, waiting for transfers between devices, at_the_source(): move = lambda x, k: lax.ppermute(x, SR, [(i, i ^ k) for i in range(n)])  11.2 us
    pallas_call x1, Pallas kernels, make_green(): pl.pallas_call(functools.partial(green_kernel, n, share), out_shape=jax.S...  9.12 us
    ppermute x4, starting transfers between devices, at_the_source(): lax.ppermute(x, ALL, [(w * n + q, (w ^ q) * n + (q ^ k)) for w, q in pairs])  7.05 us
    pallas_call x3, Pallas kernels, contract(): pl.pallas_call(kernel, out_shape=[jax.ShapeDtypeStruct((8, 128), F32)] *...  3.61 us
    unnamed x12, local copies, waits for them, and re-layouts  2.84 us
    ppermute x4, waiting for transfers between devices, at_the_source(): lax.ppermute(x, ALL, [(w * n + q, (w ^ q) * n + (q ^ k)) for w, q in pairs])  2.68 us
    pallas_call x1, Pallas kernels, select(): pl.pallas_call(functools.partial(select_kernel, n, per, share), out_shape...  2.17 us
  transfers between devices with their start and end apart: 18, of which 6 were waited for; matrix products, arithmetic and copies ran while one was open for 0% of the time, Pallas kernels for 27%

profile of v3, /device:TPU:0, one launch (start us, length us, event | category | flops | bytes accessed | tf_op | source)
XLA Modules:
  0.0 58.1 jit_solution(8816400761658914670)
XLA Ops:
  0.6 0.5 collective-permute-start
  1.1 0.0 copy-start
  1.2 1.2 %copy-done = bf16[2,256,1024]{2,1,0:T(8,128)(2,1)S(1)} copy-done((bf16[2,256,1024]{2,1,0:T(8,128)(2,1)S(1)}, bf16[2,256,1024]{2,1,0:T(8,128)(2,1)}, u32[]{:S(2)}) %copy-start) | copy-done | bytes 1048600
  2.4 0.0 copy-start.3
  2.4 0.9 %copy-done.3 = bf16[256,256]{1,0:T(8,128)(2,1)S(1)} copy-done((bf16[256,256]{1,0:T(8,128)(2,1)S(1)}, bf16[256,256]{1,0:T(8,128)(2,1)}, u32[]{:S(2)}) %copy-start.3) | copy-done | bytes 131096
  3.3 0.0 copy-start.4
  3.3 0.7 %copy-done.4 = f32[8,256]{1,0:T(8,128)S(1)} copy-done((f32[8,256]{1,0:T(8,128)S(1)}, f32[8,256]{1,0:T(8,128)}, u32[]{:S(2)}) %copy-start.4) | copy-done | bytes 8216
  4.0 0.0 copy-start.2
  4.0 0.0 copy-start.5
  4.0 0.4 message.1
  4.4 0.0 copy-start.1
  4.4 2.6 %collective-permute-start.4 = (bf16[192,1024]{1,0:T(8,128)(2,1)S(1)}, bf16[192,1024]{1,0:T(8,128)(2,1)S(1)}, u32[]{:S(2)}, u32[]{:S(2)}) collective-permute-start(bf16[192,1024]{1,0:T(8,128)(2,1)S(1)} %get-tuple-element.35), channel_id=1, source_target_pairs={{0,2},{1,3},{2,0},{3,1},{4,6},{5,7},{6,4},{7,5},{8,10},{9,11},{10,... | collective-permute-start | bytes 1179656 | tf_op jit(solution)/shard_map/ppermute | solution.py:320
  7.0 0.1 collective-permute-start.1
  7.1 0.0 copy-done.2
  7.1 0.0 copy-done.5
  7.1 2.2 %select.1 = (bf16[2,256,256]{2,1,0:T(8,128)(2,1)S(1)}, bf16[2,256,256]{2,1,0:T(8,128)(2,1)S(1)}, bf16[2,256,256]{2,1,0:T(8,128)(2,1)S(1)}, bf16[2,256,256]{2,1,0:T(8,128)(2,1)S(1)}) custom-call(s32[32]{0:T(128)S(1)} %copy-done.5, bf16[8,256,256]{2,1,0:T(8,128)(2,1)S(1)} %copy-done.2), custom_call_target="tpu_custom_call" | custom-call | tf_op jit(solution)/shard_map/select/pallas_call | solution.py:67
  9.2 7.7 %collective-permute-done.4.refs_0_ = bf16[192,1024]{1,0:T(8,128)(2,1)S(1)} collective-permute-done((bf16[192,1024]{1,0:T(8,128)(2,1)S(1)}, bf16[192,1024]{1,0:T(8,128)(2,1)S(1)}, u32[]{:S(2)}, u32[]{:S(2)}) %collective-permute-start.4) | collective-permute-done | bytes 393248 | tf_op jit(solution)/shard_map/ppermute | solution.py:320
  16.9 0.9 %collective-permute-start.5 = (bf16[2,256,256]{2,1,0:T(8,128)(2,1)S(1)}, bf16[2,256,256]{2,1,0:T(8,128)(2,1)S(1)}, u32[]{:S(2)}, u32[]{:S(2)}) collective-permute-start(bf16[2,256,256]{2,1,0:T(8,128)(2,1)S(1)} %get-tuple-element.36), channel_id=1, source_target_pairs={{0,3},{1,2},{2,1},{3,0},{4,7},{5,6},{6,5},{7,4},{8,11},{9,10},{10,... | collective-permute-start | bytes 786440 | tf_op jit(solution)/shard_map/ppermute | solution.py:320
  17.8 2.1 %collective-permute-done.1.refs_2_.refs_6_ = bf16[288,256]{1,0:T(8,128)(2,1)S(1)} collective-permute-done((bf16[288,256]{1,0:T(8,128)(2,1)S(1)}, bf16[288,256]{1,0:T(8,128)(2,1)S(1)}, u32[]{:S(2)}, u32[]{:S(2)}) %collective-permute-start.1) | collective-permute-done | bytes 147488 | tf_op jit(solution)/shard_map/ppermute | solution.py:320
  19.9 0.0 collective-permute-done.refs_1_
  19.9 1.8 %collective-permute-start.3 = (bf16[2,256,256]{2,1,0:T(8,128)(2,1)S(1)}, bf16[2,256,256]{2,1,0:T(8,128)(2,1)S(1)}, u32[]{:S(2)}, u32[]{:S(2)}) collective-permute-start(bf16[2,256,256]{2,1,0:T(8,128)(2,1)S(1)} %get-tuple-element.33), channel_id=1, source_target_pairs={{0,2},{1,3},{2,0},{3,1},{4,6},{5,7},{6,4},{7,5},{8,10},{9,11},{10,... | collective-permute-start | bytes 786440 | tf_op jit(solution)/shard_map/ppermute | solution.py:320
  21.7 0.0 collective-permute-start.2
  21.7 0.5 collective-permute-start.6
  22.2 0.0 collective-permute-start.7
  22.2 1.2 %collective-permute-done.6.refs_1_.refs_5_ = bf16[288,256]{1,0:T(8,128)(2,1)S(1)} collective-permute-done((bf16[288,256]{1,0:T(8,128)(2,1)S(1)}, bf16[288,256]{1,0:T(8,128)(2,1)S(1)}, u32[]{:S(2)}, u32[]{:S(2)}) %collective-permute-start.6) | collective-permute-done | bytes 147488 | tf_op jit(solution)/shard_map/ppermute | solution.py:320
  23.4 0.2 collective-permute-done.7.refs_3_.refs_7_
  23.6 0.6 %fields.1 = f32[4,2,256]{2,1,0:T(2,128)S(1)} custom-call(s32[32]{0:T(128)S(1)} %copy-done.5, bf16[288,256]{1,0:T(8,128)(2,1)S(1)} %get-tuple-element.27.refs_0_.refs_4_, bf16[288,256]{1,0:T(8,128)(2,1)S(1)} %collective-permute-done.6.refs_1_.refs_5_, bf16[288,256]{1,0:T(8,128)(2,1)S(1)} %collective-permute-done.1.refs_2_.refs_6_, ...), custom_call_target="tpu_custom_call" | custom-call | tf_op jit(solution)/shard_map/fields/pallas_call | solution.py:132
  24.2 0.7 %collective-permute-start.8 = (f32[4,2,256]{2,1,0:T(2,128)S(1)}, f32[4,2,256]{2,1,0:T(2,128)S(1)}, u32[]{:S(2)}, u32[]{:S(2)}) collective-permute-start(f32[4,2,256]{2,1,0:T(2,128)S(1)} %fields.1), channel_id=1, source_target_pairs={{0,0},{1,5},{2,10},{3,15},{4,4},{5,1},{6,14},{7,11},{8,8},{9,13},{... | collective-permute-start | bytes 24584 | tf_op jit(solution)/shard_map/ppermute | solution.py:322
  24.9 0.0 copy-done.1
  24.9 0.0 collective-permute-done.8.refs_8_
  25.0 6.0 %collective-permute-start.11 = (bf16[128,1024]{1,0:T(8,128)(2,1)S(1)}, bf16[128,1024]{1,0:T(8,128)(2,1)S(1)}, u32[]{:S(2)}, u32[]{:S(2)}) collective-permute-start(bf16[128,1024]{1,0:T(8,128)(2,1)S(1)} %slice.4), channel_id=1, source_target_pairs={{0,2},{1,3},{2,0},{3,1},{4,6},{5,7},{6,4},{7,5},{8,10},{9,11},{10,... | collective-permute-start | bytes 786440 | tf_op jit(solution)/shard_map/ppermute | solution.py:320
  31.0 1.8 %collective-permute-start.14 = (bf16[192,1024]{1,0:T(8,128)(2,1)S(1)}, bf16[192,1024]{1,0:T(8,128)(2,1)S(1)}, u32[]{:S(2)}, u32[]{:S(2)}) collective-permute-start(bf16[192,1024]{1,0:T(8,128)(2,1)S(1)} %collective-permute-done.4.refs_0_), channel_id=1, source_target_pairs={{0,4},{4,0},{8,12},{12,8},{1,5},{5,1},{9,13},{13,9},{2,6},{6,2},{1... | collective-permute-start | bytes 1179656 | tf_op jit(solution)/shard_map/ppermute | solution.py:321
  32.8 0.0 collective-permute-done.5.refs_3_
  32.8 0.0 collective-permute-done.3.refs_2_
  32.8 0.0 collective-permute-done.2.refs_1_
  32.8 9.1 %green.1.refs_2_.refs_4_ = bf16[1024,512]{1,0:T(8,128)(2,1)S(1)} custom-call(bf16[2,256,256]{2,1,0:T(8,128)(2,1)S(1)} %get-tuple-element.29.refs_0_, bf16[2,256,256]{2,1,0:T(8,128)(2,1)S(1)} %collective-permute-done.2.refs_1_, bf16[2,256,256]{2,1,0:T(8,128)(2,1)S(1)} %collective-permute-done.3.refs_2_, ...), custom_call_target="tpu_custom_call" | custom-call | flops 5100273664 | bytes 3145728 | tf_op jit(solution)/shard_map/green/pallas_call | solution.py:196
  41.9 0.0 collective-permute-done.14.refs_2_
  41.9 0.1 collective-permute-start.15
  42.0 0.5 collective-permute-start.13
  42.5 0.0 collective-permute-done.11.refs_0_
  42.5 0.1 collective-permute-start.12
  42.6 1.5 %contract.3 = (f32[8,128]{1,0:T(8,128)S(1)}, f32[8,128]{1,0:T(8,128)S(1)}) custom-call(bf16[512,1024]{1,0:T(8,128)(2,1)S(1)} %bitcast.6, bf16[512,1024]{1,0:T(8,128)(2,1)S(1)} %collective-permute-done.refs_1_, bf16[1024,512]{1,0:T(8,128)(2,1)S(1)} %green.1.refs_2_.refs_4_), custom_call_target="tpu_custom_call" | custom-call | flops 1073741824 | bytes 3145728 | tf_op jit(solution)/shard_map/contract/pallas_call | solution.py:266
  44.1 0.7 %collective-permute-start.9 = (f32[8,128]{1,0:T(8,128)S(1)}, f32[8,128]{1,0:T(8,128)S(1)}, u32[]{:S(2)}, u32[]{:S(2)}) collective-permute-start(f32[8,128]{1,0:T(8,128)S(1)} %get-tuple-element.37), channel_id=1, source_target_pairs={{0,0},{1,5},{2,10},{3,15},{4,4},{5,1},{6,14},{7,11},{8,8},{9,13},{... | collective-permute-start | bytes 12296 | tf_op jit(solution)/shard_map/ppermute | solution.py:323
  44.8 1.8 %collective-permute-start.10 = (f32[8,128]{1,0:T(8,128)S(1)}, f32[8,128]{1,0:T(8,128)S(1)}, u32[]{:S(2)}, u32[]{:S(2)}) collective-permute-start(f32[8,128]{1,0:T(8,128)S(1)} %get-tuple-element.38), channel_id=1, source_target_pairs={{0,1},{1,4},{2,11},{3,14},{4,5},{5,0},{6,15},{7,10},{8,9},{9,12},{... | collective-permute-start | bytes 12296 | tf_op jit(solution)/shard_map/ppermute | solution.py:323
  46.6 0.0 collective-permute-done.15.refs_3_
  46.6 0.0 collective-permute-done.13.refs_1_
  46.6 1.4 %contract.4 = (f32[8,128]{1,0:T(8,128)S(1)}, f32[8,128]{1,0:T(8,128)S(1)}, f32[128,512]{1,0:T(8,128)S(1)}, f32[128,512]{1,0:T(8,128)S(1)}) custom-call(bf16[192,1024]{1,0:T(8,128)(2,1)S(1)} %collective-permute-done.4.refs_0_, bf16[192,1024]{1,0:T(8,128)(2,1)S(1)} %collective-permute-done.13.refs_1_, bf16[192,1024]{1,0:T(8,128)(2,1)S(1)} %collective-permute-done.14.refs_2_, ...), custom_call_target="tpu_custom_call" | custom-call | flops 805306368 | bytes 2621440 | tf_op jit(solution)/shard_map/contract/pallas_call | solution.py:266
  48.0 0.0 collective-permute-done.12.refs_1_
  48.0 0.7 %contract.5 = (f32[8,128]{1,0:T(8,128)S(1)}, f32[8,128]{1,0:T(8,128)S(1)}) custom-call(bf16[128,1024]{1,0:T(8,128)(2,1)S(1)} %collective-permute-done.11.refs_0_, bf16[128,1024]{1,0:T(8,128)(2,1)S(1)} %collective-permute-done.12.refs_1_, bf16[1024,512]{1,0:T(8,128)(2,1)S(1)} %green.1.refs_2_.refs_4_, f32[128,512]{1,0:T(8,128)S(1)} %get-tuple-element.44.refs_3_, ...), custom_call_target="tpu_custom_call" | custom-call | flops 268435456 | bytes 1572864 | tf_op jit(solution)/shard_map/contract/pallas_call | solution.py:266
  48.7 2.2 %collective-permute-start.16 = (f32[8,128]{1,0:T(8,128)S(1)}, f32[8,128]{1,0:T(8,128)S(1)}, u32[]{:S(2)}, u32[]{:S(2)}) collective-permute-start(f32[8,128]{1,0:T(8,128)S(1)} %get-tuple-element.48), channel_id=1, source_target_pairs={{0,2},{1,7},{2,8},{3,13},{4,6},{5,3},{6,12},{7,9},{8,10},{9,15},{1... | collective-permute-start | bytes 12296 | tf_op jit(solution)/shard_map/ppermute | solution.py:323
  50.9 2.4 %collective-permute-start.17 = (f32[8,128]{1,0:T(8,128)S(1)}, f32[8,128]{1,0:T(8,128)S(1)}, u32[]{:S(2)}, u32[]{:S(2)}) collective-permute-start(f32[8,128]{1,0:T(8,128)S(1)} %get-tuple-element.49), channel_id=1, source_target_pairs={{0,3},{1,6},{2,9},{3,12},{4,7},{5,2},{6,13},{7,8},{8,11},{9,14},{1... | collective-permute-start | bytes 12296 | tf_op jit(solution)/shard_map/ppermute | solution.py:323
  53.9 0.0 collective-permute-done.10.refs_1_
  54.0 0.0 collective-permute-done.9.refs_0_
  54.0 1.7 %collective-permute-done.16.refs_2_ = f32[8,128]{1,0:T(8,128)S(1)} collective-permute-done((f32[8,128]{1,0:T(8,128)S(1)}, f32[8,128]{1,0:T(8,128)S(1)}, u32[]{:S(2)}, u32[]{:S(2)}) %collective-permute-start.16) | collective-permute-done | bytes 4128 | tf_op jit(solution)/shard_map/ppermute | solution.py:323
  55.7 0.9 %collective-permute-done.17.refs_3_ = f32[8,128]{1,0:T(8,128)S(1)} collective-permute-done((f32[8,128]{1,0:T(8,128)S(1)}, f32[8,128]{1,0:T(8,128)S(1)}, u32[]{:S(2)}, u32[]{:S(2)}) %collective-permute-start.17) | collective-permute-done | bytes 4128 | tf_op jit(solution)/shard_map/ppermute | solution.py:323
  56.6 1.5 %unpack.1 = (f32[2,8]{1,0:T(2,128)}, f32[2,8]{1,0:T(2,128)}) custom-call(s32[32]{0:T(128)S(1)} %copy-done.5, s32[1]{0:T(128)S(6)} %copy.8.counts, f32[8,128]{1,0:T(8,128)S(1)} %collective-permute-done.9.refs_0_, f32[8,128]{1,0:T(8,128)S(1)} %collective-permute-done.10.refs_1_, f32[8,128]{1,0:T(8,128)S(1)} %collective-permute-done.16.refs_2_, ...), custom_call_target="tpu_custom_call" | custom-call | tf_op jit(solution)/shard_map/unpack/pallas_call | solution.py:303
  (1 shorter events, 0.0 us)
Async XLA Ops:
  0.6 19.3 %collective-permute-start = (bf16[512,1024]{1,0:T(8,128)(2,1)}, bf16[512,1024]{1,0:T(8,128)(2,1)S(1)}, u32[]{:S(2)}, u32[]{:S(2)}) collective-permute-start(bf16[512,1024]{1,0:T(8,128)(2,1)} %bitcast.3), channel_id=1, source_target_pairs={{0,1},{1,0},{2,3},{3,2},{4,5},{5,4},{6,7},{7,6},{8,9},{9,8},{10,11... | collective-permute-start | bytes 3145736 | tf_op jit(solution)/shard_map/ppermute | solution.py:320
  1.1 1.2 %copy-start = (bf16[2,256,1024]{2,1,0:T(8,128)(2,1)S(1)}, bf16[2,256,1024]{2,1,0:T(8,128)(2,1)}, u32[]{:S(2)}) copy-start(bf16[2,256,1024]{2,1,0:T(8,128)(2,1)} %param.8) | copy-start | bytes 3145732
  2.4 0.9 %copy-start.3 = (bf16[256,256]{1,0:T(8,128)(2,1)S(1)}, bf16[256,256]{1,0:T(8,128)(2,1)}, u32[]{:S(2)}) copy-start(bf16[256,256]{1,0:T(8,128)(2,1)} %trial.1) | copy-start | bytes 393220
  3.3 0.7 %copy-start.4 = (f32[8,256]{1,0:T(8,128)S(1)}, f32[8,256]{1,0:T(8,128)}, u32[]{:S(2)}) copy-start(f32[8,256]{1,0:T(8,128)} %field.1) | copy-start | bytes 24580
  4.0 3.1 %copy-start.2 = (bf16[8,256,256]{2,1,0:T(8,128)(2,1)S(1)}, bf16[8,256,256]{2,1,0:T(8,128)(2,1)}, u32[]{:S(2)}) copy-start(bf16[8,256,256]{2,1,0:T(8,128)(2,1)} %walkers.1) | copy-start | bytes 3145732
  4.0 3.1 %copy-start.5 = (s32[32]{0:T(128)S(1)}, s32[32]{0:T(128)}, u32[]{:S(2)}) copy-start(s32[32]{0:T(128)} %branches.4) | copy-start | bytes 388
  4.4 20.5 %copy-start.1 = (bf16[2,256,1024]{2,1,0:T(8,128)(2,1)S(1)}, bf16[2,256,1024]{2,1,0:T(8,128)(2,1)}, u32[]{:S(2)}) copy-start(bf16[2,256,1024]{2,1,0:T(8,128)(2,1)} %param.8) | copy-start | bytes 3145732
  4.4 12.5 %collective-permute-start.4 = (bf16[192,1024]{1,0:T(8,128)(2,1)S(1)}, bf16[192,1024]{1,0:T(8,128)(2,1)S(1)}, u32[]{:S(2)}, u32[]{:S(2)}) collective-permute-start(bf16[192,1024]{1,0:T(8,128)(2,1)S(1)} %get-tuple-element.35), channel_id=1, source_target_pairs={{0,2},{1,3},{2,0},{3,1},{4,6},{5,7},{6,4},{7,5},{8,10},{9,11},{10,... | collective-permute-start | bytes 1179656 | tf_op jit(solution)/shard_map/ppermute | solution.py:320
  7.0 12.9 %collective-permute-start.1 = (bf16[288,256]{1,0:T(8,128)(2,1)S(1)}, bf16[288,256]{1,0:T(8,128)(2,1)S(1)}, u32[]{:S(2)}, u32[]{:S(2)}) collective-permute-start(bf16[288,256]{1,0:T(8,128)(2,1)S(1)} %get-tuple-element.27.refs_0_.refs_4_), channel_id=1, source_target_pairs={{0,2},{1,3},{2,0},{3,1},{4,6},{5,7},{6,4},{7,5},{8,10},{9,11},{10,... | collective-permute-start | bytes 442376 | tf_op jit(solution)/shard_map/ppermute | solution.py:320
  16.9 15.8 %collective-permute-start.5 = (bf16[2,256,256]{2,1,0:T(8,128)(2,1)S(1)}, bf16[2,256,256]{2,1,0:T(8,128)(2,1)S(1)}, u32[]{:S(2)}, u32[]{:S(2)}) collective-permute-start(bf16[2,256,256]{2,1,0:T(8,128)(2,1)S(1)} %get-tuple-element.36), channel_id=1, source_target_pairs={{0,3},{1,2},{2,1},{3,0},{4,7},{5,6},{6,5},{7,4},{8,11},{9,10},{10,... | collective-permute-start | bytes 786440 | tf_op jit(solution)/shard_map/ppermute | solution.py:320
  19.9 12.9 %collective-permute-start.3 = (bf16[2,256,256]{2,1,0:T(8,128)(2,1)S(1)}, bf16[2,256,256]{2,1,0:T(8,128)(2,1)S(1)}, u32[]{:S(2)}, u32[]{:S(2)}) collective-permute-start(bf16[2,256,256]{2,1,0:T(8,128)(2,1)S(1)} %get-tuple-element.33), channel_id=1, source_target_pairs={{0,2},{1,3},{2,0},{3,1},{4,6},{5,7},{6,4},{7,5},{8,10},{9,11},{10,... | collective-permute-start | bytes 786440 | tf_op jit(solution)/shard_map/ppermute | solution.py:320
  21.7 11.1 %collective-permute-start.2 = (bf16[2,256,256]{2,1,0:T(8,128)(2,1)S(1)}, bf16[2,256,256]{2,1,0:T(8,128)(2,1)S(1)}, u32[]{:S(2)}, u32[]{:S(2)}) collective-permute-start(bf16[2,256,256]{2,1,0:T(8,128)(2,1)S(1)} %get-tuple-element.31), channel_id=1, source_target_pairs={{0,1},{1,0},{2,3},{3,2},{4,5},{5,4},{6,7},{7,6},{8,9},{9,8},{10,11... | collective-permute-start | bytes 786440 | tf_op jit(solution)/shard_map/ppermute | solution.py:320
  21.7 1.7 %collective-permute-start.6 = (bf16[288,256]{1,0:T(8,128)(2,1)S(1)}, bf16[288,256]{1,0:T(8,128)(2,1)S(1)}, u32[]{:S(2)}, u32[]{:S(2)}) collective-permute-start(bf16[288,256]{1,0:T(8,128)(2,1)S(1)} %get-tuple-element.27.refs_0_.refs_4_), channel_id=1, source_target_pairs={{0,1},{1,0},{2,3},{3,2},{4,5},{5,4},{6,7},{7,6},{8,9},{9,8},{10,11... | collective-permute-start | bytes 442376 | tf_op jit(solution)/shard_map/ppermute | solution.py:320
  22.2 1.4 %collective-permute-start.7 = (bf16[288,256]{1,0:T(8,128)(2,1)S(1)}, bf16[288,256]{1,0:T(8,128)(2,1)S(1)}, u32[]{:S(2)}, u32[]{:S(2)}) collective-permute-start(bf16[288,256]{1,0:T(8,128)(2,1)S(1)} %collective-permute-done.1.refs_2_.refs_6_), channel_id=1, source_target_pairs={{0,1},{1,0},{2,3},{3,2},{4,5},{5,4},{6,7},{7,6},{8,9},{9,8},{10,11... | collective-permute-start | bytes 442376 | tf_op jit(solution)/shard_map/ppermute | solution.py:320
  24.2 0.7 %collective-permute-start.8 = (f32[4,2,256]{2,1,0:T(2,128)S(1)}, f32[4,2,256]{2,1,0:T(2,128)S(1)}, u32[]{:S(2)}, u32[]{:S(2)}) collective-permute-start(f32[4,2,256]{2,1,0:T(2,128)S(1)} %fields.1), channel_id=1, source_target_pairs={{0,0},{1,5},{2,10},{3,15},{4,4},{5,1},{6,14},{7,11},{8,8},{9,13},{... | collective-permute-start | bytes 24584 | tf_op jit(solution)/shard_map/ppermute | solution.py:322
  25.0 17.6 %collective-permute-start.11 = (bf16[128,1024]{1,0:T(8,128)(2,1)S(1)}, bf16[128,1024]{1,0:T(8,128)(2,1)S(1)}, u32[]{:S(2)}, u32[]{:S(2)}) collective-permute-start(bf16[128,1024]{1,0:T(8,128)(2,1)S(1)} %slice.4), channel_id=1, source_target_pairs={{0,2},{1,3},{2,0},{3,1},{4,6},{5,7},{6,4},{7,5},{8,10},{9,11},{10,... | collective-permute-start | bytes 786440 | tf_op jit(solution)/shard_map/ppermute | solution.py:320
  31.0 11.0 %collective-permute-start.14 = (bf16[192,1024]{1,0:T(8,128)(2,1)S(1)}, bf16[192,1024]{1,0:T(8,128)(2,1)S(1)}, u32[]{:S(2)}, u32[]{:S(2)}) collective-permute-start(bf16[192,1024]{1,0:T(8,128)(2,1)S(1)} %collective-permute-done.4.refs_0_), channel_id=1, source_target_pairs={{0,4},{4,0},{8,12},{12,8},{1,5},{5,1},{9,13},{13,9},{2,6},{6,2},{1... | collective-permute-start | bytes 1179656 | tf_op jit(solution)/shard_map/ppermute | solution.py:321
  41.9 4.7 %collective-permute-start.15 = (bf16[192,1024]{1,0:T(8,128)(2,1)S(1)}, bf16[192,1024]{1,0:T(8,128)(2,1)S(1)}, u32[]{:S(2)}, u32[]{:S(2)}) collective-permute-start(bf16[192,1024]{1,0:T(8,128)(2,1)S(1)} %collective-permute-done.14.refs_2_), channel_id=1, source_target_pairs={{0,1},{1,0},{2,3},{3,2},{4,5},{5,4},{6,7},{7,6},{8,9},{9,8},{10,11... | collective-permute-start | bytes 1179656 | tf_op jit(solution)/shard_map/ppermute | solution.py:320
  42.0 4.6 %collective-permute-start.13 = (bf16[192,1024]{1,0:T(8,128)(2,1)S(1)}, bf16[192,1024]{1,0:T(8,128)(2,1)S(1)}, u32[]{:S(2)}, u32[]{:S(2)}) collective-permute-start(bf16[192,1024]{1,0:T(8,128)(2,1)S(1)} %collective-permute-done.4.refs_0_), channel_id=1, source_target_pairs={{0,1},{1,0},{2,3},{3,2},{4,5},{5,4},{6,7},{7,6},{8,9},{9,8},{10,11... | collective-permute-start | bytes 1179656 | tf_op jit(solution)/shard_map/ppermute | solution.py:320
  42.5 5.5 %collective-permute-start.12 = (bf16[128,1024]{1,0:T(8,128)(2,1)S(1)}, bf16[128,1024]{1,0:T(8,128)(2,1)S(1)}, u32[]{:S(2)}, u32[]{:S(2)}) collective-permute-start(bf16[128,1024]{1,0:T(8,128)(2,1)S(1)} %collective-permute-done.11.refs_0_), channel_id=1, source_target_pairs={{0,1},{1,0},{2,3},{3,2},{4,5},{5,4},{6,7},{7,6},{8,9},{9,8},{10,11... | collective-permute-start | bytes 786440 | tf_op jit(solution)/shard_map/ppermute | solution.py:320
  44.1 9.8 %collective-permute-start.9 = (f32[8,128]{1,0:T(8,128)S(1)}, f32[8,128]{1,0:T(8,128)S(1)}, u32[]{:S(2)}, u32[]{:S(2)}) collective-permute-start(f32[8,128]{1,0:T(8,128)S(1)} %get-tuple-element.37), channel_id=1, source_target_pairs={{0,0},{1,5},{2,10},{3,15},{4,4},{5,1},{6,14},{7,11},{8,8},{9,13},{... | collective-permute-start | bytes 12296 | tf_op jit(solution)/shard_map/ppermute | solution.py:323
  44.8 9.2 %collective-permute-start.10 = (f32[8,128]{1,0:T(8,128)S(1)}, f32[8,128]{1,0:T(8,128)S(1)}, u32[]{:S(2)}, u32[]{:S(2)}) collective-permute-start(f32[8,128]{1,0:T(8,128)S(1)} %get-tuple-element.38), channel_id=1, source_target_pairs={{0,1},{1,4},{2,11},{3,14},{4,5},{5,0},{6,15},{7,10},{8,9},{9,12},{... | collective-permute-start | bytes 12296 | tf_op jit(solution)/shard_map/ppermute | solution.py:323
  48.7 7.0 %collective-permute-start.16 = (f32[8,128]{1,0:T(8,128)S(1)}, f32[8,128]{1,0:T(8,128)S(1)}, u32[]{:S(2)}, u32[]{:S(2)}) collective-permute-start(f32[8,128]{1,0:T(8,128)S(1)} %get-tuple-element.48), channel_id=1, source_target_pairs={{0,2},{1,7},{2,8},{3,13},{4,6},{5,3},{6,12},{7,9},{8,10},{9,15},{1... | collective-permute-start | bytes 12296 | tf_op jit(solution)/shard_map/ppermute | solution.py:323
  50.9 5.7 %collective-permute-start.17 = (f32[8,128]{1,0:T(8,128)S(1)}, f32[8,128]{1,0:T(8,128)S(1)}, u32[]{:S(2)}, u32[]{:S(2)}) collective-permute-start(f32[8,128]{1,0:T(8,128)S(1)} %get-tuple-element.49), channel_id=1, source_target_pairs={{0,3},{1,6},{2,9},{3,12},{4,7},{5,2},{6,13},{7,8},{8,11},{9,14},{1... | collective-permute-start | bytes 12296 | tf_op jit(solution)/shard_map/ppermute | solution.py:323

commit v4 on v3

--- a/solution.py
+++ b/solution.py
@@ -8,6 +8,7 @@
 from jax.sharding import PartitionSpec as P
 
 ITERS = 10
+EARLY = 3
 SR = ("slab", "row")
 ALL = ("walk", "slab", "row")
 F32 = jnp.float32
@@ -75,44 +76,29 @@
     )(branches, walkers)
 
 
-def message_kernel(trial, field, cholesky, out, shared, terms, sems):
-    walk, _ = place()
-    rows, height, count = trial.shape[0], cholesky.shape[0], shared.shape[0]
-    start = height - 2 * count + (walk & 1) * count
-    copies = [
-        pltpu.make_async_copy(cholesky.at[pl.ds(pl.multiple_of(start, 16), count)], shared, sems.at[0]),
-        pltpu.make_async_copy(trial, out.at[pl.ds(0, rows)], sems.at[1]),
-        pltpu.make_async_copy(terms, out.at[pl.ds(rows, terms.shape[0])], sems.at[2]),
-    ]
-    copies[0].start()
-    copies[1].start()
+def message_kernel(trial, field, out):
+    rows = trial.shape[0]
+    out[:rows, :] = trial[...]
     rest, parts = field[...], []
     for _ in range(3):
         parts.append(rest.astype(BF16).astype(F32))
         rest = rest - parts[-1]
-    spare = terms.shape[0] - 3 * field.shape[0]
+    spare = out.shape[0] - rows - 3 * field.shape[0]
     if spare:
         parts.append(jnp.zeros((spare, field.shape[1]), F32))
-    terms[...] = jnp.concatenate(parts, axis=0).astype(BF16)
-    copies[2].start()
-    for copy in copies:
-        copy.wait()
-
-
-def message(trial, field, cholesky, shared_rows):
-    extra = -(-3 * field.shape[0] // 16) * 16
+    out[rows:, :] = jnp.concatenate(parts, axis=0).astype(BF16)
+
+
+def message(trial, field):
+    height = trial.shape[0] + -(-3 * field.shape[0] // 16) * 16
     return pl.pallas_call(
         message_kernel,
-        out_shape=[
-            jax.ShapeDtypeStruct((trial.shape[0] + extra, trial.shape[1]), trial.dtype),
-            jax.ShapeDtypeStruct((shared_rows, cholesky.shape[1]), cholesky.dtype),
-        ],
-        in_specs=[whole(pl.ANY), whole(), whole(pl.ANY)],
-        out_specs=[whole(pl.ANY)] * 2,
-        scratch_shapes=[pltpu.VMEM((extra, trial.shape[1]), BF16), pltpu.SemaphoreType.DMA((3,))],
+        out_shape=jax.ShapeDtypeStruct((height, trial.shape[1]), trial.dtype),
+        in_specs=[whole()] * 2,
+        out_specs=whole(),
         compiler_params=pltpu.CompilerParams(vmem_limit_bytes=SMALL_LIMIT),
         name="message",
-    )(trial, field, cholesky)
+    )(trial, field)
 
 
 def fields_kernel(n, per, share, branches, *refs):
@@ -139,73 +125,105 @@
     )(branches, *messages)
 
 
+def turn_kernel(n, per, share, branches, counts, *refs):
+    messages, turned, masks = refs[:n], refs[n], refs[n + 1]
+    walk, q = place()
+    rows = turned.shape[1] // n
+    for k in range(n):
+        turned[:, k * rows : (k + 1) * rows] = messages[k][:rows, :].T
+    lane = lax.broadcasted_iota(jnp.int32, (1, 128), 1)
+    for k in range(n):
+        places = picks(branches, walk * per, per, walk ^ q ^ k, share)[0]
+        for r in range(share):
+            here = (lane == places[r]) & (places[r] < counts[0])
+            masks[k * share + r : k * share + r + 1, :] = here.astype(F32)
+
+
+def turn(n, per, share, branches, counts, messages):
+    electrons = messages[0].shape[1]
+    rows = n * (messages[0].shape[0] - -(-3 * per // 16) * 16)
+    return pl.pallas_call(
+        functools.partial(turn_kernel, n, per, share),
+        out_shape=[
+            jax.ShapeDtypeStruct((electrons, rows), messages[0].dtype),
+            jax.ShapeDtypeStruct((n * share, 128), F32),
+        ],
+        in_specs=[whole(pltpu.SMEM)] * 2 + [whole()] * n,
+        out_specs=[whole()] * 2,
+        compiler_params=pltpu.CompilerParams(vmem_limit_bytes=SMALL_LIMIT),
+        name="turn",
+    )(branches, counts, *messages)
+
+
+def squared(high, low):
+    mixed = dot(high, low)
+    return dot(high, high) + (mixed + mixed.T)
+
+
 def green_kernel(n, share, *refs):
-    blocks, messages, fields = refs[:n], refs[n : 2 * n], refs[2 * n]
-    green, moved, state = refs[2 * n + 1 :]
-    walk, q = place()
+    blocks, turned, fields = refs[:n], refs[n], refs[n + 1]
+    green, moved, left, right = refs[n + 2 :]
+    q = place()[1]
     rows, electrons = blocks[0].shape[1:]
     spare = jnp.zeros((-share % 8, rows), F32)
-    columns = []
     for k in range(n):
         lines = fields[pl.ds(q ^ k, 1), :, :].reshape(share, rows)
-        columns.append((jnp.concatenate([lines, spare], axis=0) if share % 8 else lines).T)
+        columns = (jnp.concatenate([lines, spare], axis=0) if share % 8 else lines).T
+        for i in range(share):
+            moved[k * rows : (k + 1) * rows, i * electrons : (i + 1) * electrons] = (
+                blocks[k][i].astype(F32) * columns[:, i : i + 1]
+            ).astype(BF16)
+    overlaps = dot(turned[...], moved[...])
     for i in range(share):
-        transposed = jnp.zeros((electrons, electrons), F32)
-        for k in range(n):
-            part = (blocks[k][i].astype(F32) * columns[k][:, i : i + 1]).astype(BF16)
-            moved[i, k * rows : (k + 1) * rows, :] = part
-            transposed = transposed + dot(part, messages[k][:rows, :], ((0,), (0,)))
-        size = jnp.abs(transposed)
+        overlap = overlaps[:, i * electrons : (i + 1) * electrons]
+        size = jnp.abs(overlap)
         scale = jnp.max(jnp.sum(size, axis=0)) * jnp.max(jnp.sum(size, axis=1))
-        start = transposed / scale
-        high, low = split(transposed)
-        start_high, start_low = split(start)
-        across = ((0,), (0,))
-        state[i, :electrons, :] = start
-        state[i, electrons:, :] = dot(high, start_high, across) + (
-            dot(high, start_low, across) + dot(low, start_high, across)
-        )
-
-    def advance(step, carry):
+        left[i] = overlap.T / scale
+        high, low = split(overlap)
+        mixed = dot(high, low, ((1,), (1,)))
+        right[i] = (dot(high, high, ((1,), (1,))) + (mixed + mixed.T)) / scale
+
+    def advance(exact, step, carry):
         for i in range(share):
-            now = state[i]
-            high, low = split(now)
-            right_high, right_low = high[electrons:], low[electrons:]
-            product = dot(high, right_high) + (dot(high, right_low) + dot(low, right_high))
-            state[i] = 2.0 * now - product
+            now, matrix = left[i], right[i]
+            high, low = split(matrix)
+            left_high, left_low = split(now)
+            product = dot(left_high, high)
+            if exact:
+                product = product + (dot(left_high, low) + dot(left_low, high))
+            left[i] = 2.0 * now - product
+            right[i] = 2.0 * matrix - squared(high, low)
         return carry
 
-    lax.fori_loop(0, ITERS - 1, advance, 0)
+    lax.fori_loop(0, EARLY, functools.partial(advance, False), 0)
+    lax.fori_loop(EARLY, ITERS - 1, functools.partial(advance, True), 0)
     for i in range(share):
-        now = state[i]
-        high, low = split(now)
-        left_high, left_low = high[:electrons], low[:electrons]
-        right_high, right_low = high[electrons:], low[electrons:]
-        product = dot(left_high, right_high) + (dot(left_high, right_low) + dot(left_low, right_high))
-        inverse = (2.0 * now[:electrons] - product).astype(BF16)
+        high, low = split(right[i])
+        left_high, left_low = split(left[i])
+        product = dot(left_high, high) + (dot(left_high, low) + dot(left_low, high))
+        inverse = (2.0 * left[i] - product).astype(BF16)
         for k in range(n):
             at = pl.multiple_of((q ^ k) * rows, rows)
             green[pl.ds(at, rows), i * electrons : (i + 1) * electrons] = dot(
-                moved[i, k * rows : (k + 1) * rows, :], inverse
+                moved[k * rows : (k + 1) * rows, i * electrons : (i + 1) * electrons], inverse
             ).astype(BF16)
 
 
-def make_green(n, share, blocks, messages, fields):
+def make_green(n, share, blocks, turned, fields):
     rows, electrons = blocks[0].shape[1:]
-    flops = share * (8 * rows * n * electrons**2 + 2 * 6 * ITERS * electrons**3)
     return pl.pallas_call(
         functools.partial(green_kernel, n, share),
         out_shape=jax.ShapeDtypeStruct((n * rows, share * electrons), BF16),
-        in_specs=[whole()] * (2 * n + 1),
+        in_specs=[whole()] * (n + 2),
         out_specs=whole(),
         scratch_shapes=[
-            pltpu.VMEM((share, n * rows, electrons), BF16),
-            pltpu.VMEM((share, 2 * electrons, electrons), F32),
+            pltpu.VMEM((n * rows, share * electrons), BF16),
+            pltpu.VMEM((share, electrons, electrons), F32),
+            pltpu.VMEM((share, electrons, electrons), F32),
         ],
         compiler_params=pltpu.CompilerParams(vmem_limit_bytes=VMEM_LIMIT),
-        cost_estimate=pl.CostEstimate(flops=flops, bytes_accessed=3 * 2**20, transcendentals=0),
         name="green",
-    )(*blocks, *messages, fields)
+    )(*blocks, turned, fields)
 
 
 def report(share, held, index, upper, lower):
@@ -213,16 +231,14 @@
     row = lax.broadcasted_iota(jnp.int32, (half, half), 0)
     column = lax.broadcasted_iota(jnp.int32, (half, half), 1)
     out_row = lax.broadcasted_iota(jnp.int32, held.shape, 0)
-    lane = lax.broadcasted_iota(jnp.int32, held.shape, 1)
     for i in range(share):
         left, middle, right = 2 * i * half, (2 * i + 1) * half, 2 * (i + 1) * half
         a, b = upper[:, left:middle], upper[:, middle:right]
         c, d = lower[:, left:middle], lower[:, middle:right]
         trace = jnp.sum(jnp.where(row == column, a + d, 0.0))
         exchange = -0.5 * jnp.sum(a * a.T + d * d.T + 2.0 * (b * c.T))
-        here = out_row == index * share + i
-        held = jnp.where(here & (lane == 0), trace, held)
-        held = jnp.where(here & (lane == 1), exchange, held)
+        held = jnp.where(out_row == index * share + i, trace, held)
+        held = jnp.where(out_row == held.shape[0] // 2 + index * share + i, exchange, held)
     return held
 
 
@@ -279,35 +295,28 @@
     )(*vectors, green, *more)
 
 
-def unpack_kernel(n, per, share, branches, counts, *refs):
-    arrived, force, exchange = refs[:n], refs[n], refs[n + 1]
-    walk, q = place()
-    vectors = force.shape[0]
-    walker = lax.broadcasted_iota(jnp.int32, force.shape, 1)
-    vector = lax.broadcasted_iota(jnp.int32, force.shape, 0)
-    force_all = jnp.zeros(force.shape, F32)
-    exchange_all = jnp.zeros(force.shape, F32)
-    for k in range(n):
-        places = picks(branches, walk * per, per, walk ^ q ^ k, share)[0]
-        for r in range(share):
-            for g in range(vectors):
-                here = (walker == places[r]) & (vector == g)
-                force_all = jnp.where(here, arrived[k][g * share + r, 0], force_all)
-                exchange_all = jnp.where(here, arrived[k][g * share + r, 1], exchange_all)
-    living = (walker < counts[0]).astype(F32)
-    force[...] = force_all * living
-    exchange[...] = exchange_all * living
-
-
-def unpack(n, per, share, vectors, branches, counts, arrived):
-    return pl.pallas_call(
-        functools.partial(unpack_kernel, n, per, share),
+def unpack_kernel(n, share, masks, *refs):
+    arrived, outs = refs[:n], refs[n:]
+    vectors, per = outs[0].shape
+    for which, out in enumerate(outs):
+        for g in range(vectors):
+            line = jnp.zeros((1, 128), F32)
+            for k in range(n):
+                for r in range(share):
+                    at = which * (arrived[k].shape[0] // 2) + g * share + r
+                    line = jnp.where(masks[k * share + r : k * share + r + 1, :] > 0.0, arrived[k][at : at + 1, :], line)
+            out[g : g + 1, :] = line[:, :per]
+
+
+def unpack(n, per, share, vectors, masks, arrived):
+    return pl.pallas_call(
+        functools.partial(unpack_kernel, n, share),
         out_shape=[jax.ShapeDtypeStruct((vectors, per), F32)] * 2,
-        in_specs=[whole(pltpu.SMEM)] * (2 + n),
+        in_specs=[whole()] * (1 + n),
         out_specs=[whole()] * 2,
         compiler_params=pltpu.CompilerParams(vmem_limit_bytes=SMALL_LIMIT),
         name="unpack",
-    )(branches, counts, *arrived)
+    )(masks, *arrived)
 
 
 def at_the_source(walkers, trial_orbitals, cholesky, branches, counts, field):
@@ -340,11 +349,13 @@
     rows = cholesky.reshape(vectors * height, cholesky.shape[2])
     direct_rows = height // 2
     shared_rows = (rows.shape[0] - direct_rows) // 2
-    own, shared = message(trial_orbitals, field, rows, shared_rows)
+    at = direct_rows + (lax.axis_index("walk") & 1) * shared_rows
+    shared = lax.dynamic_slice_in_dim(rows, at, shared_rows, 0)
+    sends = select(n, per, share, branches, walkers)
+    own = message(ordered(trial_orbitals, sends[0]), field)
     messages = {0: own, **spread(own)}
     messages.update({k: move(own, k) for k in near[1:]})
     messages = [messages[k] for k in range(n)]
-    sends = select(n, per, share, ordered(branches, own), walkers)
     crossed = {k: move(shared, k) for k in heads}
     close = [rows] + [move(rows, k) for k in near[1:]]
     early = [messages[far[0]], *close[1:]]
@@ -352,9 +363,10 @@
         move(ordered(sends[k], *(crossed.values() if k == n - 1 else early)), k) for k in range(1, n)
     ]
     asked = ask(pick_fields(n, per, share, branches, messages))
-    direct = {k: move(ordered(rows[:direct_rows], asked), k) for k in heads}
+    turned, masks = turn(n, per, share, branches, counts, messages)
+    direct = {k: move(ordered(rows[:direct_rows], asked, turned), k) for k in heads}
     other = {k: swap(x) for k, x in crossed.items()}
-    green = make_green(n, share, blocks, messages, asked)
+    green = make_green(n, share, blocks, turned, asked)
     crossed, other, direct = (along({k: ordered(x, green) for k, x in held.items()}) for held in (crossed, other, direct))
     results = contract(functools.partial(near_kernel, share, len(near), height), len(near), close, green)
     late = contract(
@@ -370,7 +382,7 @@
         *late[len(far) :], *late[: len(far)],
     )
     arrived = [answer(x, k) for k, x in enumerate(list(results) + list(late))]
-    return tuple(x.T for x in unpack(n, per, share, vectors, branches, counts, arrived))
+    return tuple(x.T for x in unpack(n, per, share, vectors, masks, arrived))
 
 
 def newton_schulz(intersection):
@@ -434,7 +446,7 @@
     walk_size, shard_count = lax.axis_size("walk"), lax.axis_size(SR)
     per = walkers.shape[0]
     if walk_size == shard_count and per % walk_size == 0 and not walk_size & (walk_size - 1):
-        if cholesky.shape[0] * (per // walk_size) <= 8 and cholesky.shape[1] % 64 == 0:
+        if cholesky.shape[0] * (per // walk_size) <= 4 and cholesky.shape[1] % 64 == 0 and per <= 128:
             return at_the_source(walkers, trial_orbitals, cholesky, branches, counts, field)
     return at_the_target(walkers, trial_orbitals, cholesky, branches, counts, field)
 

time: 58.4 us -> 55.7 us (0.954)
  Pallas kernels: 17.4 us -> 14.8 us
  waiting for transfers between devices: 13.9 us -> 15.1 us
  starting transfers between devices: 22.5 us -> 21.8 us
    ppermute x4, waiting for transfers between devices: 2.68 us -> 4.81 us  [at_the_source(): lax.ppermute(x, ALL, [(w * n + q, (w ^ q) * n + (q ^ k)) for w, q in pairs])]
    pallas_call x1, Pallas kernels: 9.12 us -> 7.02 us  [make_green(): pl.pallas_call(functools.partial(green_kernel, n, share), out_shape=jax.S...]
    unnamed x12 -> x10, local copies, waits for them, and re-layouts: 2.84 us -> 1.24 us
    dynamic_slice x0 -> x1, local copies, waits for them, and re-layouts: none -> 1.06 us  [at_the_source(): shared = lax.dynamic_slice_in_dim(rows, at, shared_rows, 0)]
    ppermute x12, waiting for transfers between devices: 11.2 us -> 10.3 us  [at_the_source(): move = lambda x, k: lax.ppermute(x, SR, [(i, i ^ k) for i in range(n)])]
    ppermute x12, starting transfers between devices: 13 us -> 12.1 us  [at_the_source(): move = lambda x, k: lax.ppermute(x, SR, [(i, i ^ k) for i in range(n)])]
    pallas_call x2 -> x3, Pallas kernels: 1.9 us -> 1.39 us  [the longest x1 0.8 us: turn(): pl.pallas_call(functools.partial(turn_kernel, n, per, share), out_shape=[...]
  transfers between devices with their start and end apart: 18 -> 18, of which waited for: 6 -> 5; matrix products, arithmetic and copies ran while one was open for 0% -> 2% of each run, Pallas kernels for 27% -> 26%
where the time goes in v4:
time: 55.7 us; the launch traced here: 55.5 us
  starting transfers between devices  21.8 us (39%)
  waiting for transfers between devices  15.1 us (27%)
  Pallas kernels  14.8 us (27%)
  local copies, waits for them, and re-layouts  2.32 us (4%)
  between operations  1.44 us (3%)
    ppermute x12, starting transfers between devices, at_the_source(): move = lambda x, k: lax.ppermute(x, SR, [(i, i ^ k) for i in range(n)])  12.1 us
    ppermute x12, waiting for transfers between devices, at_the_source(): move = lambda x, k: lax.ppermute(x, SR, [(i, i ^ k) for i in range(n)])  10.3 us
    ppermute x4, starting transfers between devices, at_the_source(): lax.ppermute(x, ALL, [(w * n + q, (w ^ q) * n + (q ^ k)) for w, q in pairs])  7.04 us
    pallas_call x1, Pallas kernels, make_green(): pl.pallas_call(functools.partial(green_kernel, n, share), out_shape=jax.S...  7.02 us
    ppermute x4, waiting for transfers between devices, at_the_source(): lax.ppermute(x, ALL, [(w * n + q, (w ^ q) * n + (q ^ k)) for w, q in pairs])  4.81 us
    pallas_call x3, Pallas kernels, contract(): pl.pallas_call(kernel, out_shape=[jax.ShapeDtypeStruct((8, 128), F32)] *...  3.63 us
    pallas_call x1, Pallas kernels, select(): pl.pallas_call(functools.partial(select_kernel, n, per, share), out_shape...  2.17 us
    ppermute x1, starting transfers between devices, at_the_source(): swap = lambda x: lax.ppermute(x, 'walk', [(w, w ^ 1) for w in range(n)])  2.03 us
  transfers between devices with their start and end apart: 18, of which 5 were waited for; matrix products, arithmetic and copies ran while one was open for 2% of the time, Pallas kernels for 26%

profile of v4, /device:TPU:0, one launch (start us, length us, event | category | flops | bytes accessed | tf_op | source)
XLA Modules:
  0.0 55.5 jit_solution(9262144814986479834)
XLA Ops:
  0.6 0.5 collective-permute-start.3
  1.1 0.0 copy-start.4
  1.2 0.0 copy-start.2
  1.2 0.0 copy-start.3
  1.2 1.1 %constant_dynamic-slice_fusion = bf16[192,1024]{1,0:T(8,128)(2,1)S(1)} fusion(bf16[512,1024]{1,0:T(8,128)(2,1)} %bitcast.4, s32[]{:T(128)S(6)} %select_n.3), kind=kLoop, calls=%fused_computation | loop fusion | bytes 786436 | tf_op jit(solution)/shard_map/dynamic_slice | solution.py:353
  2.2 2.6 %collective-permute-start.6 = (bf16[192,1024]{1,0:T(8,128)(2,1)S(1)}, bf16[192,1024]{1,0:T(8,128)(2,1)S(1)}, u32[]{:S(2)}, u32[]{:S(2)}) collective-permute-start(bf16[192,1024]{1,0:T(8,128)(2,1)S(1)} %constant_dynamic-slice_fusion), channel_id=1, source_target_pairs={{0,2},{1,3},{2,0},{3,1},{4,6},{5,7},{6,4},{7,5},{8,10},{9,11},{10,... | collective-permute-start | bytes 1179656 | tf_op jit(solution)/shard_map/ppermute | solution.py:329
  4.8 0.0 copy-done.4
  4.8 0.0 copy-start
  4.8 1.2 %copy-done = bf16[8,256,256]{2,1,0:T(8,128)(2,1)S(1)} copy-done((bf16[8,256,256]{2,1,0:T(8,128)(2,1)S(1)}, bf16[8,256,256]{2,1,0:T(8,128)(2,1)}, u32[]{:S(2)}) %copy-start) | copy-done | bytes 1048600
  6.0 0.0 copy-start.1
  6.1 2.2 %select.1 = (bf16[2,256,256]{2,1,0:T(8,128)(2,1)S(1)}, bf16[2,256,256]{2,1,0:T(8,128)(2,1)S(1)}, bf16[2,256,256]{2,1,0:T(8,128)(2,1)S(1)}, bf16[2,256,256]{2,1,0:T(8,128)(2,1)S(1)}) custom-call(s32[32]{0:T(128)S(1)} %copy-done.4, bf16[8,256,256]{2,1,0:T(8,128)(2,1)S(1)} %copy-done), custom_call_target="tpu_custom_call" | custom-call | tf_op jit(solution)/shard_map/select/pallas_call | solution.py:68
  8.2 0.0 copy-done.2
  8.2 0.0 copy-done.3
  8.3 0.1 collective-permute-start.1
  8.4 6.4 %collective-permute-done.6.refs_0_ = bf16[192,1024]{1,0:T(8,128)(2,1)S(1)} collective-permute-done((bf16[192,1024]{1,0:T(8,128)(2,1)S(1)}, bf16[192,1024]{1,0:T(8,128)(2,1)S(1)}, u32[]{:S(2)}, u32[]{:S(2)}) %collective-permute-start.6) | collective-permute-done | bytes 393248 | tf_op jit(solution)/shard_map/ppermute | solution.py:329
  14.8 2.0 %collective-permute-start.14 = (bf16[192,1024]{1,0:T(8,128)(2,1)S(1)}, bf16[192,1024]{1,0:T(8,128)(2,1)S(1)}, u32[]{:S(2)}, u32[]{:S(2)}) collective-permute-start(bf16[192,1024]{1,0:T(8,128)(2,1)S(1)} %collective-permute-done.6.refs_0_), channel_id=1, source_target_pairs={{0,4},{4,0},{8,12},{12,8},{1,5},{5,1},{9,13},{13,9},{2,6},{6,2},{1... | collective-permute-start | bytes 1179656 | tf_op jit(solution)/shard_map/ppermute | solution.py:330
  16.8 0.0 collective-permute-start
  16.8 1.6 %collective-permute-start.7 = (bf16[2,256,256]{2,1,0:T(8,128)(2,1)S(1)}, bf16[2,256,256]{2,1,0:T(8,128)(2,1)S(1)}, u32[]{:S(2)}, u32[]{:S(2)}) collective-permute-start(bf16[2,256,256]{2,1,0:T(8,128)(2,1)S(1)} %get-tuple-element.35), channel_id=1, source_target_pairs={{0,3},{1,2},{2,1},{3,0},{4,7},{5,6},{6,5},{7,4},{8,11},{9,10},{10,... | collective-permute-start | bytes 786440 | tf_op jit(solution)/shard_map/ppermute | solution.py:329
  18.4 0.0 collective-permute-done.1.refs_2_
  18.4 0.0 collective-permute-done.3.refs_1_
  18.4 0.0 collective-permute-start.4
  18.4 1.0 %collective-permute-start.5 = (bf16[2,256,256]{2,1,0:T(8,128)(2,1)S(1)}, bf16[2,256,256]{2,1,0:T(8,128)(2,1)S(1)}, u32[]{:S(2)}, u32[]{:S(2)}) collective-permute-start(bf16[2,256,256]{2,1,0:T(8,128)(2,1)S(1)} %get-tuple-element.33), channel_id=1, source_target_pairs={{0,2},{1,3},{2,0},{3,1},{4,6},{5,7},{6,4},{7,5},{8,10},{9,11},{10,... | collective-permute-start | bytes 786440 | tf_op jit(solution)/shard_map/ppermute | solution.py:329
  19.5 0.0 collective-permute-done.refs_1_
  19.5 0.2 collective-permute-start.2
  19.7 1.1 %collective-permute-done.2.refs_3_ = bf16[288,256]{1,0:T(8,128)(2,1)S(1)} collective-permute-done((bf16[288,256]{1,0:T(8,128)(2,1)S(1)}, bf16[288,256]{1,0:T(8,128)(2,1)S(1)}, u32[]{:S(2)}, u32[]{:S(2)}) %collective-permute-start.2) | collective-permute-done | bytes 147488 | tf_op jit(solution)/shard_map/ppermute | solution.py:329
  20.8 0.6 %fields.1 = f32[4,2,256]{2,1,0:T(2,128)S(1)} custom-call(s32[32]{0:T(128)S(1)} %copy-done.4, bf16[288,256]{1,0:T(8,128)(2,1)S(1)} %message.1.refs_0_, bf16[288,256]{1,0:T(8,128)(2,1)S(1)} %collective-permute-done.refs_1_, bf16[288,256]{1,0:T(8,128)(2,1)S(1)} %collective-permute-done.1.refs_2_, bf16[288,256]{1,0:T(8,128)(2,1)S(1)} %collective-permute-done.2.refs_3_), custom_call_target="tpu_custom_call" | custom-call | tf_op jit(solution)/shard_map/fields/pallas_call | solution.py:118
  21.5 0.7 %collective-permute-start.8 = (f32[4,2,256]{2,1,0:T(2,128)S(1)}, f32[4,2,256]{2,1,0:T(2,128)S(1)}, u32[]{:S(2)}, u32[]{:S(2)}) collective-permute-start(f32[4,2,256]{2,1,0:T(2,128)S(1)} %fields.1), channel_id=1, source_target_pairs={{0,0},{1,5},{2,10},{3,15},{4,4},{5,1},{6,14},{7,11},{8,8},{9,13},{... | collective-permute-start | bytes 24584 | tf_op jit(solution)/shard_map/ppermute | solution.py:331
  22.1 0.0 copy-done.1
  22.8 0.8 %turn.1 = (bf16[256,1024]{1,0:T(8,128)(2,1)S(1)}, f32[8,128]{1,0:T(8,128)S(1)}) custom-call(s32[32]{0:T(128)S(1)} %copy-done.4, s32[1]{0:T(128)S(6)} %copy.8.counts, bf16[288,256]{1,0:T(8,128)(2,1)S(1)} %message.1.refs_0_, bf16[288,256]{1,0:T(8,128)(2,1)S(1)} %collective-permute-done.refs_1_, bf16[288,256]{1,0:T(8,128)(2,1)S(1)} %collective-permute-done.1.refs_2_, ...), custom_call_target="tpu_custom_call" | custom-call | tf_op jit(solution)/shard_map/turn/pallas_call | solution.py:145
  23.6 0.0 collective-permute-done.8.refs_5_
  23.6 5.3 %collective-permute-start.11 = (bf16[128,1024]{1,0:T(8,128)(2,1)S(1)}, bf16[128,1024]{1,0:T(8,128)(2,1)S(1)}, u32[]{:S(2)}, u32[]{:S(2)}) collective-permute-start(bf16[128,1024]{1,0:T(8,128)(2,1)S(1)} %slice.4), channel_id=1, source_target_pairs={{0,2},{1,3},{2,0},{3,1},{4,6},{5,7},{6,4},{7,5},{8,10},{9,11},{10,... | collective-permute-start | bytes 786440 | tf_op jit(solution)/shard_map/ppermute | solution.py:329
  29.0 0.0 collective-permute-done.7.refs_3_
  29.0 0.0 collective-permute-done.4.refs_1_
  29.0 2.7 %collective-permute-done.5.refs_2_ = bf16[2,256,256]{2,1,0:T(8,128)(2,1)S(1)} collective-permute-done((bf16[2,256,256]{2,1,0:T(8,128)(2,1)S(1)}, bf16[2,256,256]{2,1,0:T(8,128)(2,1)S(1)}, u32[]{:S(2)}, u32[]{:S(2)}) %collective-permute-start.5) | collective-permute-done | bytes 262176 | tf_op jit(solution)/shard_map/ppermute | solution.py:329
  31.7 7.0 %green.1.refs_2_.refs_4_ = bf16[1024,512]{1,0:T(8,128)(2,1)S(1)} custom-call(bf16[2,256,256]{2,1,0:T(8,128)(2,1)S(1)} %get-tuple-element.27.refs_0_, bf16[2,256,256]{2,1,0:T(8,128)(2,1)S(1)} %collective-permute-done.4.refs_1_, bf16[2,256,256]{2,1,0:T(8,128)(2,1)S(1)} %collective-permute-done.5.refs_2_, ...), custom_call_target="tpu_custom_call" | custom-call | tf_op jit(solution)/shard_map/green/pallas_call | solution.py:214
  38.7 0.1 collective-permute-start.13
  38.8 0.0 collective-permute-done.14.refs_2_
  38.8 0.5 collective-permute-start.15
  39.3 0.0 collective-permute-done.11.refs_0_
  39.3 0.1 collective-permute-start.12
  39.4 1.5 %contract.3 = (f32[8,128]{1,0:T(8,128)S(1)}, f32[8,128]{1,0:T(8,128)S(1)}) custom-call(bf16[512,1024]{1,0:T(8,128)(2,1)S(1)} %bitcast.6, bf16[512,1024]{1,0:T(8,128)(2,1)S(1)} %collective-permute-done.3.refs_1_, bf16[1024,512]{1,0:T(8,128)(2,1)S(1)} %green.1.refs_2_.refs_4_), custom_call_target="tpu_custom_call" | custom-call | flops 1073741824 | bytes 3145728 | tf_op jit(solution)/shard_map/contract/pallas_call | solution.py:282
  40.9 0.7 %collective-permute-start.9 = (f32[8,128]{1,0:T(8,128)S(1)}, f32[8,128]{1,0:T(8,128)S(1)}, u32[]{:S(2)}, u32[]{:S(2)}) collective-permute-start(f32[8,128]{1,0:T(8,128)S(1)} %get-tuple-element.37), channel_id=1, source_target_pairs={{0,0},{1,5},{2,10},{3,15},{4,4},{5,1},{6,14},{7,11},{8,8},{9,13},{... | collective-permute-start | bytes 12296 | tf_op jit(solution)/shard_map/ppermute | solution.py:332
  41.6 1.7 %collective-permute-start.10 = (f32[8,128]{1,0:T(8,128)S(1)}, f32[8,128]{1,0:T(8,128)S(1)}, u32[]{:S(2)}, u32[]{:S(2)}) collective-permute-start(f32[8,128]{1,0:T(8,128)S(1)} %get-tuple-element.38), channel_id=1, source_target_pairs={{0,1},{1,4},{2,11},{3,14},{4,5},{5,0},{6,15},{7,10},{8,9},{9,12},{... | collective-permute-start | bytes 12296 | tf_op jit(solution)/shard_map/ppermute | solution.py:332
  43.3 0.0 collective-permute-done.13.refs_1_
  43.3 0.0 collective-permute-done.15.refs_3_
  43.3 1.4 %contract.4 = (f32[8,128]{1,0:T(8,128)S(1)}, f32[8,128]{1,0:T(8,128)S(1)}, f32[128,512]{1,0:T(8,128)S(1)}, f32[128,512]{1,0:T(8,128)S(1)}) custom-call(bf16[192,1024]{1,0:T(8,128)(2,1)S(1)} %collective-permute-done.6.refs_0_, bf16[192,1024]{1,0:T(8,128)(2,1)S(1)} %collective-permute-done.13.refs_1_, bf16[192,1024]{1,0:T(8,128)(2,1)S(1)} %collective-permute-done.14.refs_2_, ...), custom_call_target="tpu_custom_call" | custom-call | flops 805306368 | bytes 2621440 | tf_op jit(solution)/shard_map/contract/pallas_call | solution.py:282
  44.7 0.0 collective-permute-done.12.refs_1_
  44.7 0.7 %contract.5 = (f32[8,128]{1,0:T(8,128)S(1)}, f32[8,128]{1,0:T(8,128)S(1)}) custom-call(bf16[128,1024]{1,0:T(8,128)(2,1)S(1)} %collective-permute-done.11.refs_0_, bf16[128,1024]{1,0:T(8,128)(2,1)S(1)} %collective-permute-done.12.refs_1_, bf16[1024,512]{1,0:T(8,128)(2,1)S(1)} %green.1.refs_2_.refs_4_, f32[128,512]{1,0:T(8,128)S(1)} %get-tuple-element.44.refs_3_, ...), custom_call_target="tpu_custom_call" | custom-call | flops 268435456 | bytes 1572864 | tf_op jit(solution)/shard_map/contract/pallas_call | solution.py:282
  45.5 3.7 %collective-permute-start.16 = (f32[8,128]{1,0:T(8,128)S(1)}, f32[8,128]{1,0:T(8,128)S(1)}, u32[]{:S(2)}, u32[]{:S(2)}) collective-permute-start(f32[8,128]{1,0:T(8,128)S(1)} %get-tuple-element.48), channel_id=1, source_target_pairs={{0,2},{1,7},{2,8},{3,13},{4,6},{5,3},{6,12},{7,9},{8,10},{9,15},{1... | collective-permute-start | bytes 12296 | tf_op jit(solution)/shard_map/ppermute | solution.py:332
  49.2 0.9 %collective-permute-start.17 = (f32[8,128]{1,0:T(8,128)S(1)}, f32[8,128]{1,0:T(8,128)S(1)}, u32[]{:S(2)}, u32[]{:S(2)}) collective-permute-start(f32[8,128]{1,0:T(8,128)S(1)} %get-tuple-element.49), channel_id=1, source_target_pairs={{0,3},{1,6},{2,9},{3,12},{4,7},{5,2},{6,13},{7,8},{8,11},{9,14},{1... | collective-permute-start | bytes 12296 | tf_op jit(solution)/shard_map/ppermute | solution.py:332
  50.1 0.0 collective-permute-done.9.refs_0_
  50.1 0.0 collective-permute-done.10.refs_1_
  50.1 2.3 %collective-permute-done.16.refs_2_ = f32[8,128]{1,0:T(8,128)S(1)} collective-permute-done((f32[8,128]{1,0:T(8,128)S(1)}, f32[8,128]{1,0:T(8,128)S(1)}, u32[]{:S(2)}, u32[]{:S(2)}) %collective-permute-start.16) | collective-permute-done | bytes 4128 | tf_op jit(solution)/shard_map/ppermute | solution.py:332
  52.5 2.5 %collective-permute-done.17.refs_3_ = f32[8,128]{1,0:T(8,128)S(1)} collective-permute-done((f32[8,128]{1,0:T(8,128)S(1)}, f32[8,128]{1,0:T(8,128)S(1)}, u32[]{:S(2)}, u32[]{:S(2)}) %collective-permute-start.17) | collective-permute-done | bytes 4128 | tf_op jit(solution)/shard_map/ppermute | solution.py:332
  54.9 0.6 %unpack.1 = (f32[2,8]{1,0:T(2,128)}, f32[2,8]{1,0:T(2,128)}) custom-call(f32[8,128]{1,0:T(8,128)S(1)} %get-tuple-element.29.masks, f32[8,128]{1,0:T(8,128)S(1)} %collective-permute-done.9.refs_0_, f32[8,128]{1,0:T(8,128)S(1)} %collective-permute-done.10.refs_1_, f32[8,128]{1,0:T(8,128)S(1)} %collective-permute-done.16.refs_2_, ...), custom_call_target="tpu_custom_call" | custom-call | tf_op jit(solution)/shard_map/unpack/pallas_call | solution.py:312
  (2 shorter events, 0.0 us)
Async XLA Ops:
  0.6 17.8 %collective-permute-start.3 = (bf16[512,1024]{1,0:T(8,128)(2,1)}, bf16[512,1024]{1,0:T(8,128)(2,1)S(1)}, u32[]{:S(2)}, u32[]{:S(2)}) collective-permute-start(bf16[512,1024]{1,0:T(8,128)(2,1)} %bitcast.3), channel_id=1, source_target_pairs={{0,1},{1,0},{2,3},{3,2},{4,5},{5,4},{6,7},{7,6},{8,9},{9,8},{10,11... | collective-permute-start | bytes 3145736 | tf_op jit(solution)/shard_map/ppermute | solution.py:329
  1.1 3.7 %copy-start.4 = (s32[32]{0:T(128)S(1)}, s32[32]{0:T(128)}, u32[]{:S(2)}) copy-start(s32[32]{0:T(128)} %branches.5) | copy-start | bytes 388
  1.2 7.1 %copy-start.2 = (bf16[256,256]{1,0:T(8,128)(2,1)S(1)}, bf16[256,256]{1,0:T(8,128)(2,1)}, u32[]{:S(2)}) copy-start(bf16[256,256]{1,0:T(8,128)(2,1)} %trial) | copy-start | bytes 393220
  1.2 7.1 %copy-start.3 = (f32[8,256]{1,0:T(8,128)S(1)}, f32[8,256]{1,0:T(8,128)}, u32[]{:S(2)}) copy-start(f32[8,256]{1,0:T(8,128)} %field.1) | copy-start | bytes 24580
  2.2 12.6 %collective-permute-start.6 = (bf16[192,1024]{1,0:T(8,128)(2,1)S(1)}, bf16[192,1024]{1,0:T(8,128)(2,1)S(1)}, u32[]{:S(2)}, u32[]{:S(2)}) collective-permute-start(bf16[192,1024]{1,0:T(8,128)(2,1)S(1)} %constant_dynamic-slice_fusion), channel_id=1, source_target_pairs={{0,2},{1,3},{2,0},{3,1},{4,6},{5,7},{6,4},{7,5},{8,10},{9,11},{10,... | collective-permute-start | bytes 1179656 | tf_op jit(solution)/shard_map/ppermute | solution.py:329
  4.8 1.2 %copy-start = (bf16[8,256,256]{2,1,0:T(8,128)(2,1)S(1)}, bf16[8,256,256]{2,1,0:T(8,128)(2,1)}, u32[]{:S(2)}) copy-start(bf16[8,256,256]{2,1,0:T(8,128)(2,1)} %walkers.1) | copy-start | bytes 3145732
  6.0 16.1 %copy-start.1 = (bf16[2,256,1024]{2,1,0:T(8,128)(2,1)S(1)}, bf16[2,256,1024]{2,1,0:T(8,128)(2,1)}, u32[]{:S(2)}) copy-start(bf16[2,256,1024]{2,1,0:T(8,128)(2,1)} %param.8) | copy-start | bytes 3145732
  8.3 10.2 %collective-permute-start.1 = (bf16[288,256]{1,0:T(8,128)(2,1)S(1)}, bf16[288,256]{1,0:T(8,128)(2,1)S(1)}, u32[]{:S(2)}, u32[]{:S(2)}) collective-permute-start(bf16[288,256]{1,0:T(8,128)(2,1)S(1)} %message.1.refs_0_), channel_id=1, source_target_pairs={{0,2},{1,3},{2,0},{3,1},{4,6},{5,7},{6,4},{7,5},{8,10},{9,11},{10,... | collective-permute-start | bytes 442376 | tf_op jit(solution)/shard_map/ppermute | solution.py:329
  14.8 24.0 %collective-permute-start.14 = (bf16[192,1024]{1,0:T(8,128)(2,1)S(1)}, bf16[192,1024]{1,0:T(8,128)(2,1)S(1)}, u32[]{:S(2)}, u32[]{:S(2)}) collective-permute-start(bf16[192,1024]{1,0:T(8,128)(2,1)S(1)} %collective-permute-done.6.refs_0_), channel_id=1, source_target_pairs={{0,4},{4,0},{8,12},{12,8},{1,5},{5,1},{9,13},{13,9},{2,6},{6,2},{1... | collective-permute-start | bytes 1179656 | tf_op jit(solution)/shard_map/ppermute | solution.py:330
  16.8 2.6 %collective-permute-start = (bf16[288,256]{1,0:T(8,128)(2,1)S(1)}, bf16[288,256]{1,0:T(8,128)(2,1)S(1)}, u32[]{:S(2)}, u32[]{:S(2)}) collective-permute-start(bf16[288,256]{1,0:T(8,128)(2,1)S(1)} %message.1.refs_0_), channel_id=1, source_target_pairs={{0,1},{1,0},{2,3},{3,2},{4,5},{5,4},{6,7},{7,6},{8,9},{9,8},{10,11... | collective-permute-start | bytes 442376 | tf_op jit(solution)/shard_map/ppermute | solution.py:329
  16.8 12.2 %collective-permute-start.7 = (bf16[2,256,256]{2,1,0:T(8,128)(2,1)S(1)}, bf16[2,256,256]{2,1,0:T(8,128)(2,1)S(1)}, u32[]{:S(2)}, u32[]{:S(2)}) collective-permute-start(bf16[2,256,256]{2,1,0:T(8,128)(2,1)S(1)} %get-tuple-element.35), channel_id=1, source_target_pairs={{0,3},{1,2},{2,1},{3,0},{4,7},{5,6},{6,5},{7,4},{8,11},{9,10},{10,... | collective-permute-start | bytes 786440 | tf_op jit(solution)/shard_map/ppermute | solution.py:329
  18.4 10.5 %collective-permute-start.4 = (bf16[2,256,256]{2,1,0:T(8,128)(2,1)S(1)}, bf16[2,256,256]{2,1,0:T(8,128)(2,1)S(1)}, u32[]{:S(2)}, u32[]{:S(2)}) collective-permute-start(bf16[2,256,256]{2,1,0:T(8,128)(2,1)S(1)} %get-tuple-element.31), channel_id=1, source_target_pairs={{0,1},{1,0},{2,3},{3,2},{4,5},{5,4},{6,7},{7,6},{8,9},{9,8},{10,11... | collective-permute-start | bytes 786440 | tf_op jit(solution)/shard_map/ppermute | solution.py:329
  18.4 13.2 %collective-permute-start.5 = (bf16[2,256,256]{2,1,0:T(8,128)(2,1)S(1)}, bf16[2,256,256]{2,1,0:T(8,128)(2,1)S(1)}, u32[]{:S(2)}, u32[]{:S(2)}) collective-permute-start(bf16[2,256,256]{2,1,0:T(8,128)(2,1)S(1)} %get-tuple-element.33), channel_id=1, source_target_pairs={{0,2},{1,3},{2,0},{3,1},{4,6},{5,7},{6,4},{7,5},{8,10},{9,11},{10,... | collective-permute-start | bytes 786440 | tf_op jit(solution)/shard_map/ppermute | solution.py:329
  19.5 1.4 %collective-permute-start.2 = (bf16[288,256]{1,0:T(8,128)(2,1)S(1)}, bf16[288,256]{1,0:T(8,128)(2,1)S(1)}, u32[]{:S(2)}, u32[]{:S(2)}) collective-permute-start(bf16[288,256]{1,0:T(8,128)(2,1)S(1)} %collective-permute-done.1.refs_2_), channel_id=1, source_target_pairs={{0,1},{1,0},{2,3},{3,2},{4,5},{5,4},{6,7},{7,6},{8,9},{9,8},{10,11... | collective-permute-start | bytes 442376 | tf_op jit(solution)/shard_map/ppermute | solution.py:329
  21.5 2.2 %collective-permute-start.8 = (f32[4,2,256]{2,1,0:T(2,128)S(1)}, f32[4,2,256]{2,1,0:T(2,128)S(1)}, u32[]{:S(2)}, u32[]{:S(2)}) collective-permute-start(f32[4,2,256]{2,1,0:T(2,128)S(1)} %fields.1), channel_id=1, source_target_pairs={{0,0},{1,5},{2,10},{3,15},{4,4},{5,1},{6,14},{7,11},{8,8},{9,13},{... | collective-permute-start | bytes 24584 | tf_op jit(solution)/shard_map/ppermute | solution.py:331
  23.6 15.7 %collective-permute-start.11 = (bf16[128,1024]{1,0:T(8,128)(2,1)S(1)}, bf16[128,1024]{1,0:T(8,128)(2,1)S(1)}, u32[]{:S(2)}, u32[]{:S(2)}) collective-permute-start(bf16[128,1024]{1,0:T(8,128)(2,1)S(1)} %slice.4), channel_id=1, source_target_pairs={{0,2},{1,3},{2,0},{3,1},{4,6},{5,7},{6,4},{7,5},{8,10},{9,11},{10,... | collective-permute-start | bytes 786440 | tf_op jit(solution)/shard_map/ppermute | solution.py:329
  38.7 4.6 %collective-permute-start.13 = (bf16[192,1024]{1,0:T(8,128)(2,1)S(1)}, bf16[192,1024]{1,0:T(8,128)(2,1)S(1)}, u32[]{:S(2)}, u32[]{:S(2)}) collective-permute-start(bf16[192,1024]{1,0:T(8,128)(2,1)S(1)} %collective-permute-done.6.refs_0_), channel_id=1, source_target_pairs={{0,1},{1,0},{2,3},{3,2},{4,5},{5,4},{6,7},{7,6},{8,9},{9,8},{10,11... | collective-permute-start | bytes 1179656 | tf_op jit(solution)/shard_map/ppermute | solution.py:329
  38.8 4.5 %collective-permute-start.15 = (bf16[192,1024]{1,0:T(8,128)(2,1)S(1)}, bf16[192,1024]{1,0:T(8,128)(2,1)S(1)}, u32[]{:S(2)}, u32[]{:S(2)}) collective-permute-start(bf16[192,1024]{1,0:T(8,128)(2,1)S(1)} %collective-permute-done.14.refs_2_), channel_id=1, source_target_pairs={{0,1},{1,0},{2,3},{3,2},{4,5},{5,4},{6,7},{7,6},{8,9},{9,8},{10,11... | collective-permute-start | bytes 1179656 | tf_op jit(solution)/shard_map/ppermute | solution.py:329
  39.3 5.4 %collective-permute-start.12 = (bf16[128,1024]{1,0:T(8,128)(2,1)S(1)}, bf16[128,1024]{1,0:T(8,128)(2,1)S(1)}, u32[]{:S(2)}, u32[]{:S(2)}) collective-permute-start(bf16[128,1024]{1,0:T(8,128)(2,1)S(1)} %collective-permute-done.11.refs_0_), channel_id=1, source_target_pairs={{0,1},{1,0},{2,3},{3,2},{4,5},{5,4},{6,7},{7,6},{8,9},{9,8},{10,11... | collective-permute-start | bytes 786440 | tf_op jit(solution)/shard_map/ppermute | solution.py:329
  40.9 9.2 %collective-permute-start.9 = (f32[8,128]{1,0:T(8,128)S(1)}, f32[8,128]{1,0:T(8,128)S(1)}, u32[]{:S(2)}, u32[]{:S(2)}) collective-permute-start(f32[8,128]{1,0:T(8,128)S(1)} %get-tuple-element.37), channel_id=1, source_target_pairs={{0,0},{1,5},{2,10},{3,15},{4,4},{5,1},{6,14},{7,11},{8,8},{9,13},{... | collective-permute-start | bytes 12296 | tf_op jit(solution)/shard_map/ppermute | solution.py:332
  41.6 8.5 %collective-permute-start.10 = (f32[8,128]{1,0:T(8,128)S(1)}, f32[8,128]{1,0:T(8,128)S(1)}, u32[]{:S(2)}, u32[]{:S(2)}) collective-permute-start(f32[8,128]{1,0:T(8,128)S(1)} %get-tuple-element.38), channel_id=1, source_target_pairs={{0,1},{1,4},{2,11},{3,14},{4,5},{5,0},{6,15},{7,10},{8,9},{9,12},{... | collective-permute-start | bytes 12296 | tf_op jit(solution)/shard_map/ppermute | solution.py:332
  45.5 7.0 %collective-permute-start.16 = (f32[8,128]{1,0:T(8,128)S(1)}, f32[8,128]{1,0:T(8,128)S(1)}, u32[]{:S(2)}, u32[]{:S(2)}) collective-permute-start(f32[8,128]{1,0:T(8,128)S(1)} %get-tuple-element.48), channel_id=1, source_target_pairs={{0,2},{1,7},{2,8},{3,13},{4,6},{5,3},{6,12},{7,9},{8,10},{9,15},{1... | collective-permute-start | bytes 12296 | tf_op jit(solution)/shard_map/ppermute | solution.py:332
  49.2 5.7 %collective-permute-start.17 = (f32[8,128]{1,0:T(8,128)S(1)}, f32[8,128]{1,0:T(8,128)S(1)}, u32[]{:S(2)}, u32[]{:S(2)}) collective-permute-start(f32[8,128]{1,0:T(8,128)S(1)} %get-tuple-element.49), channel_id=1, source_target_pairs={{0,3},{1,6},{2,9},{3,12},{4,7},{5,2},{6,13},{7,8},{8,11},{9,14},{1... | collective-permute-start | bytes 12296 | tf_op jit(solution)/shard_map/ppermute | solution.py:332

commit v5 on v4

--- a/solution.py
+++ b/solution.py
@@ -381,7 +381,7 @@
         functools.partial(direct_kernel, share, len(far)), len(far), [direct[k] for k in far], green,
         *late[len(far) :], *late[: len(far)],
     )
-    arrived = [answer(x, k) for k, x in enumerate(list(results) + list(late))]
+    arrived = [answer(x if k in far else ordered(x, late[0]), k) for k, x in enumerate(list(results) + list(late))]
     return tuple(x.T for x in unpack(n, per, share, vectors, masks, arrived))
 
 

time: 55.7 us -> 54.7 us (0.982)
  waiting for transfers between devices: 15.1 us -> 12.5 us
  starting transfers between devices: 21.8 us -> 23.4 us
    ppermute x4, waiting for transfers between devices: 4.81 us -> 2.09 us  [at_the_source(): lax.ppermute(x, ALL, [(w * n + q, (w ^ q) * n + (q ^ k)) for w, q in pairs])]
    ppermute x4, starting transfers between devices: 7.04 us -> 8.61 us  [at_the_source(): lax.ppermute(x, ALL, [(w * n + q, (w ^ q) * n + (q ^ k)) for w, q in pairs])]
  transfers between devices with their start and end apart: 18 -> 18, of which waited for: 5 -> 5; matrix products, arithmetic and copies ran while one was open for 2% -> 2% of each run, Pallas kernels for 26% -> 25%
where the time goes in v5:
time: 54.7 us; the launch traced here: 54.5 us
  starting transfers between devices  23.4 us (43%)
  Pallas kernels  14.8 us (27%)
  waiting for transfers between devices  12.5 us (23%)
  local copies, waits for them, and re-layouts  2.32 us (4%)
  between operations  1.45 us (3%)
    ppermute x12, starting transfers between devices, at_the_source(): move = lambda x, k: lax.ppermute(x, SR, [(i, i ^ k) for i in range(n)])  12.1 us
    ppermute x12, waiting for transfers between devices, at_the_source(): move = lambda x, k: lax.ppermute(x, SR, [(i, i ^ k) for i in range(n)])  10.5 us
    ppermute x4, starting transfers between devices, at_the_source(): lax.ppermute(x, ALL, [(w * n + q, (w ^ q) * n + (q ^ k)) for w, q in pairs])  8.61 us
    pallas_call x1, Pallas kernels, make_green(): pl.pallas_call(functools.partial(green_kernel, n, share), out_shape=jax.S...  7.02 us
    pallas_call x3, Pallas kernels, contract(): pl.pallas_call(kernel, out_shape=[jax.ShapeDtypeStruct((8, 128), F32)] *...  3.62 us
    pallas_call x1, Pallas kernels, select(): pl.pallas_call(functools.partial(select_kernel, n, per, share), out_shape...  2.17 us
    ppermute x4, waiting for transfers between devices, at_the_source(): lax.ppermute(x, ALL, [(w * n + q, (w ^ q) * n + (q ^ k)) for w, q in pairs])  2.09 us
    ppermute x1, starting transfers between devices, at_the_source(): swap = lambda x: lax.ppermute(x, 'walk', [(w, w ^ 1) for w in range(n)])  2.03 us
  transfers between devices with their start and end apart: 18, of which 5 were waited for; matrix products, arithmetic and copies ran while one was open for 2% of the time, Pallas kernels for 25%

profile of v5, /device:TPU:0, one launch (start us, length us, event | category | flops | bytes accessed | tf_op | source)
XLA Modules:
  0.0 54.5 jit_solution(7405632116759513761)
XLA Ops:
  0.6 0.5 collective-permute-start.3
  1.1 0.0 copy-start.4
  1.2 0.0 copy-start.2
  1.2 0.0 copy-start.3
  1.2 1.1 %constant_dynamic-slice_fusion = bf16[192,1024]{1,0:T(8,128)(2,1)S(1)} fusion(bf16[512,1024]{1,0:T(8,128)(2,1)} %bitcast.4, s32[]{:T(128)S(6)} %select_n.3), kind=kLoop, calls=%fused_computation | loop fusion | bytes 786436 | tf_op jit(solution)/shard_map/dynamic_slice | solution.py:353
  2.2 2.6 %collective-permute-start.6 = (bf16[192,1024]{1,0:T(8,128)(2,1)S(1)}, bf16[192,1024]{1,0:T(8,128)(2,1)S(1)}, u32[]{:S(2)}, u32[]{:S(2)}) collective-permute-start(bf16[192,1024]{1,0:T(8,128)(2,1)S(1)} %constant_dynamic-slice_fusion), channel_id=1, source_target_pairs={{0,2},{1,3},{2,0},{3,1},{4,6},{5,7},{6,4},{7,5},{8,10},{9,11},{10,... | collective-permute-start | bytes 1179656 | tf_op jit(solution)/shard_map/ppermute | solution.py:329
  4.8 0.0 copy-done.4
  4.8 0.0 copy-start
  4.8 1.2 %copy-done = bf16[8,256,256]{2,1,0:T(8,128)(2,1)S(1)} copy-done((bf16[8,256,256]{2,1,0:T(8,128)(2,1)S(1)}, bf16[8,256,256]{2,1,0:T(8,128)(2,1)}, u32[]{:S(2)}) %copy-start) | copy-done | bytes 1048600
  6.0 0.0 copy-start.1
  6.1 2.2 %select.1 = (bf16[2,256,256]{2,1,0:T(8,128)(2,1)S(1)}, bf16[2,256,256]{2,1,0:T(8,128)(2,1)S(1)}, bf16[2,256,256]{2,1,0:T(8,128)(2,1)S(1)}, bf16[2,256,256]{2,1,0:T(8,128)(2,1)S(1)}) custom-call(s32[32]{0:T(128)S(1)} %copy-done.4, bf16[8,256,256]{2,1,0:T(8,128)(2,1)S(1)} %copy-done), custom_call_target="tpu_custom_call" | custom-call | tf_op jit(solution)/shard_map/select/pallas_call | solution.py:68
  8.2 0.0 copy-done.2
  8.2 0.0 copy-done.3
  8.3 0.1 collective-permute-start.1
  8.4 6.4 %collective-permute-done.6.refs_0_ = bf16[192,1024]{1,0:T(8,128)(2,1)S(1)} collective-permute-done((bf16[192,1024]{1,0:T(8,128)(2,1)S(1)}, bf16[192,1024]{1,0:T(8,128)(2,1)S(1)}, u32[]{:S(2)}, u32[]{:S(2)}) %collective-permute-start.6) | collective-permute-done | bytes 393248 | tf_op jit(solution)/shard_map/ppermute | solution.py:329
  14.8 2.0 %collective-permute-start.12 = (bf16[192,1024]{1,0:T(8,128)(2,1)S(1)}, bf16[192,1024]{1,0:T(8,128)(2,1)S(1)}, u32[]{:S(2)}, u32[]{:S(2)}) collective-permute-start(bf16[192,1024]{1,0:T(8,128)(2,1)S(1)} %collective-permute-done.6.refs_0_), channel_id=1, source_target_pairs={{0,4},{4,0},{8,12},{12,8},{1,5},{5,1},{9,13},{13,9},{2,6},{6,2},{1... | collective-permute-start | bytes 1179656 | tf_op jit(solution)/shard_map/ppermute | solution.py:330
  16.8 0.0 collective-permute-start
  16.8 1.6 %collective-permute-start.7 = (bf16[2,256,256]{2,1,0:T(8,128)(2,1)S(1)}, bf16[2,256,256]{2,1,0:T(8,128)(2,1)S(1)}, u32[]{:S(2)}, u32[]{:S(2)}) collective-permute-start(bf16[2,256,256]{2,1,0:T(8,128)(2,1)S(1)} %get-tuple-element.37), channel_id=1, source_target_pairs={{0,3},{1,2},{2,1},{3,0},{4,7},{5,6},{6,5},{7,4},{8,11},{9,10},{10,... | collective-permute-start | bytes 786440 | tf_op jit(solution)/shard_map/ppermute | solution.py:329
  18.4 0.0 collective-permute-done.1.refs_2_
  18.4 0.0 collective-permute-done.3.refs_1_
  18.4 0.0 collective-permute-start.4
  18.4 1.0 %collective-permute-start.5 = (bf16[2,256,256]{2,1,0:T(8,128)(2,1)S(1)}, bf16[2,256,256]{2,1,0:T(8,128)(2,1)S(1)}, u32[]{:S(2)}, u32[]{:S(2)}) collective-permute-start(bf16[2,256,256]{2,1,0:T(8,128)(2,1)S(1)} %get-tuple-element.35), channel_id=1, source_target_pairs={{0,2},{1,3},{2,0},{3,1},{4,6},{5,7},{6,4},{7,5},{8,10},{9,11},{10,... | collective-permute-start | bytes 786440 | tf_op jit(solution)/shard_map/ppermute | solution.py:329
  19.5 0.0 collective-permute-done.refs_1_
  19.5 0.2 collective-permute-start.2
  19.7 1.1 %collective-permute-done.2.refs_3_ = bf16[288,256]{1,0:T(8,128)(2,1)S(1)} collective-permute-done((bf16[288,256]{1,0:T(8,128)(2,1)S(1)}, bf16[288,256]{1,0:T(8,128)(2,1)S(1)}, u32[]{:S(2)}, u32[]{:S(2)}) %collective-permute-start.2) | collective-permute-done | bytes 147488 | tf_op jit(solution)/shard_map/ppermute | solution.py:329
  20.8 0.6 %fields.1 = f32[4,2,256]{2,1,0:T(2,128)S(1)} custom-call(s32[32]{0:T(128)S(1)} %copy-done.4, bf16[288,256]{1,0:T(8,128)(2,1)S(1)} %message.1.refs_0_, bf16[288,256]{1,0:T(8,128)(2,1)S(1)} %collective-permute-done.refs_1_, bf16[288,256]{1,0:T(8,128)(2,1)S(1)} %collective-permute-done.1.refs_2_, bf16[288,256]{1,0:T(8,128)(2,1)S(1)} %collective-permute-done.2.refs_3_), custom_call_target="tpu_custom_call" | custom-call | tf_op jit(solution)/shard_map/fields/pallas_call | solution.py:118
  21.5 0.7 %collective-permute-start.8 = (f32[4,2,256]{2,1,0:T(2,128)S(1)}, f32[4,2,256]{2,1,0:T(2,128)S(1)}, u32[]{:S(2)}, u32[]{:S(2)}) collective-permute-start(f32[4,2,256]{2,1,0:T(2,128)S(1)} %fields.1), channel_id=1, source_target_pairs={{0,0},{1,5},{2,10},{3,15},{4,4},{5,1},{6,14},{7,11},{8,8},{9,13},{... | collective-permute-start | bytes 24584 | tf_op jit(solution)/shard_map/ppermute | solution.py:331
  22.1 0.0 copy-done.1
  22.8 0.8 %turn.1 = (bf16[256,1024]{1,0:T(8,128)(2,1)S(1)}, f32[8,128]{1,0:T(8,128)S(1)}) custom-call(s32[32]{0:T(128)S(1)} %copy-done.4, s32[1]{0:T(128)S(6)} %copy.8.counts, bf16[288,256]{1,0:T(8,128)(2,1)S(1)} %message.1.refs_0_, bf16[288,256]{1,0:T(8,128)(2,1)S(1)} %collective-permute-done.refs_1_, bf16[288,256]{1,0:T(8,128)(2,1)S(1)} %collective-permute-done.1.refs_2_, ...), custom_call_target="tpu_custom_call" | custom-call | tf_op jit(solution)/shard_map/turn/pallas_call | solution.py:145
  23.6 0.0 collective-permute-done.8.refs_5_
  23.6 5.3 %collective-permute-start.9 = (bf16[128,1024]{1,0:T(8,128)(2,1)S(1)}, bf16[128,1024]{1,0:T(8,128)(2,1)S(1)}, u32[]{:S(2)}, u32[]{:S(2)}) collective-permute-start(bf16[128,1024]{1,0:T(8,128)(2,1)S(1)} %slice.4), channel_id=1, source_target_pairs={{0,2},{1,3},{2,0},{3,1},{4,6},{5,7},{6,4},{7,5},{8,10},{9,11},{10,... | collective-permute-start | bytes 786440 | tf_op jit(solution)/shard_map/ppermute | solution.py:329
  29.0 0.0 collective-permute-done.7.refs_3_
  29.0 0.0 collective-permute-done.4.refs_1_
  29.0 2.7 %collective-permute-done.5.refs_2_ = bf16[2,256,256]{2,1,0:T(8,128)(2,1)S(1)} collective-permute-done((bf16[2,256,256]{2,1,0:T(8,128)(2,1)S(1)}, bf16[2,256,256]{2,1,0:T(8,128)(2,1)S(1)}, u32[]{:S(2)}, u32[]{:S(2)}) %collective-permute-start.5) | collective-permute-done | bytes 262176 | tf_op jit(solution)/shard_map/ppermute | solution.py:329
  31.7 7.0 %green.1.refs_2_.refs_4_ = bf16[1024,512]{1,0:T(8,128)(2,1)S(1)} custom-call(bf16[2,256,256]{2,1,0:T(8,128)(2,1)S(1)} %get-tuple-element.29.refs_0_, bf16[2,256,256]{2,1,0:T(8,128)(2,1)S(1)} %collective-permute-done.4.refs_1_, bf16[2,256,256]{2,1,0:T(8,128)(2,1)S(1)} %collective-permute-done.5.refs_2_, ...), custom_call_target="tpu_custom_call" | custom-call | tf_op jit(solution)/shard_map/green/pallas_call | solution.py:214
  38.7 0.1 collective-permute-start.11
  38.8 0.0 collective-permute-done.12.refs_2_
  38.8 0.5 collective-permute-start.13
  39.3 0.0 collective-permute-done.9.refs_0_
  39.3 0.1 collective-permute-start.10
  39.4 1.5 %contract.3 = (f32[8,128]{1,0:T(8,128)S(1)}, f32[8,128]{1,0:T(8,128)S(1)}) custom-call(bf16[512,1024]{1,0:T(8,128)(2,1)S(1)} %bitcast.6, bf16[512,1024]{1,0:T(8,128)(2,1)S(1)} %collective-permute-done.3.refs_1_, bf16[1024,512]{1,0:T(8,128)(2,1)S(1)} %green.1.refs_2_.refs_4_), custom_call_target="tpu_custom_call" | custom-call | flops 1073741824 | bytes 3145728 | tf_op jit(solution)/shard_map/contract/pallas_call | solution.py:282
  40.9 0.0 collective-permute-done.11.refs_1_
  40.9 0.1 collective-permute-done.13.refs_3_
  41.1 1.4 %contract.4 = (f32[8,128]{1,0:T(8,128)S(1)}, f32[8,128]{1,0:T(8,128)S(1)}, f32[128,512]{1,0:T(8,128)S(1)}, f32[128,512]{1,0:T(8,128)S(1)}) custom-call(bf16[192,1024]{1,0:T(8,128)(2,1)S(1)} %collective-permute-done.6.refs_0_, bf16[192,1024]{1,0:T(8,128)(2,1)S(1)} %collective-permute-done.11.refs_1_, bf16[192,1024]{1,0:T(8,128)(2,1)S(1)} %collective-permute-done.12.refs_2_, ...), custom_call_target="tpu_custom_call" | custom-call | flops 805306368 | bytes 2621440 | tf_op jit(solution)/shard_map/contract/pallas_call | solution.py:282
  42.5 0.0 collective-permute-done.10.refs_1_
  42.5 0.7 %contract.5 = (f32[8,128]{1,0:T(8,128)S(1)}, f32[8,128]{1,0:T(8,128)S(1)}) custom-call(bf16[128,1024]{1,0:T(8,128)(2,1)S(1)} %collective-permute-done.9.refs_0_, bf16[128,1024]{1,0:T(8,128)(2,1)S(1)} %collective-permute-done.10.refs_1_, bf16[1024,512]{1,0:T(8,128)(2,1)S(1)} %green.1.refs_2_.refs_4_, f32[128,512]{1,0:T(8,128)S(1)} %get-tuple-element.45.refs_3_, ...), custom_call_target="tpu_custom_call" | custom-call | flops 268435456 | bytes 1572864 | tf_op jit(solution)/shard_map/contract/pallas_call | solution.py:282
  43.2 1.6 %collective-permute-start.16 = (f32[8,128]{1,0:T(8,128)S(1)}, f32[8,128]{1,0:T(8,128)S(1)}, u32[]{:S(2)}, u32[]{:S(2)}) collective-permute-start(f32[8,128]{1,0:T(8,128)S(1)} %get-tuple-element.49), channel_id=1, source_target_pairs={{0,2},{1,7},{2,8},{3,13},{4,6},{5,3},{6,12},{7,9},{8,10},{9,15},{1... | collective-permute-start | bytes 12296 | tf_op jit(solution)/shard_map/ppermute | solution.py:332
  44.8 0.6 %collective-permute-start.14 = (f32[8,128]{1,0:T(8,128)S(1)}, f32[8,128]{1,0:T(8,128)S(1)}, u32[]{:S(2)}, u32[]{:S(2)}) collective-permute-start(f32[8,128]{1,0:T(8,128)S(1)} %get-tuple-element.50), channel_id=1, source_target_pairs={{0,0},{1,5},{2,10},{3,15},{4,4},{5,1},{6,14},{7,11},{8,8},{9,13},{... | collective-permute-start | bytes 12296 | tf_op jit(solution)/shard_map/ppermute | solution.py:332
  45.4 2.5 %collective-permute-start.15 = (f32[8,128]{1,0:T(8,128)S(1)}, f32[8,128]{1,0:T(8,128)S(1)}, u32[]{:S(2)}, u32[]{:S(2)}) collective-permute-start(f32[8,128]{1,0:T(8,128)S(1)} %get-tuple-element.52), channel_id=1, source_target_pairs={{0,1},{1,4},{2,11},{3,14},{4,5},{5,0},{6,15},{7,10},{8,9},{9,12},{... | collective-permute-start | bytes 12296 | tf_op jit(solution)/shard_map/ppermute | solution.py:332
  47.9 3.9 %collective-permute-start.17 = (f32[8,128]{1,0:T(8,128)S(1)}, f32[8,128]{1,0:T(8,128)S(1)}, u32[]{:S(2)}, u32[]{:S(2)}) collective-permute-start(f32[8,128]{1,0:T(8,128)S(1)} %get-tuple-element.53), channel_id=1, source_target_pairs={{0,3},{1,6},{2,9},{3,12},{4,7},{5,2},{6,13},{7,8},{8,11},{9,14},{1... | collective-permute-start | bytes 12296 | tf_op jit(solution)/shard_map/ppermute | solution.py:332
  51.8 0.0 collective-permute-done.14.refs_0_
  51.8 0.0 collective-permute-done.15.refs_1_
  51.8 0.0 collective-permute-done.16.refs_2_
  51.8 2.1 %collective-permute-done.17.refs_3_ = f32[8,128]{1,0:T(8,128)S(1)} collective-permute-done((f32[8,128]{1,0:T(8,128)S(1)}, f32[8,128]{1,0:T(8,128)S(1)}, u32[]{:S(2)}, u32[]{:S(2)}) %collective-permute-start.17) | collective-permute-done | bytes 4128 | tf_op jit(solution)/shard_map/ppermute | solution.py:332
  53.9 0.6 %unpack.1 = (f32[2,8]{1,0:T(2,128)}, f32[2,8]{1,0:T(2,128)}) custom-call(f32[8,128]{1,0:T(8,128)S(1)} %get-tuple-element.31.masks, f32[8,128]{1,0:T(8,128)S(1)} %collective-permute-done.14.refs_0_, f32[8,128]{1,0:T(8,128)S(1)} %collective-permute-done.15.refs_1_, f32[8,128]{1,0:T(8,128)S(1)} %collective-permute-done.16.refs_2_, ...), custom_call_target="tpu_custom_call" | custom-call | tf_op jit(solution)/shard_map/unpack/pallas_call | solution.py:312
  (2 shorter events, 0.0 us)
Async XLA Ops:
  0.6 17.8 %collective-permute-start.3 = (bf16[512,1024]{1,0:T(8,128)(2,1)}, bf16[512,1024]{1,0:T(8,128)(2,1)S(1)}, u32[]{:S(2)}, u32[]{:S(2)}) collective-permute-start(bf16[512,1024]{1,0:T(8,128)(2,1)} %bitcast.3), channel_id=1, source_target_pairs={{0,1},{1,0},{2,3},{3,2},{4,5},{5,4},{6,7},{7,6},{8,9},{9,8},{10,11... | collective-permute-start | bytes 3145736 | tf_op jit(solution)/shard_map/ppermute | solution.py:329
  1.1 3.7 %copy-start.4 = (s32[32]{0:T(128)S(1)}, s32[32]{0:T(128)}, u32[]{:S(2)}) copy-start(s32[32]{0:T(128)} %branches.5) | copy-start | bytes 388
  1.2 7.1 %copy-start.2 = (bf16[256,256]{1,0:T(8,128)(2,1)S(1)}, bf16[256,256]{1,0:T(8,128)(2,1)}, u32[]{:S(2)}) copy-start(bf16[256,256]{1,0:T(8,128)(2,1)} %trial) | copy-start | bytes 393220
  1.2 7.1 %copy-start.3 = (f32[8,256]{1,0:T(8,128)S(1)}, f32[8,256]{1,0:T(8,128)}, u32[]{:S(2)}) copy-start(f32[8,256]{1,0:T(8,128)} %field.1) | copy-start | bytes 24580
  2.2 12.6 %collective-permute-start.6 = (bf16[192,1024]{1,0:T(8,128)(2,1)S(1)}, bf16[192,1024]{1,0:T(8,128)(2,1)S(1)}, u32[]{:S(2)}, u32[]{:S(2)}) collective-permute-start(bf16[192,1024]{1,0:T(8,128)(2,1)S(1)} %constant_dynamic-slice_fusion), channel_id=1, source_target_pairs={{0,2},{1,3},{2,0},{3,1},{4,6},{5,7},{6,4},{7,5},{8,10},{9,11},{10,... | collective-permute-start | bytes 1179656 | tf_op jit(solution)/shard_map/ppermute | solution.py:329
  4.8 1.2 %copy-start = (bf16[8,256,256]{2,1,0:T(8,128)(2,1)S(1)}, bf16[8,256,256]{2,1,0:T(8,128)(2,1)}, u32[]{:S(2)}) copy-start(bf16[8,256,256]{2,1,0:T(8,128)(2,1)} %walkers.1) | copy-start | bytes 3145732
  6.0 16.1 %copy-start.1 = (bf16[2,256,1024]{2,1,0:T(8,128)(2,1)S(1)}, bf16[2,256,1024]{2,1,0:T(8,128)(2,1)}, u32[]{:S(2)}) copy-start(bf16[2,256,1024]{2,1,0:T(8,128)(2,1)} %param.8) | copy-start | bytes 3145732
  8.3 10.2 %collective-permute-start.1 = (bf16[288,256]{1,0:T(8,128)(2,1)S(1)}, bf16[288,256]{1,0:T(8,128)(2,1)S(1)}, u32[]{:S(2)}, u32[]{:S(2)}) collective-permute-start(bf16[288,256]{1,0:T(8,128)(2,1)S(1)} %message.1.refs_0_), channel_id=1, source_target_pairs={{0,2},{1,3},{2,0},{3,1},{4,6},{5,7},{6,4},{7,5},{8,10},{9,11},{10,... | collective-permute-start | bytes 442376 | tf_op jit(solution)/shard_map/ppermute | solution.py:329
  14.8 24.0 %collective-permute-start.12 = (bf16[192,1024]{1,0:T(8,128)(2,1)S(1)}, bf16[192,1024]{1,0:T(8,128)(2,1)S(1)}, u32[]{:S(2)}, u32[]{:S(2)}) collective-permute-start(bf16[192,1024]{1,0:T(8,128)(2,1)S(1)} %collective-permute-done.6.refs_0_), channel_id=1, source_target_pairs={{0,4},{4,0},{8,12},{12,8},{1,5},{5,1},{9,13},{13,9},{2,6},{6,2},{1... | collective-permute-start | bytes 1179656 | tf_op jit(solution)/shard_map/ppermute | solution.py:330
  16.8 2.6 %collective-permute-start = (bf16[288,256]{1,0:T(8,128)(2,1)S(1)}, bf16[288,256]{1,0:T(8,128)(2,1)S(1)}, u32[]{:S(2)}, u32[]{:S(2)}) collective-permute-start(bf16[288,256]{1,0:T(8,128)(2,1)S(1)} %message.1.refs_0_), channel_id=1, source_target_pairs={{0,1},{1,0},{2,3},{3,2},{4,5},{5,4},{6,7},{7,6},{8,9},{9,8},{10,11... | collective-permute-start | bytes 442376 | tf_op jit(solution)/shard_map/ppermute | solution.py:329
  16.8 12.2 %collective-permute-start.7 = (bf16[2,256,256]{2,1,0:T(8,128)(2,1)S(1)}, bf16[2,256,256]{2,1,0:T(8,128)(2,1)S(1)}, u32[]{:S(2)}, u32[]{:S(2)}) collective-permute-start(bf16[2,256,256]{2,1,0:T(8,128)(2,1)S(1)} %get-tuple-element.37), channel_id=1, source_target_pairs={{0,3},{1,2},{2,1},{3,0},{4,7},{5,6},{6,5},{7,4},{8,11},{9,10},{10,... | collective-permute-start | bytes 786440 | tf_op jit(solution)/shard_map/ppermute | solution.py:329
  18.4 10.5 %collective-permute-start.4 = (bf16[2,256,256]{2,1,0:T(8,128)(2,1)S(1)}, bf16[2,256,256]{2,1,0:T(8,128)(2,1)S(1)}, u32[]{:S(2)}, u32[]{:S(2)}) collective-permute-start(bf16[2,256,256]{2,1,0:T(8,128)(2,1)S(1)} %get-tuple-element.33), channel_id=1, source_target_pairs={{0,1},{1,0},{2,3},{3,2},{4,5},{5,4},{6,7},{7,6},{8,9},{9,8},{10,11... | collective-permute-start | bytes 786440 | tf_op jit(solution)/shard_map/ppermute | solution.py:329
  18.4 13.2 %collective-permute-start.5 = (bf16[2,256,256]{2,1,0:T(8,128)(2,1)S(1)}, bf16[2,256,256]{2,1,0:T(8,128)(2,1)S(1)}, u32[]{:S(2)}, u32[]{:S(2)}) collective-permute-start(bf16[2,256,256]{2,1,0:T(8,128)(2,1)S(1)} %get-tuple-element.35), channel_id=1, source_target_pairs={{0,2},{1,3},{2,0},{3,1},{4,6},{5,7},{6,4},{7,5},{8,10},{9,11},{10,... | collective-permute-start | bytes 786440 | tf_op jit(solution)/shard_map/ppermute | solution.py:329
  19.5 1.4 %collective-permute-start.2 = (bf16[288,256]{1,0:T(8,128)(2,1)S(1)}, bf16[288,256]{1,0:T(8,128)(2,1)S(1)}, u32[]{:S(2)}, u32[]{:S(2)}) collective-permute-start(bf16[288,256]{1,0:T(8,128)(2,1)S(1)} %collective-permute-done.1.refs_2_), channel_id=1, source_target_pairs={{0,1},{1,0},{2,3},{3,2},{4,5},{5,4},{6,7},{7,6},{8,9},{9,8},{10,11... | collective-permute-start | bytes 442376 | tf_op jit(solution)/shard_map/ppermute | solution.py:329
  21.5 2.2 %collective-permute-start.8 = (f32[4,2,256]{2,1,0:T(2,128)S(1)}, f32[4,2,256]{2,1,0:T(2,128)S(1)}, u32[]{:S(2)}, u32[]{:S(2)}) collective-permute-start(f32[4,2,256]{2,1,0:T(2,128)S(1)} %fields.1), channel_id=1, source_target_pairs={{0,0},{1,5},{2,10},{3,15},{4,4},{5,1},{6,14},{7,11},{8,8},{9,13},{... | collective-permute-start | bytes 24584 | tf_op jit(solution)/shard_map/ppermute | solution.py:331
  23.6 15.7 %collective-permute-start.9 = (bf16[128,1024]{1,0:T(8,128)(2,1)S(1)}, bf16[128,1024]{1,0:T(8,128)(2,1)S(1)}, u32[]{:S(2)}, u32[]{:S(2)}) collective-permute-start(bf16[128,1024]{1,0:T(8,128)(2,1)S(1)} %slice.4), channel_id=1, source_target_pairs={{0,2},{1,3},{2,0},{3,1},{4,6},{5,7},{6,4},{7,5},{8,10},{9,11},{10,... | collective-permute-start | bytes 786440 | tf_op jit(solution)/shard_map/ppermute | solution.py:329
  38.7 2.2 %collective-permute-start.11 = (bf16[192,1024]{1,0:T(8,128)(2,1)S(1)}, bf16[192,1024]{1,0:T(8,128)(2,1)S(1)}, u32[]{:S(2)}, u32[]{:S(2)}) collective-permute-start(bf16[192,1024]{1,0:T(8,128)(2,1)S(1)} %collective-permute-done.6.refs_0_), channel_id=1, source_target_pairs={{0,1},{1,0},{2,3},{3,2},{4,5},{5,4},{6,7},{7,6},{8,9},{9,8},{10,11... | collective-permute-start | bytes 1179656 | tf_op jit(solution)/shard_map/ppermute | solution.py:329
  38.8 2.3 %collective-permute-start.13 = (bf16[192,1024]{1,0:T(8,128)(2,1)S(1)}, bf16[192,1024]{1,0:T(8,128)(2,1)S(1)}, u32[]{:S(2)}, u32[]{:S(2)}) collective-permute-start(bf16[192,1024]{1,0:T(8,128)(2,1)S(1)} %collective-permute-done.12.refs_2_), channel_id=1, source_target_pairs={{0,1},{1,0},{2,3},{3,2},{4,5},{5,4},{6,7},{7,6},{8,9},{9,8},{10,11... | collective-permute-start | bytes 1179656 | tf_op jit(solution)/shard_map/ppermute | solution.py:329
  39.3 3.2 %collective-permute-start.10 = (bf16[128,1024]{1,0:T(8,128)(2,1)S(1)}, bf16[128,1024]{1,0:T(8,128)(2,1)S(1)}, u32[]{:S(2)}, u32[]{:S(2)}) collective-permute-start(bf16[128,1024]{1,0:T(8,128)(2,1)S(1)} %collective-permute-done.9.refs_0_), channel_id=1, source_target_pairs={{0,1},{1,0},{2,3},{3,2},{4,5},{5,4},{6,7},{7,6},{8,9},{9,8},{10,11... | collective-permute-start | bytes 786440 | tf_op jit(solution)/shard_map/ppermute | solution.py:329
  43.2 8.6 %collective-permute-start.16 = (f32[8,128]{1,0:T(8,128)S(1)}, f32[8,128]{1,0:T(8,128)S(1)}, u32[]{:S(2)}, u32[]{:S(2)}) collective-permute-start(f32[8,128]{1,0:T(8,128)S(1)} %get-tuple-element.49), channel_id=1, source_target_pairs={{0,2},{1,7},{2,8},{3,13},{4,6},{5,3},{6,12},{7,9},{8,10},{9,15},{1... | collective-permute-start | bytes 12296 | tf_op jit(solution)/shard_map/ppermute | solution.py:332
  44.8 7.1 %collective-permute-start.14 = (f32[8,128]{1,0:T(8,128)S(1)}, f32[8,128]{1,0:T(8,128)S(1)}, u32[]{:S(2)}, u32[]{:S(2)}) collective-permute-start(f32[8,128]{1,0:T(8,128)S(1)} %get-tuple-element.50), channel_id=1, source_target_pairs={{0,0},{1,5},{2,10},{3,15},{4,4},{5,1},{6,14},{7,11},{8,8},{9,13},{... | collective-permute-start | bytes 12296 | tf_op jit(solution)/shard_map/ppermute | solution.py:332
  45.4 6.4 %collective-permute-start.15 = (f32[8,128]{1,0:T(8,128)S(1)}, f32[8,128]{1,0:T(8,128)S(1)}, u32[]{:S(2)}, u32[]{:S(2)}) collective-permute-start(f32[8,128]{1,0:T(8,128)S(1)} %get-tuple-element.52), channel_id=1, source_target_pairs={{0,1},{1,4},{2,11},{3,14},{4,5},{5,0},{6,15},{7,10},{8,9},{9,12},{... | collective-permute-start | bytes 12296 | tf_op jit(solution)/shard_map/ppermute | solution.py:332
  47.9 6.0 %collective-permute-start.17 = (f32[8,128]{1,0:T(8,128)S(1)}, f32[8,128]{1,0:T(8,128)S(1)}, u32[]{:S(2)}, u32[]{:S(2)}) collective-permute-start(f32[8,128]{1,0:T(8,128)S(1)} %get-tuple-element.53), channel_id=1, source_target_pairs={{0,3},{1,6},{2,9},{3,12},{4,7},{5,2},{6,13},{7,8},{8,11},{9,14},{1... | collective-permute-start | bytes 12296 | tf_op jit(solution)/shard_map/ppermute | solution.py:332

commit v6 on v5

--- a/solution.py
+++ b/solution.py
@@ -243,18 +243,18 @@
 
 
 def near_kernel(share, count, height, *refs):
-    vectors, green, outs = refs[:count], refs[count], refs[-count:]
+    vectors, green, outs = refs[:count], refs[count], refs[-1]
     for v in range(count):
-        held = jnp.zeros(outs[v].shape, F32)
+        held = jnp.zeros(outs.shape[1:], F32)
         for g in range(vectors[v].shape[0] // height):
             full = dot(vectors[v][g * height : (g + 1) * height, :], green[...])
             held = report(share, held, g, full[: height // 2], full[height // 2 :])
-        outs[v][...] = held
+        outs[v] = held
 
 
 def shared_kernel(share, count, height, *refs):
     firsts, seconds, green = refs[:count], refs[count : 2 * count], refs[2 * count]
-    outs, kept, both = refs[-2 * count - 1 : -count - 1], refs[-count - 1 : -1], refs[-1]
+    outs, kept, both = refs[-count - 2], refs[-count - 1 : -1], refs[-1]
     parity = lax.axis_index("walk") & 1
     half = height // 2
     for v in range(count):
@@ -262,18 +262,18 @@
         for at, piece in ((parity, firsts[v]), (1 - parity, seconds[v])):
             both[pl.ds(pl.multiple_of(at * rows, 16), rows), :] = dot(piece[...], green[...])
         kept[v][...] = both[:half, :]
-        held = jnp.zeros(outs[v].shape, F32)
+        held = jnp.zeros(outs.shape[1:], F32)
         for g in range(1, (2 * rows + half) // height):
             start = g * height - half
             held = report(share, held, g, both[start : start + half, :], both[start + half : start + height, :])
-        outs[v][...] = held
+        outs[v] = held
 
 
 def direct_kernel(share, count, *refs):
-    uppers, green, kept, before = refs[:count], refs[count], refs[count + 1 : 2 * count + 1], refs[2 * count + 1 : -count]
-    outs = refs[-count:]
+    uppers, green, kept = refs[:count], refs[count], refs[count + 1 : 2 * count + 1]
+    before, outs = refs[-2:]
     for v in range(count):
-        outs[v][...] = report(share, before[v][...], 0, dot(uppers[v][...], green[...]), kept[v][...])
+        outs[v] = report(share, before[v], 0, dot(uppers[v][...], green[...]), kept[v][...])
 
 
 def contract(kernel, count, vectors, green, *more, kept_rows=0, scratch_rows=0):
@@ -281,9 +281,9 @@
     kept = [jax.ShapeDtypeStruct((kept_rows, wide), F32)] * count if kept_rows else []
     return pl.pallas_call(
         kernel,
-        out_shape=[jax.ShapeDtypeStruct((8, 128), F32)] * count + kept,
+        out_shape=[jax.ShapeDtypeStruct((count, 8, 128), F32)] + kept,
         in_specs=[whole()] * (len(vectors) + 1 + len(more)),
-        out_specs=[whole()] * (count + len(kept)),
+        out_specs=[whole()] * (1 + len(kept)),
         scratch_shapes=[pltpu.VMEM((scratch_rows, wide), F32)] if scratch_rows else [],
         compiler_params=pltpu.CompilerParams(vmem_limit_bytes=VMEM_LIMIT),
         cost_estimate=pl.CostEstimate(
@@ -303,8 +303,10 @@
             line = jnp.zeros((1, 128), F32)
             for k in range(n):
                 for r in range(share):
-                    at = which * (arrived[k].shape[0] // 2) + g * share + r
-                    line = jnp.where(masks[k * share + r : k * share + r + 1, :] > 0.0, arrived[k][at : at + 1, :], line)
+                    cores, height = arrived[k].shape[:2]
+                    at = which * (height // 2) + g * share + r
+                    value = arrived[k][k % cores, at : at + 1, :]
+                    line = jnp.where(masks[k * share + r : k * share + r + 1, :] > 0.0, value, line)
             out[g : g + 1, :] = line[:, :per]
 
 
@@ -368,21 +370,21 @@
     other = {k: swap(x) for k, x in crossed.items()}
     green = make_green(n, share, blocks, turned, asked)
     crossed, other, direct = (along({k: ordered(x, green) for k, x in held.items()}) for held in (crossed, other, direct))
-    results = contract(functools.partial(near_kernel, share, len(near), height), len(near), close, green)
-    late = contract(
+    [results] = contract(functools.partial(near_kernel, share, len(near), height), len(near), close, green)
+    late, *kept = contract(
         functools.partial(shared_kernel, share, len(far), height),
         len(far),
         [crossed[k] for k in far] + [other[k] for k in far],
-        ordered(green, results[0]),
+        ordered(green, results),
         kept_rows=direct_rows,
         scratch_rows=2 * shared_rows,
     )
-    late = contract(
-        functools.partial(direct_kernel, share, len(far)), len(far), [direct[k] for k in far], green,
-        *late[len(far) :], *late[: len(far)],
+    [late] = contract(
+        functools.partial(direct_kernel, share, len(far)), len(far), [direct[k] for k in far], green, *kept, late
     )
-    arrived = [answer(x if k in far else ordered(x, late[0]), k) for k, x in enumerate(list(results) + list(late))]
-    return tuple(x.T for x in unpack(n, per, share, vectors, masks, arrived))
+    answers = [answer(late, far[0]), answer(ordered(results, late), 0)]
+    arrived = [[x] + [move(x, k) for k in near[1:]] for x in reversed(answers)]
+    return tuple(x.T for x in unpack(n, per, share, vectors, masks, [x for held in arrived for x in held]))
 
 
 def newton_schulz(intersection):
@@ -445,7 +447,7 @@
 def on_device(walkers, trial_orbitals, cholesky, branches, counts, field):
     walk_size, shard_count = lax.axis_size("walk"), lax.axis_size(SR)
     per = walkers.shape[0]
-    if walk_size == shard_count and per % walk_size == 0 and not walk_size & (walk_size - 1):
+    if walk_size == shard_count and lax.axis_size("slab") == 2 and per % walk_size == 0 and not walk_size & (walk_size - 1):
         if cholesky.shape[0] * (per // walk_size) <= 4 and cholesky.shape[1] % 64 == 0 and per <= 128:
             return at_the_source(walkers, trial_orbitals, cholesky, branches, counts, field)
     return at_the_target(walkers, trial_orbitals, cholesky, branches, counts, field)

time: 54.7 us -> 52.9 us (0.967)
  starting transfers between devices: 23.4 us -> 20.8 us
  waiting for transfers between devices: 12.5 us -> 13.3 us
    ppermute x4 -> x2, starting transfers between devices: 8.61 us -> 6.04 us  [at_the_source(): lax.ppermute(x, ALL, [(w * n + q, (w ^ q) * n + (q ^ k)) for w, q in pairs])]
    ppermute x12 -> x14, waiting for transfers between devices: 10.5 us -> 11.6 us  [at_the_source(): move = lambda x, k: lax.ppermute(x, SR, [(i, i ^ k) for i in range(n)])]
    ppermute x4 -> x2, waiting for transfers between devices: 2.09 us -> 1.66 us  [at_the_source(): lax.ppermute(x, ALL, [(w * n + q, (w ^ q) * n + (q ^ k)) for w, q in pairs])]
    ppermute x12 -> x14, starting transfers between devices: 12.1 us -> 12.1 us  [at_the_source(): move = lambda x, k: lax.ppermute(x, SR, [(i, i ^ k) for i in range(n)])]
  transfers between devices with their start and end apart: 18 -> 18, of which waited for: 5 -> 6; matrix products, arithmetic and copies ran while one was open for 2% -> 2% of each run, Pallas kernels for 25% -> 26%
where the time goes in v6:
time: 52.9 us; the launch traced here: 52.7 us
  starting transfers between devices  20.8 us (39%)
  Pallas kernels  14.8 us (28%)
  waiting for transfers between devices  13.3 us (25%)
  local copies, waits for them, and re-layouts  2.32 us (4%)
  between operations  1.45 us (3%)
    ppermute x14, starting transfers between devices, at_the_source(): move = lambda x, k: lax.ppermute(x, SR, [(i, i ^ k) for i in range(n)])  12.1 us
    ppermute x14, waiting for transfers between devices, at_the_source(): move = lambda x, k: lax.ppermute(x, SR, [(i, i ^ k) for i in range(n)])  11.6 us
    pallas_call x1, Pallas kernels, make_green(): pl.pallas_call(functools.partial(green_kernel, n, share), out_shape=jax.S...  7.02 us
    ppermute x2, starting transfers between devices, at_the_source(): lax.ppermute(x, ALL, [(w * n + q, (w ^ q) * n + (q ^ k)) for w, q in pairs])  6.04 us
    pallas_call x3, Pallas kernels, contract(): pl.pallas_call(kernel, out_shape=[jax.ShapeDtypeStruct((count, 8, 128), F...  3.62 us
    pallas_call x1, Pallas kernels, select(): pl.pallas_call(functools.partial(select_kernel, n, per, share), out_shape...  2.17 us
    ppermute x1, starting transfers between devices, at_the_source(): swap = lambda x: lax.ppermute(x, 'walk', [(w, w ^ 1) for w in range(n)])  2.03 us
    ppermute x2, waiting for transfers between devices, at_the_source(): lax.ppermute(x, ALL, [(w * n + q, (w ^ q) * n + (q ^ k)) for w, q in pairs])  1.66 us
  transfers between devices with their start and end apart: 18, of which 6 were waited for; matrix products, arithmetic and copies ran while one was open for 2% of the time, Pallas kernels for 26%

profile of v6, /device:TPU:0, one launch (start us, length us, event | category | flops | bytes accessed | tf_op | source)
XLA Modules:
  0.0 52.7 jit_solution(17841718722115670051)
XLA Ops:
  0.6 0.5 collective-permute-start.3
  1.1 0.0 copy-start.4
  1.2 0.0 copy-start.2
  1.2 0.0 copy-start.3
  1.2 1.1 %constant_dynamic-slice_fusion = bf16[192,1024]{1,0:T(8,128)(2,1)S(1)} fusion(bf16[512,1024]{1,0:T(8,128)(2,1)} %bitcast.4, s32[]{:T(128)S(6)} %select_n.3), kind=kLoop, calls=%fused_computation | loop fusion | bytes 786436 | tf_op jit(solution)/shard_map/dynamic_slice | solution.py:355
  2.2 2.6 %collective-permute-start.6 = (bf16[192,1024]{1,0:T(8,128)(2,1)S(1)}, bf16[192,1024]{1,0:T(8,128)(2,1)S(1)}, u32[]{:S(2)}, u32[]{:S(2)}) collective-permute-start(bf16[192,1024]{1,0:T(8,128)(2,1)S(1)} %constant_dynamic-slice_fusion), channel_id=1, source_target_pairs={{0,2},{1,3},{2,0},{3,1},{4,6},{5,7},{6,4},{7,5},{8,10},{9,11},{10,... | collective-permute-start | bytes 1179656 | tf_op jit(solution)/shard_map/ppermute | solution.py:331
  4.8 0.0 copy-done.4
  4.8 0.0 copy-start
  4.8 1.2 %copy-done = bf16[8,256,256]{2,1,0:T(8,128)(2,1)S(1)} copy-done((bf16[8,256,256]{2,1,0:T(8,128)(2,1)S(1)}, bf16[8,256,256]{2,1,0:T(8,128)(2,1)}, u32[]{:S(2)}) %copy-start) | copy-done | bytes 1048600
  6.0 0.0 copy-start.1
  6.1 2.2 %select.1 = (bf16[2,256,256]{2,1,0:T(8,128)(2,1)S(1)}, bf16[2,256,256]{2,1,0:T(8,128)(2,1)S(1)}, bf16[2,256,256]{2,1,0:T(8,128)(2,1)S(1)}, bf16[2,256,256]{2,1,0:T(8,128)(2,1)S(1)}) custom-call(s32[32]{0:T(128)S(1)} %copy-done.4, bf16[8,256,256]{2,1,0:T(8,128)(2,1)S(1)} %copy-done), custom_call_target="tpu_custom_call" | custom-call | tf_op jit(solution)/shard_map/select/pallas_call | solution.py:68
  8.2 0.0 copy-done.2
  8.2 0.0 copy-done.3
  8.3 0.1 collective-permute-start.1
  8.4 6.4 %collective-permute-done.6.refs_0_ = bf16[192,1024]{1,0:T(8,128)(2,1)S(1)} collective-permute-done((bf16[192,1024]{1,0:T(8,128)(2,1)S(1)}, bf16[192,1024]{1,0:T(8,128)(2,1)S(1)}, u32[]{:S(2)}, u32[]{:S(2)}) %collective-permute-start.6) | collective-permute-done | bytes 393248 | tf_op jit(solution)/shard_map/ppermute | solution.py:331
  14.8 2.0 %collective-permute-start.12 = (bf16[192,1024]{1,0:T(8,128)(2,1)S(1)}, bf16[192,1024]{1,0:T(8,128)(2,1)S(1)}, u32[]{:S(2)}, u32[]{:S(2)}) collective-permute-start(bf16[192,1024]{1,0:T(8,128)(2,1)S(1)} %collective-permute-done.6.refs_0_), channel_id=1, source_target_pairs={{0,4},{4,0},{8,12},{12,8},{1,5},{5,1},{9,13},{13,9},{2,6},{6,2},{1... | collective-permute-start | bytes 1179656 | tf_op jit(solution)/shard_map/ppermute | solution.py:332
  16.8 0.0 collective-permute-start
  16.8 1.6 %collective-permute-start.7 = (bf16[2,256,256]{2,1,0:T(8,128)(2,1)S(1)}, bf16[2,256,256]{2,1,0:T(8,128)(2,1)S(1)}, u32[]{:S(2)}, u32[]{:S(2)}) collective-permute-start(bf16[2,256,256]{2,1,0:T(8,128)(2,1)S(1)} %get-tuple-element.31), channel_id=1, source_target_pairs={{0,3},{1,2},{2,1},{3,0},{4,7},{5,6},{6,5},{7,4},{8,11},{9,10},{10,... | collective-permute-start | bytes 786440 | tf_op jit(solution)/shard_map/ppermute | solution.py:331
  18.4 0.0 collective-permute-done.1.refs_2_
  18.4 0.0 collective-permute-done.3.refs_1_
  18.4 0.0 collective-permute-start.4
  18.4 1.0 %collective-permute-start.5 = (bf16[2,256,256]{2,1,0:T(8,128)(2,1)S(1)}, bf16[2,256,256]{2,1,0:T(8,128)(2,1)S(1)}, u32[]{:S(2)}, u32[]{:S(2)}) collective-permute-start(bf16[2,256,256]{2,1,0:T(8,128)(2,1)S(1)} %get-tuple-element.29), channel_id=1, source_target_pairs={{0,2},{1,3},{2,0},{3,1},{4,6},{5,7},{6,4},{7,5},{8,10},{9,11},{10,... | collective-permute-start | bytes 786440 | tf_op jit(solution)/shard_map/ppermute | solution.py:331
  19.5 0.0 collective-permute-done.refs_1_
  19.5 0.2 collective-permute-start.2
  19.7 1.1 %collective-permute-done.2.refs_3_ = bf16[288,256]{1,0:T(8,128)(2,1)S(1)} collective-permute-done((bf16[288,256]{1,0:T(8,128)(2,1)S(1)}, bf16[288,256]{1,0:T(8,128)(2,1)S(1)}, u32[]{:S(2)}, u32[]{:S(2)}) %collective-permute-start.2) | collective-permute-done | bytes 147488 | tf_op jit(solution)/shard_map/ppermute | solution.py:331
  20.8 0.6 %fields.1 = f32[4,2,256]{2,1,0:T(2,128)S(1)} custom-call(s32[32]{0:T(128)S(1)} %copy-done.4, bf16[288,256]{1,0:T(8,128)(2,1)S(1)} %message.1.refs_0_, bf16[288,256]{1,0:T(8,128)(2,1)S(1)} %collective-permute-done.refs_1_, bf16[288,256]{1,0:T(8,128)(2,1)S(1)} %collective-permute-done.1.refs_2_, bf16[288,256]{1,0:T(8,128)(2,1)S(1)} %collective-permute-done.2.refs_3_), custom_call_target="tpu_custom_call" | custom-call | tf_op jit(solution)/shard_map/fields/pallas_call | solution.py:118
  21.5 0.7 %collective-permute-start.8 = (f32[4,2,256]{2,1,0:T(2,128)S(1)}, f32[4,2,256]{2,1,0:T(2,128)S(1)}, u32[]{:S(2)}, u32[]{:S(2)}) collective-permute-start(f32[4,2,256]{2,1,0:T(2,128)S(1)} %fields.1), channel_id=1, source_target_pairs={{0,0},{1,5},{2,10},{3,15},{4,4},{5,1},{6,14},{7,11},{8,8},{9,13},{... | collective-permute-start | bytes 24584 | tf_op jit(solution)/shard_map/ppermute | solution.py:333
  22.1 0.0 copy-done.1
  22.8 0.8 %turn.1 = (bf16[256,1024]{1,0:T(8,128)(2,1)S(1)}, f32[8,128]{1,0:T(8,128)S(1)}) custom-call(s32[32]{0:T(128)S(1)} %copy-done.4, s32[1]{0:T(128)S(6)} %copy.8.counts, bf16[288,256]{1,0:T(8,128)(2,1)S(1)} %message.1.refs_0_, bf16[288,256]{1,0:T(8,128)(2,1)S(1)} %collective-permute-done.refs_1_, bf16[288,256]{1,0:T(8,128)(2,1)S(1)} %collective-permute-done.1.refs_2_, ...), custom_call_target="tpu_custom_call" | custom-call | tf_op jit(solution)/shard_map/turn/pallas_call | solution.py:145
  23.6 0.0 collective-permute-done.8.refs_5_
  23.6 5.3 %collective-permute-start.9 = (bf16[128,1024]{1,0:T(8,128)(2,1)S(1)}, bf16[128,1024]{1,0:T(8,128)(2,1)S(1)}, u32[]{:S(2)}, u32[]{:S(2)}) collective-permute-start(bf16[128,1024]{1,0:T(8,128)(2,1)S(1)} %slice.4), channel_id=1, source_target_pairs={{0,2},{1,3},{2,0},{3,1},{4,6},{5,7},{6,4},{7,5},{8,10},{9,11},{10,... | collective-permute-start | bytes 786440 | tf_op jit(solution)/shard_map/ppermute | solution.py:331
  29.0 0.0 collective-permute-done.7.refs_3_
  29.0 0.0 collective-permute-done.4.refs_1_
  29.0 2.7 %collective-permute-done.5.refs_2_ = bf16[2,256,256]{2,1,0:T(8,128)(2,1)S(1)} collective-permute-done((bf16[2,256,256]{2,1,0:T(8,128)(2,1)S(1)}, bf16[2,256,256]{2,1,0:T(8,128)(2,1)S(1)}, u32[]{:S(2)}, u32[]{:S(2)}) %collective-permute-start.5) | collective-permute-done | bytes 262176 | tf_op jit(solution)/shard_map/ppermute | solution.py:331
  31.7 7.0 %green.1.refs_2_.refs_4_ = bf16[1024,512]{1,0:T(8,128)(2,1)S(1)} custom-call(bf16[2,256,256]{2,1,0:T(8,128)(2,1)S(1)} %get-tuple-element.23.refs_0_, bf16[2,256,256]{2,1,0:T(8,128)(2,1)S(1)} %collective-permute-done.4.refs_1_, bf16[2,256,256]{2,1,0:T(8,128)(2,1)S(1)} %collective-permute-done.5.refs_2_, ...), custom_call_target="tpu_custom_call" | custom-call | tf_op jit(solution)/shard_map/green/pallas_call | solution.py:214
  38.7 0.1 collective-permute-start.11
  38.8 0.0 collective-permute-done.12.refs_2_
  38.8 0.5 collective-permute-start.13
  39.3 0.0 collective-permute-done.9.refs_0_
  39.3 0.1 collective-permute-start.10
  39.4 1.5 %contract.3 = f32[2,8,128]{2,1,0:T(8,128)S(1)} custom-call(bf16[512,1024]{1,0:T(8,128)(2,1)S(1)} %bitcast.6, bf16[512,1024]{1,0:T(8,128)(2,1)S(1)} %collective-permute-done.3.refs_1_, bf16[1024,512]{1,0:T(8,128)(2,1)S(1)} %green.1.refs_2_.refs_4_), custom_call_target="tpu_custom_call" | custom-call | flops 1073741824 | bytes 3145728 | tf_op jit(solution)/shard_map/contract/pallas_call | solution.py:282
  40.9 0.0 collective-permute-done.11.refs_1_
  40.9 0.1 collective-permute-done.13.refs_3_
  41.1 1.4 %contract.4 = (f32[2,8,128]{2,1,0:T(8,128)S(1)}, f32[128,512]{1,0:T(8,128)S(1)}, f32[128,512]{1,0:T(8,128)S(1)}) custom-call(bf16[192,1024]{1,0:T(8,128)(2,1)S(1)} %collective-permute-done.6.refs_0_, bf16[192,1024]{1,0:T(8,128)(2,1)S(1)} %collective-permute-done.11.refs_1_, bf16[192,1024]{1,0:T(8,128)(2,1)S(1)} %collective-permute-done.12.refs_2_, ...), custom_call_target="tpu_custom_call" | custom-call | flops 805306368 | bytes 2621440 | tf_op jit(solution)/shard_map/contract/pallas_call | solution.py:282
  42.5 0.0 collective-permute-done.10.refs_1_
  42.5 0.7 %contract.5 = f32[2,8,128]{2,1,0:T(8,128)S(1)} custom-call(bf16[128,1024]{1,0:T(8,128)(2,1)S(1)} %collective-permute-done.9.refs_0_, bf16[128,1024]{1,0:T(8,128)(2,1)S(1)} %collective-permute-done.10.refs_1_, bf16[1024,512]{1,0:T(8,128)(2,1)S(1)} %green.1.refs_2_.refs_4_, f32[128,512]{1,0:T(8,128)S(1)} %get-tuple-element.38.refs_3_, ...), custom_call_target="tpu_custom_call" | custom-call | flops 268435456 | bytes 1572864 | tf_op jit(solution)/shard_map/contract/pallas_call | solution.py:282
  43.2 0.7 %collective-permute-start.14 = (f32[2,8,128]{2,1,0:T(8,128)S(1)}, f32[2,8,128]{2,1,0:T(8,128)S(1)}, u32[]{:S(2)}, u32[]{:S(2)}) collective-permute-start(f32[2,8,128]{2,1,0:T(8,128)S(1)} %contract.3), channel_id=1, source_target_pairs={{0,0},{1,5},{2,10},{3,15},{4,4},{5,1},{6,14},{7,11},{8,8},{9,13},{... | collective-permute-start | bytes 24584 | tf_op jit(solution)/shard_map/ppermute | solution.py:334
  43.9 5.4 %collective-permute-start.16 = (f32[2,8,128]{2,1,0:T(8,128)S(1)}, f32[2,8,128]{2,1,0:T(8,128)S(1)}, u32[]{:S(2)}, u32[]{:S(2)}) collective-permute-start(f32[2,8,128]{2,1,0:T(8,128)S(1)} %contract.5), channel_id=1, source_target_pairs={{0,2},{1,7},{2,8},{3,13},{4,6},{5,3},{6,12},{7,9},{8,10},{9,15},{1... | collective-permute-start | bytes 24584 | tf_op jit(solution)/shard_map/ppermute | solution.py:334
  49.3 0.0 collective-permute-done.14.refs_0_
  49.3 0.0 collective-permute-start.15
  49.3 1.7 %collective-permute-done.16.refs_2_ = f32[2,8,128]{2,1,0:T(8,128)S(1)} collective-permute-done((f32[2,8,128]{2,1,0:T(8,128)S(1)}, f32[2,8,128]{2,1,0:T(8,128)S(1)}, u32[]{:S(2)}, u32[]{:S(2)}) %collective-permute-start.16) | collective-permute-done | bytes 8224 | tf_op jit(solution)/shard_map/ppermute | solution.py:334
  50.9 0.0 collective-permute-start.17
  50.9 0.0 collective-permute-done.15.refs_1_
  50.9 1.2 %collective-permute-done.17.refs_3_ = f32[2,8,128]{2,1,0:T(8,128)S(1)} collective-permute-done((f32[2,8,128]{2,1,0:T(8,128)S(1)}, f32[2,8,128]{2,1,0:T(8,128)S(1)}, u32[]{:S(2)}, u32[]{:S(2)}) %collective-permute-start.17) | collective-permute-done | bytes 8224 | tf_op jit(solution)/shard_map/ppermute | solution.py:331
  52.1 0.6 %unpack.1 = (f32[2,8]{1,0:T(2,128)}, f32[2,8]{1,0:T(2,128)}) custom-call(f32[8,128]{1,0:T(8,128)S(1)} %get-tuple-element.25.masks, f32[2,8,128]{2,1,0:T(8,128)S(1)} %collective-permute-done.14.refs_0_, f32[2,8,128]{2,1,0:T(8,128)S(1)} %collective-permute-done.15.refs_1_, f32[2,8,128]{2,1,0:T(8,128)S(1)} %collective-permute-done.16.refs_2_, ...), custom_call_target="tpu_custom_call" | custom-call | tf_op jit(solution)/shard_map/unpack/pallas_call | solution.py:314
  (2 shorter events, 0.0 us)
Async XLA Ops:
  0.6 17.8 %collective-permute-start.3 = (bf16[512,1024]{1,0:T(8,128)(2,1)}, bf16[512,1024]{1,0:T(8,128)(2,1)S(1)}, u32[]{:S(2)}, u32[]{:S(2)}) collective-permute-start(bf16[512,1024]{1,0:T(8,128)(2,1)} %bitcast.3), channel_id=1, source_target_pairs={{0,1},{1,0},{2,3},{3,2},{4,5},{5,4},{6,7},{7,6},{8,9},{9,8},{10,11... | collective-permute-start | bytes 3145736 | tf_op jit(solution)/shard_map/ppermute | solution.py:331
  1.1 3.7 %copy-start.4 = (s32[32]{0:T(128)S(1)}, s32[32]{0:T(128)}, u32[]{:S(2)}) copy-start(s32[32]{0:T(128)} %branches.5) | copy-start | bytes 388
  1.2 7.1 %copy-start.2 = (bf16[256,256]{1,0:T(8,128)(2,1)S(1)}, bf16[256,256]{1,0:T(8,128)(2,1)}, u32[]{:S(2)}) copy-start(bf16[256,256]{1,0:T(8,128)(2,1)} %trial) | copy-start | bytes 393220
  1.2 7.1 %copy-start.3 = (f32[8,256]{1,0:T(8,128)S(1)}, f32[8,256]{1,0:T(8,128)}, u32[]{:S(2)}) copy-start(f32[8,256]{1,0:T(8,128)} %field.1) | copy-start | bytes 24580
  2.2 12.6 %collective-permute-start.6 = (bf16[192,1024]{1,0:T(8,128)(2,1)S(1)}, bf16[192,1024]{1,0:T(8,128)(2,1)S(1)}, u32[]{:S(2)}, u32[]{:S(2)}) collective-permute-start(bf16[192,1024]{1,0:T(8,128)(2,1)S(1)} %constant_dynamic-slice_fusion), channel_id=1, source_target_pairs={{0,2},{1,3},{2,0},{3,1},{4,6},{5,7},{6,4},{7,5},{8,10},{9,11},{10,... | collective-permute-start | bytes 1179656 | tf_op jit(solution)/shard_map/ppermute | solution.py:331
  4.8 1.2 %copy-start = (bf16[8,256,256]{2,1,0:T(8,128)(2,1)S(1)}, bf16[8,256,256]{2,1,0:T(8,128)(2,1)}, u32[]{:S(2)}) copy-start(bf16[8,256,256]{2,1,0:T(8,128)(2,1)} %walkers.1) | copy-start | bytes 3145732
  6.0 16.1 %copy-start.1 = (bf16[2,256,1024]{2,1,0:T(8,128)(2,1)S(1)}, bf16[2,256,1024]{2,1,0:T(8,128)(2,1)}, u32[]{:S(2)}) copy-start(bf16[2,256,1024]{2,1,0:T(8,128)(2,1)} %param.8) | copy-start | bytes 3145732
  8.3 10.2 %collective-permute-start.1 = (bf16[288,256]{1,0:T(8,128)(2,1)S(1)}, bf16[288,256]{1,0:T(8,128)(2,1)S(1)}, u32[]{:S(2)}, u32[]{:S(2)}) collective-permute-start(bf16[288,256]{1,0:T(8,128)(2,1)S(1)} %message.1.refs_0_), channel_id=1, source_target_pairs={{0,2},{1,3},{2,0},{3,1},{4,6},{5,7},{6,4},{7,5},{8,10},{9,11},{10,... | collective-permute-start | bytes 442376 | tf_op jit(solution)/shard_map/ppermute | solution.py:331
  14.8 24.0 %collective-permute-start.12 = (bf16[192,1024]{1,0:T(8,128)(2,1)S(1)}, bf16[192,1024]{1,0:T(8,128)(2,1)S(1)}, u32[]{:S(2)}, u32[]{:S(2)}) collective-permute-start(bf16[192,1024]{1,0:T(8,128)(2,1)S(1)} %collective-permute-done.6.refs_0_), channel_id=1, source_target_pairs={{0,4},{4,0},{8,12},{12,8},{1,5},{5,1},{9,13},{13,9},{2,6},{6,2},{1... | collective-permute-start | bytes 1179656 | tf_op jit(solution)/shard_map/ppermute | solution.py:332
  16.8 2.6 %collective-permute-start = (bf16[288,256]{1,0:T(8,128)(2,1)S(1)}, bf16[288,256]{1,0:T(8,128)(2,1)S(1)}, u32[]{:S(2)}, u32[]{:S(2)}) collective-permute-start(bf16[288,256]{1,0:T(8,128)(2,1)S(1)} %message.1.refs_0_), channel_id=1, source_target_pairs={{0,1},{1,0},{2,3},{3,2},{4,5},{5,4},{6,7},{7,6},{8,9},{9,8},{10,11... | collective-permute-start | bytes 442376 | tf_op jit(solution)/shard_map/ppermute | solution.py:331
  16.8 12.2 %collective-permute-start.7 = (bf16[2,256,256]{2,1,0:T(8,128)(2,1)S(1)}, bf16[2,256,256]{2,1,0:T(8,128)(2,1)S(1)}, u32[]{:S(2)}, u32[]{:S(2)}) collective-permute-start(bf16[2,256,256]{2,1,0:T(8,128)(2,1)S(1)} %get-tuple-element.31), channel_id=1, source_target_pairs={{0,3},{1,2},{2,1},{3,0},{4,7},{5,6},{6,5},{7,4},{8,11},{9,10},{10,... | collective-permute-start | bytes 786440 | tf_op jit(solution)/shard_map/ppermute | solution.py:331
  18.4 10.5 %collective-permute-start.4 = (bf16[2,256,256]{2,1,0:T(8,128)(2,1)S(1)}, bf16[2,256,256]{2,1,0:T(8,128)(2,1)S(1)}, u32[]{:S(2)}, u32[]{:S(2)}) collective-permute-start(bf16[2,256,256]{2,1,0:T(8,128)(2,1)S(1)} %get-tuple-element.27), channel_id=1, source_target_pairs={{0,1},{1,0},{2,3},{3,2},{4,5},{5,4},{6,7},{7,6},{8,9},{9,8},{10,11... | collective-permute-start | bytes 786440 | tf_op jit(solution)/shard_map/ppermute | solution.py:331
  18.4 13.2 %collective-permute-start.5 = (bf16[2,256,256]{2,1,0:T(8,128)(2,1)S(1)}, bf16[2,256,256]{2,1,0:T(8,128)(2,1)S(1)}, u32[]{:S(2)}, u32[]{:S(2)}) collective-permute-start(bf16[2,256,256]{2,1,0:T(8,128)(2,1)S(1)} %get-tuple-element.29), channel_id=1, source_target_pairs={{0,2},{1,3},{2,0},{3,1},{4,6},{5,7},{6,4},{7,5},{8,10},{9,11},{10,... | collective-permute-start | bytes 786440 | tf_op jit(solution)/shard_map/ppermute | solution.py:331
  19.5 1.4 %collective-permute-start.2 = (bf16[288,256]{1,0:T(8,128)(2,1)S(1)}, bf16[288,256]{1,0:T(8,128)(2,1)S(1)}, u32[]{:S(2)}, u32[]{:S(2)}) collective-permute-start(bf16[288,256]{1,0:T(8,128)(2,1)S(1)} %collective-permute-done.1.refs_2_), channel_id=1, source_target_pairs={{0,1},{1,0},{2,3},{3,2},{4,5},{5,4},{6,7},{7,6},{8,9},{9,8},{10,11... | collective-permute-start | bytes 442376 | tf_op jit(solution)/shard_map/ppermute | solution.py:331
  21.5 2.2 %collective-permute-start.8 = (f32[4,2,256]{2,1,0:T(2,128)S(1)}, f32[4,2,256]{2,1,0:T(2,128)S(1)}, u32[]{:S(2)}, u32[]{:S(2)}) collective-permute-start(f32[4,2,256]{2,1,0:T(2,128)S(1)} %fields.1), channel_id=1, source_target_pairs={{0,0},{1,5},{2,10},{3,15},{4,4},{5,1},{6,14},{7,11},{8,8},{9,13},{... | collective-permute-start | bytes 24584 | tf_op jit(solution)/shard_map/ppermute | solution.py:333
  23.6 15.7 %collective-permute-start.9 = (bf16[128,1024]{1,0:T(8,128)(2,1)S(1)}, bf16[128,1024]{1,0:T(8,128)(2,1)S(1)}, u32[]{:S(2)}, u32[]{:S(2)}) collective-permute-start(bf16[128,1024]{1,0:T(8,128)(2,1)S(1)} %slice.4), channel_id=1, source_target_pairs={{0,2},{1,3},{2,0},{3,1},{4,6},{5,7},{6,4},{7,5},{8,10},{9,11},{10,... | collective-permute-start | bytes 786440 | tf_op jit(solution)/shard_map/ppermute | solution.py:331
  38.7 2.2 %collective-permute-start.11 = (bf16[192,1024]{1,0:T(8,128)(2,1)S(1)}, bf16[192,1024]{1,0:T(8,128)(2,1)S(1)}, u32[]{:S(2)}, u32[]{:S(2)}) collective-permute-start(bf16[192,1024]{1,0:T(8,128)(2,1)S(1)} %collective-permute-done.6.refs_0_), channel_id=1, source_target_pairs={{0,1},{1,0},{2,3},{3,2},{4,5},{5,4},{6,7},{7,6},{8,9},{9,8},{10,11... | collective-permute-start | bytes 1179656 | tf_op jit(solution)/shard_map/ppermute | solution.py:331
  38.8 2.3 %collective-permute-start.13 = (bf16[192,1024]{1,0:T(8,128)(2,1)S(1)}, bf16[192,1024]{1,0:T(8,128)(2,1)S(1)}, u32[]{:S(2)}, u32[]{:S(2)}) collective-permute-start(bf16[192,1024]{1,0:T(8,128)(2,1)S(1)} %collective-permute-done.12.refs_2_), channel_id=1, source_target_pairs={{0,1},{1,0},{2,3},{3,2},{4,5},{5,4},{6,7},{7,6},{8,9},{9,8},{10,11... | collective-permute-start | bytes 1179656 | tf_op jit(solution)/shard_map/ppermute | solution.py:331
  39.3 3.2 %collective-permute-start.10 = (bf16[128,1024]{1,0:T(8,128)(2,1)S(1)}, bf16[128,1024]{1,0:T(8,128)(2,1)S(1)}, u32[]{:S(2)}, u32[]{:S(2)}) collective-permute-start(bf16[128,1024]{1,0:T(8,128)(2,1)S(1)} %collective-permute-done.9.refs_0_), channel_id=1, source_target_pairs={{0,1},{1,0},{2,3},{3,2},{4,5},{5,4},{6,7},{7,6},{8,9},{9,8},{10,11... | collective-permute-start | bytes 786440 | tf_op jit(solution)/shard_map/ppermute | solution.py:331
  43.2 6.1 %collective-permute-start.14 = (f32[2,8,128]{2,1,0:T(8,128)S(1)}, f32[2,8,128]{2,1,0:T(8,128)S(1)}, u32[]{:S(2)}, u32[]{:S(2)}) collective-permute-start(f32[2,8,128]{2,1,0:T(8,128)S(1)} %contract.3), channel_id=1, source_target_pairs={{0,0},{1,5},{2,10},{3,15},{4,4},{5,1},{6,14},{7,11},{8,8},{9,13},{... | collective-permute-start | bytes 24584 | tf_op jit(solution)/shard_map/ppermute | solution.py:334
  43.9 7.0 %collective-permute-start.16 = (f32[2,8,128]{2,1,0:T(8,128)S(1)}, f32[2,8,128]{2,1,0:T(8,128)S(1)}, u32[]{:S(2)}, u32[]{:S(2)}) collective-permute-start(f32[2,8,128]{2,1,0:T(8,128)S(1)} %contract.5), channel_id=1, source_target_pairs={{0,2},{1,7},{2,8},{3,13},{4,6},{5,3},{6,12},{7,9},{8,10},{9,15},{1... | collective-permute-start | bytes 24584 | tf_op jit(solution)/shard_map/ppermute | solution.py:334
  49.3 1.7 %collective-permute-start.15 = (f32[2,8,128]{2,1,0:T(8,128)S(1)}, f32[2,8,128]{2,1,0:T(8,128)S(1)}, u32[]{:S(2)}, u32[]{:S(2)}) collective-permute-start(f32[2,8,128]{2,1,0:T(8,128)S(1)} %collective-permute-done.14.refs_0_), channel_id=1, source_target_pairs={{0,1},{1,0},{2,3},{3,2},{4,5},{5,4},{6,7},{7,6},{8,9},{9,8},{10,11... | collective-permute-start | bytes 24584 | tf_op jit(solution)/shard_map/ppermute | solution.py:331
  50.9 1.2 %collective-permute-start.17 = (f32[2,8,128]{2,1,0:T(8,128)S(1)}, f32[2,8,128]{2,1,0:T(8,128)S(1)}, u32[]{:S(2)}, u32[]{:S(2)}) collective-permute-start(f32[2,8,128]{2,1,0:T(8,128)S(1)} %collective-permute-done.16.refs_2_), channel_id=1, source_target_pairs={{0,1},{1,0},{2,3},{3,2},{4,5},{5,4},{6,7},{7,6},{8,9},{9,8},{10,11... | collective-permute-start | bytes 24584 | tf_op jit(solution)/shard_map/ppermute | solution.py:331

commit v7 on v6

--- a/solution.py
+++ b/solution.py
@@ -15,6 +15,7 @@
 BF16 = jnp.bfloat16
 VMEM_LIMIT = 24 * 2**20
 SMALL_LIMIT = 2**20
+AHEAD = pl.CostEstimate(flops=2**36, bytes_accessed=2**22, transcendentals=0)
 HIGHEST = lax.Precision.HIGHEST
 
 
@@ -160,20 +161,50 @@
     return dot(high, high) + (mixed + mixed.T)
 
 
+def propagate(share, k, block, fields, moved, start):
+    q = place()[1]
+    rows, electrons = block.shape[1:]
+    lines = fields[pl.ds(q ^ k, 1), :, :].reshape(share, rows)
+    if share % 8:
+        lines = jnp.concatenate([lines, jnp.zeros((-share % 8, rows), F32)], axis=0)
+    columns = lines.T
+    for i in range(share):
+        moved[start : start + rows, i * electrons : (i + 1) * electrons] = (
+            block[i].astype(F32) * columns[:, i : i + 1]
+        ).astype(BF16)
+
+
+def first_kernel(n, share, *refs):
+    blocks, turned, fields, moved, overlaps = refs[: n - 1], *refs[n - 1 :]
+    rows = blocks[0].shape[1]
+    for k in range(n - 1):
+        propagate(share, k, blocks[k], fields, moved, k * rows)
+    overlaps[...] = dot(turned[:, : (n - 1) * rows], moved[...])
+
+
+def first_blocks(n, share, blocks, turned, fields):
+    rows, electrons = blocks[0].shape[1:]
+    return pl.pallas_call(
+        functools.partial(first_kernel, n, share),
+        out_shape=[
+            jax.ShapeDtypeStruct(((n - 1) * rows, share * electrons), BF16),
+            jax.ShapeDtypeStruct((electrons, share * electrons), F32),
+        ],
+        in_specs=[whole()] * (n + 1),
+        out_specs=[whole()] * 2,
+        compiler_params=pltpu.CompilerParams(vmem_limit_bytes=VMEM_LIMIT),
+        cost_estimate=AHEAD,
+        name="first",
+    )(*blocks, turned, fields)
+
+
 def green_kernel(n, share, *refs):
-    blocks, turned, fields = refs[:n], refs[n], refs[n + 1]
-    green, moved, left, right = refs[n + 2 :]
+    block, turned, fields, earlier, begun = refs[:5]
+    green, moved, left, right = refs[5:]
     q = place()[1]
-    rows, electrons = blocks[0].shape[1:]
-    spare = jnp.zeros((-share % 8, rows), F32)
-    for k in range(n):
-        lines = fields[pl.ds(q ^ k, 1), :, :].reshape(share, rows)
-        columns = (jnp.concatenate([lines, spare], axis=0) if share % 8 else lines).T
-        for i in range(share):
-            moved[k * rows : (k + 1) * rows, i * electrons : (i + 1) * electrons] = (
-                blocks[k][i].astype(F32) * columns[:, i : i + 1]
-            ).astype(BF16)
-    overlaps = dot(turned[...], moved[...])
+    rows, electrons = block.shape[1:]
+    propagate(share, n - 1, block, fields, moved, 0)
+    overlaps = begun[...] + dot(turned[:, (n - 1) * rows :], moved[...])
     for i in range(share):
         overlap = overlaps[:, i * electrons : (i + 1) * electrons]
         size = jnp.abs(overlap)
@@ -204,26 +235,27 @@
         inverse = (2.0 * left[i] - product).astype(BF16)
         for k in range(n):
             at = pl.multiple_of((q ^ k) * rows, rows)
+            held, start = (moved, 0) if k == n - 1 else (earlier, k * rows)
             green[pl.ds(at, rows), i * electrons : (i + 1) * electrons] = dot(
-                moved[k * rows : (k + 1) * rows, i * electrons : (i + 1) * electrons], inverse
+                held[start : start + rows, i * electrons : (i + 1) * electrons], inverse
             ).astype(BF16)
 
 
-def make_green(n, share, blocks, turned, fields):
-    rows, electrons = blocks[0].shape[1:]
+def make_green(n, share, block, turned, fields, earlier, begun):
+    rows, electrons = block.shape[1:]
     return pl.pallas_call(
         functools.partial(green_kernel, n, share),
         out_shape=jax.ShapeDtypeStruct((n * rows, share * electrons), BF16),
-        in_specs=[whole()] * (n + 2),
+        in_specs=[whole()] * 5,
         out_specs=whole(),
         scratch_shapes=[
-            pltpu.VMEM((n * rows, share * electrons), BF16),
+            pltpu.VMEM((rows, share * electrons), BF16),
             pltpu.VMEM((share, electrons, electrons), F32),
             pltpu.VMEM((share, electrons, electrons), F32),
         ],
         compiler_params=pltpu.CompilerParams(vmem_limit_bytes=VMEM_LIMIT),
         name="green",
-    )(*blocks, turned, fields)
+    )(block, turned, fields, earlier, begun)
 
 
 def report(share, held, index, upper, lower):
@@ -360,15 +392,16 @@
     messages = [messages[k] for k in range(n)]
     crossed = {k: move(shared, k) for k in heads}
     close = [rows] + [move(rows, k) for k in near[1:]]
-    early = [messages[far[0]], *close[1:]]
+    early = close[1:]
     blocks = [sends[0]] + [
         move(ordered(sends[k], *(crossed.values() if k == n - 1 else early)), k) for k in range(1, n)
     ]
     asked = ask(pick_fields(n, per, share, branches, messages))
     turned, masks = turn(n, per, share, branches, counts, messages)
-    direct = {k: move(ordered(rows[:direct_rows], asked, turned), k) for k in heads}
     other = {k: swap(x) for k, x in crossed.items()}
-    green = make_green(n, share, blocks, turned, asked)
+    earlier, begun = first_blocks(n, share, blocks[:-1], turned, asked)
+    direct = {k: move(ordered(rows[:direct_rows], begun), k) for k in heads}
+    green = make_green(n, share, blocks[n - 1], turned, asked, earlier, begun)
     crossed, other, direct = (along({k: ordered(x, green) for k, x in held.items()}) for held in (crossed, other, direct))
     [results] = contract(functools.partial(near_kernel, share, len(near), height), len(near), close, green)
     late, *kept = contract(

time: 52.9 us -> 56.6 us (1.070)
  waiting for transfers between devices: 13.3 us -> 18.2 us
  starting transfers between devices: 20.8 us -> 19.2 us
    ppermute x14, waiting for transfers between devices: 11.6 us -> 14.7 us  [at_the_source(): move = lambda x, k: lax.ppermute(x, SR, [(i, i ^ k) for i in range(n)])]
    ppermute x14, starting transfers between devices: 12.1 us -> 14.3 us  [at_the_source(): move = lambda x, k: lax.ppermute(x, SR, [(i, i ^ k) for i in range(n)])]
    ppermute x1, starting transfers between devices: 2.03 us -> 0.01 us  [at_the_source(): swap = lambda x: lax.ppermute(x, 'walk', [(w, w ^ 1) for w in range(n)])]
    ppermute x2, starting transfers between devices: 6.04 us -> 4.17 us  [at_the_source(): lax.ppermute(x, ALL, [(w * n + q, (w ^ q) * n + (q ^ k)) for w, q in pairs])]
    ppermute x2, waiting for transfers between devices: 1.66 us -> 3.49 us  [at_the_source(): lax.ppermute(x, ALL, [(w * n + q, (w ^ q) * n + (q ^ k)) for w, q in pairs])]
    pallas_call x0 -> x1, Pallas kernels: none -> 0.79 us  [first_blocks(): pl.pallas_call(functools.partial(first_kernel, n, share), out_shape=[jax....]
  transfers between devices with their start and end apart: 18 -> 18, of which waited for: 6 -> 6; matrix products, arithmetic and copies ran while one was open for 2% -> 2% of each run, Pallas kernels for 26% -> 25%
where the time goes in v7:
time: 56.6 us; the launch traced here: 56.4 us
  starting transfers between devices  19.2 us (34%)
  waiting for transfers between devices  18.2 us (32%)
  Pallas kernels  15.3 us (27%)
  local copies, waits for them, and re-layouts  2.32 us (4%)
  between operations  1.47 us (3%)
    ppermute x14, waiting for transfers between devices, at_the_source(): move = lambda x, k: lax.ppermute(x, SR, [(i, i ^ k) for i in range(n)])  14.7 us
    ppermute x14, starting transfers between devices, at_the_source(): move = lambda x, k: lax.ppermute(x, SR, [(i, i ^ k) for i in range(n)])  14.3 us
    pallas_call x1, Pallas kernels, make_green(): pl.pallas_call(functools.partial(green_kernel, n, share), out_shape=jax.S...  6.67 us
    ppermute x2, starting transfers between devices, at_the_source(): lax.ppermute(x, ALL, [(w * n + q, (w ^ q) * n + (q ^ k)) for w, q in pairs])  4.17 us
    pallas_call x3, Pallas kernels, contract(): pl.pallas_call(kernel, out_shape=[jax.ShapeDtypeStruct((count, 8, 128), F...  3.62 us
    ppermute x2, waiting for transfers between devices, at_the_source(): lax.ppermute(x, ALL, [(w * n + q, (w ^ q) * n + (q ^ k)) for w, q in pairs])  3.49 us
    pallas_call x1, Pallas kernels, select(): pl.pallas_call(functools.partial(select_kernel, n, per, share), out_shape...  2.17 us
    unnamed x10, local copies, waits for them, and re-layouts  1.24 us
  transfers between devices with their start and end apart: 18, of which 6 were waited for; matrix products, arithmetic and copies ran while one was open for 2% of the time, Pallas kernels for 25%

profile of v7, /device:TPU:0, one launch (start us, length us, event | category | flops | bytes accessed | tf_op | source)
XLA Modules:
  0.0 56.4 jit_solution(1831971696341341633)
XLA Ops:
  0.6 0.5 collective-permute-start.3
  1.1 0.0 copy-start.4
  1.2 0.0 copy-start.2
  1.2 0.0 copy-start.3
  1.2 1.1 %constant_dynamic-slice_fusion = bf16[192,1024]{1,0:T(8,128)(2,1)S(1)} fusion(bf16[512,1024]{1,0:T(8,128)(2,1)} %bitcast.4, s32[]{:T(128)S(6)} %select_n.3), kind=kLoop, calls=%fused_computation | loop fusion | bytes 786436 | tf_op jit(solution)/shard_map/dynamic_slice | solution.py:387
  2.2 2.6 %collective-permute-start.4 = (bf16[192,1024]{1,0:T(8,128)(2,1)S(1)}, bf16[192,1024]{1,0:T(8,128)(2,1)S(1)}, u32[]{:S(2)}, u32[]{:S(2)}) collective-permute-start(bf16[192,1024]{1,0:T(8,128)(2,1)S(1)} %constant_dynamic-slice_fusion), channel_id=1, source_target_pairs={{0,2},{1,3},{2,0},{3,1},{4,6},{5,7},{6,4},{7,5},{8,10},{9,11},{10,... | collective-permute-start | bytes 1179656 | tf_op jit(solution)/shard_map/ppermute | solution.py:363
  4.8 0.0 copy-done.4
  4.8 0.0 copy-start
  4.8 1.2 %copy-done = bf16[8,256,256]{2,1,0:T(8,128)(2,1)S(1)} copy-done((bf16[8,256,256]{2,1,0:T(8,128)(2,1)S(1)}, bf16[8,256,256]{2,1,0:T(8,128)(2,1)}, u32[]{:S(2)}) %copy-start) | copy-done | bytes 1048600
  6.0 0.0 copy-start.1
  6.1 2.2 %select.1 = (bf16[2,256,256]{2,1,0:T(8,128)(2,1)S(1)}, bf16[2,256,256]{2,1,0:T(8,128)(2,1)S(1)}, bf16[2,256,256]{2,1,0:T(8,128)(2,1)S(1)}, bf16[2,256,256]{2,1,0:T(8,128)(2,1)S(1)}) custom-call(s32[32]{0:T(128)S(1)} %copy-done.4, bf16[8,256,256]{2,1,0:T(8,128)(2,1)S(1)} %copy-done), custom_call_target="tpu_custom_call" | custom-call | tf_op jit(solution)/shard_map/select/pallas_call | solution.py:69
  8.2 0.0 copy-done.2
  8.2 0.0 copy-done.3
  8.3 0.1 collective-permute-start.1
  8.4 0.0 collective-permute-done.3.refs_1_
  8.4 0.2 collective-permute-start.7
  8.6 1.8 %collective-permute-start.8 = (bf16[2,256,256]{2,1,0:T(8,128)(2,1)S(1)}, bf16[2,256,256]{2,1,0:T(8,128)(2,1)S(1)}, u32[]{:S(2)}, u32[]{:S(2)}) collective-permute-start(bf16[2,256,256]{2,1,0:T(8,128)(2,1)S(1)} %get-tuple-element.34), channel_id=1, source_target_pairs={{0,2},{1,3},{2,0},{3,1},{4,6},{5,7},{6,4},{7,5},{8,10},{9,11},{10,... | collective-permute-start | bytes 786440 | tf_op jit(solution)/shard_map/ppermute | solution.py:363
  10.4 0.2 collective-permute-start
  10.6 7.3 %collective-permute-done.1.refs_2_ = bf16[288,256]{1,0:T(8,128)(2,1)S(1)} collective-permute-done((bf16[288,256]{1,0:T(8,128)(2,1)S(1)}, bf16[288,256]{1,0:T(8,128)(2,1)S(1)}, u32[]{:S(2)}, u32[]{:S(2)}) %collective-permute-start.1) | collective-permute-done | bytes 147488 | tf_op jit(solution)/shard_map/ppermute | solution.py:363
  17.9 0.0 collective-permute-start.2
  18.0 0.0 collective-permute-done.refs_1_
  18.0 1.4 %collective-permute-done.2.refs_3_ = bf16[288,256]{1,0:T(8,128)(2,1)S(1)} collective-permute-done((bf16[288,256]{1,0:T(8,128)(2,1)S(1)}, bf16[288,256]{1,0:T(8,128)(2,1)S(1)}, u32[]{:S(2)}, u32[]{:S(2)}) %collective-permute-start.2) | collective-permute-done | bytes 147488 | tf_op jit(solution)/shard_map/ppermute | solution.py:363
  19.3 0.6 %fields.1 = f32[4,2,256]{2,1,0:T(2,128)S(1)} custom-call(s32[32]{0:T(128)S(1)} %copy-done.4, bf16[288,256]{1,0:T(8,128)(2,1)S(1)} %message.1.refs_0_, bf16[288,256]{1,0:T(8,128)(2,1)S(1)} %collective-permute-done.refs_1_, bf16[288,256]{1,0:T(8,128)(2,1)S(1)} %collective-permute-done.1.refs_2_, bf16[288,256]{1,0:T(8,128)(2,1)S(1)} %collective-permute-done.2.refs_3_), custom_call_target="tpu_custom_call" | custom-call | tf_op jit(solution)/shard_map/fields/pallas_call | solution.py:119
  19.9 0.7 %collective-permute-start.6 = (f32[4,2,256]{2,1,0:T(2,128)S(1)}, f32[4,2,256]{2,1,0:T(2,128)S(1)}, u32[]{:S(2)}, u32[]{:S(2)}) collective-permute-start(f32[4,2,256]{2,1,0:T(2,128)S(1)} %fields.1), channel_id=1, source_target_pairs={{0,0},{1,5},{2,10},{3,15},{4,4},{5,1},{6,14},{7,11},{8,8},{9,13},{... | collective-permute-start | bytes 24584 | tf_op jit(solution)/shard_map/ppermute | solution.py:365
  20.6 0.0 copy-done.1
  21.3 0.8 %turn.1 = (bf16[256,1024]{1,0:T(8,128)(2,1)S(1)}, f32[8,128]{1,0:T(8,128)S(1)}) custom-call(s32[32]{0:T(128)S(1)} %copy-done.4, s32[1]{0:T(128)S(6)} %copy.8.counts, bf16[288,256]{1,0:T(8,128)(2,1)S(1)} %message.1.refs_0_, bf16[288,256]{1,0:T(8,128)(2,1)S(1)} %collective-permute-done.refs_1_, bf16[288,256]{1,0:T(8,128)(2,1)S(1)} %collective-permute-done.1.refs_2_, ...), custom_call_target="tpu_custom_call" | custom-call | tf_op jit(solution)/shard_map/turn/pallas_call | solution.py:146
  22.1 0.0 collective-permute-done.4.refs_0_
  22.1 6.3 %collective-permute-start.5 = (bf16[2,256,256]{2,1,0:T(8,128)(2,1)S(1)}, bf16[2,256,256]{2,1,0:T(8,128)(2,1)S(1)}, u32[]{:S(2)}, u32[]{:S(2)}) collective-permute-start(bf16[2,256,256]{2,1,0:T(8,128)(2,1)S(1)} %get-tuple-element.29), channel_id=1, source_target_pairs={{0,3},{1,2},{2,1},{3,0},{4,7},{5,6},{6,5},{7,4},{8,11},{9,10},{10,... | collective-permute-start | bytes 786440 | tf_op jit(solution)/shard_map/ppermute | solution.py:363
  28.4 0.0 collective-permute-start.12
  28.4 0.0 collective-permute-done.6.refs_4_.refs_2_
  28.4 0.0 collective-permute-done.7.refs_1_
  28.4 0.0 collective-permute-done.8.refs_2_
  28.5 0.8 %first.1 = (bf16[768,512]{1,0:T(8,128)(2,1)S(1)}, f32[256,512]{1,0:T(8,128)S(1)}) custom-call(bf16[2,256,256]{2,1,0:T(8,128)(2,1)S(1)} %get-tuple-element.25.refs_0_, bf16[2,256,256]{2,1,0:T(8,128)(2,1)S(1)} %collective-permute-done.7.refs_1_, bf16[2,256,256]{2,1,0:T(8,128)(2,1)S(1)} %collective-permute-done.8.refs_2_, ...), custom_call_target="tpu_custom_call" | custom-call | flops 68719476736 | bytes 4194304 | tf_op jit(solution)/shard_map/first/pallas_call | solution.py:187
  29.3 1.2 %collective-permute-start.9 = (bf16[128,1024]{1,0:T(8,128)(2,1)S(1)}, bf16[128,1024]{1,0:T(8,128)(2,1)S(1)}, u32[]{:S(2)}, u32[]{:S(2)}) collective-permute-start(bf16[128,1024]{1,0:T(8,128)(2,1)S(1)} %slice.4), channel_id=1, source_target_pairs={{0,2},{1,3},{2,0},{3,1},{4,6},{5,7},{6,4},{7,5},{8,10},{9,11},{10,... | collective-permute-start | bytes 786440 | tf_op jit(solution)/shard_map/ppermute | solution.py:363
  30.5 4.8 %collective-permute-done.5.refs_0_ = bf16[2,256,256]{2,1,0:T(8,128)(2,1)S(1)} collective-permute-done((bf16[2,256,256]{2,1,0:T(8,128)(2,1)S(1)}, bf16[2,256,256]{2,1,0:T(8,128)(2,1)S(1)}, u32[]{:S(2)}, u32[]{:S(2)}) %collective-permute-start.5) | collective-permute-done | bytes 262176 | tf_op jit(solution)/shard_map/ppermute | solution.py:363
  35.3 6.7 %green.1.refs_2_.refs_4_ = bf16[1024,512]{1,0:T(8,128)(2,1)S(1)} custom-call(bf16[2,256,256]{2,1,0:T(8,128)(2,1)S(1)} %collective-permute-done.5.refs_0_, bf16[256,1024]{1,0:T(8,128)(2,1)S(1)} %get-tuple-element.30.refs_3_.refs_1_, f32[4,2,256]{2,1,0:T(2,128)S(1)} %collective-permute-done.6.refs_4_.refs_2_, bf16[768,512]{1,0:T(8,128)(2,1)S(1)} %get-tuple-element.35.refs_3_, ...), custom_call_target="tpu_custom_call" | custom-call | tf_op jit(solution)/shard_map/green/pallas_call | solution.py:246
  42.0 0.1 collective-permute-start.11
  42.1 0.0 collective-permute-done.12.refs_2_
  42.1 0.5 collective-permute-start.13
  42.6 0.0 collective-permute-done.9.refs_0_
  42.6 0.1 collective-permute-start.10
  42.7 1.5 %contract.3 = f32[2,8,128]{2,1,0:T(8,128)S(1)} custom-call(bf16[512,1024]{1,0:T(8,128)(2,1)S(1)} %bitcast.6, bf16[512,1024]{1,0:T(8,128)(2,1)S(1)} %collective-permute-done.3.refs_1_, bf16[1024,512]{1,0:T(8,128)(2,1)S(1)} %green.1.refs_2_.refs_4_), custom_call_target="tpu_custom_call" | custom-call | flops 1073741824 | bytes 3145728 | tf_op jit(solution)/shard_map/contract/pallas_call | solution.py:314
  44.2 0.0 collective-permute-done.11.refs_1_
  44.2 0.1 collective-permute-done.13.refs_3_
  44.3 1.4 %contract.4 = (f32[2,8,128]{2,1,0:T(8,128)S(1)}, f32[128,512]{1,0:T(8,128)S(1)}, f32[128,512]{1,0:T(8,128)S(1)}) custom-call(bf16[192,1024]{1,0:T(8,128)(2,1)S(1)} %collective-permute-done.4.refs_0_, bf16[192,1024]{1,0:T(8,128)(2,1)S(1)} %collective-permute-done.11.refs_1_, bf16[192,1024]{1,0:T(8,128)(2,1)S(1)} %collective-permute-done.12.refs_2_, ...), custom_call_target="tpu_custom_call" | custom-call | flops 805306368 | bytes 2621440 | tf_op jit(solution)/shard_map/contract/pallas_call | solution.py:314
  45.7 0.0 collective-permute-done.10.refs_1_
  45.7 0.7 %contract.5 = f32[2,8,128]{2,1,0:T(8,128)S(1)} custom-call(bf16[128,1024]{1,0:T(8,128)(2,1)S(1)} %collective-permute-done.9.refs_0_, bf16[128,1024]{1,0:T(8,128)(2,1)S(1)} %collective-permute-done.10.refs_1_, bf16[1024,512]{1,0:T(8,128)(2,1)S(1)} %green.1.refs_2_.refs_4_, f32[128,512]{1,0:T(8,128)S(1)} %get-tuple-element.42.refs_3_, ...), custom_call_target="tpu_custom_call" | custom-call | flops 268435456 | bytes 1572864 | tf_op jit(solution)/shard_map/contract/pallas_call | solution.py:314
  46.5 0.7 %collective-permute-start.14 = (f32[2,8,128]{2,1,0:T(8,128)S(1)}, f32[2,8,128]{2,1,0:T(8,128)S(1)}, u32[]{:S(2)}, u32[]{:S(2)}) collective-permute-start(f32[2,8,128]{2,1,0:T(8,128)S(1)} %contract.3), channel_id=1, source_target_pairs={{0,0},{1,5},{2,10},{3,15},{4,4},{5,1},{6,14},{7,11},{8,8},{9,13},{... | collective-permute-start | bytes 24584 | tf_op jit(solution)/shard_map/ppermute | solution.py:366
  47.1 3.5 %collective-permute-start.16 = (f32[2,8,128]{2,1,0:T(8,128)S(1)}, f32[2,8,128]{2,1,0:T(8,128)S(1)}, u32[]{:S(2)}, u32[]{:S(2)}) collective-permute-start(f32[2,8,128]{2,1,0:T(8,128)S(1)} %contract.5), channel_id=1, source_target_pairs={{0,2},{1,7},{2,8},{3,13},{4,6},{5,3},{6,12},{7,9},{8,10},{9,15},{1... | collective-permute-start | bytes 24584 | tf_op jit(solution)/shard_map/ppermute | solution.py:366
  50.6 0.0 collective-permute-done.14.refs_0_
  50.6 0.5 collective-permute-start.15
  51.2 3.5 %collective-permute-done.16.refs_2_ = f32[2,8,128]{2,1,0:T(8,128)S(1)} collective-permute-done((f32[2,8,128]{2,1,0:T(8,128)S(1)}, f32[2,8,128]{2,1,0:T(8,128)S(1)}, u32[]{:S(2)}, u32[]{:S(2)}) %collective-permute-start.16) | collective-permute-done | bytes 8224 | tf_op jit(solution)/shard_map/ppermute | solution.py:366
  54.6 0.2 collective-permute-start.17
  54.8 0.0 collective-permute-done.15.refs_1_
  54.8 1.0 %collective-permute-done.17.refs_3_ = f32[2,8,128]{2,1,0:T(8,128)S(1)} collective-permute-done((f32[2,8,128]{2,1,0:T(8,128)S(1)}, f32[2,8,128]{2,1,0:T(8,128)S(1)}, u32[]{:S(2)}, u32[]{:S(2)}) %collective-permute-start.17) | collective-permute-done | bytes 8224 | tf_op jit(solution)/shard_map/ppermute | solution.py:363
  55.8 0.6 %unpack.1 = (f32[2,8]{1,0:T(2,128)}, f32[2,8]{1,0:T(2,128)}) custom-call(f32[8,128]{1,0:T(8,128)S(1)} %get-tuple-element.27.masks, f32[2,8,128]{2,1,0:T(8,128)S(1)} %collective-permute-done.14.refs_0_, f32[2,8,128]{2,1,0:T(8,128)S(1)} %collective-permute-done.15.refs_1_, f32[2,8,128]{2,1,0:T(8,128)S(1)} %collective-permute-done.16.refs_2_, ...), custom_call_target="tpu_custom_call" | custom-call | tf_op jit(solution)/shard_map/unpack/pallas_call | solution.py:346
  (2 shorter events, 0.0 us)
Async XLA Ops:
  0.6 7.7 %collective-permute-start.3 = (bf16[512,1024]{1,0:T(8,128)(2,1)}, bf16[512,1024]{1,0:T(8,128)(2,1)S(1)}, u32[]{:S(2)}, u32[]{:S(2)}) collective-permute-start(bf16[512,1024]{1,0:T(8,128)(2,1)} %bitcast.3), channel_id=1, source_target_pairs={{0,1},{1,0},{2,3},{3,2},{4,5},{5,4},{6,7},{7,6},{8,9},{9,8},{10,11... | collective-permute-start | bytes 3145736 | tf_op jit(solution)/shard_map/ppermute | solution.py:363
  1.1 3.7 %copy-start.4 = (s32[32]{0:T(128)S(1)}, s32[32]{0:T(128)}, u32[]{:S(2)}) copy-start(s32[32]{0:T(128)} %branches.5) | copy-start | bytes 388
  1.2 7.1 %copy-start.2 = (bf16[256,256]{1,0:T(8,128)(2,1)S(1)}, bf16[256,256]{1,0:T(8,128)(2,1)}, u32[]{:S(2)}) copy-start(bf16[256,256]{1,0:T(8,128)(2,1)} %trial) | copy-start | bytes 393220
  1.2 7.1 %copy-start.3 = (f32[8,256]{1,0:T(8,128)S(1)}, f32[8,256]{1,0:T(8,128)}, u32[]{:S(2)}) copy-start(f32[8,256]{1,0:T(8,128)} %field.1) | copy-start | bytes 24580
  2.2 19.9 %collective-permute-start.4 = (bf16[192,1024]{1,0:T(8,128)(2,1)S(1)}, bf16[192,1024]{1,0:T(8,128)(2,1)S(1)}, u32[]{:S(2)}, u32[]{:S(2)}) collective-permute-start(bf16[192,1024]{1,0:T(8,128)(2,1)S(1)} %constant_dynamic-slice_fusion), channel_id=1, source_target_pairs={{0,2},{1,3},{2,0},{3,1},{4,6},{5,7},{6,4},{7,5},{8,10},{9,11},{10,... | collective-permute-start | bytes 1179656 | tf_op jit(solution)/shard_map/ppermute | solution.py:363
  4.8 1.2 %copy-start = (bf16[8,256,256]{2,1,0:T(8,128)(2,1)S(1)}, bf16[8,256,256]{2,1,0:T(8,128)(2,1)}, u32[]{:S(2)}) copy-start(bf16[8,256,256]{2,1,0:T(8,128)(2,1)} %walkers.1) | copy-start | bytes 3145732
  6.0 14.6 %copy-start.1 = (bf16[2,256,1024]{2,1,0:T(8,128)(2,1)S(1)}, bf16[2,256,1024]{2,1,0:T(8,128)(2,1)}, u32[]{:S(2)}) copy-start(bf16[2,256,1024]{2,1,0:T(8,128)(2,1)} %param.8) | copy-start | bytes 3145732
  8.3 9.7 %collective-permute-start.1 = (bf16[288,256]{1,0:T(8,128)(2,1)S(1)}, bf16[288,256]{1,0:T(8,128)(2,1)S(1)}, u32[]{:S(2)}, u32[]{:S(2)}) collective-permute-start(bf16[288,256]{1,0:T(8,128)(2,1)S(1)} %message.1.refs_0_), channel_id=1, source_target_pairs={{0,2},{1,3},{2,0},{3,1},{4,6},{5,7},{6,4},{7,5},{8,10},{9,11},{10,... | collective-permute-start | bytes 442376 | tf_op jit(solution)/shard_map/ppermute | solution.py:363
  8.4 20.1 %collective-permute-start.7 = (bf16[2,256,256]{2,1,0:T(8,128)(2,1)S(1)}, bf16[2,256,256]{2,1,0:T(8,128)(2,1)S(1)}, u32[]{:S(2)}, u32[]{:S(2)}) collective-permute-start(bf16[2,256,256]{2,1,0:T(8,128)(2,1)S(1)} %get-tuple-element.32), channel_id=1, source_target_pairs={{0,1},{1,0},{2,3},{3,2},{4,5},{5,4},{6,7},{7,6},{8,9},{9,8},{10,11... | collective-permute-start | bytes 786440 | tf_op jit(solution)/shard_map/ppermute | solution.py:363
  8.6 19.8 %collective-permute-start.8 = (bf16[2,256,256]{2,1,0:T(8,128)(2,1)S(1)}, bf16[2,256,256]{2,1,0:T(8,128)(2,1)S(1)}, u32[]{:S(2)}, u32[]{:S(2)}) collective-permute-start(bf16[2,256,256]{2,1,0:T(8,128)(2,1)S(1)} %get-tuple-element.34), channel_id=1, source_target_pairs={{0,2},{1,3},{2,0},{3,1},{4,6},{5,7},{6,4},{7,5},{8,10},{9,11},{10,... | collective-permute-start | bytes 786440 | tf_op jit(solution)/shard_map/ppermute | solution.py:363
  10.4 7.6 %collective-permute-start = (bf16[288,256]{1,0:T(8,128)(2,1)S(1)}, bf16[288,256]{1,0:T(8,128)(2,1)S(1)}, u32[]{:S(2)}, u32[]{:S(2)}) collective-permute-start(bf16[288,256]{1,0:T(8,128)(2,1)S(1)} %message.1.refs_0_), channel_id=1, source_target_pairs={{0,1},{1,0},{2,3},{3,2},{4,5},{5,4},{6,7},{7,6},{8,9},{9,8},{10,11... | collective-permute-start | bytes 442376 | tf_op jit(solution)/shard_map/ppermute | solution.py:363
  17.9 1.4 %collective-permute-start.2 = (bf16[288,256]{1,0:T(8,128)(2,1)S(1)}, bf16[288,256]{1,0:T(8,128)(2,1)S(1)}, u32[]{:S(2)}, u32[]{:S(2)}) collective-permute-start(bf16[288,256]{1,0:T(8,128)(2,1)S(1)} %collective-permute-done.1.refs_2_), channel_id=1, source_target_pairs={{0,1},{1,0},{2,3},{3,2},{4,5},{5,4},{6,7},{7,6},{8,9},{9,8},{10,11... | collective-permute-start | bytes 442376 | tf_op jit(solution)/shard_map/ppermute | solution.py:363
  19.9 8.5 %collective-permute-start.6 = (f32[4,2,256]{2,1,0:T(2,128)S(1)}, f32[4,2,256]{2,1,0:T(2,128)S(1)}, u32[]{:S(2)}, u32[]{:S(2)}) collective-permute-start(f32[4,2,256]{2,1,0:T(2,128)S(1)} %fields.1), channel_id=1, source_target_pairs={{0,0},{1,5},{2,10},{3,15},{4,4},{5,1},{6,14},{7,11},{8,8},{9,13},{... | collective-permute-start | bytes 24584 | tf_op jit(solution)/shard_map/ppermute | solution.py:365
  22.1 13.2 %collective-permute-start.5 = (bf16[2,256,256]{2,1,0:T(8,128)(2,1)S(1)}, bf16[2,256,256]{2,1,0:T(8,128)(2,1)S(1)}, u32[]{:S(2)}, u32[]{:S(2)}) collective-permute-start(bf16[2,256,256]{2,1,0:T(8,128)(2,1)S(1)} %get-tuple-element.29), channel_id=1, source_target_pairs={{0,3},{1,2},{2,1},{3,0},{4,7},{5,6},{6,5},{7,4},{8,11},{9,10},{10,... | collective-permute-start | bytes 786440 | tf_op jit(solution)/shard_map/ppermute | solution.py:363
  28.4 13.6 %collective-permute-start.12 = (bf16[192,1024]{1,0:T(8,128)(2,1)S(1)}, bf16[192,1024]{1,0:T(8,128)(2,1)S(1)}, u32[]{:S(2)}, u32[]{:S(2)}) collective-permute-start(bf16[192,1024]{1,0:T(8,128)(2,1)S(1)} %collective-permute-done.4.refs_0_), channel_id=1, source_target_pairs={{0,4},{4,0},{8,12},{12,8},{1,5},{5,1},{9,13},{13,9},{2,6},{6,2},{1... | collective-permute-start | bytes 1179656 | tf_op jit(solution)/shard_map/ppermute | solution.py:364
  29.3 13.3 %collective-permute-start.9 = (bf16[128,1024]{1,0:T(8,128)(2,1)S(1)}, bf16[128,1024]{1,0:T(8,128)(2,1)S(1)}, u32[]{:S(2)}, u32[]{:S(2)}) collective-permute-start(bf16[128,1024]{1,0:T(8,128)(2,1)S(1)} %slice.4), channel_id=1, source_target_pairs={{0,2},{1,3},{2,0},{3,1},{4,6},{5,7},{6,4},{7,5},{8,10},{9,11},{10,... | collective-permute-start | bytes 786440 | tf_op jit(solution)/shard_map/ppermute | solution.py:363
  42.0 2.2 %collective-permute-start.11 = (bf16[192,1024]{1,0:T(8,128)(2,1)S(1)}, bf16[192,1024]{1,0:T(8,128)(2,1)S(1)}, u32[]{:S(2)}, u32[]{:S(2)}) collective-permute-start(bf16[192,1024]{1,0:T(8,128)(2,1)S(1)} %collective-permute-done.4.refs_0_), channel_id=1, source_target_pairs={{0,1},{1,0},{2,3},{3,2},{4,5},{5,4},{6,7},{7,6},{8,9},{9,8},{10,11... | collective-permute-start | bytes 1179656 | tf_op jit(solution)/shard_map/ppermute | solution.py:363
  42.1 2.3 %collective-permute-start.13 = (bf16[192,1024]{1,0:T(8,128)(2,1)S(1)}, bf16[192,1024]{1,0:T(8,128)(2,1)S(1)}, u32[]{:S(2)}, u32[]{:S(2)}) collective-permute-start(bf16[192,1024]{1,0:T(8,128)(2,1)S(1)} %collective-permute-done.12.refs_2_), channel_id=1, source_target_pairs={{0,1},{1,0},{2,3},{3,2},{4,5},{5,4},{6,7},{7,6},{8,9},{9,8},{10,11... | collective-permute-start | bytes 1179656 | tf_op jit(solution)/shard_map/ppermute | solution.py:363
  42.6 3.2 %collective-permute-start.10 = (bf16[128,1024]{1,0:T(8,128)(2,1)S(1)}, bf16[128,1024]{1,0:T(8,128)(2,1)S(1)}, u32[]{:S(2)}, u32[]{:S(2)}) collective-permute-start(bf16[128,1024]{1,0:T(8,128)(2,1)S(1)} %collective-permute-done.9.refs_0_), channel_id=1, source_target_pairs={{0,1},{1,0},{2,3},{3,2},{4,5},{5,4},{6,7},{7,6},{8,9},{9,8},{10,11... | collective-permute-start | bytes 786440 | tf_op jit(solution)/shard_map/ppermute | solution.py:363
  46.5 4.2 %collective-permute-start.14 = (f32[2,8,128]{2,1,0:T(8,128)S(1)}, f32[2,8,128]{2,1,0:T(8,128)S(1)}, u32[]{:S(2)}, u32[]{:S(2)}) collective-permute-start(f32[2,8,128]{2,1,0:T(8,128)S(1)} %contract.3), channel_id=1, source_target_pairs={{0,0},{1,5},{2,10},{3,15},{4,4},{5,1},{6,14},{7,11},{8,8},{9,13},{... | collective-permute-start | bytes 24584 | tf_op jit(solution)/shard_map/ppermute | solution.py:366
  47.1 7.5 %collective-permute-start.16 = (f32[2,8,128]{2,1,0:T(8,128)S(1)}, f32[2,8,128]{2,1,0:T(8,128)S(1)}, u32[]{:S(2)}, u32[]{:S(2)}) collective-permute-start(f32[2,8,128]{2,1,0:T(8,128)S(1)} %contract.5), channel_id=1, source_target_pairs={{0,2},{1,7},{2,8},{3,13},{4,6},{5,3},{6,12},{7,9},{8,10},{9,15},{1... | collective-permute-start | bytes 24584 | tf_op jit(solution)/shard_map/ppermute | solution.py:366
  50.6 4.2 %collective-permute-start.15 = (f32[2,8,128]{2,1,0:T(8,128)S(1)}, f32[2,8,128]{2,1,0:T(8,128)S(1)}, u32[]{:S(2)}, u32[]{:S(2)}) collective-permute-start(f32[2,8,128]{2,1,0:T(8,128)S(1)} %collective-permute-done.14.refs_0_), channel_id=1, source_target_pairs={{0,1},{1,0},{2,3},{3,2},{4,5},{5,4},{6,7},{7,6},{8,9},{9,8},{10,11... | collective-permute-start | bytes 24584 | tf_op jit(solution)/shard_map/ppermute | solution.py:363
  54.6 1.2 %collective-permute-start.17 = (f32[2,8,128]{2,1,0:T(8,128)S(1)}, f32[2,8,128]{2,1,0:T(8,128)S(1)}, u32[]{:S(2)}, u32[]{:S(2)}) collective-permute-start(f32[2,8,128]{2,1,0:T(8,128)S(1)} %collective-permute-done.16.refs_2_), channel_id=1, source_target_pairs={{0,1},{1,0},{2,3},{3,2},{4,5},{5,4},{6,7},{7,6},{8,9},{9,8},{10,11... | collective-permute-start | bytes 24584 | tf_op jit(solution)/shard_map/ppermute | solution.py:363

commit v8 on v7

--- a/solution.py
+++ b/solution.py
@@ -15,7 +15,7 @@
 BF16 = jnp.bfloat16
 VMEM_LIMIT = 24 * 2**20
 SMALL_LIMIT = 2**20
-AHEAD = pl.CostEstimate(flops=2**36, bytes_accessed=2**22, transcendentals=0)
+AHEAD = pl.CostEstimate(flops=2**30, bytes_accessed=2**20, transcendentals=0)
 HIGHEST = lax.Precision.HIGHEST
 
 

time: 56.6 us -> 50.7 us (0.90)
  waiting for transfers between devices: 18.2 us -> 8.34 us
  starting transfers between devices: 19.2 us -> 23.2 us
    ppermute x14, waiting for transfers between devices: 14.7 us -> 6.97 us  [at_the_source(): move = lambda x, k: lax.ppermute(x, SR, [(i, i ^ k) for i in range(n)])]
    ppermute x2, waiting for transfers between devices: 3.49 us -> 1.36 us  [at_the_source(): lax.ppermute(x, ALL, [(w * n + q, (w ^ q) * n + (q ^ k)) for w, q in pairs])]
    ppermute x1, starting transfers between devices: 0.01 us -> 2.03 us  [at_the_source(): swap = lambda x: lax.ppermute(x, 'walk', [(w, w ^ 1) for w in range(n)])]
    ppermute x2, starting transfers between devices: 4.17 us -> 6.07 us  [at_the_source(): lax.ppermute(x, ALL, [(w * n + q, (w ^ q) * n + (q ^ k)) for w, q in pairs])]
  transfers between devices with their start and end apart: 18 -> 18, of which waited for: 6 -> 6; matrix products, arithmetic and copies ran while one was open for 2% -> 2% of each run, Pallas kernels for 25% -> 28%
where the time goes in v8:
time: 50.7 us; the launch traced here: 50.5 us
  starting transfers between devices  23.2 us (46%)
  Pallas kernels  15.3 us (30%)
  waiting for transfers between devices  8.34 us (16%)
  local copies, waits for them, and re-layouts  2.32 us (5%)
  between operations  1.45 us (3%)
    ppermute x14, starting transfers between devices, at_the_source(): move = lambda x, k: lax.ppermute(x, SR, [(i, i ^ k) for i in range(n)])  14.4 us
    ppermute x14, waiting for transfers between devices, at_the_source(): move = lambda x, k: lax.ppermute(x, SR, [(i, i ^ k) for i in range(n)])  6.97 us
    pallas_call x1, Pallas kernels, make_green(): pl.pallas_call(functools.partial(green_kernel, n, share), out_shape=jax.S...  6.67 us
    ppermute x2, starting transfers between devices, at_the_source(): lax.ppermute(x, ALL, [(w * n + q, (w ^ q) * n + (q ^ k)) for w, q in pairs])  6.07 us
    pallas_call x3, Pallas kernels, contract(): pl.pallas_call(kernel, out_shape=[jax.ShapeDtypeStruct((count, 8, 128), F...  3.62 us
    pallas_call x1, Pallas kernels, select(): pl.pallas_call(functools.partial(select_kernel, n, per, share), out_shape...  2.17 us
    ppermute x1, starting transfers between devices, at_the_source(): swap = lambda x: lax.ppermute(x, 'walk', [(w, w ^ 1) for w in range(n)])  2.03 us
    ppermute x2, waiting for transfers between devices, at_the_source(): lax.ppermute(x, ALL, [(w * n + q, (w ^ q) * n + (q ^ k)) for w, q in pairs])  1.36 us
  transfers between devices with their start and end apart: 18, of which 6 were waited for; matrix products, arithmetic and copies ran while one was open for 2% of the time, Pallas kernels for 28%

profile of v8, /device:TPU:0, one launch (start us, length us, event | category | flops | bytes accessed | tf_op | source)
XLA Modules:
  0.0 50.5 jit_solution(18301323528546357728)
XLA Ops:
  0.6 0.5 %collective-permute-start.3 = (bf16[512,1024]{1,0:T(8,128)(2,1)}, bf16[512,1024]{1,0:T(8,128)(2,1)S(1)}, u32[]{:S(2)}, u32[]{:S(2)}) collective-permute-start(bf16[512,1024]{1,0:T(8,128)(2,1)} %bitcast.3), channel_id=1, source_target_pairs={{0,1},{1,0},{2,3},{3,2},{4,5},{5,4},{6,7},{7,6},{8,9},{9,8},{10,11... | collective-permute-start | bytes 3145736 | tf_op jit(solution)/shard_map/ppermute | solution.py:363
  1.1 0.0 copy-start.4
  1.2 0.0 copy-start.2
  1.2 0.0 copy-start.3
  1.2 1.1 %constant_dynamic-slice_fusion = bf16[192,1024]{1,0:T(8,128)(2,1)S(1)} fusion(bf16[512,1024]{1,0:T(8,128)(2,1)} %bitcast.4, s32[]{:T(128)S(6)} %select_n.3), kind=kLoop, calls=%fused_computation | loop fusion | bytes 786436 | tf_op jit(solution)/shard_map/dynamic_slice | solution.py:387
  2.2 2.6 %collective-permute-start.4 = (bf16[192,1024]{1,0:T(8,128)(2,1)S(1)}, bf16[192,1024]{1,0:T(8,128)(2,1)S(1)}, u32[]{:S(2)}, u32[]{:S(2)}) collective-permute-start(bf16[192,1024]{1,0:T(8,128)(2,1)S(1)} %constant_dynamic-slice_fusion), channel_id=1, source_target_pairs={{0,2},{1,3},{2,0},{3,1},{4,6},{5,7},{6,4},{7,5},{8,10},{9,11},{10,... | collective-permute-start | bytes 1179656 | tf_op jit(solution)/shard_map/ppermute | solution.py:363
  4.8 0.0 copy-done.4
  4.8 0.0 copy-start
  4.8 1.2 %copy-done = bf16[8,256,256]{2,1,0:T(8,128)(2,1)S(1)} copy-done((bf16[8,256,256]{2,1,0:T(8,128)(2,1)S(1)}, bf16[8,256,256]{2,1,0:T(8,128)(2,1)}, u32[]{:S(2)}) %copy-start) | copy-done | bytes 1048600
  6.0 0.0 copy-start.1
  6.1 2.2 %select.1 = (bf16[2,256,256]{2,1,0:T(8,128)(2,1)S(1)}, bf16[2,256,256]{2,1,0:T(8,128)(2,1)S(1)}, bf16[2,256,256]{2,1,0:T(8,128)(2,1)S(1)}, bf16[2,256,256]{2,1,0:T(8,128)(2,1)S(1)}) custom-call(s32[32]{0:T(128)S(1)} %copy-done.4, bf16[8,256,256]{2,1,0:T(8,128)(2,1)S(1)} %copy-done), custom_call_target="tpu_custom_call" | custom-call | tf_op jit(solution)/shard_map/select/pallas_call | solution.py:69
  8.2 0.0 copy-done.2
  8.2 0.0 copy-done.3
  8.3 0.1 collective-permute-start.1
  8.4 0.0 collective-permute-done.3.refs_1_
  8.4 0.2 collective-permute-start.7
  8.6 1.8 %collective-permute-start.8 = (bf16[2,256,256]{2,1,0:T(8,128)(2,1)S(1)}, bf16[2,256,256]{2,1,0:T(8,128)(2,1)S(1)}, u32[]{:S(2)}, u32[]{:S(2)}) collective-permute-start(bf16[2,256,256]{2,1,0:T(8,128)(2,1)S(1)} %get-tuple-element.34), channel_id=1, source_target_pairs={{0,2},{1,3},{2,0},{3,1},{4,6},{5,7},{6,4},{7,5},{8,10},{9,11},{10,... | collective-permute-start | bytes 786440 | tf_op jit(solution)/shard_map/ppermute | solution.py:363
  10.4 0.2 collective-permute-start
  10.6 4.2 %collective-permute-done.4.refs_0_ = bf16[192,1024]{1,0:T(8,128)(2,1)S(1)} collective-permute-done((bf16[192,1024]{1,0:T(8,128)(2,1)S(1)}, bf16[192,1024]{1,0:T(8,128)(2,1)S(1)}, u32[]{:S(2)}, u32[]{:S(2)}) %collective-permute-start.4) | collective-permute-done | bytes 393248 | tf_op jit(solution)/shard_map/ppermute | solution.py:363
  14.8 2.0 %collective-permute-start.12 = (bf16[192,1024]{1,0:T(8,128)(2,1)S(1)}, bf16[192,1024]{1,0:T(8,128)(2,1)S(1)}, u32[]{:S(2)}, u32[]{:S(2)}) collective-permute-start(bf16[192,1024]{1,0:T(8,128)(2,1)S(1)} %collective-permute-done.4.refs_0_), channel_id=1, source_target_pairs={{0,4},{4,0},{8,12},{12,8},{1,5},{5,1},{9,13},{13,9},{2,6},{6,2},{1... | collective-permute-start | bytes 1179656 | tf_op jit(solution)/shard_map/ppermute | solution.py:364
  16.8 1.1 %collective-permute-done.1.refs_2_ = bf16[288,256]{1,0:T(8,128)(2,1)S(1)} collective-permute-done((bf16[288,256]{1,0:T(8,128)(2,1)S(1)}, bf16[288,256]{1,0:T(8,128)(2,1)S(1)}, u32[]{:S(2)}, u32[]{:S(2)}) %collective-permute-start.1) | collective-permute-done | bytes 147488 | tf_op jit(solution)/shard_map/ppermute | solution.py:363
  17.9 0.0 collective-permute-start.2
  18.0 0.0 collective-permute-done.refs_1_
  18.0 2.1 %collective-permute-start.5 = (bf16[2,256,256]{2,1,0:T(8,128)(2,1)S(1)}, bf16[2,256,256]{2,1,0:T(8,128)(2,1)S(1)}, u32[]{:S(2)}, u32[]{:S(2)}) collective-permute-start(bf16[2,256,256]{2,1,0:T(8,128)(2,1)S(1)} %get-tuple-element.29), channel_id=1, source_target_pairs={{0,3},{1,2},{2,1},{3,0},{4,7},{5,6},{6,5},{7,4},{8,11},{9,10},{10,... | collective-permute-start | bytes 786440 | tf_op jit(solution)/shard_map/ppermute | solution.py:363
  20.0 0.0 collective-permute-done.2.refs_3_
  20.0 0.6 %fields.1 = f32[4,2,256]{2,1,0:T(2,128)S(1)} custom-call(s32[32]{0:T(128)S(1)} %copy-done.4, bf16[288,256]{1,0:T(8,128)(2,1)S(1)} %message.1.refs_0_, bf16[288,256]{1,0:T(8,128)(2,1)S(1)} %collective-permute-done.refs_1_, bf16[288,256]{1,0:T(8,128)(2,1)S(1)} %collective-permute-done.1.refs_2_, bf16[288,256]{1,0:T(8,128)(2,1)S(1)} %collective-permute-done.2.refs_3_), custom_call_target="tpu_custom_call" | custom-call | tf_op jit(solution)/shard_map/fields/pallas_call | solution.py:119
  20.6 0.7 %collective-permute-start.6 = (f32[4,2,256]{2,1,0:T(2,128)S(1)}, f32[4,2,256]{2,1,0:T(2,128)S(1)}, u32[]{:S(2)}, u32[]{:S(2)}) collective-permute-start(f32[4,2,256]{2,1,0:T(2,128)S(1)} %fields.1), channel_id=1, source_target_pairs={{0,0},{1,5},{2,10},{3,15},{4,4},{5,1},{6,14},{7,11},{8,8},{9,13},{... | collective-permute-start | bytes 24584 | tf_op jit(solution)/shard_map/ppermute | solution.py:365
  21.3 0.0 copy-done.1
  22.0 0.8 %turn.1 = (bf16[256,1024]{1,0:T(8,128)(2,1)S(1)}, f32[8,128]{1,0:T(8,128)S(1)}) custom-call(s32[32]{0:T(128)S(1)} %copy-done.4, s32[1]{0:T(128)S(6)} %copy.8.counts, bf16[288,256]{1,0:T(8,128)(2,1)S(1)} %message.1.refs_0_, bf16[288,256]{1,0:T(8,128)(2,1)S(1)} %collective-permute-done.refs_1_, bf16[288,256]{1,0:T(8,128)(2,1)S(1)} %collective-permute-done.1.refs_2_, ...), custom_call_target="tpu_custom_call" | custom-call | tf_op jit(solution)/shard_map/turn/pallas_call | solution.py:146
  22.8 0.0 collective-permute-done.6.refs_4_.refs_2_
  22.8 0.0 collective-permute-done.7.refs_1_
  22.8 0.8 %collective-permute-done.8.refs_2_ = bf16[2,256,256]{2,1,0:T(8,128)(2,1)S(1)} collective-permute-done((bf16[2,256,256]{2,1,0:T(8,128)(2,1)S(1)}, bf16[2,256,256]{2,1,0:T(8,128)(2,1)S(1)}, u32[]{:S(2)}, u32[]{:S(2)}) %collective-permute-start.8) | collective-permute-done | bytes 262176 | tf_op jit(solution)/shard_map/ppermute | solution.py:363
  23.6 0.8 %first.1 = (bf16[768,512]{1,0:T(8,128)(2,1)S(1)}, f32[256,512]{1,0:T(8,128)S(1)}) custom-call(bf16[2,256,256]{2,1,0:T(8,128)(2,1)S(1)} %get-tuple-element.25.refs_0_, bf16[2,256,256]{2,1,0:T(8,128)(2,1)S(1)} %collective-permute-done.7.refs_1_, bf16[2,256,256]{2,1,0:T(8,128)(2,1)S(1)} %collective-permute-done.8.refs_2_, ...), custom_call_target="tpu_custom_call" | custom-call | flops 1073741824 | bytes 1048576 | tf_op jit(solution)/shard_map/first/pallas_call | solution.py:187
  24.4 4.8 %collective-permute-start.9 = (bf16[128,1024]{1,0:T(8,128)(2,1)S(1)}, bf16[128,1024]{1,0:T(8,128)(2,1)S(1)}, u32[]{:S(2)}, u32[]{:S(2)}) collective-permute-start(bf16[128,1024]{1,0:T(8,128)(2,1)S(1)} %slice.4), channel_id=1, source_target_pairs={{0,2},{1,3},{2,0},{3,1},{4,6},{5,7},{6,4},{7,5},{8,10},{9,11},{10,... | collective-permute-start | bytes 786440 | tf_op jit(solution)/shard_map/ppermute | solution.py:363
  29.2 0.0 collective-permute-done.5.refs_0_
  29.2 6.7 %green.1.refs_2_.refs_4_ = bf16[1024,512]{1,0:T(8,128)(2,1)S(1)} custom-call(bf16[2,256,256]{2,1,0:T(8,128)(2,1)S(1)} %collective-permute-done.5.refs_0_, bf16[256,1024]{1,0:T(8,128)(2,1)S(1)} %get-tuple-element.30.refs_3_.refs_1_, f32[4,2,256]{2,1,0:T(2,128)S(1)} %collective-permute-done.6.refs_4_.refs_2_, bf16[768,512]{1,0:T(8,128)(2,1)S(1)} %get-tuple-element.35.refs_3_, ...), custom_call_target="tpu_custom_call" | custom-call | tf_op jit(solution)/shard_map/green/pallas_call | solution.py:246
  35.9 0.2 collective-permute-start.11
  36.1 0.0 collective-permute-done.12.refs_2_
  36.1 0.3 collective-permute-start.13
  36.5 0.0 collective-permute-done.9.refs_0_
  36.5 0.2 collective-permute-start.10
  36.6 1.5 %contract.3 = f32[2,8,128]{2,1,0:T(8,128)S(1)} custom-call(bf16[512,1024]{1,0:T(8,128)(2,1)S(1)} %bitcast.6, bf16[512,1024]{1,0:T(8,128)(2,1)S(1)} %collective-permute-done.3.refs_1_, bf16[1024,512]{1,0:T(8,128)(2,1)S(1)} %green.1.refs_2_.refs_4_), custom_call_target="tpu_custom_call" | custom-call | flops 1073741824 | bytes 3145728 | tf_op jit(solution)/shard_map/contract/pallas_call | solution.py:314
  38.2 0.0 collective-permute-done.11.refs_1_
  38.2 0.1 collective-permute-done.13.refs_3_
  38.2 1.4 %contract.4 = (f32[2,8,128]{2,1,0:T(8,128)S(1)}, f32[128,512]{1,0:T(8,128)S(1)}, f32[128,512]{1,0:T(8,128)S(1)}) custom-call(bf16[192,1024]{1,0:T(8,128)(2,1)S(1)} %collective-permute-done.4.refs_0_, bf16[192,1024]{1,0:T(8,128)(2,1)S(1)} %collective-permute-done.11.refs_1_, bf16[192,1024]{1,0:T(8,128)(2,1)S(1)} %collective-permute-done.12.refs_2_, ...), custom_call_target="tpu_custom_call" | custom-call | flops 805306368 | bytes 2621440 | tf_op jit(solution)/shard_map/contract/pallas_call | solution.py:314
  39.6 0.0 collective-permute-done.10.refs_1_
  39.6 0.7 %contract.5 = f32[2,8,128]{2,1,0:T(8,128)S(1)} custom-call(bf16[128,1024]{1,0:T(8,128)(2,1)S(1)} %collective-permute-done.9.refs_0_, bf16[128,1024]{1,0:T(8,128)(2,1)S(1)} %collective-permute-done.10.refs_1_, bf16[1024,512]{1,0:T(8,128)(2,1)S(1)} %green.1.refs_2_.refs_4_, f32[128,512]{1,0:T(8,128)S(1)} %get-tuple-element.42.refs_3_, ...), custom_call_target="tpu_custom_call" | custom-call | flops 268435456 | bytes 1572864 | tf_op jit(solution)/shard_map/contract/pallas_call | solution.py:314
  40.4 0.7 %collective-permute-start.14 = (f32[2,8,128]{2,1,0:T(8,128)S(1)}, f32[2,8,128]{2,1,0:T(8,128)S(1)}, u32[]{:S(2)}, u32[]{:S(2)}) collective-permute-start(f32[2,8,128]{2,1,0:T(8,128)S(1)} %contract.3), channel_id=1, source_target_pairs={{0,0},{1,5},{2,10},{3,15},{4,4},{5,1},{6,14},{7,11},{8,8},{9,13},{... | collective-permute-start | bytes 24584 | tf_op jit(solution)/shard_map/ppermute | solution.py:366
  41.0 5.4 %collective-permute-start.16 = (f32[2,8,128]{2,1,0:T(8,128)S(1)}, f32[2,8,128]{2,1,0:T(8,128)S(1)}, u32[]{:S(2)}, u32[]{:S(2)}) collective-permute-start(f32[2,8,128]{2,1,0:T(8,128)S(1)} %contract.5), channel_id=1, source_target_pairs={{0,2},{1,7},{2,8},{3,13},{4,6},{5,3},{6,12},{7,9},{8,10},{9,15},{1... | collective-permute-start | bytes 24584 | tf_op jit(solution)/shard_map/ppermute | solution.py:366
  46.4 0.0 collective-permute-done.14.refs_0_
  46.5 0.0 collective-permute-start.15
  46.5 1.4 %collective-permute-done.16.refs_2_ = f32[2,8,128]{2,1,0:T(8,128)S(1)} collective-permute-done((f32[2,8,128]{2,1,0:T(8,128)S(1)}, f32[2,8,128]{2,1,0:T(8,128)S(1)}, u32[]{:S(2)}, u32[]{:S(2)}) %collective-permute-start.16) | collective-permute-done | bytes 8224 | tf_op jit(solution)/shard_map/ppermute | solution.py:366
  47.8 1.3 %collective-permute-start.17 = (f32[2,8,128]{2,1,0:T(8,128)S(1)}, f32[2,8,128]{2,1,0:T(8,128)S(1)}, u32[]{:S(2)}, u32[]{:S(2)}) collective-permute-start(f32[2,8,128]{2,1,0:T(8,128)S(1)} %collective-permute-done.16.refs_2_), channel_id=1, source_target_pairs={{0,1},{1,0},{2,3},{3,2},{4,5},{5,4},{6,7},{7,6},{8,9},{9,8},{10,11... | collective-permute-start | bytes 24584 | tf_op jit(solution)/shard_map/ppermute | solution.py:363
  49.1 0.0 collective-permute-done.15.refs_1_
  49.1 0.8 %collective-permute-done.17.refs_3_ = f32[2,8,128]{2,1,0:T(8,128)S(1)} collective-permute-done((f32[2,8,128]{2,1,0:T(8,128)S(1)}, f32[2,8,128]{2,1,0:T(8,128)S(1)}, u32[]{:S(2)}, u32[]{:S(2)}) %collective-permute-start.17) | collective-permute-done | bytes 8224 | tf_op jit(solution)/shard_map/ppermute | solution.py:363
  50.0 0.6 %unpack.1 = (f32[2,8]{1,0:T(2,128)}, f32[2,8]{1,0:T(2,128)}) custom-call(f32[8,128]{1,0:T(8,128)S(1)} %get-tuple-element.27.masks, f32[2,8,128]{2,1,0:T(8,128)S(1)} %collective-permute-done.14.refs_0_, f32[2,8,128]{2,1,0:T(8,128)S(1)} %collective-permute-done.15.refs_1_, f32[2,8,128]{2,1,0:T(8,128)S(1)} %collective-permute-done.16.refs_2_, ...), custom_call_target="tpu_custom_call" | custom-call | tf_op jit(solution)/shard_map/unpack/pallas_call | solution.py:346
  (2 shorter events, 0.0 us)
Async XLA Ops:
  0.6 7.7 %collective-permute-start.3 = (bf16[512,1024]{1,0:T(8,128)(2,1)}, bf16[512,1024]{1,0:T(8,128)(2,1)S(1)}, u32[]{:S(2)}, u32[]{:S(2)}) collective-permute-start(bf16[512,1024]{1,0:T(8,128)(2,1)} %bitcast.3), channel_id=1, source_target_pairs={{0,1},{1,0},{2,3},{3,2},{4,5},{5,4},{6,7},{7,6},{8,9},{9,8},{10,11... | collective-permute-start | bytes 3145736 | tf_op jit(solution)/shard_map/ppermute | solution.py:363
  1.1 3.7 %copy-start.4 = (s32[32]{0:T(128)S(1)}, s32[32]{0:T(128)}, u32[]{:S(2)}) copy-start(s32[32]{0:T(128)} %branches.5) | copy-start | bytes 388
  1.2 7.1 %copy-start.2 = (bf16[256,256]{1,0:T(8,128)(2,1)S(1)}, bf16[256,256]{1,0:T(8,128)(2,1)}, u32[]{:S(2)}) copy-start(bf16[256,256]{1,0:T(8,128)(2,1)} %trial) | copy-start | bytes 393220
  1.2 7.1 %copy-start.3 = (f32[8,256]{1,0:T(8,128)S(1)}, f32[8,256]{1,0:T(8,128)}, u32[]{:S(2)}) copy-start(f32[8,256]{1,0:T(8,128)} %field.1) | copy-start | bytes 24580
  2.2 12.6 %collective-permute-start.4 = (bf16[192,1024]{1,0:T(8,128)(2,1)S(1)}, bf16[192,1024]{1,0:T(8,128)(2,1)S(1)}, u32[]{:S(2)}, u32[]{:S(2)}) collective-permute-start(bf16[192,1024]{1,0:T(8,128)(2,1)S(1)} %constant_dynamic-slice_fusion), channel_id=1, source_target_pairs={{0,2},{1,3},{2,0},{3,1},{4,6},{5,7},{6,4},{7,5},{8,10},{9,11},{10,... | collective-permute-start | bytes 1179656 | tf_op jit(solution)/shard_map/ppermute | solution.py:363
  4.8 1.2 %copy-start = (bf16[8,256,256]{2,1,0:T(8,128)(2,1)S(1)}, bf16[8,256,256]{2,1,0:T(8,128)(2,1)}, u32[]{:S(2)}) copy-start(bf16[8,256,256]{2,1,0:T(8,128)(2,1)} %walkers.1) | copy-start | bytes 3145732
  6.0 15.3 %copy-start.1 = (bf16[2,256,1024]{2,1,0:T(8,128)(2,1)S(1)}, bf16[2,256,1024]{2,1,0:T(8,128)(2,1)}, u32[]{:S(2)}) copy-start(bf16[2,256,1024]{2,1,0:T(8,128)(2,1)} %param.8) | copy-start | bytes 3145732
  8.3 9.7 %collective-permute-start.1 = (bf16[288,256]{1,0:T(8,128)(2,1)S(1)}, bf16[288,256]{1,0:T(8,128)(2,1)S(1)}, u32[]{:S(2)}, u32[]{:S(2)}) collective-permute-start(bf16[288,256]{1,0:T(8,128)(2,1)S(1)} %message.1.refs_0_), channel_id=1, source_target_pairs={{0,2},{1,3},{2,0},{3,1},{4,6},{5,7},{6,4},{7,5},{8,10},{9,11},{10,... | collective-permute-start | bytes 442376 | tf_op jit(solution)/shard_map/ppermute | solution.py:363
  8.4 14.4 %collective-permute-start.7 = (bf16[2,256,256]{2,1,0:T(8,128)(2,1)S(1)}, bf16[2,256,256]{2,1,0:T(8,128)(2,1)S(1)}, u32[]{:S(2)}, u32[]{:S(2)}) collective-permute-start(bf16[2,256,256]{2,1,0:T(8,128)(2,1)S(1)} %get-tuple-element.32), channel_id=1, source_target_pairs={{0,1},{1,0},{2,3},{3,2},{4,5},{5,4},{6,7},{7,6},{8,9},{9,8},{10,11... | collective-permute-start | bytes 786440 | tf_op jit(solution)/shard_map/ppermute | solution.py:363
  8.6 15.0 %collective-permute-start.8 = (bf16[2,256,256]{2,1,0:T(8,128)(2,1)S(1)}, bf16[2,256,256]{2,1,0:T(8,128)(2,1)S(1)}, u32[]{:S(2)}, u32[]{:S(2)}) collective-permute-start(bf16[2,256,256]{2,1,0:T(8,128)(2,1)S(1)} %get-tuple-element.34), channel_id=1, source_target_pairs={{0,2},{1,3},{2,0},{3,1},{4,6},{5,7},{6,4},{7,5},{8,10},{9,11},{10,... | collective-permute-start | bytes 786440 | tf_op jit(solution)/shard_map/ppermute | solution.py:363
  10.4 7.6 %collective-permute-start = (bf16[288,256]{1,0:T(8,128)(2,1)S(1)}, bf16[288,256]{1,0:T(8,128)(2,1)S(1)}, u32[]{:S(2)}, u32[]{:S(2)}) collective-permute-start(bf16[288,256]{1,0:T(8,128)(2,1)S(1)} %message.1.refs_0_), channel_id=1, source_target_pairs={{0,1},{1,0},{2,3},{3,2},{4,5},{5,4},{6,7},{7,6},{8,9},{9,8},{10,11... | collective-permute-start | bytes 442376 | tf_op jit(solution)/shard_map/ppermute | solution.py:363
  14.8 21.3 %collective-permute-start.12 = (bf16[192,1024]{1,0:T(8,128)(2,1)S(1)}, bf16[192,1024]{1,0:T(8,128)(2,1)S(1)}, u32[]{:S(2)}, u32[]{:S(2)}) collective-permute-start(bf16[192,1024]{1,0:T(8,128)(2,1)S(1)} %collective-permute-done.4.refs_0_), channel_id=1, source_target_pairs={{0,4},{4,0},{8,12},{12,8},{1,5},{5,1},{9,13},{13,9},{2,6},{6,2},{1... | collective-permute-start | bytes 1179656 | tf_op jit(solution)/shard_map/ppermute | solution.py:364
  17.9 2.1 %collective-permute-start.2 = (bf16[288,256]{1,0:T(8,128)(2,1)S(1)}, bf16[288,256]{1,0:T(8,128)(2,1)S(1)}, u32[]{:S(2)}, u32[]{:S(2)}) collective-permute-start(bf16[288,256]{1,0:T(8,128)(2,1)S(1)} %collective-permute-done.1.refs_2_), channel_id=1, source_target_pairs={{0,1},{1,0},{2,3},{3,2},{4,5},{5,4},{6,7},{7,6},{8,9},{9,8},{10,11... | collective-permute-start | bytes 442376 | tf_op jit(solution)/shard_map/ppermute | solution.py:363
  18.0 11.2 %collective-permute-start.5 = (bf16[2,256,256]{2,1,0:T(8,128)(2,1)S(1)}, bf16[2,256,256]{2,1,0:T(8,128)(2,1)S(1)}, u32[]{:S(2)}, u32[]{:S(2)}) collective-permute-start(bf16[2,256,256]{2,1,0:T(8,128)(2,1)S(1)} %get-tuple-element.29), channel_id=1, source_target_pairs={{0,3},{1,2},{2,1},{3,0},{4,7},{5,6},{6,5},{7,4},{8,11},{9,10},{10,... | collective-permute-start | bytes 786440 | tf_op jit(solution)/shard_map/ppermute | solution.py:363
  20.6 2.2 %collective-permute-start.6 = (f32[4,2,256]{2,1,0:T(2,128)S(1)}, f32[4,2,256]{2,1,0:T(2,128)S(1)}, u32[]{:S(2)}, u32[]{:S(2)}) collective-permute-start(f32[4,2,256]{2,1,0:T(2,128)S(1)} %fields.1), channel_id=1, source_target_pairs={{0,0},{1,5},{2,10},{3,15},{4,4},{5,1},{6,14},{7,11},{8,8},{9,13},{... | collective-permute-start | bytes 24584 | tf_op jit(solution)/shard_map/ppermute | solution.py:365
  24.4 12.1 %collective-permute-start.9 = (bf16[128,1024]{1,0:T(8,128)(2,1)S(1)}, bf16[128,1024]{1,0:T(8,128)(2,1)S(1)}, u32[]{:S(2)}, u32[]{:S(2)}) collective-permute-start(bf16[128,1024]{1,0:T(8,128)(2,1)S(1)} %slice.4), channel_id=1, source_target_pairs={{0,2},{1,3},{2,0},{3,1},{4,6},{5,7},{6,4},{7,5},{8,10},{9,11},{10,... | collective-permute-start | bytes 786440 | tf_op jit(solution)/shard_map/ppermute | solution.py:363
  35.9 2.3 %collective-permute-start.11 = (bf16[192,1024]{1,0:T(8,128)(2,1)S(1)}, bf16[192,1024]{1,0:T(8,128)(2,1)S(1)}, u32[]{:S(2)}, u32[]{:S(2)}) collective-permute-start(bf16[192,1024]{1,0:T(8,128)(2,1)S(1)} %collective-permute-done.4.refs_0_), channel_id=1, source_target_pairs={{0,1},{1,0},{2,3},{3,2},{4,5},{5,4},{6,7},{7,6},{8,9},{9,8},{10,11... | collective-permute-start | bytes 1179656 | tf_op jit(solution)/shard_map/ppermute | solution.py:363
  36.1 2.1 %collective-permute-start.13 = (bf16[192,1024]{1,0:T(8,128)(2,1)S(1)}, bf16[192,1024]{1,0:T(8,128)(2,1)S(1)}, u32[]{:S(2)}, u32[]{:S(2)}) collective-permute-start(bf16[192,1024]{1,0:T(8,128)(2,1)S(1)} %collective-permute-done.12.refs_2_), channel_id=1, source_target_pairs={{0,1},{1,0},{2,3},{3,2},{4,5},{5,4},{6,7},{7,6},{8,9},{9,8},{10,11... | collective-permute-start | bytes 1179656 | tf_op jit(solution)/shard_map/ppermute | solution.py:363
  36.5 3.2 %collective-permute-start.10 = (bf16[128,1024]{1,0:T(8,128)(2,1)S(1)}, bf16[128,1024]{1,0:T(8,128)(2,1)S(1)}, u32[]{:S(2)}, u32[]{:S(2)}) collective-permute-start(bf16[128,1024]{1,0:T(8,128)(2,1)S(1)} %collective-permute-done.9.refs_0_), channel_id=1, source_target_pairs={{0,1},{1,0},{2,3},{3,2},{4,5},{5,4},{6,7},{7,6},{8,9},{9,8},{10,11... | collective-permute-start | bytes 786440 | tf_op jit(solution)/shard_map/ppermute | solution.py:363
  40.4 6.1 %collective-permute-start.14 = (f32[2,8,128]{2,1,0:T(8,128)S(1)}, f32[2,8,128]{2,1,0:T(8,128)S(1)}, u32[]{:S(2)}, u32[]{:S(2)}) collective-permute-start(f32[2,8,128]{2,1,0:T(8,128)S(1)} %contract.3), channel_id=1, source_target_pairs={{0,0},{1,5},{2,10},{3,15},{4,4},{5,1},{6,14},{7,11},{8,8},{9,13},{... | collective-permute-start | bytes 24584 | tf_op jit(solution)/shard_map/ppermute | solution.py:366
  41.0 6.8 %collective-permute-start.16 = (f32[2,8,128]{2,1,0:T(8,128)S(1)}, f32[2,8,128]{2,1,0:T(8,128)S(1)}, u32[]{:S(2)}, u32[]{:S(2)}) collective-permute-start(f32[2,8,128]{2,1,0:T(8,128)S(1)} %contract.5), channel_id=1, source_target_pairs={{0,2},{1,7},{2,8},{3,13},{4,6},{5,3},{6,12},{7,9},{8,10},{9,15},{1... | collective-permute-start | bytes 24584 | tf_op jit(solution)/shard_map/ppermute | solution.py:366
  46.5 2.7 %collective-permute-start.15 = (f32[2,8,128]{2,1,0:T(8,128)S(1)}, f32[2,8,128]{2,1,0:T(8,128)S(1)}, u32[]{:S(2)}, u32[]{:S(2)}) collective-permute-start(f32[2,8,128]{2,1,0:T(8,128)S(1)} %collective-permute-done.14.refs_0_), channel_id=1, source_target_pairs={{0,1},{1,0},{2,3},{3,2},{4,5},{5,4},{6,7},{7,6},{8,9},{9,8},{10,11... | collective-permute-start | bytes 24584 | tf_op jit(solution)/shard_map/ppermute | solution.py:363
  47.8 2.1 %collective-permute-start.17 = (f32[2,8,128]{2,1,0:T(8,128)S(1)}, f32[2,8,128]{2,1,0:T(8,128)S(1)}, u32[]{:S(2)}, u32[]{:S(2)}) collective-permute-start(f32[2,8,128]{2,1,0:T(8,128)S(1)} %collective-permute-done.16.refs_2_), channel_id=1, source_target_pairs={{0,1},{1,0},{2,3},{3,2},{4,5},{5,4},{6,7},{7,6},{8,9},{9,8},{10,11... | collective-permute-start | bytes 24584 | tf_op jit(solution)/shard_map/ppermute | solution.py:363

commit v9 on v8

--- a/solution.py
+++ b/solution.py
@@ -214,7 +214,7 @@
         mixed = dot(high, low, ((1,), (1,)))
         right[i] = (dot(high, high, ((1,), (1,))) + (mixed + mixed.T)) / scale
 
-    def advance(exact, step, carry):
+    def advance(exact):
         for i in range(share):
             now, matrix = left[i], right[i]
             high, low = split(matrix)
@@ -224,10 +224,9 @@
                 product = product + (dot(left_high, low) + dot(left_low, high))
             left[i] = 2.0 * now - product
             right[i] = 2.0 * matrix - squared(high, low)
-        return carry
-
-    lax.fori_loop(0, EARLY, functools.partial(advance, False), 0)
-    lax.fori_loop(EARLY, ITERS - 1, functools.partial(advance, True), 0)
+
+    for step in range(ITERS - 1):
+        advance(step >= EARLY)
     for i in range(share):
         high, low = split(right[i])
         left_high, left_low = split(left[i])
@@ -402,7 +401,8 @@
     earlier, begun = first_blocks(n, share, blocks[:-1], turned, asked)
     direct = {k: move(ordered(rows[:direct_rows], begun), k) for k in heads}
     green = make_green(n, share, blocks[n - 1], turned, asked, earlier, begun)
-    crossed, other, direct = (along({k: ordered(x, green) for k, x in held.items()}) for held in (crossed, other, direct))
+    crossed = along(crossed)
+    other, direct = (along({k: ordered(x, green) for k, x in held.items()}) for held in (other, direct))
     [results] = contract(functools.partial(near_kernel, share, len(near), height), len(near), close, green)
     late, *kept = contract(
         functools.partial(shared_kernel, share, len(far), height),

time: 50.7 us -> 49.5 us (0.976)
  waiting for transfers between devices: 8.34 us -> 11 us
  starting transfers between devices: 23.2 us -> 20.8 us
  Pallas kernels: 15.3 us -> 13.7 us
    pallas_call x1, Pallas kernels: 6.67 us -> 5.13 us  [make_green(): pl.pallas_call(functools.partial(green_kernel, n, share), out_shape=jax.S...]
    ppermute x2, waiting for transfers between devices: 1.36 us -> 2.81 us  [at_the_source(): lax.ppermute(x, ALL, [(w * n + q, (w ^ q) * n + (q ^ k)) for w, q in pairs])]
    ppermute x2, starting transfers between devices: 6.07 us -> 4.74 us  [at_the_source(): lax.ppermute(x, ALL, [(w * n + q, (w ^ q) * n + (q ^ k)) for w, q in pairs])]
    ppermute x14, waiting for transfers between devices: 6.97 us -> 8.2 us  [at_the_source(): move = lambda x, k: lax.ppermute(x, SR, [(i, i ^ k) for i in range(n)])]
    ppermute x14, starting transfers between devices: 14.4 us -> 13.4 us  [at_the_source(): move = lambda x, k: lax.ppermute(x, SR, [(i, i ^ k) for i in range(n)])]
  transfers between devices with their start and end apart: 18 -> 18, of which waited for: 6 -> 6; matrix products, arithmetic and copies ran while one was open for 2% -> 2% of each run, Pallas kernels for 28% -> 25%
where the time goes in v9:
time: 49.5 us; the launch traced here: 49.3 us
  starting transfers between devices  20.8 us (42%)
  Pallas kernels  13.7 us (28%)
  waiting for transfers between devices  11 us (22%)
  local copies, waits for them, and re-layouts  2.32 us (5%)
  between operations  1.46 us (3%)
    ppermute x14, starting transfers between devices, at_the_source(): move = lambda x, k: lax.ppermute(x, SR, [(i, i ^ k) for i in range(n)])  13.4 us
    ppermute x14, waiting for transfers between devices, at_the_source(): move = lambda x, k: lax.ppermute(x, SR, [(i, i ^ k) for i in range(n)])  8.2 us
    pallas_call x1, Pallas kernels, make_green(): pl.pallas_call(functools.partial(green_kernel, n, share), out_shape=jax.S...  5.13 us
    ppermute x2, starting transfers between devices, at_the_source(): lax.ppermute(x, ALL, [(w * n + q, (w ^ q) * n + (q ^ k)) for w, q in pairs])  4.74 us
    pallas_call x3, Pallas kernels, contract(): pl.pallas_call(kernel, out_shape=[jax.ShapeDtypeStruct((count, 8, 128), F...  3.62 us
    ppermute x2, waiting for transfers between devices, at_the_source(): lax.ppermute(x, ALL, [(w * n + q, (w ^ q) * n + (q ^ k)) for w, q in pairs])  2.81 us
    pallas_call x1, Pallas kernels, select(): pl.pallas_call(functools.partial(select_kernel, n, per, share), out_shape...  2.17 us
    ppermute x1, starting transfers between devices, at_the_source(): swap = lambda x: lax.ppermute(x, 'walk', [(w, w ^ 1) for w in range(n)])  2.03 us
  transfers between devices with their start and end apart: 18, of which 6 were waited for; matrix products, arithmetic and copies ran while one was open for 2% of the time, Pallas kernels for 25%

profile of v9, /device:TPU:0, one launch (start us, length us, event | category | flops | bytes accessed | tf_op | source)
XLA Modules:
  0.0 49.3 jit_solution(12335960868619117844)
XLA Ops:
  0.6 0.5 %collective-permute-start.3 = (bf16[512,1024]{1,0:T(8,128)(2,1)}, bf16[512,1024]{1,0:T(8,128)(2,1)S(1)}, u32[]{:S(2)}, u32[]{:S(2)}) collective-permute-start(bf16[512,1024]{1,0:T(8,128)(2,1)} %bitcast.3), channel_id=1, source_target_pairs={{0,1},{1,0},{2,3},{3,2},{4,5},{5,4},{6,7},{7,6},{8,9},{9,8},{10,11... | collective-permute-start | bytes 3145736 | tf_op jit(solution)/shard_map/ppermute | solution.py:362
  1.1 0.0 copy-start.4
  1.2 0.0 copy-start.2
  1.2 0.0 copy-start.3
  1.2 1.1 %constant_dynamic-slice_fusion = bf16[192,1024]{1,0:T(8,128)(2,1)S(1)} fusion(bf16[512,1024]{1,0:T(8,128)(2,1)} %bitcast.4, s32[]{:T(128)S(6)} %select_n.3), kind=kLoop, calls=%fused_computation | loop fusion | bytes 786436 | tf_op jit(solution)/shard_map/dynamic_slice | solution.py:386
  2.2 2.6 %collective-permute-start.4 = (bf16[192,1024]{1,0:T(8,128)(2,1)S(1)}, bf16[192,1024]{1,0:T(8,128)(2,1)S(1)}, u32[]{:S(2)}, u32[]{:S(2)}) collective-permute-start(bf16[192,1024]{1,0:T(8,128)(2,1)S(1)} %constant_dynamic-slice_fusion), channel_id=1, source_target_pairs={{0,2},{1,3},{2,0},{3,1},{4,6},{5,7},{6,4},{7,5},{8,10},{9,11},{10,... | collective-permute-start | bytes 1179656 | tf_op jit(solution)/shard_map/ppermute | solution.py:362
  4.8 0.0 copy-done.4
  4.8 0.0 copy-start
  4.8 1.2 %copy-done = bf16[8,256,256]{2,1,0:T(8,128)(2,1)S(1)} copy-done((bf16[8,256,256]{2,1,0:T(8,128)(2,1)S(1)}, bf16[8,256,256]{2,1,0:T(8,128)(2,1)}, u32[]{:S(2)}) %copy-start) | copy-done | bytes 1048600
  6.0 0.0 copy-start.1
  6.1 2.2 %select.1 = (bf16[2,256,256]{2,1,0:T(8,128)(2,1)S(1)}, bf16[2,256,256]{2,1,0:T(8,128)(2,1)S(1)}, bf16[2,256,256]{2,1,0:T(8,128)(2,1)S(1)}, bf16[2,256,256]{2,1,0:T(8,128)(2,1)S(1)}) custom-call(s32[32]{0:T(128)S(1)} %copy-done.4, bf16[8,256,256]{2,1,0:T(8,128)(2,1)S(1)} %copy-done), custom_call_target="tpu_custom_call" | custom-call | tf_op jit(solution)/shard_map/select/pallas_call | solution.py:69
  8.2 0.0 copy-done.2
  8.2 0.0 copy-done.3
  8.3 0.1 collective-permute-start.1
  8.4 0.0 collective-permute-done.3.refs_1_
  8.4 0.2 collective-permute-start.7
  8.6 1.8 %collective-permute-start.8 = (bf16[2,256,256]{2,1,0:T(8,128)(2,1)S(1)}, bf16[2,256,256]{2,1,0:T(8,128)(2,1)S(1)}, u32[]{:S(2)}, u32[]{:S(2)}) collective-permute-start(bf16[2,256,256]{2,1,0:T(8,128)(2,1)S(1)} %get-tuple-element.33), channel_id=1, source_target_pairs={{0,2},{1,3},{2,0},{3,1},{4,6},{5,7},{6,4},{7,5},{8,10},{9,11},{10,... | collective-permute-start | bytes 786440 | tf_op jit(solution)/shard_map/ppermute | solution.py:362
  10.4 0.2 collective-permute-start
  10.6 4.2 %collective-permute-done.4.refs_0_ = bf16[192,1024]{1,0:T(8,128)(2,1)S(1)} collective-permute-done((bf16[192,1024]{1,0:T(8,128)(2,1)S(1)}, bf16[192,1024]{1,0:T(8,128)(2,1)S(1)}, u32[]{:S(2)}, u32[]{:S(2)}) %collective-permute-start.4) | collective-permute-done | bytes 393248 | tf_op jit(solution)/shard_map/ppermute | solution.py:362
  14.8 2.0 %collective-permute-start.12 = (bf16[192,1024]{1,0:T(8,128)(2,1)S(1)}, bf16[192,1024]{1,0:T(8,128)(2,1)S(1)}, u32[]{:S(2)}, u32[]{:S(2)}) collective-permute-start(bf16[192,1024]{1,0:T(8,128)(2,1)S(1)} %collective-permute-done.4.refs_0_), channel_id=1, source_target_pairs={{0,4},{4,0},{8,12},{12,8},{1,5},{5,1},{9,13},{13,9},{2,6},{6,2},{1... | collective-permute-start | bytes 1179656 | tf_op jit(solution)/shard_map/ppermute | solution.py:363
  16.8 1.1 %collective-permute-done.1.refs_2_ = bf16[288,256]{1,0:T(8,128)(2,1)S(1)} collective-permute-done((bf16[288,256]{1,0:T(8,128)(2,1)S(1)}, bf16[288,256]{1,0:T(8,128)(2,1)S(1)}, u32[]{:S(2)}, u32[]{:S(2)}) %collective-permute-start.1) | collective-permute-done | bytes 147488 | tf_op jit(solution)/shard_map/ppermute | solution.py:362
  17.9 0.0 collective-permute-start.2
  18.0 0.0 collective-permute-done.refs_1_
  18.0 2.1 %collective-permute-start.5 = (bf16[2,256,256]{2,1,0:T(8,128)(2,1)S(1)}, bf16[2,256,256]{2,1,0:T(8,128)(2,1)S(1)}, u32[]{:S(2)}, u32[]{:S(2)}) collective-permute-start(bf16[2,256,256]{2,1,0:T(8,128)(2,1)S(1)} %get-tuple-element.28), channel_id=1, source_target_pairs={{0,3},{1,2},{2,1},{3,0},{4,7},{5,6},{6,5},{7,4},{8,11},{9,10},{10,... | collective-permute-start | bytes 786440 | tf_op jit(solution)/shard_map/ppermute | solution.py:362
  20.0 0.0 collective-permute-done.2.refs_3_
  20.0 0.6 %fields.1 = f32[4,2,256]{2,1,0:T(2,128)S(1)} custom-call(s32[32]{0:T(128)S(1)} %copy-done.4, bf16[288,256]{1,0:T(8,128)(2,1)S(1)} %message.1.refs_0_, bf16[288,256]{1,0:T(8,128)(2,1)S(1)} %collective-permute-done.refs_1_, bf16[288,256]{1,0:T(8,128)(2,1)S(1)} %collective-permute-done.1.refs_2_, bf16[288,256]{1,0:T(8,128)(2,1)S(1)} %collective-permute-done.2.refs_3_), custom_call_target="tpu_custom_call" | custom-call | tf_op jit(solution)/shard_map/fields/pallas_call | solution.py:119
  20.6 0.7 %collective-permute-start.6 = (f32[4,2,256]{2,1,0:T(2,128)S(1)}, f32[4,2,256]{2,1,0:T(2,128)S(1)}, u32[]{:S(2)}, u32[]{:S(2)}) collective-permute-start(f32[4,2,256]{2,1,0:T(2,128)S(1)} %fields.1), channel_id=1, source_target_pairs={{0,0},{1,5},{2,10},{3,15},{4,4},{5,1},{6,14},{7,11},{8,8},{9,13},{... | collective-permute-start | bytes 24584 | tf_op jit(solution)/shard_map/ppermute | solution.py:364
  21.3 0.0 copy-done.1
  22.0 0.8 %turn.1 = (bf16[256,1024]{1,0:T(8,128)(2,1)S(1)}, f32[8,128]{1,0:T(8,128)S(1)}) custom-call(s32[32]{0:T(128)S(1)} %copy-done.4, s32[1]{0:T(128)S(6)} %copy.8.counts, bf16[288,256]{1,0:T(8,128)(2,1)S(1)} %message.1.refs_0_, bf16[288,256]{1,0:T(8,128)(2,1)S(1)} %collective-permute-done.refs_1_, bf16[288,256]{1,0:T(8,128)(2,1)S(1)} %collective-permute-done.1.refs_2_, ...), custom_call_target="tpu_custom_call" | custom-call | tf_op jit(solution)/shard_map/turn/pallas_call | solution.py:146
  22.8 0.0 collective-permute-done.6.refs_4_.refs_2_
  22.8 0.0 collective-permute-done.7.refs_1_
  22.8 0.8 %collective-permute-done.8.refs_2_ = bf16[2,256,256]{2,1,0:T(8,128)(2,1)S(1)} collective-permute-done((bf16[2,256,256]{2,1,0:T(8,128)(2,1)S(1)}, bf16[2,256,256]{2,1,0:T(8,128)(2,1)S(1)}, u32[]{:S(2)}, u32[]{:S(2)}) %collective-permute-start.8) | collective-permute-done | bytes 262176 | tf_op jit(solution)/shard_map/ppermute | solution.py:362
  23.6 0.8 %first.1 = (bf16[768,512]{1,0:T(8,128)(2,1)S(1)}, f32[256,512]{1,0:T(8,128)S(1)}) custom-call(bf16[2,256,256]{2,1,0:T(8,128)(2,1)S(1)} %get-tuple-element.24.refs_0_, bf16[2,256,256]{2,1,0:T(8,128)(2,1)S(1)} %collective-permute-done.7.refs_1_, bf16[2,256,256]{2,1,0:T(8,128)(2,1)S(1)} %collective-permute-done.8.refs_2_, ...), custom_call_target="tpu_custom_call" | custom-call | flops 1073741824 | bytes 1048576 | tf_op jit(solution)/shard_map/first/pallas_call | solution.py:187
  24.4 4.8 %collective-permute-start.9 = (bf16[128,1024]{1,0:T(8,128)(2,1)S(1)}, bf16[128,1024]{1,0:T(8,128)(2,1)S(1)}, u32[]{:S(2)}, u32[]{:S(2)}) collective-permute-start(bf16[128,1024]{1,0:T(8,128)(2,1)S(1)} %slice.4), channel_id=1, source_target_pairs={{0,2},{1,3},{2,0},{3,1},{4,6},{5,7},{6,4},{7,5},{8,10},{9,11},{10,... | collective-permute-start | bytes 786440 | tf_op jit(solution)/shard_map/ppermute | solution.py:362
  29.2 0.2 collective-permute-start.11
  29.4 0.0 collective-permute-done.5.refs_0_
  29.4 5.1 %green.1.refs_2_.refs_4_ = bf16[1024,512]{1,0:T(8,128)(2,1)S(1)} custom-call(bf16[2,256,256]{2,1,0:T(8,128)(2,1)S(1)} %collective-permute-done.5.refs_0_, bf16[256,1024]{1,0:T(8,128)(2,1)S(1)} %get-tuple-element.29.refs_3_.refs_1_, f32[4,2,256]{2,1,0:T(2,128)S(1)} %collective-permute-done.6.refs_4_.refs_2_, bf16[768,512]{1,0:T(8,128)(2,1)S(1)} %get-tuple-element.34.refs_3_, ...), custom_call_target="tpu_custom_call" | custom-call | tf_op jit(solution)/shard_map/green/pallas_call | solution.py:245
  34.5 0.0 collective-permute-done.12.refs_2_
  34.5 0.4 collective-permute-start.13
  34.9 1.2 %collective-permute-done.9.refs_0_ = bf16[128,1024]{1,0:T(8,128)(2,1)S(1)} collective-permute-done((bf16[128,1024]{1,0:T(8,128)(2,1)S(1)}, bf16[128,1024]{1,0:T(8,128)(2,1)S(1)}, u32[]{:S(2)}, u32[]{:S(2)}) %collective-permute-start.9) | collective-permute-done | bytes 262176 | tf_op jit(solution)/shard_map/ppermute | solution.py:362
  36.1 0.0 collective-permute-start.10
  36.1 1.5 %contract.3 = f32[2,8,128]{2,1,0:T(8,128)S(1)} custom-call(bf16[512,1024]{1,0:T(8,128)(2,1)S(1)} %bitcast.6, bf16[512,1024]{1,0:T(8,128)(2,1)S(1)} %collective-permute-done.3.refs_1_, bf16[1024,512]{1,0:T(8,128)(2,1)S(1)} %green.1.refs_2_.refs_4_), custom_call_target="tpu_custom_call" | custom-call | flops 1073741824 | bytes 3145728 | tf_op jit(solution)/shard_map/contract/pallas_call | solution.py:313
  37.7 0.0 collective-permute-done.11.refs_1_
  37.7 0.0 collective-permute-done.13.refs_3_
  37.7 1.4 %contract.4 = (f32[2,8,128]{2,1,0:T(8,128)S(1)}, f32[128,512]{1,0:T(8,128)S(1)}, f32[128,512]{1,0:T(8,128)S(1)}) custom-call(bf16[192,1024]{1,0:T(8,128)(2,1)S(1)} %collective-permute-done.4.refs_0_, bf16[192,1024]{1,0:T(8,128)(2,1)S(1)} %collective-permute-done.11.refs_1_, bf16[192,1024]{1,0:T(8,128)(2,1)S(1)} %collective-permute-done.12.refs_2_, ...), custom_call_target="tpu_custom_call" | custom-call | flops 805306368 | bytes 2621440 | tf_op jit(solution)/shard_map/contract/pallas_call | solution.py:313
  39.1 0.0 collective-permute-done.10.refs_1_
  39.1 0.7 %contract.5 = f32[2,8,128]{2,1,0:T(8,128)S(1)} custom-call(bf16[128,1024]{1,0:T(8,128)(2,1)S(1)} %collective-permute-done.9.refs_0_, bf16[128,1024]{1,0:T(8,128)(2,1)S(1)} %collective-permute-done.10.refs_1_, bf16[1024,512]{1,0:T(8,128)(2,1)S(1)} %green.1.refs_2_.refs_4_, f32[128,512]{1,0:T(8,128)S(1)} %get-tuple-element.40.refs_3_, ...), custom_call_target="tpu_custom_call" | custom-call | flops 268435456 | bytes 1572864 | tf_op jit(solution)/shard_map/contract/pallas_call | solution.py:313
  39.8 0.7 %collective-permute-start.14 = (f32[2,8,128]{2,1,0:T(8,128)S(1)}, f32[2,8,128]{2,1,0:T(8,128)S(1)}, u32[]{:S(2)}, u32[]{:S(2)}) collective-permute-start(f32[2,8,128]{2,1,0:T(8,128)S(1)} %contract.3), channel_id=1, source_target_pairs={{0,0},{1,5},{2,10},{3,15},{4,4},{5,1},{6,14},{7,11},{8,8},{9,13},{... | collective-permute-start | bytes 24584 | tf_op jit(solution)/shard_map/ppermute | solution.py:365
  40.5 4.1 %collective-permute-start.16 = (f32[2,8,128]{2,1,0:T(8,128)S(1)}, f32[2,8,128]{2,1,0:T(8,128)S(1)}, u32[]{:S(2)}, u32[]{:S(2)}) collective-permute-start(f32[2,8,128]{2,1,0:T(8,128)S(1)} %contract.5), channel_id=1, source_target_pairs={{0,2},{1,7},{2,8},{3,13},{4,6},{5,3},{6,12},{7,9},{8,10},{9,15},{1... | collective-permute-start | bytes 24584 | tf_op jit(solution)/shard_map/ppermute | solution.py:365
  44.5 0.0 collective-permute-done.14.refs_0_
  44.5 0.2 collective-permute-start.15
  44.7 2.8 %collective-permute-done.16.refs_2_ = f32[2,8,128]{2,1,0:T(8,128)S(1)} collective-permute-done((f32[2,8,128]{2,1,0:T(8,128)S(1)}, f32[2,8,128]{2,1,0:T(8,128)S(1)}, u32[]{:S(2)}, u32[]{:S(2)}) %collective-permute-start.16) | collective-permute-done | bytes 8224 | tf_op jit(solution)/shard_map/ppermute | solution.py:365
  47.5 0.3 collective-permute-start.17
  47.8 0.0 collective-permute-done.15.refs_1_
  47.8 0.9 %collective-permute-done.17.refs_3_ = f32[2,8,128]{2,1,0:T(8,128)S(1)} collective-permute-done((f32[2,8,128]{2,1,0:T(8,128)S(1)}, f32[2,8,128]{2,1,0:T(8,128)S(1)}, u32[]{:S(2)}, u32[]{:S(2)}) %collective-permute-start.17) | collective-permute-done | bytes 8224 | tf_op jit(solution)/shard_map/ppermute | solution.py:362
  48.7 0.6 %unpack.1 = (f32[2,8]{1,0:T(2,128)}, f32[2,8]{1,0:T(2,128)}) custom-call(f32[8,128]{1,0:T(8,128)S(1)} %get-tuple-element.26.masks, f32[2,8,128]{2,1,0:T(8,128)S(1)} %collective-permute-done.14.refs_0_, f32[2,8,128]{2,1,0:T(8,128)S(1)} %collective-permute-done.15.refs_1_, f32[2,8,128]{2,1,0:T(8,128)S(1)} %collective-permute-done.16.refs_2_, ...), custom_call_target="tpu_custom_call" | custom-call | tf_op jit(solution)/shard_map/unpack/pallas_call | solution.py:345
  (2 shorter events, 0.0 us)
Async XLA Ops:
  0.6 7.7 %collective-permute-start.3 = (bf16[512,1024]{1,0:T(8,128)(2,1)}, bf16[512,1024]{1,0:T(8,128)(2,1)S(1)}, u32[]{:S(2)}, u32[]{:S(2)}) collective-permute-start(bf16[512,1024]{1,0:T(8,128)(2,1)} %bitcast.3), channel_id=1, source_target_pairs={{0,1},{1,0},{2,3},{3,2},{4,5},{5,4},{6,7},{7,6},{8,9},{9,8},{10,11... | collective-permute-start | bytes 3145736 | tf_op jit(solution)/shard_map/ppermute | solution.py:362
  1.1 3.7 %copy-start.4 = (s32[32]{0:T(128)S(1)}, s32[32]{0:T(128)}, u32[]{:S(2)}) copy-start(s32[32]{0:T(128)} %branches.5) | copy-start | bytes 388
  1.2 7.1 %copy-start.2 = (bf16[256,256]{1,0:T(8,128)(2,1)S(1)}, bf16[256,256]{1,0:T(8,128)(2,1)}, u32[]{:S(2)}) copy-start(bf16[256,256]{1,0:T(8,128)(2,1)} %trial) | copy-start | bytes 393220
  1.2 7.1 %copy-start.3 = (f32[8,256]{1,0:T(8,128)S(1)}, f32[8,256]{1,0:T(8,128)}, u32[]{:S(2)}) copy-start(f32[8,256]{1,0:T(8,128)} %field.1) | copy-start | bytes 24580
  2.2 12.6 %collective-permute-start.4 = (bf16[192,1024]{1,0:T(8,128)(2,1)S(1)}, bf16[192,1024]{1,0:T(8,128)(2,1)S(1)}, u32[]{:S(2)}, u32[]{:S(2)}) collective-permute-start(bf16[192,1024]{1,0:T(8,128)(2,1)S(1)} %constant_dynamic-slice_fusion), channel_id=1, source_target_pairs={{0,2},{1,3},{2,0},{3,1},{4,6},{5,7},{6,4},{7,5},{8,10},{9,11},{10,... | collective-permute-start | bytes 1179656 | tf_op jit(solution)/shard_map/ppermute | solution.py:362
  4.8 1.2 %copy-start = (bf16[8,256,256]{2,1,0:T(8,128)(2,1)S(1)}, bf16[8,256,256]{2,1,0:T(8,128)(2,1)}, u32[]{:S(2)}) copy-start(bf16[8,256,256]{2,1,0:T(8,128)(2,1)} %walkers.1) | copy-start | bytes 3145732
  6.0 15.3 %copy-start.1 = (bf16[2,256,1024]{2,1,0:T(8,128)(2,1)S(1)}, bf16[2,256,1024]{2,1,0:T(8,128)(2,1)}, u32[]{:S(2)}) copy-start(bf16[2,256,1024]{2,1,0:T(8,128)(2,1)} %param.8) | copy-start | bytes 3145732
  8.3 9.7 %collective-permute-start.1 = (bf16[288,256]{1,0:T(8,128)(2,1)S(1)}, bf16[288,256]{1,0:T(8,128)(2,1)S(1)}, u32[]{:S(2)}, u32[]{:S(2)}) collective-permute-start(bf16[288,256]{1,0:T(8,128)(2,1)S(1)} %message.1.refs_0_), channel_id=1, source_target_pairs={{0,2},{1,3},{2,0},{3,1},{4,6},{5,7},{6,4},{7,5},{8,10},{9,11},{10,... | collective-permute-start | bytes 442376 | tf_op jit(solution)/shard_map/ppermute | solution.py:362
  8.4 14.4 %collective-permute-start.7 = (bf16[2,256,256]{2,1,0:T(8,128)(2,1)S(1)}, bf16[2,256,256]{2,1,0:T(8,128)(2,1)S(1)}, u32[]{:S(2)}, u32[]{:S(2)}) collective-permute-start(bf16[2,256,256]{2,1,0:T(8,128)(2,1)S(1)} %get-tuple-element.31), channel_id=1, source_target_pairs={{0,1},{1,0},{2,3},{3,2},{4,5},{5,4},{6,7},{7,6},{8,9},{9,8},{10,11... | collective-permute-start | bytes 786440 | tf_op jit(solution)/shard_map/ppermute | solution.py:362
  8.6 15.0 %collective-permute-start.8 = (bf16[2,256,256]{2,1,0:T(8,128)(2,1)S(1)}, bf16[2,256,256]{2,1,0:T(8,128)(2,1)S(1)}, u32[]{:S(2)}, u32[]{:S(2)}) collective-permute-start(bf16[2,256,256]{2,1,0:T(8,128)(2,1)S(1)} %get-tuple-element.33), channel_id=1, source_target_pairs={{0,2},{1,3},{2,0},{3,1},{4,6},{5,7},{6,4},{7,5},{8,10},{9,11},{10,... | collective-permute-start | bytes 786440 | tf_op jit(solution)/shard_map/ppermute | solution.py:362
  10.4 7.6 %collective-permute-start = (bf16[288,256]{1,0:T(8,128)(2,1)S(1)}, bf16[288,256]{1,0:T(8,128)(2,1)S(1)}, u32[]{:S(2)}, u32[]{:S(2)}) collective-permute-start(bf16[288,256]{1,0:T(8,128)(2,1)S(1)} %message.1.refs_0_), channel_id=1, source_target_pairs={{0,1},{1,0},{2,3},{3,2},{4,5},{5,4},{6,7},{7,6},{8,9},{9,8},{10,11... | collective-permute-start | bytes 442376 | tf_op jit(solution)/shard_map/ppermute | solution.py:362
  14.8 19.7 %collective-permute-start.12 = (bf16[192,1024]{1,0:T(8,128)(2,1)S(1)}, bf16[192,1024]{1,0:T(8,128)(2,1)S(1)}, u32[]{:S(2)}, u32[]{:S(2)}) collective-permute-start(bf16[192,1024]{1,0:T(8,128)(2,1)S(1)} %collective-permute-done.4.refs_0_), channel_id=1, source_target_pairs={{0,4},{4,0},{8,12},{12,8},{1,5},{5,1},{9,13},{13,9},{2,6},{6,2},{1... | collective-permute-start | bytes 1179656 | tf_op jit(solution)/shard_map/ppermute | solution.py:363
  17.9 2.1 %collective-permute-start.2 = (bf16[288,256]{1,0:T(8,128)(2,1)S(1)}, bf16[288,256]{1,0:T(8,128)(2,1)S(1)}, u32[]{:S(2)}, u32[]{:S(2)}) collective-permute-start(bf16[288,256]{1,0:T(8,128)(2,1)S(1)} %collective-permute-done.1.refs_2_), channel_id=1, source_target_pairs={{0,1},{1,0},{2,3},{3,2},{4,5},{5,4},{6,7},{7,6},{8,9},{9,8},{10,11... | collective-permute-start | bytes 442376 | tf_op jit(solution)/shard_map/ppermute | solution.py:362
  18.0 11.4 %collective-permute-start.5 = (bf16[2,256,256]{2,1,0:T(8,128)(2,1)S(1)}, bf16[2,256,256]{2,1,0:T(8,128)(2,1)S(1)}, u32[]{:S(2)}, u32[]{:S(2)}) collective-permute-start(bf16[2,256,256]{2,1,0:T(8,128)(2,1)S(1)} %get-tuple-element.28), channel_id=1, source_target_pairs={{0,3},{1,2},{2,1},{3,0},{4,7},{5,6},{6,5},{7,4},{8,11},{9,10},{10,... | collective-permute-start | bytes 786440 | tf_op jit(solution)/shard_map/ppermute | solution.py:362
  20.6 2.2 %collective-permute-start.6 = (f32[4,2,256]{2,1,0:T(2,128)S(1)}, f32[4,2,256]{2,1,0:T(2,128)S(1)}, u32[]{:S(2)}, u32[]{:S(2)}) collective-permute-start(f32[4,2,256]{2,1,0:T(2,128)S(1)} %fields.1), channel_id=1, source_target_pairs={{0,0},{1,5},{2,10},{3,15},{4,4},{5,1},{6,14},{7,11},{8,8},{9,13},{... | collective-permute-start | bytes 24584 | tf_op jit(solution)/shard_map/ppermute | solution.py:364
  24.4 11.8 %collective-permute-start.9 = (bf16[128,1024]{1,0:T(8,128)(2,1)S(1)}, bf16[128,1024]{1,0:T(8,128)(2,1)S(1)}, u32[]{:S(2)}, u32[]{:S(2)}) collective-permute-start(bf16[128,1024]{1,0:T(8,128)(2,1)S(1)} %slice.4), channel_id=1, source_target_pairs={{0,2},{1,3},{2,0},{3,1},{4,6},{5,7},{6,4},{7,5},{8,10},{9,11},{10,... | collective-permute-start | bytes 786440 | tf_op jit(solution)/shard_map/ppermute | solution.py:362
  29.2 8.5 %collective-permute-start.11 = (bf16[192,1024]{1,0:T(8,128)(2,1)S(1)}, bf16[192,1024]{1,0:T(8,128)(2,1)S(1)}, u32[]{:S(2)}, u32[]{:S(2)}) collective-permute-start(bf16[192,1024]{1,0:T(8,128)(2,1)S(1)} %collective-permute-done.4.refs_0_), channel_id=1, source_target_pairs={{0,1},{1,0},{2,3},{3,2},{4,5},{5,4},{6,7},{7,6},{8,9},{9,8},{10,11... | collective-permute-start | bytes 1179656 | tf_op jit(solution)/shard_map/ppermute | solution.py:362
  34.5 3.1 %collective-permute-start.13 = (bf16[192,1024]{1,0:T(8,128)(2,1)S(1)}, bf16[192,1024]{1,0:T(8,128)(2,1)S(1)}, u32[]{:S(2)}, u32[]{:S(2)}) collective-permute-start(bf16[192,1024]{1,0:T(8,128)(2,1)S(1)} %collective-permute-done.12.refs_2_), channel_id=1, source_target_pairs={{0,1},{1,0},{2,3},{3,2},{4,5},{5,4},{6,7},{7,6},{8,9},{9,8},{10,11... | collective-permute-start | bytes 1179656 | tf_op jit(solution)/shard_map/ppermute | solution.py:362
  36.1 2.9 %collective-permute-start.10 = (bf16[128,1024]{1,0:T(8,128)(2,1)S(1)}, bf16[128,1024]{1,0:T(8,128)(2,1)S(1)}, u32[]{:S(2)}, u32[]{:S(2)}) collective-permute-start(bf16[128,1024]{1,0:T(8,128)(2,1)S(1)} %collective-permute-done.9.refs_0_), channel_id=1, source_target_pairs={{0,1},{1,0},{2,3},{3,2},{4,5},{5,4},{6,7},{7,6},{8,9},{9,8},{10,11... | collective-permute-start | bytes 786440 | tf_op jit(solution)/shard_map/ppermute | solution.py:362
  39.8 4.7 %collective-permute-start.14 = (f32[2,8,128]{2,1,0:T(8,128)S(1)}, f32[2,8,128]{2,1,0:T(8,128)S(1)}, u32[]{:S(2)}, u32[]{:S(2)}) collective-permute-start(f32[2,8,128]{2,1,0:T(8,128)S(1)} %contract.3), channel_id=1, source_target_pairs={{0,0},{1,5},{2,10},{3,15},{4,4},{5,1},{6,14},{7,11},{8,8},{9,13},{... | collective-permute-start | bytes 24584 | tf_op jit(solution)/shard_map/ppermute | solution.py:365
  40.5 7.1 %collective-permute-start.16 = (f32[2,8,128]{2,1,0:T(8,128)S(1)}, f32[2,8,128]{2,1,0:T(8,128)S(1)}, u32[]{:S(2)}, u32[]{:S(2)}) collective-permute-start(f32[2,8,128]{2,1,0:T(8,128)S(1)} %contract.5), channel_id=1, source_target_pairs={{0,2},{1,7},{2,8},{3,13},{4,6},{5,3},{6,12},{7,9},{8,10},{9,15},{1... | collective-permute-start | bytes 24584 | tf_op jit(solution)/shard_map/ppermute | solution.py:365
  44.5 3.2 %collective-permute-start.15 = (f32[2,8,128]{2,1,0:T(8,128)S(1)}, f32[2,8,128]{2,1,0:T(8,128)S(1)}, u32[]{:S(2)}, u32[]{:S(2)}) collective-permute-start(f32[2,8,128]{2,1,0:T(8,128)S(1)} %collective-permute-done.14.refs_0_), channel_id=1, source_target_pairs={{0,1},{1,0},{2,3},{3,2},{4,5},{5,4},{6,7},{7,6},{8,9},{9,8},{10,11... | collective-permute-start | bytes 24584 | tf_op jit(solution)/shard_map/ppermute | solution.py:362
  47.5 1.2 %collective-permute-start.17 = (f32[2,8,128]{2,1,0:T(8,128)S(1)}, f32[2,8,128]{2,1,0:T(8,128)S(1)}, u32[]{:S(2)}, u32[]{:S(2)}) collective-permute-start(f32[2,8,128]{2,1,0:T(8,128)S(1)} %collective-permute-done.16.refs_2_), channel_id=1, source_target_pairs={{0,1},{1,0},{2,3},{3,2},{4,5},{5,4},{6,7},{7,6},{8,9},{9,8},{10,11... | collective-permute-start | bytes 24584 | tf_op jit(solution)/shard_map/ppermute | solution.py:362

commit v10 on v9

--- a/solution.py
+++ b/solution.py
@@ -402,8 +402,9 @@
     direct = {k: move(ordered(rows[:direct_rows], begun), k) for k in heads}
     green = make_green(n, share, blocks[n - 1], turned, asked, earlier, begun)
     crossed = along(crossed)
-    other, direct = (along({k: ordered(x, green) for k, x in held.items()}) for held in (other, direct))
+    other = along({k: ordered(x, green) for k, x in other.items()})
     [results] = contract(functools.partial(near_kernel, share, len(near), height), len(near), close, green)
+    direct = along({k: ordered(x, results) for k, x in direct.items()})
     late, *kept = contract(
         functools.partial(shared_kernel, share, len(far), height),
         len(far),

time: 49.5 us -> 49.3 us (level)
  waiting for transfers between devices: 11 us -> 8.42 us
  starting transfers between devices: 20.8 us -> 23.2 us
    ppermute x14, starting transfers between devices: 13.4 us -> 14.7 us  [at_the_source(): move = lambda x, k: lax.ppermute(x, SR, [(i, i ^ k) for i in range(n)])]
    ppermute x2, waiting for transfers between devices: 2.81 us -> 1.5 us  [at_the_source(): lax.ppermute(x, ALL, [(w * n + q, (w ^ q) * n + (q ^ k)) for w, q in pairs])]
    ppermute x14, waiting for transfers between devices: 8.2 us -> 6.92 us  [at_the_source(): move = lambda x, k: lax.ppermute(x, SR, [(i, i ^ k) for i in range(n)])]
    ppermute x2, starting transfers between devices: 4.74 us -> 5.75 us  [at_the_source(): lax.ppermute(x, ALL, [(w * n + q, (w ^ q) * n + (q ^ k)) for w, q in pairs])]
  transfers between devices with their start and end apart: 18 -> 18, of which waited for: 6 -> 5; matrix products, arithmetic and copies ran while one was open for 2% -> 2% of each run, Pallas kernels for 25% -> 25%
where the time goes in v10:
time: 49.3 us; the launch traced here: 49.1 us
  starting transfers between devices  23.2 us (47%)
  Pallas kernels  13.7 us (28%)
  waiting for transfers between devices  8.42 us (17%)
  local copies, waits for them, and re-layouts  2.32 us (5%)
  between operations  1.46 us (3%)
    ppermute x14, starting transfers between devices, at_the_source(): move = lambda x, k: lax.ppermute(x, SR, [(i, i ^ k) for i in range(n)])  14.7 us
    ppermute x14, waiting for transfers between devices, at_the_source(): move = lambda x, k: lax.ppermute(x, SR, [(i, i ^ k) for i in range(n)])  6.92 us
    ppermute x2, starting transfers between devices, at_the_source(): lax.ppermute(x, ALL, [(w * n + q, (w ^ q) * n + (q ^ k)) for w, q in pairs])  5.75 us
    pallas_call x1, Pallas kernels, make_green(): pl.pallas_call(functools.partial(green_kernel, n, share), out_shape=jax.S...  5.13 us
    pallas_call x3, Pallas kernels, contract(): pl.pallas_call(kernel, out_shape=[jax.ShapeDtypeStruct((count, 8, 128), F...  3.62 us
    pallas_call x1, Pallas kernels, select(): pl.pallas_call(functools.partial(select_kernel, n, per, share), out_shape...  2.17 us
    ppermute x1, starting transfers between devices, at_the_source(): swap = lambda x: lax.ppermute(x, 'walk', [(w, w ^ 1) for w in range(n)])  2.03 us
    ppermute x2, waiting for transfers between devices, at_the_source(): lax.ppermute(x, ALL, [(w * n + q, (w ^ q) * n + (q ^ k)) for w, q in pairs])  1.5 us
  transfers between devices with their start and end apart: 18, of which 5 were waited for; matrix products, arithmetic and copies ran while one was open for 2% of the time, Pallas kernels for 25%

profile of v10, /device:TPU:0, one launch (start us, length us, event | category | flops | bytes accessed | tf_op | source)
XLA Modules:
  0.0 49.1 jit_solution(446951447510443434)
XLA Ops:
  0.6 0.5 %collective-permute-start.3 = (bf16[512,1024]{1,0:T(8,128)(2,1)}, bf16[512,1024]{1,0:T(8,128)(2,1)S(1)}, u32[]{:S(2)}, u32[]{:S(2)}) collective-permute-start(bf16[512,1024]{1,0:T(8,128)(2,1)} %bitcast.3), channel_id=1, source_target_pairs={{0,1},{1,0},{2,3},{3,2},{4,5},{5,4},{6,7},{7,6},{8,9},{9,8},{10,11... | collective-permute-start | bytes 3145736 | tf_op jit(solution)/shard_map/ppermute | solution.py:362
  1.1 0.0 copy-start.4
  1.2 0.0 copy-start.2
  1.2 0.0 copy-start.3
  1.2 1.1 %constant_dynamic-slice_fusion = bf16[192,1024]{1,0:T(8,128)(2,1)S(1)} fusion(bf16[512,1024]{1,0:T(8,128)(2,1)} %bitcast.4, s32[]{:T(128)S(6)} %select_n.3), kind=kLoop, calls=%fused_computation | loop fusion | bytes 786436 | tf_op jit(solution)/shard_map/dynamic_slice | solution.py:386
  2.2 2.6 %collective-permute-start.4 = (bf16[192,1024]{1,0:T(8,128)(2,1)S(1)}, bf16[192,1024]{1,0:T(8,128)(2,1)S(1)}, u32[]{:S(2)}, u32[]{:S(2)}) collective-permute-start(bf16[192,1024]{1,0:T(8,128)(2,1)S(1)} %constant_dynamic-slice_fusion), channel_id=1, source_target_pairs={{0,2},{1,3},{2,0},{3,1},{4,6},{5,7},{6,4},{7,5},{8,10},{9,11},{10,... | collective-permute-start | bytes 1179656 | tf_op jit(solution)/shard_map/ppermute | solution.py:362
  4.8 0.0 copy-done.4
  4.8 0.0 copy-start
  4.8 1.2 %copy-done = bf16[8,256,256]{2,1,0:T(8,128)(2,1)S(1)} copy-done((bf16[8,256,256]{2,1,0:T(8,128)(2,1)S(1)}, bf16[8,256,256]{2,1,0:T(8,128)(2,1)}, u32[]{:S(2)}) %copy-start) | copy-done | bytes 1048600
  6.0 0.0 copy-start.1
  6.1 2.2 %select.1 = (bf16[2,256,256]{2,1,0:T(8,128)(2,1)S(1)}, bf16[2,256,256]{2,1,0:T(8,128)(2,1)S(1)}, bf16[2,256,256]{2,1,0:T(8,128)(2,1)S(1)}, bf16[2,256,256]{2,1,0:T(8,128)(2,1)S(1)}) custom-call(s32[32]{0:T(128)S(1)} %copy-done.4, bf16[8,256,256]{2,1,0:T(8,128)(2,1)S(1)} %copy-done), custom_call_target="tpu_custom_call" | custom-call | tf_op jit(solution)/shard_map/select/pallas_call | solution.py:69
  8.2 0.0 copy-done.2
  8.2 0.0 copy-done.3
  8.3 0.1 collective-permute-start.1
  8.4 0.0 collective-permute-done.3.refs_1_
  8.4 0.2 collective-permute-start.7
  8.6 1.8 %collective-permute-start.8 = (bf16[2,256,256]{2,1,0:T(8,128)(2,1)S(1)}, bf16[2,256,256]{2,1,0:T(8,128)(2,1)S(1)}, u32[]{:S(2)}, u32[]{:S(2)}) collective-permute-start(bf16[2,256,256]{2,1,0:T(8,128)(2,1)S(1)} %get-tuple-element.33), channel_id=1, source_target_pairs={{0,2},{1,3},{2,0},{3,1},{4,6},{5,7},{6,4},{7,5},{8,10},{9,11},{10,... | collective-permute-start | bytes 786440 | tf_op jit(solution)/shard_map/ppermute | solution.py:362
  10.4 0.2 collective-permute-start
  10.6 4.2 %collective-permute-done.4.refs_0_ = bf16[192,1024]{1,0:T(8,128)(2,1)S(1)} collective-permute-done((bf16[192,1024]{1,0:T(8,128)(2,1)S(1)}, bf16[192,1024]{1,0:T(8,128)(2,1)S(1)}, u32[]{:S(2)}, u32[]{:S(2)}) %collective-permute-start.4) | collective-permute-done | bytes 393248 | tf_op jit(solution)/shard_map/ppermute | solution.py:362
  14.8 2.0 %collective-permute-start.12 = (bf16[192,1024]{1,0:T(8,128)(2,1)S(1)}, bf16[192,1024]{1,0:T(8,128)(2,1)S(1)}, u32[]{:S(2)}, u32[]{:S(2)}) collective-permute-start(bf16[192,1024]{1,0:T(8,128)(2,1)S(1)} %collective-permute-done.4.refs_0_), channel_id=1, source_target_pairs={{0,4},{4,0},{8,12},{12,8},{1,5},{5,1},{9,13},{13,9},{2,6},{6,2},{1... | collective-permute-start | bytes 1179656 | tf_op jit(solution)/shard_map/ppermute | solution.py:363
  16.8 1.1 %collective-permute-done.1.refs_2_ = bf16[288,256]{1,0:T(8,128)(2,1)S(1)} collective-permute-done((bf16[288,256]{1,0:T(8,128)(2,1)S(1)}, bf16[288,256]{1,0:T(8,128)(2,1)S(1)}, u32[]{:S(2)}, u32[]{:S(2)}) %collective-permute-start.1) | collective-permute-done | bytes 147488 | tf_op jit(solution)/shard_map/ppermute | solution.py:362
  17.9 0.0 collective-permute-start.2
  18.0 0.0 collective-permute-done.refs_1_
  18.0 2.1 %collective-permute-start.5 = (bf16[2,256,256]{2,1,0:T(8,128)(2,1)S(1)}, bf16[2,256,256]{2,1,0:T(8,128)(2,1)S(1)}, u32[]{:S(2)}, u32[]{:S(2)}) collective-permute-start(bf16[2,256,256]{2,1,0:T(8,128)(2,1)S(1)} %get-tuple-element.28), channel_id=1, source_target_pairs={{0,3},{1,2},{2,1},{3,0},{4,7},{5,6},{6,5},{7,4},{8,11},{9,10},{10,... | collective-permute-start | bytes 786440 | tf_op jit(solution)/shard_map/ppermute | solution.py:362
  20.0 0.0 collective-permute-done.2.refs_3_
  20.0 0.6 %fields.1 = f32[4,2,256]{2,1,0:T(2,128)S(1)} custom-call(s32[32]{0:T(128)S(1)} %copy-done.4, bf16[288,256]{1,0:T(8,128)(2,1)S(1)} %message.1.refs_0_, bf16[288,256]{1,0:T(8,128)(2,1)S(1)} %collective-permute-done.refs_1_, bf16[288,256]{1,0:T(8,128)(2,1)S(1)} %collective-permute-done.1.refs_2_, bf16[288,256]{1,0:T(8,128)(2,1)S(1)} %collective-permute-done.2.refs_3_), custom_call_target="tpu_custom_call" | custom-call | tf_op jit(solution)/shard_map/fields/pallas_call | solution.py:119
  20.6 0.7 %collective-permute-start.6 = (f32[4,2,256]{2,1,0:T(2,128)S(1)}, f32[4,2,256]{2,1,0:T(2,128)S(1)}, u32[]{:S(2)}, u32[]{:S(2)}) collective-permute-start(f32[4,2,256]{2,1,0:T(2,128)S(1)} %fields.1), channel_id=1, source_target_pairs={{0,0},{1,5},{2,10},{3,15},{4,4},{5,1},{6,14},{7,11},{8,8},{9,13},{... | collective-permute-start | bytes 24584 | tf_op jit(solution)/shard_map/ppermute | solution.py:364
  21.3 0.0 copy-done.1
  22.0 0.8 %turn.1 = (bf16[256,1024]{1,0:T(8,128)(2,1)S(1)}, f32[8,128]{1,0:T(8,128)S(1)}) custom-call(s32[32]{0:T(128)S(1)} %copy-done.4, s32[1]{0:T(128)S(6)} %copy.8.counts, bf16[288,256]{1,0:T(8,128)(2,1)S(1)} %message.1.refs_0_, bf16[288,256]{1,0:T(8,128)(2,1)S(1)} %collective-permute-done.refs_1_, bf16[288,256]{1,0:T(8,128)(2,1)S(1)} %collective-permute-done.1.refs_2_, ...), custom_call_target="tpu_custom_call" | custom-call | tf_op jit(solution)/shard_map/turn/pallas_call | solution.py:146
  22.8 0.0 collective-permute-done.6.refs_4_.refs_2_
  22.8 0.0 collective-permute-done.7.refs_1_
  22.8 0.8 %collective-permute-done.8.refs_2_ = bf16[2,256,256]{2,1,0:T(8,128)(2,1)S(1)} collective-permute-done((bf16[2,256,256]{2,1,0:T(8,128)(2,1)S(1)}, bf16[2,256,256]{2,1,0:T(8,128)(2,1)S(1)}, u32[]{:S(2)}, u32[]{:S(2)}) %collective-permute-start.8) | collective-permute-done | bytes 262176 | tf_op jit(solution)/shard_map/ppermute | solution.py:362
  23.6 0.8 %first.1 = (bf16[768,512]{1,0:T(8,128)(2,1)S(1)}, f32[256,512]{1,0:T(8,128)S(1)}) custom-call(bf16[2,256,256]{2,1,0:T(8,128)(2,1)S(1)} %get-tuple-element.24.refs_0_, bf16[2,256,256]{2,1,0:T(8,128)(2,1)S(1)} %collective-permute-done.7.refs_1_, bf16[2,256,256]{2,1,0:T(8,128)(2,1)S(1)} %collective-permute-done.8.refs_2_, ...), custom_call_target="tpu_custom_call" | custom-call | flops 1073741824 | bytes 1048576 | tf_op jit(solution)/shard_map/first/pallas_call | solution.py:187
  24.4 4.8 %collective-permute-start.9 = (bf16[128,1024]{1,0:T(8,128)(2,1)S(1)}, bf16[128,1024]{1,0:T(8,128)(2,1)S(1)}, u32[]{:S(2)}, u32[]{:S(2)}) collective-permute-start(bf16[128,1024]{1,0:T(8,128)(2,1)S(1)} %slice.4), channel_id=1, source_target_pairs={{0,2},{1,3},{2,0},{3,1},{4,6},{5,7},{6,4},{7,5},{8,10},{9,11},{10,... | collective-permute-start | bytes 786440 | tf_op jit(solution)/shard_map/ppermute | solution.py:362
  29.2 0.2 collective-permute-start.11
  29.4 0.0 collective-permute-done.5.refs_0_
  29.4 5.1 %green.1.refs_2_.refs_4_ = bf16[1024,512]{1,0:T(8,128)(2,1)S(1)} custom-call(bf16[2,256,256]{2,1,0:T(8,128)(2,1)S(1)} %collective-permute-done.5.refs_0_, bf16[256,1024]{1,0:T(8,128)(2,1)S(1)} %get-tuple-element.29.refs_3_.refs_1_, f32[4,2,256]{2,1,0:T(2,128)S(1)} %collective-permute-done.6.refs_4_.refs_2_, bf16[768,512]{1,0:T(8,128)(2,1)S(1)} %get-tuple-element.34.refs_3_, ...), custom_call_target="tpu_custom_call" | custom-call | tf_op jit(solution)/shard_map/green/pallas_call | solution.py:245
  34.5 0.0 collective-permute-done.12.refs_2_
  34.5 0.4 collective-permute-start.13
  34.9 1.5 %contract.3 = f32[2,8,128]{2,1,0:T(8,128)S(1)} custom-call(bf16[512,1024]{1,0:T(8,128)(2,1)S(1)} %bitcast.6, bf16[512,1024]{1,0:T(8,128)(2,1)S(1)} %collective-permute-done.3.refs_1_, bf16[1024,512]{1,0:T(8,128)(2,1)S(1)} %green.1.refs_2_.refs_4_), custom_call_target="tpu_custom_call" | custom-call | flops 1073741824 | bytes 3145728 | tf_op jit(solution)/shard_map/contract/pallas_call | solution.py:313
  36.5 0.0 collective-permute-done.9.refs_0_
  36.5 0.2 collective-permute-start.10
  36.7 0.0 collective-permute-done.11.refs_1_
  36.7 0.0 collective-permute-done.13.refs_3_
  36.7 1.4 %contract.4 = (f32[2,8,128]{2,1,0:T(8,128)S(1)}, f32[128,512]{1,0:T(8,128)S(1)}, f32[128,512]{1,0:T(8,128)S(1)}) custom-call(bf16[192,1024]{1,0:T(8,128)(2,1)S(1)} %collective-permute-done.4.refs_0_, bf16[192,1024]{1,0:T(8,128)(2,1)S(1)} %collective-permute-done.11.refs_1_, bf16[192,1024]{1,0:T(8,128)(2,1)S(1)} %collective-permute-done.12.refs_2_, ...), custom_call_target="tpu_custom_call" | custom-call | flops 805306368 | bytes 2621440 | tf_op jit(solution)/shard_map/contract/pallas_call | solution.py:313
  38.1 0.0 collective-permute-done.10.refs_1_
  38.1 0.7 %contract.5 = f32[2,8,128]{2,1,0:T(8,128)S(1)} custom-call(bf16[128,1024]{1,0:T(8,128)(2,1)S(1)} %collective-permute-done.9.refs_0_, bf16[128,1024]{1,0:T(8,128)(2,1)S(1)} %collective-permute-done.10.refs_1_, bf16[1024,512]{1,0:T(8,128)(2,1)S(1)} %green.1.refs_2_.refs_4_, f32[128,512]{1,0:T(8,128)S(1)} %get-tuple-element.40.refs_3_, ...), custom_call_target="tpu_custom_call" | custom-call | flops 268435456 | bytes 1572864 | tf_op jit(solution)/shard_map/contract/pallas_call | solution.py:313
  38.8 0.7 %collective-permute-start.14 = (f32[2,8,128]{2,1,0:T(8,128)S(1)}, f32[2,8,128]{2,1,0:T(8,128)S(1)}, u32[]{:S(2)}, u32[]{:S(2)}) collective-permute-start(f32[2,8,128]{2,1,0:T(8,128)S(1)} %contract.3), channel_id=1, source_target_pairs={{0,0},{1,5},{2,10},{3,15},{4,4},{5,1},{6,14},{7,11},{8,8},{9,13},{... | collective-permute-start | bytes 24584 | tf_op jit(solution)/shard_map/ppermute | solution.py:365
  39.5 5.1 %collective-permute-start.16 = (f32[2,8,128]{2,1,0:T(8,128)S(1)}, f32[2,8,128]{2,1,0:T(8,128)S(1)}, u32[]{:S(2)}, u32[]{:S(2)}) collective-permute-start(f32[2,8,128]{2,1,0:T(8,128)S(1)} %contract.5), channel_id=1, source_target_pairs={{0,2},{1,7},{2,8},{3,13},{4,6},{5,3},{6,12},{7,9},{8,10},{9,15},{1... | collective-permute-start | bytes 24584 | tf_op jit(solution)/shard_map/ppermute | solution.py:365
  44.6 0.0 collective-permute-done.14.refs_0_
  44.6 0.0 collective-permute-start.15
  44.6 1.5 %collective-permute-done.16.refs_2_ = f32[2,8,128]{2,1,0:T(8,128)S(1)} collective-permute-done((f32[2,8,128]{2,1,0:T(8,128)S(1)}, f32[2,8,128]{2,1,0:T(8,128)S(1)}, u32[]{:S(2)}, u32[]{:S(2)}) %collective-permute-start.16) | collective-permute-done | bytes 8224 | tf_op jit(solution)/shard_map/ppermute | solution.py:365
  46.1 1.6 %collective-permute-start.17 = (f32[2,8,128]{2,1,0:T(8,128)S(1)}, f32[2,8,128]{2,1,0:T(8,128)S(1)}, u32[]{:S(2)}, u32[]{:S(2)}) collective-permute-start(f32[2,8,128]{2,1,0:T(8,128)S(1)} %collective-permute-done.16.refs_2_), channel_id=1, source_target_pairs={{0,1},{1,0},{2,3},{3,2},{4,5},{5,4},{6,7},{7,6},{8,9},{9,8},{10,11... | collective-permute-start | bytes 24584 | tf_op jit(solution)/shard_map/ppermute | solution.py:362
  47.7 0.0 collective-permute-done.15.refs_1_
  47.7 0.8 %collective-permute-done.17.refs_3_ = f32[2,8,128]{2,1,0:T(8,128)S(1)} collective-permute-done((f32[2,8,128]{2,1,0:T(8,128)S(1)}, f32[2,8,128]{2,1,0:T(8,128)S(1)}, u32[]{:S(2)}, u32[]{:S(2)}) %collective-permute-start.17) | collective-permute-done | bytes 8224 | tf_op jit(solution)/shard_map/ppermute | solution.py:362
  48.5 0.6 %unpack.1 = (f32[2,8]{1,0:T(2,128)}, f32[2,8]{1,0:T(2,128)}) custom-call(f32[8,128]{1,0:T(8,128)S(1)} %get-tuple-element.26.masks, f32[2,8,128]{2,1,0:T(8,128)S(1)} %collective-permute-done.14.refs_0_, f32[2,8,128]{2,1,0:T(8,128)S(1)} %collective-permute-done.15.refs_1_, f32[2,8,128]{2,1,0:T(8,128)S(1)} %collective-permute-done.16.refs_2_, ...), custom_call_target="tpu_custom_call" | custom-call | tf_op jit(solution)/shard_map/unpack/pallas_call | solution.py:345
  (2 shorter events, 0.0 us)
Async XLA Ops:
  0.6 7.7 %collective-permute-start.3 = (bf16[512,1024]{1,0:T(8,128)(2,1)}, bf16[512,1024]{1,0:T(8,128)(2,1)S(1)}, u32[]{:S(2)}, u32[]{:S(2)}) collective-permute-start(bf16[512,1024]{1,0:T(8,128)(2,1)} %bitcast.3), channel_id=1, source_target_pairs={{0,1},{1,0},{2,3},{3,2},{4,5},{5,4},{6,7},{7,6},{8,9},{9,8},{10,11... | collective-permute-start | bytes 3145736 | tf_op jit(solution)/shard_map/ppermute | solution.py:362
  1.1 3.7 %copy-start.4 = (s32[32]{0:T(128)S(1)}, s32[32]{0:T(128)}, u32[]{:S(2)}) copy-start(s32[32]{0:T(128)} %branches.5) | copy-start | bytes 388
  1.2 7.1 %copy-start.2 = (bf16[256,256]{1,0:T(8,128)(2,1)S(1)}, bf16[256,256]{1,0:T(8,128)(2,1)}, u32[]{:S(2)}) copy-start(bf16[256,256]{1,0:T(8,128)(2,1)} %trial) | copy-start | bytes 393220
  1.2 7.1 %copy-start.3 = (f32[8,256]{1,0:T(8,128)S(1)}, f32[8,256]{1,0:T(8,128)}, u32[]{:S(2)}) copy-start(f32[8,256]{1,0:T(8,128)} %field.1) | copy-start | bytes 24580
  2.2 12.6 %collective-permute-start.4 = (bf16[192,1024]{1,0:T(8,128)(2,1)S(1)}, bf16[192,1024]{1,0:T(8,128)(2,1)S(1)}, u32[]{:S(2)}, u32[]{:S(2)}) collective-permute-start(bf16[192,1024]{1,0:T(8,128)(2,1)S(1)} %constant_dynamic-slice_fusion), channel_id=1, source_target_pairs={{0,2},{1,3},{2,0},{3,1},{4,6},{5,7},{6,4},{7,5},{8,10},{9,11},{10,... | collective-permute-start | bytes 1179656 | tf_op jit(solution)/shard_map/ppermute | solution.py:362
  4.8 1.2 %copy-start = (bf16[8,256,256]{2,1,0:T(8,128)(2,1)S(1)}, bf16[8,256,256]{2,1,0:T(8,128)(2,1)}, u32[]{:S(2)}) copy-start(bf16[8,256,256]{2,1,0:T(8,128)(2,1)} %walkers.1) | copy-start | bytes 3145732
  6.0 15.3 %copy-start.1 = (bf16[2,256,1024]{2,1,0:T(8,128)(2,1)S(1)}, bf16[2,256,1024]{2,1,0:T(8,128)(2,1)}, u32[]{:S(2)}) copy-start(bf16[2,256,1024]{2,1,0:T(8,128)(2,1)} %param.8) | copy-start | bytes 3145732
  8.3 9.7 %collective-permute-start.1 = (bf16[288,256]{1,0:T(8,128)(2,1)S(1)}, bf16[288,256]{1,0:T(8,128)(2,1)S(1)}, u32[]{:S(2)}, u32[]{:S(2)}) collective-permute-start(bf16[288,256]{1,0:T(8,128)(2,1)S(1)} %message.1.refs_0_), channel_id=1, source_target_pairs={{0,2},{1,3},{2,0},{3,1},{4,6},{5,7},{6,4},{7,5},{8,10},{9,11},{10,... | collective-permute-start | bytes 442376 | tf_op jit(solution)/shard_map/ppermute | solution.py:362
  8.4 14.4 %collective-permute-start.7 = (bf16[2,256,256]{2,1,0:T(8,128)(2,1)S(1)}, bf16[2,256,256]{2,1,0:T(8,128)(2,1)S(1)}, u32[]{:S(2)}, u32[]{:S(2)}) collective-permute-start(bf16[2,256,256]{2,1,0:T(8,128)(2,1)S(1)} %get-tuple-element.31), channel_id=1, source_target_pairs={{0,1},{1,0},{2,3},{3,2},{4,5},{5,4},{6,7},{7,6},{8,9},{9,8},{10,11... | collective-permute-start | bytes 786440 | tf_op jit(solution)/shard_map/ppermute | solution.py:362
  8.6 15.0 %collective-permute-start.8 = (bf16[2,256,256]{2,1,0:T(8,128)(2,1)S(1)}, bf16[2,256,256]{2,1,0:T(8,128)(2,1)S(1)}, u32[]{:S(2)}, u32[]{:S(2)}) collective-permute-start(bf16[2,256,256]{2,1,0:T(8,128)(2,1)S(1)} %get-tuple-element.33), channel_id=1, source_target_pairs={{0,2},{1,3},{2,0},{3,1},{4,6},{5,7},{6,4},{7,5},{8,10},{9,11},{10,... | collective-permute-start | bytes 786440 | tf_op jit(solution)/shard_map/ppermute | solution.py:362
  10.4 7.6 %collective-permute-start = (bf16[288,256]{1,0:T(8,128)(2,1)S(1)}, bf16[288,256]{1,0:T(8,128)(2,1)S(1)}, u32[]{:S(2)}, u32[]{:S(2)}) collective-permute-start(bf16[288,256]{1,0:T(8,128)(2,1)S(1)} %message.1.refs_0_), channel_id=1, source_target_pairs={{0,1},{1,0},{2,3},{3,2},{4,5},{5,4},{6,7},{7,6},{8,9},{9,8},{10,11... | collective-permute-start | bytes 442376 | tf_op jit(solution)/shard_map/ppermute | solution.py:362
  14.8 19.7 %collective-permute-start.12 = (bf16[192,1024]{1,0:T(8,128)(2,1)S(1)}, bf16[192,1024]{1,0:T(8,128)(2,1)S(1)}, u32[]{:S(2)}, u32[]{:S(2)}) collective-permute-start(bf16[192,1024]{1,0:T(8,128)(2,1)S(1)} %collective-permute-done.4.refs_0_), channel_id=1, source_target_pairs={{0,4},{4,0},{8,12},{12,8},{1,5},{5,1},{9,13},{13,9},{2,6},{6,2},{1... | collective-permute-start | bytes 1179656 | tf_op jit(solution)/shard_map/ppermute | solution.py:363
  17.9 2.1 %collective-permute-start.2 = (bf16[288,256]{1,0:T(8,128)(2,1)S(1)}, bf16[288,256]{1,0:T(8,128)(2,1)S(1)}, u32[]{:S(2)}, u32[]{:S(2)}) collective-permute-start(bf16[288,256]{1,0:T(8,128)(2,1)S(1)} %collective-permute-done.1.refs_2_), channel_id=1, source_target_pairs={{0,1},{1,0},{2,3},{3,2},{4,5},{5,4},{6,7},{7,6},{8,9},{9,8},{10,11... | collective-permute-start | bytes 442376 | tf_op jit(solution)/shard_map/ppermute | solution.py:362
  18.0 11.4 %collective-permute-start.5 = (bf16[2,256,256]{2,1,0:T(8,128)(2,1)S(1)}, bf16[2,256,256]{2,1,0:T(8,128)(2,1)S(1)}, u32[]{:S(2)}, u32[]{:S(2)}) collective-permute-start(bf16[2,256,256]{2,1,0:T(8,128)(2,1)S(1)} %get-tuple-element.28), channel_id=1, source_target_pairs={{0,3},{1,2},{2,1},{3,0},{4,7},{5,6},{6,5},{7,4},{8,11},{9,10},{10,... | collective-permute-start | bytes 786440 | tf_op jit(solution)/shard_map/ppermute | solution.py:362
  20.6 2.2 %collective-permute-start.6 = (f32[4,2,256]{2,1,0:T(2,128)S(1)}, f32[4,2,256]{2,1,0:T(2,128)S(1)}, u32[]{:S(2)}, u32[]{:S(2)}) collective-permute-start(f32[4,2,256]{2,1,0:T(2,128)S(1)} %fields.1), channel_id=1, source_target_pairs={{0,0},{1,5},{2,10},{3,15},{4,4},{5,1},{6,14},{7,11},{8,8},{9,13},{... | collective-permute-start | bytes 24584 | tf_op jit(solution)/shard_map/ppermute | solution.py:364
  24.4 12.1 %collective-permute-start.9 = (bf16[128,1024]{1,0:T(8,128)(2,1)S(1)}, bf16[128,1024]{1,0:T(8,128)(2,1)S(1)}, u32[]{:S(2)}, u32[]{:S(2)}) collective-permute-start(bf16[128,1024]{1,0:T(8,128)(2,1)S(1)} %slice.4), channel_id=1, source_target_pairs={{0,2},{1,3},{2,0},{3,1},{4,6},{5,7},{6,4},{7,5},{8,10},{9,11},{10,... | collective-permute-start | bytes 786440 | tf_op jit(solution)/shard_map/ppermute | solution.py:362
  29.2 7.5 %collective-permute-start.11 = (bf16[192,1024]{1,0:T(8,128)(2,1)S(1)}, bf16[192,1024]{1,0:T(8,128)(2,1)S(1)}, u32[]{:S(2)}, u32[]{:S(2)}) collective-permute-start(bf16[192,1024]{1,0:T(8,128)(2,1)S(1)} %collective-permute-done.4.refs_0_), channel_id=1, source_target_pairs={{0,1},{1,0},{2,3},{3,2},{4,5},{5,4},{6,7},{7,6},{8,9},{9,8},{10,11... | collective-permute-start | bytes 1179656 | tf_op jit(solution)/shard_map/ppermute | solution.py:362
  34.5 2.2 %collective-permute-start.13 = (bf16[192,1024]{1,0:T(8,128)(2,1)S(1)}, bf16[192,1024]{1,0:T(8,128)(2,1)S(1)}, u32[]{:S(2)}, u32[]{:S(2)}) collective-permute-start(bf16[192,1024]{1,0:T(8,128)(2,1)S(1)} %collective-permute-done.12.refs_2_), channel_id=1, source_target_pairs={{0,1},{1,0},{2,3},{3,2},{4,5},{5,4},{6,7},{7,6},{8,9},{9,8},{10,11... | collective-permute-start | bytes 1179656 | tf_op jit(solution)/shard_map/ppermute | solution.py:362
  36.5 1.6 %collective-permute-start.10 = (bf16[128,1024]{1,0:T(8,128)(2,1)S(1)}, bf16[128,1024]{1,0:T(8,128)(2,1)S(1)}, u32[]{:S(2)}, u32[]{:S(2)}) collective-permute-start(bf16[128,1024]{1,0:T(8,128)(2,1)S(1)} %collective-permute-done.9.refs_0_), channel_id=1, source_target_pairs={{0,1},{1,0},{2,3},{3,2},{4,5},{5,4},{6,7},{7,6},{8,9},{9,8},{10,11... | collective-permute-start | bytes 786440 | tf_op jit(solution)/shard_map/ppermute | solution.py:362
  38.8 5.8 %collective-permute-start.14 = (f32[2,8,128]{2,1,0:T(8,128)S(1)}, f32[2,8,128]{2,1,0:T(8,128)S(1)}, u32[]{:S(2)}, u32[]{:S(2)}) collective-permute-start(f32[2,8,128]{2,1,0:T(8,128)S(1)} %contract.3), channel_id=1, source_target_pairs={{0,0},{1,5},{2,10},{3,15},{4,4},{5,1},{6,14},{7,11},{8,8},{9,13},{... | collective-permute-start | bytes 24584 | tf_op jit(solution)/shard_map/ppermute | solution.py:365
  39.5 6.6 %collective-permute-start.16 = (f32[2,8,128]{2,1,0:T(8,128)S(1)}, f32[2,8,128]{2,1,0:T(8,128)S(1)}, u32[]{:S(2)}, u32[]{:S(2)}) collective-permute-start(f32[2,8,128]{2,1,0:T(8,128)S(1)} %contract.5), channel_id=1, source_target_pairs={{0,2},{1,7},{2,8},{3,13},{4,6},{5,3},{6,12},{7,9},{8,10},{9,15},{1... | collective-permute-start | bytes 24584 | tf_op jit(solution)/shard_map/ppermute | solution.py:365
  44.6 3.1 %collective-permute-start.15 = (f32[2,8,128]{2,1,0:T(8,128)S(1)}, f32[2,8,128]{2,1,0:T(8,128)S(1)}, u32[]{:S(2)}, u32[]{:S(2)}) collective-permute-start(f32[2,8,128]{2,1,0:T(8,128)S(1)} %collective-permute-done.14.refs_0_), channel_id=1, source_target_pairs={{0,1},{1,0},{2,3},{3,2},{4,5},{5,4},{6,7},{7,6},{8,9},{9,8},{10,11... | collective-permute-start | bytes 24584 | tf_op jit(solution)/shard_map/ppermute | solution.py:362
  46.1 2.4 %collective-permute-start.17 = (f32[2,8,128]{2,1,0:T(8,128)S(1)}, f32[2,8,128]{2,1,0:T(8,128)S(1)}, u32[]{:S(2)}, u32[]{:S(2)}) collective-permute-start(f32[2,8,128]{2,1,0:T(8,128)S(1)} %collective-permute-done.16.refs_2_), channel_id=1, source_target_pairs={{0,1},{1,0},{2,3},{3,2},{4,5},{5,4},{6,7},{7,6},{8,9},{9,8},{10,11... | collective-permute-start | bytes 24584 | tf_op jit(solution)/shard_map/ppermute | solution.py:362

commit v11 on v10

--- a/solution.py
+++ b/solution.py
@@ -302,19 +302,20 @@
 
 def direct_kernel(share, count, *refs):
     uppers, green, kept = refs[:count], refs[count], refs[count + 1 : 2 * count + 1]
-    before, outs = refs[-2:]
+    before, near, outs, near_out = refs[-4:]
+    near_out[...] = near[...]
     for v in range(count):
         outs[v] = report(share, before[v], 0, dot(uppers[v][...], green[...]), kept[v][...])
 
 
-def contract(kernel, count, vectors, green, *more, kept_rows=0, scratch_rows=0):
+def contract(kernel, count, vectors, green, *more, kept_rows=0, scratch_rows=0, outs=1):
     wide = green.shape[1]
     kept = [jax.ShapeDtypeStruct((kept_rows, wide), F32)] * count if kept_rows else []
     return pl.pallas_call(
         kernel,
-        out_shape=[jax.ShapeDtypeStruct((count, 8, 128), F32)] + kept,
+        out_shape=[jax.ShapeDtypeStruct((count, 8, 128), F32)] * outs + kept,
         in_specs=[whole()] * (len(vectors) + 1 + len(more)),
-        out_specs=[whole()] * (1 + len(kept)),
+        out_specs=[whole()] * (outs + len(kept)),
         scratch_shapes=[pltpu.VMEM((scratch_rows, wide), F32)] if scratch_rows else [],
         compiler_params=pltpu.CompilerParams(vmem_limit_bytes=VMEM_LIMIT),
         cost_estimate=pl.CostEstimate(
@@ -326,8 +327,8 @@
     )(*vectors, green, *more)
 
 
-def unpack_kernel(n, share, masks, *refs):
-    arrived, outs = refs[:n], refs[n:]
+def unpack_kernel(n, share, order, masks, *refs):
+    arrived, outs = dict(zip(order, refs)), refs[n:]
     vectors, per = outs[0].shape
     for which, out in enumerate(outs):
         for g in range(vectors):
@@ -341,9 +342,9 @@
             out[g : g + 1, :] = line[:, :per]
 
 
-def unpack(n, per, share, vectors, masks, arrived):
-    return pl.pallas_call(
-        functools.partial(unpack_kernel, n, share),
+def unpack(n, per, share, vectors, order, masks, arrived):
+    return pl.pallas_call(
+        functools.partial(unpack_kernel, n, share, order),
         out_shape=[jax.ShapeDtypeStruct((vectors, per), F32)] * 2,
         in_specs=[whole()] * (1 + n),
         out_specs=[whole()] * 2,
@@ -413,12 +414,13 @@
         kept_rows=direct_rows,
         scratch_rows=2 * shared_rows,
     )
-    [late] = contract(
-        functools.partial(direct_kernel, share, len(far)), len(far), [direct[k] for k in far], green, *kept, late
+    late, results = contract(
+        functools.partial(direct_kernel, share, len(far)), len(far), [direct[k] for k in far], green, *kept, late,
+        results, outs=2,
     )
-    answers = [answer(late, far[0]), answer(ordered(results, late), 0)]
-    arrived = [[x] + [move(x, k) for k in near[1:]] for x in reversed(answers)]
-    return tuple(x.T for x in unpack(n, per, share, vectors, masks, [x for held in arrived for x in held]))
+    answers = [answer(late, far[0]), answer(results, 0)]
+    arrived = [[x] + [move(x, k) for k in near[1:]] for x in answers]
+    return tuple(x.T for x in unpack(n, per, share, vectors, far + near, masks, [x for held in arrived for x in held]))
 
 
 def newton_schulz(intersection):
@@ -481,7 +483,7 @@
 def on_device(walkers, trial_orbitals, cholesky, branches, counts, field):
     walk_size, shard_count = lax.axis_size("walk"), lax.axis_size(SR)
     per = walkers.shape[0]
-    if walk_size == shard_count and lax.axis_size("slab") == 2 and per % walk_size == 0 and not walk_size & (walk_size - 1):
+    if walk_size == shard_count and lax.axis_size("slab") == lax.axis_size("row") == 2 and per % walk_size == 0 and not walk_size & (walk_size - 1):
         if cholesky.shape[0] * (per // walk_size) <= 4 and cholesky.shape[1] % 64 == 0 and per <= 128:
             return at_the_source(walkers, trial_orbitals, cholesky, branches, counts, field)
     return at_the_target(walkers, trial_orbitals, cholesky, branches, counts, field)

time: 49.3 us -> 49.5 us (level)
  the two profiles are of different devices: /device:TPU:0 before, /device:TPU:3 now
where the time goes in v11:
time: 49.5 us; the launch traced here: 49.2 us
  starting transfers between devices  17.9 us (36%)
  waiting for transfers between devices  13.9 us (28%)
  Pallas kernels  13.7 us (28%)
  local copies, waits for them, and re-layouts  2.31 us (5%)
  between operations  1.5 us (3%)
    ppermute x14, waiting for transfers between devices, at_the_source(): move = lambda x, k: lax.ppermute(x, SR, [(i, i ^ k) for i in range(n)])  9.63 us
    ppermute x14, starting transfers between devices, at_the_source(): move = lambda x, k: lax.ppermute(x, SR, [(i, i ^ k) for i in range(n)])  5.9 us
    ppermute x2, starting transfers between devices, at_the_source(): lax.ppermute(x, ALL, [(w * n + q, (w ^ q) * n + (q ^ k)) for w, q in pairs])  5.43 us
    ppermute x1, starting transfers between devices, at_the_source(): lax.ppermute(x, ALL, [(w * n + q, (w ^ q) * n + q) for w, q in pairs])  5.23 us
    pallas_call x1, Pallas kernels, make_green(): pl.pallas_call(functools.partial(green_kernel, n, share), out_shape=jax.S...  5.13 us
    ppermute x2, waiting for transfers between devices, at_the_source(): lax.ppermute(x, ALL, [(w * n + q, (w ^ q) * n + (q ^ k)) for w, q in pairs])  4.22 us
    pallas_call x3, Pallas kernels, contract(): pl.pallas_call(kernel, out_shape=[jax.ShapeDtypeStruct((count, 8, 128), F...  3.63 us
    pallas_call x1, Pallas kernels, select(): pl.pallas_call(functools.partial(select_kernel, n, per, share), out_shape...  2.17 us
  transfers between devices with their start and end apart: 18, of which 6 were waited for; matrix products, arithmetic and copies ran while one was open for 2% of the time, Pallas kernels for 25%

profile of v11, /device:TPU:3, one launch (start us, length us, event | category | flops | bytes accessed | tf_op | source)
XLA Modules:
  0.0 49.2 jit_solution(7403324151986147544)
XLA Ops:
  0.6 0.7 %collective-permute-start.3 = (bf16[512,1024]{1,0:T(8,128)(2,1)}, bf16[512,1024]{1,0:T(8,128)(2,1)S(1)}, u32[]{:S(2)}, u32[]{:S(2)}) collective-permute-start(bf16[512,1024]{1,0:T(8,128)(2,1)} %bitcast.3), channel_id=1, source_target_pairs={{0,1},{1,0},{2,3},{3,2},{4,5},{5,4},{6,7},{7,6},{8,9},{9,8},{10,11... | collective-permute-start | bytes 3145736 | tf_op jit(solution)/shard_map/ppermute | solution.py:363
  1.4 0.0 copy-start.4
  1.4 0.0 copy-start.2
  1.4 0.0 copy-start.3
  1.4 1.1 %constant_dynamic-slice_fusion = bf16[192,1024]{1,0:T(8,128)(2,1)S(1)} fusion(bf16[512,1024]{1,0:T(8,128)(2,1)} %bitcast.4, s32[]{:T(128)S(6)} %select_n.3), kind=kLoop, calls=%fused_computation | loop fusion | bytes 786436 | tf_op jit(solution)/shard_map/dynamic_slice | solution.py:387
  2.4 0.1 collective-permute-start.8
  2.5 0.0 copy-done.4
  2.5 0.0 copy-start
  2.5 1.2 %copy-done = bf16[8,256,256]{2,1,0:T(8,128)(2,1)S(1)} copy-done((bf16[8,256,256]{2,1,0:T(8,128)(2,1)S(1)}, bf16[8,256,256]{2,1,0:T(8,128)(2,1)}, u32[]{:S(2)}) %copy-start) | copy-done | bytes 1048600
  3.8 0.0 copy-start.1
  3.8 2.2 %select.1 = (bf16[2,256,256]{2,1,0:T(8,128)(2,1)S(1)}, bf16[2,256,256]{2,1,0:T(8,128)(2,1)S(1)}, bf16[2,256,256]{2,1,0:T(8,128)(2,1)S(1)}, bf16[2,256,256]{2,1,0:T(8,128)(2,1)S(1)}) custom-call(s32[32]{0:T(128)S(1)} %copy-done.4, bf16[8,256,256]{2,1,0:T(8,128)(2,1)S(1)} %copy-done), custom_call_target="tpu_custom_call" | custom-call | tf_op jit(solution)/shard_map/select/pallas_call | solution.py:69
  5.9 0.0 copy-done.2
  5.9 0.0 copy-done.3
  6.0 1.5 %collective-permute-start.1 = (bf16[288,256]{1,0:T(8,128)(2,1)S(1)}, bf16[288,256]{1,0:T(8,128)(2,1)S(1)}, u32[]{:S(2)}, u32[]{:S(2)}) collective-permute-start(bf16[288,256]{1,0:T(8,128)(2,1)S(1)} %message.1.refs_0_), channel_id=1, source_target_pairs={{0,2},{1,3},{2,0},{3,1},{4,6},{5,7},{6,4},{7,5},{8,10},{9,11},{10,... | collective-permute-start | bytes 442376 | tf_op jit(solution)/shard_map/ppermute | solution.py:363
  7.5 0.0 collective-permute-done.3.refs_1_
  7.5 0.6 %collective-permute-start.4 = (bf16[2,256,256]{2,1,0:T(8,128)(2,1)S(1)}, bf16[2,256,256]{2,1,0:T(8,128)(2,1)S(1)}, u32[]{:S(2)}, u32[]{:S(2)}) collective-permute-start(bf16[2,256,256]{2,1,0:T(8,128)(2,1)S(1)} %get-tuple-element.29), channel_id=1, source_target_pairs={{0,1},{1,0},{2,3},{3,2},{4,5},{5,4},{6,7},{7,6},{8,9},{9,8},{10,11... | collective-permute-start | bytes 786440 | tf_op jit(solution)/shard_map/ppermute | solution.py:363
  8.1 0.0 collective-permute-start.5
  8.1 0.3 collective-permute-start
  8.4 4.8 %collective-permute-done.8.refs_0_ = bf16[192,1024]{1,0:T(8,128)(2,1)S(1)} collective-permute-done((bf16[192,1024]{1,0:T(8,128)(2,1)S(1)}, bf16[192,1024]{1,0:T(8,128)(2,1)S(1)}, u32[]{:S(2)}, u32[]{:S(2)}) %collective-permute-start.8) | collective-permute-done | bytes 393248 | tf_op jit(solution)/shard_map/ppermute | solution.py:363
  13.2 1.3 %collective-permute-start.12 = (bf16[192,1024]{1,0:T(8,128)(2,1)S(1)}, bf16[192,1024]{1,0:T(8,128)(2,1)S(1)}, u32[]{:S(2)}, u32[]{:S(2)}) collective-permute-start(bf16[192,1024]{1,0:T(8,128)(2,1)S(1)} %collective-permute-done.8.refs_0_), channel_id=1, source_target_pairs={{0,4},{4,0},{8,12},{12,8},{1,5},{5,1},{9,13},{13,9},{2,6},{6,2},{1... | collective-permute-start | bytes 1179656 | tf_op jit(solution)/shard_map/ppermute | solution.py:364
  14.5 1.9 %collective-permute-done.1.refs_2_ = bf16[288,256]{1,0:T(8,128)(2,1)S(1)} collective-permute-done((bf16[288,256]{1,0:T(8,128)(2,1)S(1)}, bf16[288,256]{1,0:T(8,128)(2,1)S(1)}, u32[]{:S(2)}, u32[]{:S(2)}) %collective-permute-start.1) | collective-permute-done | bytes 147488 | tf_op jit(solution)/shard_map/ppermute | solution.py:363
  16.4 1.3 %collective-permute-start.2 = (bf16[288,256]{1,0:T(8,128)(2,1)S(1)}, bf16[288,256]{1,0:T(8,128)(2,1)S(1)}, u32[]{:S(2)}, u32[]{:S(2)}) collective-permute-start(bf16[288,256]{1,0:T(8,128)(2,1)S(1)} %collective-permute-done.1.refs_2_), channel_id=1, source_target_pairs={{0,1},{1,0},{2,3},{3,2},{4,5},{5,4},{6,7},{7,6},{8,9},{9,8},{10,11... | collective-permute-start | bytes 442376 | tf_op jit(solution)/shard_map/ppermute | solution.py:363
  17.6 0.0 collective-permute-done.refs_1_
  17.6 0.0 collective-permute-start.9
  17.6 1.0 %collective-permute-done.2.refs_3_ = bf16[288,256]{1,0:T(8,128)(2,1)S(1)} collective-permute-done((bf16[288,256]{1,0:T(8,128)(2,1)S(1)}, bf16[288,256]{1,0:T(8,128)(2,1)S(1)}, u32[]{:S(2)}, u32[]{:S(2)}) %collective-permute-start.2) | collective-permute-done | bytes 147488 | tf_op jit(solution)/shard_map/ppermute | solution.py:363
  18.6 0.6 %fields.1 = f32[4,2,256]{2,1,0:T(2,128)S(1)} custom-call(s32[32]{0:T(128)S(1)} %copy-done.4, bf16[288,256]{1,0:T(8,128)(2,1)S(1)} %message.1.refs_0_, bf16[288,256]{1,0:T(8,128)(2,1)S(1)} %collective-permute-done.refs_1_, bf16[288,256]{1,0:T(8,128)(2,1)S(1)} %collective-permute-done.1.refs_2_, bf16[288,256]{1,0:T(8,128)(2,1)S(1)} %collective-permute-done.2.refs_3_), custom_call_target="tpu_custom_call" | custom-call | tf_op jit(solution)/shard_map/fields/pallas_call | solution.py:119
  19.3 5.2 %collective-permute-start.6 = (f32[4,2,256]{2,1,0:T(2,128)S(1)}, f32[4,2,256]{2,1,0:T(2,128)S(1)}, u32[]{:S(2)}, u32[]{:S(2)}) collective-permute-start(f32[4,2,256]{2,1,0:T(2,128)S(1)} %fields.1), channel_id=1, source_target_pairs={{0,0},{1,5},{2,10},{3,15},{4,4},{5,1},{6,14},{7,11},{8,8},{9,13},{... | collective-permute-start | bytes 24584 | tf_op jit(solution)/shard_map/ppermute | solution.py:365
  24.5 0.0 copy-done.1
  25.2 0.8 %turn.1 = (bf16[256,1024]{1,0:T(8,128)(2,1)S(1)}, f32[8,128]{1,0:T(8,128)S(1)}) custom-call(s32[32]{0:T(128)S(1)} %copy-done.4, s32[1]{0:T(128)S(6)} %copy.8.counts, bf16[288,256]{1,0:T(8,128)(2,1)S(1)} %message.1.refs_0_, bf16[288,256]{1,0:T(8,128)(2,1)S(1)} %collective-permute-done.refs_1_, bf16[288,256]{1,0:T(8,128)(2,1)S(1)} %collective-permute-done.1.refs_2_, ...), custom_call_target="tpu_custom_call" | custom-call | tf_op jit(solution)/shard_map/turn/pallas_call | solution.py:146
  26.0 0.0 collective-permute-done.6.refs_4_.refs_2_
  26.0 0.0 collective-permute-done.4.refs_1_
  26.0 0.0 collective-permute-done.5.refs_2_
  26.0 0.8 %first.1 = (bf16[768,512]{1,0:T(8,128)(2,1)S(1)}, f32[256,512]{1,0:T(8,128)S(1)}) custom-call(bf16[2,256,256]{2,1,0:T(8,128)(2,1)S(1)} %get-tuple-element.25.refs_0_, bf16[2,256,256]{2,1,0:T(8,128)(2,1)S(1)} %collective-permute-done.4.refs_1_, bf16[2,256,256]{2,1,0:T(8,128)(2,1)S(1)} %collective-permute-done.5.refs_2_, ...), custom_call_target="tpu_custom_call" | custom-call | flops 1073741824 | bytes 1048576 | tf_op jit(solution)/shard_map/first/pallas_call | solution.py:187
  26.8 0.1 collective-permute-start.7
  26.9 0.1 collective-permute-start.11
  27.0 0.7 %collective-permute-done.9.refs_0_ = bf16[2,256,256]{2,1,0:T(8,128)(2,1)S(1)} collective-permute-done((bf16[2,256,256]{2,1,0:T(8,128)(2,1)S(1)}, bf16[2,256,256]{2,1,0:T(8,128)(2,1)S(1)}, u32[]{:S(2)}, u32[]{:S(2)}) %collective-permute-start.9) | collective-permute-done | bytes 262176 | tf_op jit(solution)/shard_map/ppermute | solution.py:363
  27.7 5.1 %green.1.refs_2_.refs_4_ = bf16[1024,512]{1,0:T(8,128)(2,1)S(1)} custom-call(bf16[2,256,256]{2,1,0:T(8,128)(2,1)S(1)} %collective-permute-done.9.refs_0_, bf16[256,1024]{1,0:T(8,128)(2,1)S(1)} %get-tuple-element.32.refs_3_.refs_1_, f32[4,2,256]{2,1,0:T(2,128)S(1)} %collective-permute-done.6.refs_4_.refs_2_, bf16[768,512]{1,0:T(8,128)(2,1)S(1)} %get-tuple-element.37.refs_3_, ...), custom_call_target="tpu_custom_call" | custom-call | tf_op jit(solution)/shard_map/green/pallas_call | solution.py:245
  32.9 0.0 collective-permute-done.12.refs_2_
  32.9 0.3 collective-permute-start.13
  33.2 1.5 %contract.3.refs_6_ = f32[2,8,128]{2,1,0:T(8,128)S(1)} custom-call(bf16[512,1024]{1,0:T(8,128)(2,1)S(1)} %bitcast.6, bf16[512,1024]{1,0:T(8,128)(2,1)S(1)} %collective-permute-done.3.refs_1_, bf16[1024,512]{1,0:T(8,128)(2,1)S(1)} %green.1.refs_2_.refs_4_), custom_call_target="tpu_custom_call" | custom-call | flops 1073741824 | bytes 3145728 | tf_op jit(solution)/shard_map/contract/pallas_call | solution.py:314
  34.7 0.0 collective-permute-done.7.refs_0_
  34.8 0.8 %collective-permute-start.10 = (bf16[128,1024]{1,0:T(8,128)(2,1)S(1)}, bf16[128,1024]{1,0:T(8,128)(2,1)S(1)}, u32[]{:S(2)}, u32[]{:S(2)}) collective-permute-start(bf16[128,1024]{1,0:T(8,128)(2,1)S(1)} %collective-permute-done.7.refs_0_), channel_id=1, source_target_pairs={{0,1},{1,0},{2,3},{3,2},{4,5},{5,4},{6,7},{7,6},{8,9},{9,8},{10,11... | collective-permute-start | bytes 786440 | tf_op jit(solution)/shard_map/ppermute | solution.py:363
  35.6 0.0 collective-permute-done.11.refs_1_
  35.6 0.0 collective-permute-done.13.refs_3_
  35.6 1.4 %contract.4 = (f32[2,8,128]{2,1,0:T(8,128)S(1)}, f32[128,512]{1,0:T(8,128)S(1)}, f32[128,512]{1,0:T(8,128)S(1)}) custom-call(bf16[192,1024]{1,0:T(8,128)(2,1)S(1)} %collective-permute-done.8.refs_0_, bf16[192,1024]{1,0:T(8,128)(2,1)S(1)} %collective-permute-done.11.refs_1_, bf16[192,1024]{1,0:T(8,128)(2,1)S(1)} %collective-permute-done.12.refs_2_, ...), custom_call_target="tpu_custom_call" | custom-call | flops 805306368 | bytes 2621440 | tf_op jit(solution)/shard_map/contract/pallas_call | solution.py:314
  37.0 0.0 collective-permute-done.10.refs_1_
  37.0 0.7 %contract.5 = (f32[2,8,128]{2,1,0:T(8,128)S(1)}, f32[2,8,128]{2,1,0:T(8,128)S(1)}) custom-call(bf16[128,1024]{1,0:T(8,128)(2,1)S(1)} %collective-permute-done.7.refs_0_, bf16[128,1024]{1,0:T(8,128)(2,1)S(1)} %collective-permute-done.10.refs_1_, bf16[1024,512]{1,0:T(8,128)(2,1)S(1)} %green.1.refs_2_.refs_4_, f32[128,512]{1,0:T(8,128)S(1)} %get-tuple-element.41.refs_3_, ...), custom_call_target="tpu_custom_call" | custom-call | flops 268435456 | bytes 1572864 | tf_op jit(solution)/shard_map/contract/pallas_call | solution.py:314
  37.7 3.5 %collective-permute-start.14 = (f32[2,8,128]{2,1,0:T(8,128)S(1)}, f32[2,8,128]{2,1,0:T(8,128)S(1)}, u32[]{:S(2)}, u32[]{:S(2)}) collective-permute-start(f32[2,8,128]{2,1,0:T(8,128)S(1)} %get-tuple-element.44), channel_id=1, source_target_pairs={{0,2},{1,7},{2,8},{3,13},{4,6},{5,3},{6,12},{7,9},{8,10},{9,15},{1... | collective-permute-start | bytes 24584 | tf_op jit(solution)/shard_map/ppermute | solution.py:366
  41.3 1.9 %collective-permute-start.16 = (f32[2,8,128]{2,1,0:T(8,128)S(1)}, f32[2,8,128]{2,1,0:T(8,128)S(1)}, u32[]{:S(2)}, u32[]{:S(2)}) collective-permute-start(f32[2,8,128]{2,1,0:T(8,128)S(1)} %get-tuple-element.45), channel_id=1, source_target_pairs={{0,0},{1,5},{2,10},{3,15},{4,4},{5,1},{6,14},{7,11},{8,8},{9,13},{... | collective-permute-start | bytes 24584 | tf_op jit(solution)/shard_map/ppermute | solution.py:366
  43.2 0.0 collective-permute-done.14.refs_0_
  43.2 0.1 collective-permute-start.15
  43.3 4.2 %collective-permute-done.16.refs_2_ = f32[2,8,128]{2,1,0:T(8,128)S(1)} collective-permute-done((f32[2,8,128]{2,1,0:T(8,128)S(1)}, f32[2,8,128]{2,1,0:T(8,128)S(1)}, u32[]{:S(2)}, u32[]{:S(2)}) %collective-permute-start.16) | collective-permute-done | bytes 8224 | tf_op jit(solution)/shard_map/ppermute | solution.py:366
  47.5 0.0 collective-permute-start.17
  47.5 0.0 collective-permute-done.15.refs_1_
  47.5 1.2 %collective-permute-done.17.refs_3_ = f32[2,8,128]{2,1,0:T(8,128)S(1)} collective-permute-done((f32[2,8,128]{2,1,0:T(8,128)S(1)}, f32[2,8,128]{2,1,0:T(8,128)S(1)}, u32[]{:S(2)}, u32[]{:S(2)}) %collective-permute-start.17) | collective-permute-done | bytes 8224 | tf_op jit(solution)/shard_map/ppermute | solution.py:363
  48.7 0.6 %unpack.1 = (f32[2,8]{1,0:T(2,128)}, f32[2,8]{1,0:T(2,128)}) custom-call(f32[8,128]{1,0:T(8,128)S(1)} %get-tuple-element.27.masks, f32[2,8,128]{2,1,0:T(8,128)S(1)} %collective-permute-done.14.refs_0_, f32[2,8,128]{2,1,0:T(8,128)S(1)} %collective-permute-done.15.refs_1_, f32[2,8,128]{2,1,0:T(8,128)S(1)} %collective-permute-done.16.refs_2_, ...), custom_call_target="tpu_custom_call" | custom-call | tf_op jit(solution)/shard_map/unpack/pallas_call | solution.py:346
  (2 shorter events, 0.0 us)
Async XLA Ops:
  0.6 6.9 %collective-permute-start.3 = (bf16[512,1024]{1,0:T(8,128)(2,1)}, bf16[512,1024]{1,0:T(8,128)(2,1)S(1)}, u32[]{:S(2)}, u32[]{:S(2)}) collective-permute-start(bf16[512,1024]{1,0:T(8,128)(2,1)} %bitcast.3), channel_id=1, source_target_pairs={{0,1},{1,0},{2,3},{3,2},{4,5},{5,4},{6,7},{7,6},{8,9},{9,8},{10,11... | collective-permute-start | bytes 3145736 | tf_op jit(solution)/shard_map/ppermute | solution.py:363
  1.4 1.1 %copy-start.4 = (s32[32]{0:T(128)S(1)}, s32[32]{0:T(128)}, u32[]{:S(2)}) copy-start(s32[32]{0:T(128)} %branches.5) | copy-start | bytes 388
  1.4 4.6 %copy-start.2 = (bf16[256,256]{1,0:T(8,128)(2,1)S(1)}, bf16[256,256]{1,0:T(8,128)(2,1)}, u32[]{:S(2)}) copy-start(bf16[256,256]{1,0:T(8,128)(2,1)} %trial) | copy-start | bytes 393220
  1.4 4.6 %copy-start.3 = (f32[8,256]{1,0:T(8,128)S(1)}, f32[8,256]{1,0:T(8,128)}, u32[]{:S(2)}) copy-start(f32[8,256]{1,0:T(8,128)} %field.1) | copy-start | bytes 24580
  2.4 10.8 %collective-permute-start.8 = (bf16[192,1024]{1,0:T(8,128)(2,1)S(1)}, bf16[192,1024]{1,0:T(8,128)(2,1)S(1)}, u32[]{:S(2)}, u32[]{:S(2)}) collective-permute-start(bf16[192,1024]{1,0:T(8,128)(2,1)S(1)} %constant_dynamic-slice_fusion), channel_id=1, source_target_pairs={{0,2},{1,3},{2,0},{3,1},{4,6},{5,7},{6,4},{7,5},{8,10},{9,11},{10,... | collective-permute-start | bytes 1179656 | tf_op jit(solution)/shard_map/ppermute | solution.py:363
  2.5 1.2 %copy-start = (bf16[8,256,256]{2,1,0:T(8,128)(2,1)S(1)}, bf16[8,256,256]{2,1,0:T(8,128)(2,1)}, u32[]{:S(2)}) copy-start(bf16[8,256,256]{2,1,0:T(8,128)(2,1)} %walkers.1) | copy-start | bytes 3145732
  3.8 20.7 %copy-start.1 = (bf16[2,256,1024]{2,1,0:T(8,128)(2,1)S(1)}, bf16[2,256,1024]{2,1,0:T(8,128)(2,1)}, u32[]{:S(2)}) copy-start(bf16[2,256,1024]{2,1,0:T(8,128)(2,1)} %param.8) | copy-start | bytes 3145732
  6.0 10.4 %collective-permute-start.1 = (bf16[288,256]{1,0:T(8,128)(2,1)S(1)}, bf16[288,256]{1,0:T(8,128)(2,1)S(1)}, u32[]{:S(2)}, u32[]{:S(2)}) collective-permute-start(bf16[288,256]{1,0:T(8,128)(2,1)S(1)} %message.1.refs_0_), channel_id=1, source_target_pairs={{0,2},{1,3},{2,0},{3,1},{4,6},{5,7},{6,4},{7,5},{8,10},{9,11},{10,... | collective-permute-start | bytes 442376 | tf_op jit(solution)/shard_map/ppermute | solution.py:363
  7.5 18.5 %collective-permute-start.4 = (bf16[2,256,256]{2,1,0:T(8,128)(2,1)S(1)}, bf16[2,256,256]{2,1,0:T(8,128)(2,1)S(1)}, u32[]{:S(2)}, u32[]{:S(2)}) collective-permute-start(bf16[2,256,256]{2,1,0:T(8,128)(2,1)S(1)} %get-tuple-element.29), channel_id=1, source_target_pairs={{0,1},{1,0},{2,3},{3,2},{4,5},{5,4},{6,7},{7,6},{8,9},{9,8},{10,11... | collective-permute-start | bytes 786440 | tf_op jit(solution)/shard_map/ppermute | solution.py:363
  8.1 17.9 %collective-permute-start.5 = (bf16[2,256,256]{2,1,0:T(8,128)(2,1)S(1)}, bf16[2,256,256]{2,1,0:T(8,128)(2,1)S(1)}, u32[]{:S(2)}, u32[]{:S(2)}) collective-permute-start(bf16[2,256,256]{2,1,0:T(8,128)(2,1)S(1)} %get-tuple-element.31), channel_id=1, source_target_pairs={{0,2},{1,3},{2,0},{3,1},{4,6},{5,7},{6,4},{7,5},{8,10},{9,11},{10,... | collective-permute-start | bytes 786440 | tf_op jit(solution)/shard_map/ppermute | solution.py:363
  8.1 9.5 %collective-permute-start = (bf16[288,256]{1,0:T(8,128)(2,1)S(1)}, bf16[288,256]{1,0:T(8,128)(2,1)S(1)}, u32[]{:S(2)}, u32[]{:S(2)}) collective-permute-start(bf16[288,256]{1,0:T(8,128)(2,1)S(1)} %message.1.refs_0_), channel_id=1, source_target_pairs={{0,1},{1,0},{2,3},{3,2},{4,5},{5,4},{6,7},{7,6},{8,9},{9,8},{10,11... | collective-permute-start | bytes 442376 | tf_op jit(solution)/shard_map/ppermute | solution.py:363
  13.2 19.7 %collective-permute-start.12 = (bf16[192,1024]{1,0:T(8,128)(2,1)S(1)}, bf16[192,1024]{1,0:T(8,128)(2,1)S(1)}, u32[]{:S(2)}, u32[]{:S(2)}) collective-permute-start(bf16[192,1024]{1,0:T(8,128)(2,1)S(1)} %collective-permute-done.8.refs_0_), channel_id=1, source_target_pairs={{0,4},{4,0},{8,12},{12,8},{1,5},{5,1},{9,13},{13,9},{2,6},{6,2},{1... | collective-permute-start | bytes 1179656 | tf_op jit(solution)/shard_map/ppermute | solution.py:364
  16.4 2.3 %collective-permute-start.2 = (bf16[288,256]{1,0:T(8,128)(2,1)S(1)}, bf16[288,256]{1,0:T(8,128)(2,1)S(1)}, u32[]{:S(2)}, u32[]{:S(2)}) collective-permute-start(bf16[288,256]{1,0:T(8,128)(2,1)S(1)} %collective-permute-done.1.refs_2_), channel_id=1, source_target_pairs={{0,1},{1,0},{2,3},{3,2},{4,5},{5,4},{6,7},{7,6},{8,9},{9,8},{10,11... | collective-permute-start | bytes 442376 | tf_op jit(solution)/shard_map/ppermute | solution.py:363
  17.6 10.1 %collective-permute-start.9 = (bf16[2,256,256]{2,1,0:T(8,128)(2,1)S(1)}, bf16[2,256,256]{2,1,0:T(8,128)(2,1)S(1)}, u32[]{:S(2)}, u32[]{:S(2)}) collective-permute-start(bf16[2,256,256]{2,1,0:T(8,128)(2,1)S(1)} %get-tuple-element.36), channel_id=1, source_target_pairs={{0,3},{1,2},{2,1},{3,0},{4,7},{5,6},{6,5},{7,4},{8,11},{9,10},{10,... | collective-permute-start | bytes 786440 | tf_op jit(solution)/shard_map/ppermute | solution.py:363
  19.3 6.7 %collective-permute-start.6 = (f32[4,2,256]{2,1,0:T(2,128)S(1)}, f32[4,2,256]{2,1,0:T(2,128)S(1)}, u32[]{:S(2)}, u32[]{:S(2)}) collective-permute-start(f32[4,2,256]{2,1,0:T(2,128)S(1)} %fields.1), channel_id=1, source_target_pairs={{0,0},{1,5},{2,10},{3,15},{4,4},{5,1},{6,14},{7,11},{8,8},{9,13},{... | collective-permute-start | bytes 24584 | tf_op jit(solution)/shard_map/ppermute | solution.py:365
  26.8 7.9 %collective-permute-start.7 = (bf16[128,1024]{1,0:T(8,128)(2,1)S(1)}, bf16[128,1024]{1,0:T(8,128)(2,1)S(1)}, u32[]{:S(2)}, u32[]{:S(2)}) collective-permute-start(bf16[128,1024]{1,0:T(8,128)(2,1)S(1)} %slice.4), channel_id=1, source_target_pairs={{0,2},{1,3},{2,0},{3,1},{4,6},{5,7},{6,4},{7,5},{8,10},{9,11},{10,... | collective-permute-start | bytes 786440 | tf_op jit(solution)/shard_map/ppermute | solution.py:363
  26.9 8.7 %collective-permute-start.11 = (bf16[192,1024]{1,0:T(8,128)(2,1)S(1)}, bf16[192,1024]{1,0:T(8,128)(2,1)S(1)}, u32[]{:S(2)}, u32[]{:S(2)}) collective-permute-start(bf16[192,1024]{1,0:T(8,128)(2,1)S(1)} %collective-permute-done.8.refs_0_), channel_id=1, source_target_pairs={{0,1},{1,0},{2,3},{3,2},{4,5},{5,4},{6,7},{7,6},{8,9},{9,8},{10,11... | collective-permute-start | bytes 1179656 | tf_op jit(solution)/shard_map/ppermute | solution.py:363
  32.9 2.7 %collective-permute-start.13 = (bf16[192,1024]{1,0:T(8,128)(2,1)S(1)}, bf16[192,1024]{1,0:T(8,128)(2,1)S(1)}, u32[]{:S(2)}, u32[]{:S(2)}) collective-permute-start(bf16[192,1024]{1,0:T(8,128)(2,1)S(1)} %collective-permute-done.12.refs_2_), channel_id=1, source_target_pairs={{0,1},{1,0},{2,3},{3,2},{4,5},{5,4},{6,7},{7,6},{8,9},{9,8},{10,11... | collective-permute-start | bytes 1179656 | tf_op jit(solution)/shard_map/ppermute | solution.py:363
  34.8 2.3 %collective-permute-start.10 = (bf16[128,1024]{1,0:T(8,128)(2,1)S(1)}, bf16[128,1024]{1,0:T(8,128)(2,1)S(1)}, u32[]{:S(2)}, u32[]{:S(2)}) collective-permute-start(bf16[128,1024]{1,0:T(8,128)(2,1)S(1)} %collective-permute-done.7.refs_0_), channel_id=1, source_target_pairs={{0,1},{1,0},{2,3},{3,2},{4,5},{5,4},{6,7},{7,6},{8,9},{9,8},{10,11... | collective-permute-start | bytes 786440 | tf_op jit(solution)/shard_map/ppermute | solution.py:363
  37.7 5.4 %collective-permute-start.14 = (f32[2,8,128]{2,1,0:T(8,128)S(1)}, f32[2,8,128]{2,1,0:T(8,128)S(1)}, u32[]{:S(2)}, u32[]{:S(2)}) collective-permute-start(f32[2,8,128]{2,1,0:T(8,128)S(1)} %get-tuple-element.44), channel_id=1, source_target_pairs={{0,2},{1,7},{2,8},{3,13},{4,6},{5,3},{6,12},{7,9},{8,10},{9,15},{1... | collective-permute-start | bytes 24584 | tf_op jit(solution)/shard_map/ppermute | solution.py:366
  41.3 6.2 %collective-permute-start.16 = (f32[2,8,128]{2,1,0:T(8,128)S(1)}, f32[2,8,128]{2,1,0:T(8,128)S(1)}, u32[]{:S(2)}, u32[]{:S(2)}) collective-permute-start(f32[2,8,128]{2,1,0:T(8,128)S(1)} %get-tuple-element.45), channel_id=1, source_target_pairs={{0,0},{1,5},{2,10},{3,15},{4,4},{5,1},{6,14},{7,11},{8,8},{9,13},{... | collective-permute-start | bytes 24584 | tf_op jit(solution)/shard_map/ppermute | solution.py:366
  43.2 4.3 %collective-permute-start.15 = (f32[2,8,128]{2,1,0:T(8,128)S(1)}, f32[2,8,128]{2,1,0:T(8,128)S(1)}, u32[]{:S(2)}, u32[]{:S(2)}) collective-permute-start(f32[2,8,128]{2,1,0:T(8,128)S(1)} %collective-permute-done.14.refs_0_), channel_id=1, source_target_pairs={{0,1},{1,0},{2,3},{3,2},{4,5},{5,4},{6,7},{7,6},{8,9},{9,8},{10,11... | collective-permute-start | bytes 24584 | tf_op jit(solution)/shard_map/ppermute | solution.py:363
  47.5 1.2 %collective-permute-start.17 = (f32[2,8,128]{2,1,0:T(8,128)S(1)}, f32[2,8,128]{2,1,0:T(8,128)S(1)}, u32[]{:S(2)}, u32[]{:S(2)}) collective-permute-start(f32[2,8,128]{2,1,0:T(8,128)S(1)} %collective-permute-done.16.refs_2_), channel_id=1, source_target_pairs={{0,1},{1,0},{2,3},{3,2},{4,5},{5,4},{6,7},{7,6},{8,9},{9,8},{10,11... | collective-permute-start | bytes 24584 | tf_op jit(solution)/shard_map/ppermute | solution.py:363

commit v12 on v11

--- a/solution.py
+++ b/solution.py
@@ -400,7 +400,7 @@
     turned, masks = turn(n, per, share, branches, counts, messages)
     other = {k: swap(x) for k, x in crossed.items()}
     earlier, begun = first_blocks(n, share, blocks[:-1], turned, asked)
-    direct = {k: move(ordered(rows[:direct_rows], begun), k) for k in heads}
+    direct = {k: move(ordered(rows[:direct_rows], turned), k) for k in heads}
     green = make_green(n, share, blocks[n - 1], turned, asked, earlier, begun)
     crossed = along(crossed)
     other = along({k: ordered(x, green) for k, x in other.items()})

time: 49.5 us -> 50.4 us (1.018)
  starting transfers between devices: 17.9 us -> 19.4 us
  waiting for transfers between devices: 13.9 us -> 13.3 us
    ppermute x14, starting transfers between devices: 5.9 us -> 8.07 us  [at_the_source(): move = lambda x, k: lax.ppermute(x, SR, [(i, i ^ k) for i in range(n)])]
    ppermute x2, waiting for transfers between devices: 4.22 us -> 3.19 us  [at_the_source(): lax.ppermute(x, ALL, [(w * n + q, (w ^ q) * n + (q ^ k)) for w, q in pairs])]
  transfers between devices with their start and end apart: 18 -> 18, of which waited for: 6 -> 5; matrix products, arithmetic and copies ran while one was open for 2% -> 2% of each run, Pallas kernels for 25% -> 25%
where the time goes in v12:
time: 50.4 us; the launch traced here: 50.2 us
  starting transfers between devices  19.4 us (38%)
  Pallas kernels  13.7 us (27%)
  waiting for transfers between devices  13.3 us (26%)
  local copies, waits for them, and re-layouts  2.31 us (5%)
  between operations  1.51 us (3%)
    ppermute x14, waiting for transfers between devices, at_the_source(): move = lambda x, k: lax.ppermute(x, SR, [(i, i ^ k) for i in range(n)])  10.1 us
    ppermute x14, starting transfers between devices, at_the_source(): move = lambda x, k: lax.ppermute(x, SR, [(i, i ^ k) for i in range(n)])  8.07 us
    ppermute x2, starting transfers between devices, at_the_source(): lax.ppermute(x, ALL, [(w * n + q, (w ^ q) * n + (q ^ k)) for w, q in pairs])  5.17 us
    pallas_call x1, Pallas kernels, make_green(): pl.pallas_call(functools.partial(green_kernel, n, share), out_shape=jax.S...  5.14 us
    ppermute x1, starting transfers between devices, at_the_source(): lax.ppermute(x, ALL, [(w * n + q, (w ^ q) * n + q) for w, q in pairs])  4.87 us
    pallas_call x3, Pallas kernels, contract(): pl.pallas_call(kernel, out_shape=[jax.ShapeDtypeStruct((count, 8, 128), F...  3.63 us
    ppermute x2, waiting for transfers between devices, at_the_source(): lax.ppermute(x, ALL, [(w * n + q, (w ^ q) * n + (q ^ k)) for w, q in pairs])  3.19 us
    pallas_call x1, Pallas kernels, select(): pl.pallas_call(functools.partial(select_kernel, n, per, share), out_shape...  2.17 us
  transfers between devices with their start and end apart: 18, of which 5 were waited for; matrix products, arithmetic and copies ran while one was open for 2% of the time, Pallas kernels for 25%

profile of v12, /device:TPU:3, one launch (start us, length us, event | category | flops | bytes accessed | tf_op | source)
XLA Modules:
  0.0 50.2 jit_solution(5567599030510578741)
XLA Ops:
  0.6 0.7 %collective-permute-start.4 = (bf16[512,1024]{1,0:T(8,128)(2,1)}, bf16[512,1024]{1,0:T(8,128)(2,1)S(1)}, u32[]{:S(2)}, u32[]{:S(2)}) collective-permute-start(bf16[512,1024]{1,0:T(8,128)(2,1)} %bitcast.3), channel_id=1, source_target_pairs={{0,1},{1,0},{2,3},{3,2},{4,5},{5,4},{6,7},{7,6},{8,9},{9,8},{10,11... | collective-permute-start | bytes 3145736 | tf_op jit(solution)/shard_map/ppermute | solution.py:363
  1.4 0.0 copy-start.4
  1.4 0.0 copy-start.2
  1.4 0.0 copy-start.3
  1.4 1.1 %constant_dynamic-slice_fusion = bf16[192,1024]{1,0:T(8,128)(2,1)S(1)} fusion(bf16[512,1024]{1,0:T(8,128)(2,1)} %bitcast.4, s32[]{:T(128)S(6)} %select_n.3), kind=kLoop, calls=%fused_computation | loop fusion | bytes 786436 | tf_op jit(solution)/shard_map/dynamic_slice | solution.py:387
  2.4 0.1 collective-permute-start.5
  2.5 0.0 copy-done.4
  2.5 0.0 copy-start
  2.5 1.2 %copy-done = bf16[8,256,256]{2,1,0:T(8,128)(2,1)S(1)} copy-done((bf16[8,256,256]{2,1,0:T(8,128)(2,1)S(1)}, bf16[8,256,256]{2,1,0:T(8,128)(2,1)}, u32[]{:S(2)}) %copy-start) | copy-done | bytes 1048600
  3.8 0.0 copy-start.1
  3.8 2.2 %select.1 = (bf16[2,256,256]{2,1,0:T(8,128)(2,1)S(1)}, bf16[2,256,256]{2,1,0:T(8,128)(2,1)S(1)}, bf16[2,256,256]{2,1,0:T(8,128)(2,1)S(1)}, bf16[2,256,256]{2,1,0:T(8,128)(2,1)S(1)}) custom-call(s32[32]{0:T(128)S(1)} %copy-done.4, bf16[8,256,256]{2,1,0:T(8,128)(2,1)S(1)} %copy-done), custom_call_target="tpu_custom_call" | custom-call | tf_op jit(solution)/shard_map/select/pallas_call | solution.py:69
  5.9 0.0 copy-done.2
  5.9 0.0 copy-done.3
  6.0 1.5 %collective-permute-start.1 = (bf16[288,256]{1,0:T(8,128)(2,1)S(1)}, bf16[288,256]{1,0:T(8,128)(2,1)S(1)}, u32[]{:S(2)}, u32[]{:S(2)}) collective-permute-start(bf16[288,256]{1,0:T(8,128)(2,1)S(1)} %message.1.refs_0_), channel_id=1, source_target_pairs={{0,2},{1,3},{2,0},{3,1},{4,6},{5,7},{6,4},{7,5},{8,10},{9,11},{10,... | collective-permute-start | bytes 442376 | tf_op jit(solution)/shard_map/ppermute | solution.py:363
  7.5 0.6 %collective-permute-start = (bf16[288,256]{1,0:T(8,128)(2,1)S(1)}, bf16[288,256]{1,0:T(8,128)(2,1)S(1)}, u32[]{:S(2)}, u32[]{:S(2)}) collective-permute-start(bf16[288,256]{1,0:T(8,128)(2,1)S(1)} %message.1.refs_0_), channel_id=1, source_target_pairs={{0,1},{1,0},{2,3},{3,2},{4,5},{5,4},{6,7},{7,6},{8,9},{9,8},{10,11... | collective-permute-start | bytes 442376 | tf_op jit(solution)/shard_map/ppermute | solution.py:363
  8.1 5.1 %collective-permute-done.5.refs_0_ = bf16[192,1024]{1,0:T(8,128)(2,1)S(1)} collective-permute-done((bf16[192,1024]{1,0:T(8,128)(2,1)S(1)}, bf16[192,1024]{1,0:T(8,128)(2,1)S(1)}, u32[]{:S(2)}, u32[]{:S(2)}) %collective-permute-start.5) | collective-permute-done | bytes 393248 | tf_op jit(solution)/shard_map/ppermute | solution.py:363
  13.2 1.3 %collective-permute-start.12 = (bf16[192,1024]{1,0:T(8,128)(2,1)S(1)}, bf16[192,1024]{1,0:T(8,128)(2,1)S(1)}, u32[]{:S(2)}, u32[]{:S(2)}) collective-permute-start(bf16[192,1024]{1,0:T(8,128)(2,1)S(1)} %collective-permute-done.5.refs_0_), channel_id=1, source_target_pairs={{0,4},{4,0},{8,12},{12,8},{1,5},{5,1},{9,13},{13,9},{2,6},{6,2},{1... | collective-permute-start | bytes 1179656 | tf_op jit(solution)/shard_map/ppermute | solution.py:364
  14.5 0.0 collective-permute-done.4.refs_1_
  14.5 1.6 %collective-permute-start.8 = (bf16[2,256,256]{2,1,0:T(8,128)(2,1)S(1)}, bf16[2,256,256]{2,1,0:T(8,128)(2,1)S(1)}, u32[]{:S(2)}, u32[]{:S(2)}) collective-permute-start(bf16[2,256,256]{2,1,0:T(8,128)(2,1)S(1)} %get-tuple-element.33), channel_id=1, source_target_pairs={{0,1},{1,0},{2,3},{3,2},{4,5},{5,4},{6,7},{7,6},{8,9},{9,8},{10,11... | collective-permute-start | bytes 786440 | tf_op jit(solution)/shard_map/ppermute | solution.py:363
  16.1 0.3 collective-permute-start.9
  16.3 0.0 collective-permute-done.1.refs_2_
  16.4 1.3 %collective-permute-start.6 = (bf16[2,256,256]{2,1,0:T(8,128)(2,1)S(1)}, bf16[2,256,256]{2,1,0:T(8,128)(2,1)S(1)}, u32[]{:S(2)}, u32[]{:S(2)}) collective-permute-start(bf16[2,256,256]{2,1,0:T(8,128)(2,1)S(1)} %get-tuple-element.31), channel_id=1, source_target_pairs={{0,3},{1,2},{2,1},{3,0},{4,7},{5,6},{6,5},{7,4},{8,11},{9,10},{10,... | collective-permute-start | bytes 786440 | tf_op jit(solution)/shard_map/ppermute | solution.py:363
  17.7 0.0 collective-permute-done.refs_1_
  17.7 0.2 collective-permute-start.2
  17.9 1.1 %collective-permute-done.2.refs_3_ = bf16[288,256]{1,0:T(8,128)(2,1)S(1)} collective-permute-done((bf16[288,256]{1,0:T(8,128)(2,1)S(1)}, bf16[288,256]{1,0:T(8,128)(2,1)S(1)}, u32[]{:S(2)}, u32[]{:S(2)}) %collective-permute-start.2) | collective-permute-done | bytes 147488 | tf_op jit(solution)/shard_map/ppermute | solution.py:363
  19.1 0.6 %fields.1 = f32[4,2,256]{2,1,0:T(2,128)S(1)} custom-call(s32[32]{0:T(128)S(1)} %copy-done.4, bf16[288,256]{1,0:T(8,128)(2,1)S(1)} %message.1.refs_0_, bf16[288,256]{1,0:T(8,128)(2,1)S(1)} %collective-permute-done.refs_1_, bf16[288,256]{1,0:T(8,128)(2,1)S(1)} %collective-permute-done.1.refs_2_, bf16[288,256]{1,0:T(8,128)(2,1)S(1)} %collective-permute-done.2.refs_3_), custom_call_target="tpu_custom_call" | custom-call | tf_op jit(solution)/shard_map/fields/pallas_call | solution.py:119
  19.7 4.9 %collective-permute-start.7 = (f32[4,2,256]{2,1,0:T(2,128)S(1)}, f32[4,2,256]{2,1,0:T(2,128)S(1)}, u32[]{:S(2)}, u32[]{:S(2)}) collective-permute-start(f32[4,2,256]{2,1,0:T(2,128)S(1)} %fields.1), channel_id=1, source_target_pairs={{0,0},{1,5},{2,10},{3,15},{4,4},{5,1},{6,14},{7,11},{8,8},{9,13},{... | collective-permute-start | bytes 24584 | tf_op jit(solution)/shard_map/ppermute | solution.py:365
  24.6 0.0 copy-done.1
  25.2 0.8 %turn.1 = (bf16[256,1024]{1,0:T(8,128)(2,1)S(1)}, f32[8,128]{1,0:T(8,128)S(1)}) custom-call(s32[32]{0:T(128)S(1)} %copy-done.4, s32[1]{0:T(128)S(6)} %copy.8.counts, bf16[288,256]{1,0:T(8,128)(2,1)S(1)} %message.1.refs_0_, bf16[288,256]{1,0:T(8,128)(2,1)S(1)} %collective-permute-done.refs_1_, bf16[288,256]{1,0:T(8,128)(2,1)S(1)} %collective-permute-done.1.refs_2_, ...), custom_call_target="tpu_custom_call" | custom-call | tf_op jit(solution)/shard_map/turn/pallas_call | solution.py:146
  26.1 0.0 collective-permute-done.7.refs_4_.refs_2_
  26.1 0.1 collective-permute-start.3
  26.1 0.0 collective-permute-done.8.refs_1_
  26.2 0.2 collective-permute-start.11
  26.4 0.0 collective-permute-done.9.refs_2_
  26.4 0.8 %first.1 = (bf16[768,512]{1,0:T(8,128)(2,1)S(1)}, f32[256,512]{1,0:T(8,128)S(1)}) custom-call(bf16[2,256,256]{2,1,0:T(8,128)(2,1)S(1)} %get-tuple-element.25.refs_0_, bf16[2,256,256]{2,1,0:T(8,128)(2,1)S(1)} %collective-permute-done.8.refs_1_, bf16[2,256,256]{2,1,0:T(8,128)(2,1)S(1)} %collective-permute-done.9.refs_2_, ...), custom_call_target="tpu_custom_call" | custom-call | flops 1073741824 | bytes 1048576 | tf_op jit(solution)/shard_map/first/pallas_call | solution.py:187
  27.2 2.9 %collective-permute-done.6.refs_0_ = bf16[2,256,256]{2,1,0:T(8,128)(2,1)S(1)} collective-permute-done((bf16[2,256,256]{2,1,0:T(8,128)(2,1)S(1)}, bf16[2,256,256]{2,1,0:T(8,128)(2,1)S(1)}, u32[]{:S(2)}, u32[]{:S(2)}) %collective-permute-start.6) | collective-permute-done | bytes 262176 | tf_op jit(solution)/shard_map/ppermute | solution.py:363
  30.1 5.1 %green.1.refs_2_.refs_4_ = bf16[1024,512]{1,0:T(8,128)(2,1)S(1)} custom-call(bf16[2,256,256]{2,1,0:T(8,128)(2,1)S(1)} %collective-permute-done.6.refs_0_, bf16[256,1024]{1,0:T(8,128)(2,1)S(1)} %get-tuple-element.28.refs_3_.refs_1_, f32[4,2,256]{2,1,0:T(2,128)S(1)} %collective-permute-done.7.refs_4_.refs_2_, bf16[768,512]{1,0:T(8,128)(2,1)S(1)} %get-tuple-element.36.refs_3_, ...), custom_call_target="tpu_custom_call" | custom-call | tf_op jit(solution)/shard_map/green/pallas_call | solution.py:245
  35.2 0.0 collective-permute-done.12.refs_2_
  35.2 0.1 collective-permute-start.13
  35.3 1.5 %contract.3.refs_6_ = f32[2,8,128]{2,1,0:T(8,128)S(1)} custom-call(bf16[512,1024]{1,0:T(8,128)(2,1)S(1)} %bitcast.6, bf16[512,1024]{1,0:T(8,128)(2,1)S(1)} %collective-permute-done.4.refs_1_, bf16[1024,512]{1,0:T(8,128)(2,1)S(1)} %green.1.refs_2_.refs_4_), custom_call_target="tpu_custom_call" | custom-call | flops 1073741824 | bytes 3145728 | tf_op jit(solution)/shard_map/contract/pallas_call | solution.py:314
  36.8 0.0 collective-permute-done.3.refs_0_
  36.9 0.6 %collective-permute-start.10 = (bf16[128,1024]{1,0:T(8,128)(2,1)S(1)}, bf16[128,1024]{1,0:T(8,128)(2,1)S(1)}, u32[]{:S(2)}, u32[]{:S(2)}) collective-permute-start(bf16[128,1024]{1,0:T(8,128)(2,1)S(1)} %collective-permute-done.3.refs_0_), channel_id=1, source_target_pairs={{0,1},{1,0},{2,3},{3,2},{4,5},{5,4},{6,7},{7,6},{8,9},{9,8},{10,11... | collective-permute-start | bytes 786440 | tf_op jit(solution)/shard_map/ppermute | solution.py:363
  37.4 0.0 collective-permute-done.11.refs_1_
  37.4 0.0 collective-permute-done.13.refs_3_
  37.4 1.4 %contract.4 = (f32[2,8,128]{2,1,0:T(8,128)S(1)}, f32[128,512]{1,0:T(8,128)S(1)}, f32[128,512]{1,0:T(8,128)S(1)}) custom-call(bf16[192,1024]{1,0:T(8,128)(2,1)S(1)} %collective-permute-done.5.refs_0_, bf16[192,1024]{1,0:T(8,128)(2,1)S(1)} %collective-permute-done.11.refs_1_, bf16[192,1024]{1,0:T(8,128)(2,1)S(1)} %collective-permute-done.12.refs_2_, ...), custom_call_target="tpu_custom_call" | custom-call | flops 805306368 | bytes 2621440 | tf_op jit(solution)/shard_map/contract/pallas_call | solution.py:314
  38.8 0.0 collective-permute-done.10.refs_1_
  38.8 0.7 %contract.5 = (f32[2,8,128]{2,1,0:T(8,128)S(1)}, f32[2,8,128]{2,1,0:T(8,128)S(1)}) custom-call(bf16[128,1024]{1,0:T(8,128)(2,1)S(1)} %collective-permute-done.3.refs_0_, bf16[128,1024]{1,0:T(8,128)(2,1)S(1)} %collective-permute-done.10.refs_1_, bf16[1024,512]{1,0:T(8,128)(2,1)S(1)} %green.1.refs_2_.refs_4_, f32[128,512]{1,0:T(8,128)S(1)} %get-tuple-element.41.refs_3_, ...), custom_call_target="tpu_custom_call" | custom-call | flops 268435456 | bytes 1572864 | tf_op jit(solution)/shard_map/contract/pallas_call | solution.py:314
  39.6 2.2 %collective-permute-start.14 = (f32[2,8,128]{2,1,0:T(8,128)S(1)}, f32[2,8,128]{2,1,0:T(8,128)S(1)}, u32[]{:S(2)}, u32[]{:S(2)}) collective-permute-start(f32[2,8,128]{2,1,0:T(8,128)S(1)} %get-tuple-element.44), channel_id=1, source_target_pairs={{0,2},{1,7},{2,8},{3,13},{4,6},{5,3},{6,12},{7,9},{8,10},{9,15},{1... | collective-permute-start | bytes 24584 | tf_op jit(solution)/shard_map/ppermute | solution.py:366
  41.8 2.9 %collective-permute-start.16 = (f32[2,8,128]{2,1,0:T(8,128)S(1)}, f32[2,8,128]{2,1,0:T(8,128)S(1)}, u32[]{:S(2)}, u32[]{:S(2)}) collective-permute-start(f32[2,8,128]{2,1,0:T(8,128)S(1)} %get-tuple-element.45), channel_id=1, source_target_pairs={{0,0},{1,5},{2,10},{3,15},{4,4},{5,1},{6,14},{7,11},{8,8},{9,13},{... | collective-permute-start | bytes 24584 | tf_op jit(solution)/shard_map/ppermute | solution.py:366
  44.7 0.0 collective-permute-done.14.refs_0_
  44.7 0.1 collective-permute-start.15
  44.8 3.2 %collective-permute-done.16.refs_2_ = f32[2,8,128]{2,1,0:T(8,128)S(1)} collective-permute-done((f32[2,8,128]{2,1,0:T(8,128)S(1)}, f32[2,8,128]{2,1,0:T(8,128)S(1)}, u32[]{:S(2)}, u32[]{:S(2)}) %collective-permute-start.16) | collective-permute-done | bytes 8224 | tf_op jit(solution)/shard_map/ppermute | solution.py:366
  48.0 0.8 %collective-permute-start.17 = (f32[2,8,128]{2,1,0:T(8,128)S(1)}, f32[2,8,128]{2,1,0:T(8,128)S(1)}, u32[]{:S(2)}, u32[]{:S(2)}) collective-permute-start(f32[2,8,128]{2,1,0:T(8,128)S(1)} %collective-permute-done.16.refs_2_), channel_id=1, source_target_pairs={{0,1},{1,0},{2,3},{3,2},{4,5},{5,4},{6,7},{7,6},{8,9},{9,8},{10,11... | collective-permute-start | bytes 24584 | tf_op jit(solution)/shard_map/ppermute | solution.py:363
  48.8 0.0 collective-permute-done.15.refs_1_
  48.8 0.8 %collective-permute-done.17.refs_3_ = f32[2,8,128]{2,1,0:T(8,128)S(1)} collective-permute-done((f32[2,8,128]{2,1,0:T(8,128)S(1)}, f32[2,8,128]{2,1,0:T(8,128)S(1)}, u32[]{:S(2)}, u32[]{:S(2)}) %collective-permute-start.17) | collective-permute-done | bytes 8224 | tf_op jit(solution)/shard_map/ppermute | solution.py:363
  49.6 0.6 %unpack.1 = (f32[2,8]{1,0:T(2,128)}, f32[2,8]{1,0:T(2,128)}) custom-call(f32[8,128]{1,0:T(8,128)S(1)} %get-tuple-element.27.masks, f32[2,8,128]{2,1,0:T(8,128)S(1)} %collective-permute-done.14.refs_0_, f32[2,8,128]{2,1,0:T(8,128)S(1)} %collective-permute-done.15.refs_1_, f32[2,8,128]{2,1,0:T(8,128)S(1)} %collective-permute-done.16.refs_2_, ...), custom_call_target="tpu_custom_call" | custom-call | tf_op jit(solution)/shard_map/unpack/pallas_call | solution.py:346
  (2 shorter events, 0.0 us)
Async XLA Ops:
  0.6 13.9 %collective-permute-start.4 = (bf16[512,1024]{1,0:T(8,128)(2,1)}, bf16[512,1024]{1,0:T(8,128)(2,1)S(1)}, u32[]{:S(2)}, u32[]{:S(2)}) collective-permute-start(bf16[512,1024]{1,0:T(8,128)(2,1)} %bitcast.3), channel_id=1, source_target_pairs={{0,1},{1,0},{2,3},{3,2},{4,5},{5,4},{6,7},{7,6},{8,9},{9,8},{10,11... | collective-permute-start | bytes 3145736 | tf_op jit(solution)/shard_map/ppermute | solution.py:363
  1.4 1.1 %copy-start.4 = (s32[32]{0:T(128)S(1)}, s32[32]{0:T(128)}, u32[]{:S(2)}) copy-start(s32[32]{0:T(128)} %branches.5) | copy-start | bytes 388
  1.4 4.6 %copy-start.2 = (bf16[256,256]{1,0:T(8,128)(2,1)S(1)}, bf16[256,256]{1,0:T(8,128)(2,1)}, u32[]{:S(2)}) copy-start(bf16[256,256]{1,0:T(8,128)(2,1)} %trial) | copy-start | bytes 393220
  1.4 4.6 %copy-start.3 = (f32[8,256]{1,0:T(8,128)S(1)}, f32[8,256]{1,0:T(8,128)}, u32[]{:S(2)}) copy-start(f32[8,256]{1,0:T(8,128)} %field.1) | copy-start | bytes 24580
  2.4 10.8 %collective-permute-start.5 = (bf16[192,1024]{1,0:T(8,128)(2,1)S(1)}, bf16[192,1024]{1,0:T(8,128)(2,1)S(1)}, u32[]{:S(2)}, u32[]{:S(2)}) collective-permute-start(bf16[192,1024]{1,0:T(8,128)(2,1)S(1)} %constant_dynamic-slice_fusion), channel_id=1, source_target_pairs={{0,2},{1,3},{2,0},{3,1},{4,6},{5,7},{6,4},{7,5},{8,10},{9,11},{10,... | collective-permute-start | bytes 1179656 | tf_op jit(solution)/shard_map/ppermute | solution.py:363
  2.5 1.2 %copy-start = (bf16[8,256,256]{2,1,0:T(8,128)(2,1)S(1)}, bf16[8,256,256]{2,1,0:T(8,128)(2,1)}, u32[]{:S(2)}) copy-start(bf16[8,256,256]{2,1,0:T(8,128)(2,1)} %walkers.1) | copy-start | bytes 3145732
  3.8 20.8 %copy-start.1 = (bf16[2,256,1024]{2,1,0:T(8,128)(2,1)S(1)}, bf16[2,256,1024]{2,1,0:T(8,128)(2,1)}, u32[]{:S(2)}) copy-start(bf16[2,256,1024]{2,1,0:T(8,128)(2,1)} %param.8) | copy-start | bytes 3145732
  6.0 10.4 %collective-permute-start.1 = (bf16[288,256]{1,0:T(8,128)(2,1)S(1)}, bf16[288,256]{1,0:T(8,128)(2,1)S(1)}, u32[]{:S(2)}, u32[]{:S(2)}) collective-permute-start(bf16[288,256]{1,0:T(8,128)(2,1)S(1)} %message.1.refs_0_), channel_id=1, source_target_pairs={{0,2},{1,3},{2,0},{3,1},{4,6},{5,7},{6,4},{7,5},{8,10},{9,11},{10,... | collective-permute-start | bytes 442376 | tf_op jit(solution)/shard_map/ppermute | solution.py:363
  7.5 10.2 %collective-permute-start = (bf16[288,256]{1,0:T(8,128)(2,1)S(1)}, bf16[288,256]{1,0:T(8,128)(2,1)S(1)}, u32[]{:S(2)}, u32[]{:S(2)}) collective-permute-start(bf16[288,256]{1,0:T(8,128)(2,1)S(1)} %message.1.refs_0_), channel_id=1, source_target_pairs={{0,1},{1,0},{2,3},{3,2},{4,5},{5,4},{6,7},{7,6},{8,9},{9,8},{10,11... | collective-permute-start | bytes 442376 | tf_op jit(solution)/shard_map/ppermute | solution.py:363
  13.2 22.0 %collective-permute-start.12 = (bf16[192,1024]{1,0:T(8,128)(2,1)S(1)}, bf16[192,1024]{1,0:T(8,128)(2,1)S(1)}, u32[]{:S(2)}, u32[]{:S(2)}) collective-permute-start(bf16[192,1024]{1,0:T(8,128)(2,1)S(1)} %collective-permute-done.5.refs_0_), channel_id=1, source_target_pairs={{0,4},{4,0},{8,12},{12,8},{1,5},{5,1},{9,13},{13,9},{2,6},{6,2},{1... | collective-permute-start | bytes 1179656 | tf_op jit(solution)/shard_map/ppermute | solution.py:364
  14.5 11.6 %collective-permute-start.8 = (bf16[2,256,256]{2,1,0:T(8,128)(2,1)S(1)}, bf16[2,256,256]{2,1,0:T(8,128)(2,1)S(1)}, u32[]{:S(2)}, u32[]{:S(2)}) collective-permute-start(bf16[2,256,256]{2,1,0:T(8,128)(2,1)S(1)} %get-tuple-element.33), channel_id=1, source_target_pairs={{0,1},{1,0},{2,3},{3,2},{4,5},{5,4},{6,7},{7,6},{8,9},{9,8},{10,11... | collective-permute-start | bytes 786440 | tf_op jit(solution)/shard_map/ppermute | solution.py:363
  16.1 10.3 %collective-permute-start.9 = (bf16[2,256,256]{2,1,0:T(8,128)(2,1)S(1)}, bf16[2,256,256]{2,1,0:T(8,128)(2,1)S(1)}, u32[]{:S(2)}, u32[]{:S(2)}) collective-permute-start(bf16[2,256,256]{2,1,0:T(8,128)(2,1)S(1)} %get-tuple-element.35), channel_id=1, source_target_pairs={{0,2},{1,3},{2,0},{3,1},{4,6},{5,7},{6,4},{7,5},{8,10},{9,11},{10,... | collective-permute-start | bytes 786440 | tf_op jit(solution)/shard_map/ppermute | solution.py:363
  16.4 13.7 %collective-permute-start.6 = (bf16[2,256,256]{2,1,0:T(8,128)(2,1)S(1)}, bf16[2,256,256]{2,1,0:T(8,128)(2,1)S(1)}, u32[]{:S(2)}, u32[]{:S(2)}) collective-permute-start(bf16[2,256,256]{2,1,0:T(8,128)(2,1)S(1)} %get-tuple-element.31), channel_id=1, source_target_pairs={{0,3},{1,2},{2,1},{3,0},{4,7},{5,6},{6,5},{7,4},{8,11},{9,10},{10,... | collective-permute-start | bytes 786440 | tf_op jit(solution)/shard_map/ppermute | solution.py:363
  17.7 1.4 %collective-permute-start.2 = (bf16[288,256]{1,0:T(8,128)(2,1)S(1)}, bf16[288,256]{1,0:T(8,128)(2,1)S(1)}, u32[]{:S(2)}, u32[]{:S(2)}) collective-permute-start(bf16[288,256]{1,0:T(8,128)(2,1)S(1)} %collective-permute-done.1.refs_2_), channel_id=1, source_target_pairs={{0,1},{1,0},{2,3},{3,2},{4,5},{5,4},{6,7},{7,6},{8,9},{9,8},{10,11... | collective-permute-start | bytes 442376 | tf_op jit(solution)/shard_map/ppermute | solution.py:363
  19.7 6.4 %collective-permute-start.7 = (f32[4,2,256]{2,1,0:T(2,128)S(1)}, f32[4,2,256]{2,1,0:T(2,128)S(1)}, u32[]{:S(2)}, u32[]{:S(2)}) collective-permute-start(f32[4,2,256]{2,1,0:T(2,128)S(1)} %fields.1), channel_id=1, source_target_pairs={{0,0},{1,5},{2,10},{3,15},{4,4},{5,1},{6,14},{7,11},{8,8},{9,13},{... | collective-permute-start | bytes 24584 | tf_op jit(solution)/shard_map/ppermute | solution.py:365
  26.1 10.8 %collective-permute-start.3 = (bf16[128,1024]{1,0:T(8,128)(2,1)S(1)}, bf16[128,1024]{1,0:T(8,128)(2,1)S(1)}, u32[]{:S(2)}, u32[]{:S(2)}) collective-permute-start(bf16[128,1024]{1,0:T(8,128)(2,1)S(1)} %slice.4), channel_id=1, source_target_pairs={{0,2},{1,3},{2,0},{3,1},{4,6},{5,7},{6,4},{7,5},{8,10},{9,11},{10,... | collective-permute-start | bytes 786440 | tf_op jit(solution)/shard_map/ppermute | solution.py:363
  26.2 11.3 %collective-permute-start.11 = (bf16[192,1024]{1,0:T(8,128)(2,1)S(1)}, bf16[192,1024]{1,0:T(8,128)(2,1)S(1)}, u32[]{:S(2)}, u32[]{:S(2)}) collective-permute-start(bf16[192,1024]{1,0:T(8,128)(2,1)S(1)} %collective-permute-done.5.refs_0_), channel_id=1, source_target_pairs={{0,1},{1,0},{2,3},{3,2},{4,5},{5,4},{6,7},{7,6},{8,9},{9,8},{10,11... | collective-permute-start | bytes 1179656 | tf_op jit(solution)/shard_map/ppermute | solution.py:363
  35.2 2.2 %collective-permute-start.13 = (bf16[192,1024]{1,0:T(8,128)(2,1)S(1)}, bf16[192,1024]{1,0:T(8,128)(2,1)S(1)}, u32[]{:S(2)}, u32[]{:S(2)}) collective-permute-start(bf16[192,1024]{1,0:T(8,128)(2,1)S(1)} %collective-permute-done.12.refs_2_), channel_id=1, source_target_pairs={{0,1},{1,0},{2,3},{3,2},{4,5},{5,4},{6,7},{7,6},{8,9},{9,8},{10,11... | collective-permute-start | bytes 1179656 | tf_op jit(solution)/shard_map/ppermute | solution.py:363
  36.9 2.0 %collective-permute-start.10 = (bf16[128,1024]{1,0:T(8,128)(2,1)S(1)}, bf16[128,1024]{1,0:T(8,128)(2,1)S(1)}, u32[]{:S(2)}, u32[]{:S(2)}) collective-permute-start(bf16[128,1024]{1,0:T(8,128)(2,1)S(1)} %collective-permute-done.3.refs_0_), channel_id=1, source_target_pairs={{0,1},{1,0},{2,3},{3,2},{4,5},{5,4},{6,7},{7,6},{8,9},{9,8},{10,11... | collective-permute-start | bytes 786440 | tf_op jit(solution)/shard_map/ppermute | solution.py:363
  39.6 5.2 %collective-permute-start.14 = (f32[2,8,128]{2,1,0:T(8,128)S(1)}, f32[2,8,128]{2,1,0:T(8,128)S(1)}, u32[]{:S(2)}, u32[]{:S(2)}) collective-permute-start(f32[2,8,128]{2,1,0:T(8,128)S(1)} %get-tuple-element.44), channel_id=1, source_target_pairs={{0,2},{1,7},{2,8},{3,13},{4,6},{5,3},{6,12},{7,9},{8,10},{9,15},{1... | collective-permute-start | bytes 24584 | tf_op jit(solution)/shard_map/ppermute | solution.py:366
  41.8 6.2 %collective-permute-start.16 = (f32[2,8,128]{2,1,0:T(8,128)S(1)}, f32[2,8,128]{2,1,0:T(8,128)S(1)}, u32[]{:S(2)}, u32[]{:S(2)}) collective-permute-start(f32[2,8,128]{2,1,0:T(8,128)S(1)} %get-tuple-element.45), channel_id=1, source_target_pairs={{0,0},{1,5},{2,10},{3,15},{4,4},{5,1},{6,14},{7,11},{8,8},{9,13},{... | collective-permute-start | bytes 24584 | tf_op jit(solution)/shard_map/ppermute | solution.py:366
  44.7 4.0 %collective-permute-start.15 = (f32[2,8,128]{2,1,0:T(8,128)S(1)}, f32[2,8,128]{2,1,0:T(8,128)S(1)}, u32[]{:S(2)}, u32[]{:S(2)}) collective-permute-start(f32[2,8,128]{2,1,0:T(8,128)S(1)} %collective-permute-done.14.refs_0_), channel_id=1, source_target_pairs={{0,1},{1,0},{2,3},{3,2},{4,5},{5,4},{6,7},{7,6},{8,9},{9,8},{10,11... | collective-permute-start | bytes 24584 | tf_op jit(solution)/shard_map/ppermute | solution.py:363
  48.0 1.6 %collective-permute-start.17 = (f32[2,8,128]{2,1,0:T(8,128)S(1)}, f32[2,8,128]{2,1,0:T(8,128)S(1)}, u32[]{:S(2)}, u32[]{:S(2)}) collective-permute-start(f32[2,8,128]{2,1,0:T(8,128)S(1)} %collective-permute-done.16.refs_2_), channel_id=1, source_target_pairs={{0,1},{1,0},{2,3},{3,2},{4,5},{5,4},{6,7},{7,6},{8,9},{9,8},{10,11... | collective-permute-start | bytes 24584 | tf_op jit(solution)/shard_map/ppermute | solution.py:363

commit v13 on v11

--- a/solution.py
+++ b/solution.py
@@ -419,7 +419,7 @@
         results, outs=2,
     )
     answers = [answer(late, far[0]), answer(results, 0)]
-    arrived = [[x] + [move(x, k) for k in near[1:]] for x in answers]
+    arrived = [[answer(late, k) for k in far], [answers[1]] + [move(answers[1], k) for k in near[1:]]]
     return tuple(x.T for x in unpack(n, per, share, vectors, far + near, masks, [x for held in arrived for x in held]))
 
 

time: 49.5 us -> 51.2 us (1.034)
  the two profiles are of different devices: /device:TPU:3 before, /device:TPU:0 now
where the time goes in v13:
time: 51.2 us; the launch traced here: 51 us
  starting transfers between devices  22.7 us (44%)
  Pallas kernels  13.7 us (27%)
  waiting for transfers between devices  10.8 us (21%)
  local copies, waits for them, and re-layouts  2.32 us (5%)
  between operations  1.46 us (3%)
    ppermute x13, starting transfers between devices, at_the_source(): move = lambda x, k: lax.ppermute(x, SR, [(i, i ^ k) for i in range(n)])  13.2 us
    ppermute x3, starting transfers between devices, at_the_source(): lax.ppermute(x, ALL, [(w * n + q, (w ^ q) * n + (q ^ k)) for w, q in pairs])  6.87 us
    ppermute x13, waiting for transfers between devices, at_the_source(): move = lambda x, k: lax.ppermute(x, SR, [(i, i ^ k) for i in range(n)])  6.09 us
    pallas_call x1, Pallas kernels, make_green(): pl.pallas_call(functools.partial(green_kernel, n, share), out_shape=jax.S...  5.13 us
    ppermute x3, waiting for transfers between devices, at_the_source(): lax.ppermute(x, ALL, [(w * n + q, (w ^ q) * n + (q ^ k)) for w, q in pairs])  4.66 us
    pallas_call x3, Pallas kernels, contract(): pl.pallas_call(kernel, out_shape=[jax.ShapeDtypeStruct((count, 8, 128), F...  3.62 us
    pallas_call x1, Pallas kernels, select(): pl.pallas_call(functools.partial(select_kernel, n, per, share), out_shape...  2.17 us
    ppermute x1, starting transfers between devices, at_the_source(): swap = lambda x: lax.ppermute(x, 'walk', [(w, w ^ 1) for w in range(n)])  2.03 us
  transfers between devices with their start and end apart: 18, of which 5 were waited for; matrix products, arithmetic and copies ran while one was open for 2% of the time, Pallas kernels for 24%

profile of v13, /device:TPU:0, one launch (start us, length us, event | category | flops | bytes accessed | tf_op | source)
XLA Modules:
  0.0 51.0 jit_solution(1917664942770715183)
XLA Ops:
  0.6 0.5 %collective-permute-start.3 = (bf16[512,1024]{1,0:T(8,128)(2,1)}, bf16[512,1024]{1,0:T(8,128)(2,1)S(1)}, u32[]{:S(2)}, u32[]{:S(2)}) collective-permute-start(bf16[512,1024]{1,0:T(8,128)(2,1)} %bitcast.3), channel_id=1, source_target_pairs={{0,1},{1,0},{2,3},{3,2},{4,5},{5,4},{6,7},{7,6},{8,9},{9,8},{10,11... | collective-permute-start | bytes 3145736 | tf_op jit(solution)/shard_map/ppermute | solution.py:363
  1.1 0.0 copy-start.4
  1.2 0.0 copy-start.2
  1.2 0.0 copy-start.3
  1.2 1.1 %constant_dynamic-slice_fusion = bf16[192,1024]{1,0:T(8,128)(2,1)S(1)} fusion(bf16[512,1024]{1,0:T(8,128)(2,1)} %bitcast.4, s32[]{:T(128)S(6)} %select_n.3), kind=kLoop, calls=%fused_computation | loop fusion | bytes 786436 | tf_op jit(solution)/shard_map/dynamic_slice | solution.py:387
  2.2 2.6 %collective-permute-start.8 = (bf16[192,1024]{1,0:T(8,128)(2,1)S(1)}, bf16[192,1024]{1,0:T(8,128)(2,1)S(1)}, u32[]{:S(2)}, u32[]{:S(2)}) collective-permute-start(bf16[192,1024]{1,0:T(8,128)(2,1)S(1)} %constant_dynamic-slice_fusion), channel_id=1, source_target_pairs={{0,2},{1,3},{2,0},{3,1},{4,6},{5,7},{6,4},{7,5},{8,10},{9,11},{10,... | collective-permute-start | bytes 1179656 | tf_op jit(solution)/shard_map/ppermute | solution.py:363
  4.8 0.0 copy-done.4
  4.8 0.0 copy-start
  4.8 1.2 %copy-done = bf16[8,256,256]{2,1,0:T(8,128)(2,1)S(1)} copy-done((bf16[8,256,256]{2,1,0:T(8,128)(2,1)S(1)}, bf16[8,256,256]{2,1,0:T(8,128)(2,1)}, u32[]{:S(2)}) %copy-start) | copy-done | bytes 1048600
  6.0 0.0 copy-start.1
  6.1 2.2 %select.1 = (bf16[2,256,256]{2,1,0:T(8,128)(2,1)S(1)}, bf16[2,256,256]{2,1,0:T(8,128)(2,1)S(1)}, bf16[2,256,256]{2,1,0:T(8,128)(2,1)S(1)}, bf16[2,256,256]{2,1,0:T(8,128)(2,1)S(1)}) custom-call(s32[32]{0:T(128)S(1)} %copy-done.4, bf16[8,256,256]{2,1,0:T(8,128)(2,1)S(1)} %copy-done), custom_call_target="tpu_custom_call" | custom-call | tf_op jit(solution)/shard_map/select/pallas_call | solution.py:69
  8.2 0.0 copy-done.2
  8.2 0.0 copy-done.3
  8.3 0.1 collective-permute-start.1
  8.4 0.0 collective-permute-done.3.refs_1_
  8.4 0.2 collective-permute-start.4
  8.6 1.8 %collective-permute-start.5 = (bf16[2,256,256]{2,1,0:T(8,128)(2,1)S(1)}, bf16[2,256,256]{2,1,0:T(8,128)(2,1)S(1)}, u32[]{:S(2)}, u32[]{:S(2)}) collective-permute-start(bf16[2,256,256]{2,1,0:T(8,128)(2,1)S(1)} %get-tuple-element.31), channel_id=1, source_target_pairs={{0,2},{1,3},{2,0},{3,1},{4,6},{5,7},{6,4},{7,5},{8,10},{9,11},{10,... | collective-permute-start | bytes 786440 | tf_op jit(solution)/shard_map/ppermute | solution.py:363
  10.4 0.2 collective-permute-start
  10.6 4.2 %collective-permute-done.8.refs_0_ = bf16[192,1024]{1,0:T(8,128)(2,1)S(1)} collective-permute-done((bf16[192,1024]{1,0:T(8,128)(2,1)S(1)}, bf16[192,1024]{1,0:T(8,128)(2,1)S(1)}, u32[]{:S(2)}, u32[]{:S(2)}) %collective-permute-start.8) | collective-permute-done | bytes 393248 | tf_op jit(solution)/shard_map/ppermute | solution.py:363
  14.8 2.0 %collective-permute-start.12 = (bf16[192,1024]{1,0:T(8,128)(2,1)S(1)}, bf16[192,1024]{1,0:T(8,128)(2,1)S(1)}, u32[]{:S(2)}, u32[]{:S(2)}) collective-permute-start(bf16[192,1024]{1,0:T(8,128)(2,1)S(1)} %collective-permute-done.8.refs_0_), channel_id=1, source_target_pairs={{0,4},{4,0},{8,12},{12,8},{1,5},{5,1},{9,13},{13,9},{2,6},{6,2},{1... | collective-permute-start | bytes 1179656 | tf_op jit(solution)/shard_map/ppermute | solution.py:364
  16.8 1.1 %collective-permute-done.1.refs_2_ = bf16[288,256]{1,0:T(8,128)(2,1)S(1)} collective-permute-done((bf16[288,256]{1,0:T(8,128)(2,1)S(1)}, bf16[288,256]{1,0:T(8,128)(2,1)S(1)}, u32[]{:S(2)}, u32[]{:S(2)}) %collective-permute-start.1) | collective-permute-done | bytes 147488 | tf_op jit(solution)/shard_map/ppermute | solution.py:363
  17.9 0.0 collective-permute-start.2
  18.0 0.0 collective-permute-done.refs_1_
  18.0 2.1 %collective-permute-start.9 = (bf16[2,256,256]{2,1,0:T(8,128)(2,1)S(1)}, bf16[2,256,256]{2,1,0:T(8,128)(2,1)S(1)}, u32[]{:S(2)}, u32[]{:S(2)}) collective-permute-start(bf16[2,256,256]{2,1,0:T(8,128)(2,1)S(1)} %get-tuple-element.36), channel_id=1, source_target_pairs={{0,3},{1,2},{2,1},{3,0},{4,7},{5,6},{6,5},{7,4},{8,11},{9,10},{10,... | collective-permute-start | bytes 786440 | tf_op jit(solution)/shard_map/ppermute | solution.py:363
  20.0 0.0 collective-permute-done.2.refs_3_
  20.0 0.6 %fields.1 = f32[4,2,256]{2,1,0:T(2,128)S(1)} custom-call(s32[32]{0:T(128)S(1)} %copy-done.4, bf16[288,256]{1,0:T(8,128)(2,1)S(1)} %message.1.refs_0_, bf16[288,256]{1,0:T(8,128)(2,1)S(1)} %collective-permute-done.refs_1_, bf16[288,256]{1,0:T(8,128)(2,1)S(1)} %collective-permute-done.1.refs_2_, bf16[288,256]{1,0:T(8,128)(2,1)S(1)} %collective-permute-done.2.refs_3_), custom_call_target="tpu_custom_call" | custom-call | tf_op jit(solution)/shard_map/fields/pallas_call | solution.py:119
  20.6 0.7 %collective-permute-start.6 = (f32[4,2,256]{2,1,0:T(2,128)S(1)}, f32[4,2,256]{2,1,0:T(2,128)S(1)}, u32[]{:S(2)}, u32[]{:S(2)}) collective-permute-start(f32[4,2,256]{2,1,0:T(2,128)S(1)} %fields.1), channel_id=1, source_target_pairs={{0,0},{1,5},{2,10},{3,15},{4,4},{5,1},{6,14},{7,11},{8,8},{9,13},{... | collective-permute-start | bytes 24584 | tf_op jit(solution)/shard_map/ppermute | solution.py:365
  21.3 0.0 copy-done.1
  22.0 0.8 %turn.1 = (bf16[256,1024]{1,0:T(8,128)(2,1)S(1)}, f32[8,128]{1,0:T(8,128)S(1)}) custom-call(s32[32]{0:T(128)S(1)} %copy-done.4, s32[1]{0:T(128)S(6)} %copy.8.counts, bf16[288,256]{1,0:T(8,128)(2,1)S(1)} %message.1.refs_0_, bf16[288,256]{1,0:T(8,128)(2,1)S(1)} %collective-permute-done.refs_1_, bf16[288,256]{1,0:T(8,128)(2,1)S(1)} %collective-permute-done.1.refs_2_, ...), custom_call_target="tpu_custom_call" | custom-call | tf_op jit(solution)/shard_map/turn/pallas_call | solution.py:146
  22.8 0.0 collective-permute-done.6.refs_4_.refs_2_
  22.8 0.0 collective-permute-done.4.refs_1_
  22.8 0.8 %collective-permute-done.5.refs_2_ = bf16[2,256,256]{2,1,0:T(8,128)(2,1)S(1)} collective-permute-done((bf16[2,256,256]{2,1,0:T(8,128)(2,1)S(1)}, bf16[2,256,256]{2,1,0:T(8,128)(2,1)S(1)}, u32[]{:S(2)}, u32[]{:S(2)}) %collective-permute-start.5) | collective-permute-done | bytes 262176 | tf_op jit(solution)/shard_map/ppermute | solution.py:363
  23.6 0.8 %first.1 = (bf16[768,512]{1,0:T(8,128)(2,1)S(1)}, f32[256,512]{1,0:T(8,128)S(1)}) custom-call(bf16[2,256,256]{2,1,0:T(8,128)(2,1)S(1)} %get-tuple-element.25.refs_0_, bf16[2,256,256]{2,1,0:T(8,128)(2,1)S(1)} %collective-permute-done.4.refs_1_, bf16[2,256,256]{2,1,0:T(8,128)(2,1)S(1)} %collective-permute-done.5.refs_2_, ...), custom_call_target="tpu_custom_call" | custom-call | flops 1073741824 | bytes 1048576 | tf_op jit(solution)/shard_map/first/pallas_call | solution.py:187
  24.4 4.8 %collective-permute-start.7 = (bf16[128,1024]{1,0:T(8,128)(2,1)S(1)}, bf16[128,1024]{1,0:T(8,128)(2,1)S(1)}, u32[]{:S(2)}, u32[]{:S(2)}) collective-permute-start(bf16[128,1024]{1,0:T(8,128)(2,1)S(1)} %slice.4), channel_id=1, source_target_pairs={{0,2},{1,3},{2,0},{3,1},{4,6},{5,7},{6,4},{7,5},{8,10},{9,11},{10,... | collective-permute-start | bytes 786440 | tf_op jit(solution)/shard_map/ppermute | solution.py:363
  29.2 0.2 collective-permute-start.11
  29.4 0.0 collective-permute-done.9.refs_0_
  29.4 5.1 %green.1.refs_2_.refs_4_ = bf16[1024,512]{1,0:T(8,128)(2,1)S(1)} custom-call(bf16[2,256,256]{2,1,0:T(8,128)(2,1)S(1)} %collective-permute-done.9.refs_0_, bf16[256,1024]{1,0:T(8,128)(2,1)S(1)} %get-tuple-element.32.refs_3_.refs_1_, f32[4,2,256]{2,1,0:T(2,128)S(1)} %collective-permute-done.6.refs_4_.refs_2_, bf16[768,512]{1,0:T(8,128)(2,1)S(1)} %get-tuple-element.37.refs_3_, ...), custom_call_target="tpu_custom_call" | custom-call | tf_op jit(solution)/shard_map/green/pallas_call | solution.py:245
  34.5 0.0 collective-permute-done.12.refs_2_
  34.5 0.4 collective-permute-start.13
  34.9 1.5 %contract.3.refs_6_ = f32[2,8,128]{2,1,0:T(8,128)S(1)} custom-call(bf16[512,1024]{1,0:T(8,128)(2,1)S(1)} %bitcast.6, bf16[512,1024]{1,0:T(8,128)(2,1)S(1)} %collective-permute-done.3.refs_1_, bf16[1024,512]{1,0:T(8,128)(2,1)S(1)} %green.1.refs_2_.refs_4_), custom_call_target="tpu_custom_call" | custom-call | flops 1073741824 | bytes 3145728 | tf_op jit(solution)/shard_map/contract/pallas_call | solution.py:314
  36.5 0.0 collective-permute-done.7.refs_0_
  36.5 0.2 collective-permute-start.10
  36.7 0.0 collective-permute-done.11.refs_1_
  36.7 0.0 collective-permute-done.13.refs_3_
  36.7 1.4 %contract.4 = (f32[2,8,128]{2,1,0:T(8,128)S(1)}, f32[128,512]{1,0:T(8,128)S(1)}, f32[128,512]{1,0:T(8,128)S(1)}) custom-call(bf16[192,1024]{1,0:T(8,128)(2,1)S(1)} %collective-permute-done.8.refs_0_, bf16[192,1024]{1,0:T(8,128)(2,1)S(1)} %collective-permute-done.11.refs_1_, bf16[192,1024]{1,0:T(8,128)(2,1)S(1)} %collective-permute-done.12.refs_2_, ...), custom_call_target="tpu_custom_call" | custom-call | flops 805306368 | bytes 2621440 | tf_op jit(solution)/shard_map/contract/pallas_call | solution.py:314
  38.1 0.0 collective-permute-done.10.refs_1_
  38.1 0.7 %contract.5 = (f32[2,8,128]{2,1,0:T(8,128)S(1)}, f32[2,8,128]{2,1,0:T(8,128)S(1)}) custom-call(bf16[128,1024]{1,0:T(8,128)(2,1)S(1)} %collective-permute-done.7.refs_0_, bf16[128,1024]{1,0:T(8,128)(2,1)S(1)} %collective-permute-done.10.refs_1_, bf16[1024,512]{1,0:T(8,128)(2,1)S(1)} %green.1.refs_2_.refs_4_, f32[128,512]{1,0:T(8,128)S(1)} %get-tuple-element.41.refs_3_, ...), custom_call_target="tpu_custom_call" | custom-call | flops 268435456 | bytes 1572864 | tf_op jit(solution)/shard_map/contract/pallas_call | solution.py:314
  38.8 0.7 %collective-permute-start.16 = (f32[2,8,128]{2,1,0:T(8,128)S(1)}, f32[2,8,128]{2,1,0:T(8,128)S(1)}, u32[]{:S(2)}, u32[]{:S(2)}) collective-permute-start(f32[2,8,128]{2,1,0:T(8,128)S(1)} %get-tuple-element.45), channel_id=1, source_target_pairs={{0,0},{1,5},{2,10},{3,15},{4,4},{5,1},{6,14},{7,11},{8,8},{9,13},{... | collective-permute-start | bytes 24584 | tf_op jit(solution)/shard_map/ppermute | solution.py:366
  39.5 5.1 %collective-permute-start.14 = (f32[2,8,128]{2,1,0:T(8,128)S(1)}, f32[2,8,128]{2,1,0:T(8,128)S(1)}, u32[]{:S(2)}, u32[]{:S(2)}) collective-permute-start(f32[2,8,128]{2,1,0:T(8,128)S(1)} %get-tuple-element.44), channel_id=1, source_target_pairs={{0,2},{1,7},{2,8},{3,13},{4,6},{5,3},{6,12},{7,9},{8,10},{9,15},{1... | collective-permute-start | bytes 24584 | tf_op jit(solution)/shard_map/ppermute | solution.py:366
  44.6 1.1 %collective-permute-start.15 = (f32[2,8,128]{2,1,0:T(8,128)S(1)}, f32[2,8,128]{2,1,0:T(8,128)S(1)}, u32[]{:S(2)}, u32[]{:S(2)}) collective-permute-start(f32[2,8,128]{2,1,0:T(8,128)S(1)} %get-tuple-element.44), channel_id=1, source_target_pairs={{0,3},{1,6},{2,9},{3,12},{4,7},{5,2},{6,13},{7,8},{8,11},{9,14},{1... | collective-permute-start | bytes 24584 | tf_op jit(solution)/shard_map/ppermute | solution.py:366
  45.7 0.0 collective-permute-done.16.refs_2_
  45.7 0.0 collective-permute-start.17
  45.7 0.4 collective-permute-done.14.refs_0_
  46.1 4.3 %collective-permute-done.15.refs_1_ = f32[2,8,128]{2,1,0:T(8,128)S(1)} collective-permute-done((f32[2,8,128]{2,1,0:T(8,128)S(1)}, f32[2,8,128]{2,1,0:T(8,128)S(1)}, u32[]{:S(2)}, u32[]{:S(2)}) %collective-permute-start.15) | collective-permute-done | bytes 8224 | tf_op jit(solution)/shard_map/ppermute | solution.py:366
  50.4 0.0 collective-permute-done.17.refs_3_
  50.4 0.6 %unpack.1 = (f32[2,8]{1,0:T(2,128)}, f32[2,8]{1,0:T(2,128)}) custom-call(f32[8,128]{1,0:T(8,128)S(1)} %get-tuple-element.27.masks, f32[2,8,128]{2,1,0:T(8,128)S(1)} %collective-permute-done.14.refs_0_, f32[2,8,128]{2,1,0:T(8,128)S(1)} %collective-permute-done.15.refs_1_, f32[2,8,128]{2,1,0:T(8,128)S(1)} %collective-permute-done.16.refs_2_, ...), custom_call_target="tpu_custom_call" | custom-call | tf_op jit(solution)/shard_map/unpack/pallas_call | solution.py:346
  (2 shorter events, 0.0 us)
Async XLA Ops:
  0.6 7.7 %collective-permute-start.3 = (bf16[512,1024]{1,0:T(8,128)(2,1)}, bf16[512,1024]{1,0:T(8,128)(2,1)S(1)}, u32[]{:S(2)}, u32[]{:S(2)}) collective-permute-start(bf16[512,1024]{1,0:T(8,128)(2,1)} %bitcast.3), channel_id=1, source_target_pairs={{0,1},{1,0},{2,3},{3,2},{4,5},{5,4},{6,7},{7,6},{8,9},{9,8},{10,11... | collective-permute-start | bytes 3145736 | tf_op jit(solution)/shard_map/ppermute | solution.py:363
  1.1 3.7 %copy-start.4 = (s32[32]{0:T(128)S(1)}, s32[32]{0:T(128)}, u32[]{:S(2)}) copy-start(s32[32]{0:T(128)} %branches.5) | copy-start | bytes 388
  1.2 7.1 %copy-start.2 = (bf16[256,256]{1,0:T(8,128)(2,1)S(1)}, bf16[256,256]{1,0:T(8,128)(2,1)}, u32[]{:S(2)}) copy-start(bf16[256,256]{1,0:T(8,128)(2,1)} %trial) | copy-start | bytes 393220
  1.2 7.1 %copy-start.3 = (f32[8,256]{1,0:T(8,128)S(1)}, f32[8,256]{1,0:T(8,128)}, u32[]{:S(2)}) copy-start(f32[8,256]{1,0:T(8,128)} %field.1) | copy-start | bytes 24580
  2.2 12.6 %collective-permute-start.8 = (bf16[192,1024]{1,0:T(8,128)(2,1)S(1)}, bf16[192,1024]{1,0:T(8,128)(2,1)S(1)}, u32[]{:S(2)}, u32[]{:S(2)}) collective-permute-start(bf16[192,1024]{1,0:T(8,128)(2,1)S(1)} %constant_dynamic-slice_fusion), channel_id=1, source_target_pairs={{0,2},{1,3},{2,0},{3,1},{4,6},{5,7},{6,4},{7,5},{8,10},{9,11},{10,... | collective-permute-start | bytes 1179656 | tf_op jit(solution)/shard_map/ppermute | solution.py:363
  4.8 1.2 %copy-start = (bf16[8,256,256]{2,1,0:T(8,128)(2,1)S(1)}, bf16[8,256,256]{2,1,0:T(8,128)(2,1)}, u32[]{:S(2)}) copy-start(bf16[8,256,256]{2,1,0:T(8,128)(2,1)} %walkers.1) | copy-start | bytes 3145732
  6.0 15.3 %copy-start.1 = (bf16[2,256,1024]{2,1,0:T(8,128)(2,1)S(1)}, bf16[2,256,1024]{2,1,0:T(8,128)(2,1)}, u32[]{:S(2)}) copy-start(bf16[2,256,1024]{2,1,0:T(8,128)(2,1)} %param.8) | copy-start | bytes 3145732
  8.3 9.7 %collective-permute-start.1 = (bf16[288,256]{1,0:T(8,128)(2,1)S(1)}, bf16[288,256]{1,0:T(8,128)(2,1)S(1)}, u32[]{:S(2)}, u32[]{:S(2)}) collective-permute-start(bf16[288,256]{1,0:T(8,128)(2,1)S(1)} %message.1.refs_0_), channel_id=1, source_target_pairs={{0,2},{1,3},{2,0},{3,1},{4,6},{5,7},{6,4},{7,5},{8,10},{9,11},{10,... | collective-permute-start | bytes 442376 | tf_op jit(solution)/shard_map/ppermute | solution.py:363
  8.4 14.4 %collective-permute-start.4 = (bf16[2,256,256]{2,1,0:T(8,128)(2,1)S(1)}, bf16[2,256,256]{2,1,0:T(8,128)(2,1)S(1)}, u32[]{:S(2)}, u32[]{:S(2)}) collective-permute-start(bf16[2,256,256]{2,1,0:T(8,128)(2,1)S(1)} %get-tuple-element.29), channel_id=1, source_target_pairs={{0,1},{1,0},{2,3},{3,2},{4,5},{5,4},{6,7},{7,6},{8,9},{9,8},{10,11... | collective-permute-start | bytes 786440 | tf_op jit(solution)/shard_map/ppermute | solution.py:363
  8.6 15.0 %collective-permute-start.5 = (bf16[2,256,256]{2,1,0:T(8,128)(2,1)S(1)}, bf16[2,256,256]{2,1,0:T(8,128)(2,1)S(1)}, u32[]{:S(2)}, u32[]{:S(2)}) collective-permute-start(bf16[2,256,256]{2,1,0:T(8,128)(2,1)S(1)} %get-tuple-element.31), channel_id=1, source_target_pairs={{0,2},{1,3},{2,0},{3,1},{4,6},{5,7},{6,4},{7,5},{8,10},{9,11},{10,... | collective-permute-start | bytes 786440 | tf_op jit(solution)/shard_map/ppermute | solution.py:363
  10.4 7.6 %collective-permute-start = (bf16[288,256]{1,0:T(8,128)(2,1)S(1)}, bf16[288,256]{1,0:T(8,128)(2,1)S(1)}, u32[]{:S(2)}, u32[]{:S(2)}) collective-permute-start(bf16[288,256]{1,0:T(8,128)(2,1)S(1)} %message.1.refs_0_), channel_id=1, source_target_pairs={{0,1},{1,0},{2,3},{3,2},{4,5},{5,4},{6,7},{7,6},{8,9},{9,8},{10,11... | collective-permute-start | bytes 442376 | tf_op jit(solution)/shard_map/ppermute | solution.py:363
  14.8 19.7 %collective-permute-start.12 = (bf16[192,1024]{1,0:T(8,128)(2,1)S(1)}, bf16[192,1024]{1,0:T(8,128)(2,1)S(1)}, u32[]{:S(2)}, u32[]{:S(2)}) collective-permute-start(bf16[192,1024]{1,0:T(8,128)(2,1)S(1)} %collective-permute-done.8.refs_0_), channel_id=1, source_target_pairs={{0,4},{4,0},{8,12},{12,8},{1,5},{5,1},{9,13},{13,9},{2,6},{6,2},{1... | collective-permute-start | bytes 1179656 | tf_op jit(solution)/shard_map/ppermute | solution.py:364
  17.9 2.1 %collective-permute-start.2 = (bf16[288,256]{1,0:T(8,128)(2,1)S(1)}, bf16[288,256]{1,0:T(8,128)(2,1)S(1)}, u32[]{:S(2)}, u32[]{:S(2)}) collective-permute-start(bf16[288,256]{1,0:T(8,128)(2,1)S(1)} %collective-permute-done.1.refs_2_), channel_id=1, source_target_pairs={{0,1},{1,0},{2,3},{3,2},{4,5},{5,4},{6,7},{7,6},{8,9},{9,8},{10,11... | collective-permute-start | bytes 442376 | tf_op jit(solution)/shard_map/ppermute | solution.py:363
  18.0 11.4 %collective-permute-start.9 = (bf16[2,256,256]{2,1,0:T(8,128)(2,1)S(1)}, bf16[2,256,256]{2,1,0:T(8,128)(2,1)S(1)}, u32[]{:S(2)}, u32[]{:S(2)}) collective-permute-start(bf16[2,256,256]{2,1,0:T(8,128)(2,1)S(1)} %get-tuple-element.36), channel_id=1, source_target_pairs={{0,3},{1,2},{2,1},{3,0},{4,7},{5,6},{6,5},{7,4},{8,11},{9,10},{10,... | collective-permute-start | bytes 786440 | tf_op jit(solution)/shard_map/ppermute | solution.py:363
  20.6 2.2 %collective-permute-start.6 = (f32[4,2,256]{2,1,0:T(2,128)S(1)}, f32[4,2,256]{2,1,0:T(2,128)S(1)}, u32[]{:S(2)}, u32[]{:S(2)}) collective-permute-start(f32[4,2,256]{2,1,0:T(2,128)S(1)} %fields.1), channel_id=1, source_target_pairs={{0,0},{1,5},{2,10},{3,15},{4,4},{5,1},{6,14},{7,11},{8,8},{9,13},{... | collective-permute-start | bytes 24584 | tf_op jit(solution)/shard_map/ppermute | solution.py:365
  24.4 12.1 %collective-permute-start.7 = (bf16[128,1024]{1,0:T(8,128)(2,1)S(1)}, bf16[128,1024]{1,0:T(8,128)(2,1)S(1)}, u32[]{:S(2)}, u32[]{:S(2)}) collective-permute-start(bf16[128,1024]{1,0:T(8,128)(2,1)S(1)} %slice.4), channel_id=1, source_target_pairs={{0,2},{1,3},{2,0},{3,1},{4,6},{5,7},{6,4},{7,5},{8,10},{9,11},{10,... | collective-permute-start | bytes 786440 | tf_op jit(solution)/shard_map/ppermute | solution.py:363
  29.2 7.5 %collective-permute-start.11 = (bf16[192,1024]{1,0:T(8,128)(2,1)S(1)}, bf16[192,1024]{1,0:T(8,128)(2,1)S(1)}, u32[]{:S(2)}, u32[]{:S(2)}) collective-permute-start(bf16[192,1024]{1,0:T(8,128)(2,1)S(1)} %collective-permute-done.8.refs_0_), channel_id=1, source_target_pairs={{0,1},{1,0},{2,3},{3,2},{4,5},{5,4},{6,7},{7,6},{8,9},{9,8},{10,11... | collective-permute-start | bytes 1179656 | tf_op jit(solution)/shard_map/ppermute | solution.py:363
  34.5 2.2 %collective-permute-start.13 = (bf16[192,1024]{1,0:T(8,128)(2,1)S(1)}, bf16[192,1024]{1,0:T(8,128)(2,1)S(1)}, u32[]{:S(2)}, u32[]{:S(2)}) collective-permute-start(bf16[192,1024]{1,0:T(8,128)(2,1)S(1)} %collective-permute-done.12.refs_2_), channel_id=1, source_target_pairs={{0,1},{1,0},{2,3},{3,2},{4,5},{5,4},{6,7},{7,6},{8,9},{9,8},{10,11... | collective-permute-start | bytes 1179656 | tf_op jit(solution)/shard_map/ppermute | solution.py:363
  36.5 1.6 %collective-permute-start.10 = (bf16[128,1024]{1,0:T(8,128)(2,1)S(1)}, bf16[128,1024]{1,0:T(8,128)(2,1)S(1)}, u32[]{:S(2)}, u32[]{:S(2)}) collective-permute-start(bf16[128,1024]{1,0:T(8,128)(2,1)S(1)} %collective-permute-done.7.refs_0_), channel_id=1, source_target_pairs={{0,1},{1,0},{2,3},{3,2},{4,5},{5,4},{6,7},{7,6},{8,9},{9,8},{10,11... | collective-permute-start | bytes 786440 | tf_op jit(solution)/shard_map/ppermute | solution.py:363
  38.8 6.9 %collective-permute-start.16 = (f32[2,8,128]{2,1,0:T(8,128)S(1)}, f32[2,8,128]{2,1,0:T(8,128)S(1)}, u32[]{:S(2)}, u32[]{:S(2)}) collective-permute-start(f32[2,8,128]{2,1,0:T(8,128)S(1)} %get-tuple-element.45), channel_id=1, source_target_pairs={{0,0},{1,5},{2,10},{3,15},{4,4},{5,1},{6,14},{7,11},{8,8},{9,13},{... | collective-permute-start | bytes 24584 | tf_op jit(solution)/shard_map/ppermute | solution.py:366
  39.5 6.6 %collective-permute-start.14 = (f32[2,8,128]{2,1,0:T(8,128)S(1)}, f32[2,8,128]{2,1,0:T(8,128)S(1)}, u32[]{:S(2)}, u32[]{:S(2)}) collective-permute-start(f32[2,8,128]{2,1,0:T(8,128)S(1)} %get-tuple-element.44), channel_id=1, source_target_pairs={{0,2},{1,7},{2,8},{3,13},{4,6},{5,3},{6,12},{7,9},{8,10},{9,15},{1... | collective-permute-start | bytes 24584 | tf_op jit(solution)/shard_map/ppermute | solution.py:366
  44.6 5.8 %collective-permute-start.15 = (f32[2,8,128]{2,1,0:T(8,128)S(1)}, f32[2,8,128]{2,1,0:T(8,128)S(1)}, u32[]{:S(2)}, u32[]{:S(2)}) collective-permute-start(f32[2,8,128]{2,1,0:T(8,128)S(1)} %get-tuple-element.44), channel_id=1, source_target_pairs={{0,3},{1,6},{2,9},{3,12},{4,7},{5,2},{6,13},{7,8},{8,11},{9,14},{1... | collective-permute-start | bytes 24584 | tf_op jit(solution)/shard_map/ppermute | solution.py:366
  45.7 4.7 %collective-permute-start.17 = (f32[2,8,128]{2,1,0:T(8,128)S(1)}, f32[2,8,128]{2,1,0:T(8,128)S(1)}, u32[]{:S(2)}, u32[]{:S(2)}) collective-permute-start(f32[2,8,128]{2,1,0:T(8,128)S(1)} %collective-permute-done.16.refs_2_), channel_id=1, source_target_pairs={{0,1},{1,0},{2,3},{3,2},{4,5},{5,4},{6,7},{7,6},{8,9},{9,8},{10,11... | collective-permute-start | bytes 24584 | tf_op jit(solution)/shard_map/ppermute | solution.py:363

commit v14 on v10

--- a/solution.py
+++ b/solution.py
@@ -8,7 +8,7 @@
 from jax.sharding import PartitionSpec as P
 
 ITERS = 10
-EARLY = 3
+EARLY = 4
 SR = ("slab", "row")
 ALL = ("walk", "slab", "row")
 F32 = jnp.float32

time: 49.3 us -> 49.2 us (level)
  no operation moved by 1% of the time
where the time goes in v14:
time: 49.2 us; the launch traced here: 49 us
  starting transfers between devices  23.1 us (47%)
  Pallas kernels  13.7 us (28%)
  waiting for transfers between devices  8.45 us (17%)
  local copies, waits for them, and re-layouts  2.32 us (5%)
  between operations  1.46 us (3%)
    ppermute x14, starting transfers between devices, at_the_source(): move = lambda x, k: lax.ppermute(x, SR, [(i, i ^ k) for i in range(n)])  14.7 us
    ppermute x14, waiting for transfers between devices, at_the_source(): move = lambda x, k: lax.ppermute(x, SR, [(i, i ^ k) for i in range(n)])  6.92 us
    ppermute x2, starting transfers between devices, at_the_source(): lax.ppermute(x, ALL, [(w * n + q, (w ^ q) * n + (q ^ k)) for w, q in pairs])  5.74 us
    pallas_call x1, Pallas kernels, make_green(): pl.pallas_call(functools.partial(green_kernel, n, share), out_shape=jax.S...  5.1 us
    pallas_call x3, Pallas kernels, contract(): pl.pallas_call(kernel, out_shape=[jax.ShapeDtypeStruct((count, 8, 128), F...  3.63 us
    pallas_call x1, Pallas kernels, select(): pl.pallas_call(functools.partial(select_kernel, n, per, share), out_shape...  2.17 us
    ppermute x1, starting transfers between devices, at_the_source(): swap = lambda x: lax.ppermute(x, 'walk', [(w, w ^ 1) for w in range(n)])  2.03 us
    ppermute x2, waiting for transfers between devices, at_the_source(): lax.ppermute(x, ALL, [(w * n + q, (w ^ q) * n + (q ^ k)) for w, q in pairs])  1.53 us
  transfers between devices with their start and end apart: 18, of which 5 were waited for; matrix products, arithmetic and copies ran while one was open for 2% of the time, Pallas kernels for 25%

profile of v14, /device:TPU:0, one launch (start us, length us, event | category | flops | bytes accessed | tf_op | source)
XLA Modules:
  0.0 49.0 jit_solution(12191953832627871967)
XLA Ops:
  0.6 0.5 %collective-permute-start.3 = (bf16[512,1024]{1,0:T(8,128)(2,1)}, bf16[512,1024]{1,0:T(8,128)(2,1)S(1)}, u32[]{:S(2)}, u32[]{:S(2)}) collective-permute-start(bf16[512,1024]{1,0:T(8,128)(2,1)} %bitcast.3), channel_id=1, source_target_pairs={{0,1},{1,0},{2,3},{3,2},{4,5},{5,4},{6,7},{7,6},{8,9},{9,8},{10,11... | collective-permute-start | bytes 3145736 | tf_op jit(solution)/shard_map/ppermute | solution.py:362
  1.1 0.0 copy-start.4
  1.2 0.0 copy-start.2
  1.2 0.0 copy-start.3
  1.2 1.1 %constant_dynamic-slice_fusion = bf16[192,1024]{1,0:T(8,128)(2,1)S(1)} fusion(bf16[512,1024]{1,0:T(8,128)(2,1)} %bitcast.4, s32[]{:T(128)S(6)} %select_n.3), kind=kLoop, calls=%fused_computation | loop fusion | bytes 786436 | tf_op jit(solution)/shard_map/dynamic_slice | solution.py:386
  2.2 2.6 %collective-permute-start.4 = (bf16[192,1024]{1,0:T(8,128)(2,1)S(1)}, bf16[192,1024]{1,0:T(8,128)(2,1)S(1)}, u32[]{:S(2)}, u32[]{:S(2)}) collective-permute-start(bf16[192,1024]{1,0:T(8,128)(2,1)S(1)} %constant_dynamic-slice_fusion), channel_id=1, source_target_pairs={{0,2},{1,3},{2,0},{3,1},{4,6},{5,7},{6,4},{7,5},{8,10},{9,11},{10,... | collective-permute-start | bytes 1179656 | tf_op jit(solution)/shard_map/ppermute | solution.py:362
  4.8 0.0 copy-done.4
  4.8 0.0 copy-start
  4.8 1.2 %copy-done = bf16[8,256,256]{2,1,0:T(8,128)(2,1)S(1)} copy-done((bf16[8,256,256]{2,1,0:T(8,128)(2,1)S(1)}, bf16[8,256,256]{2,1,0:T(8,128)(2,1)}, u32[]{:S(2)}) %copy-start) | copy-done | bytes 1048600
  6.0 0.0 copy-start.1
  6.1 2.2 %select.1 = (bf16[2,256,256]{2,1,0:T(8,128)(2,1)S(1)}, bf16[2,256,256]{2,1,0:T(8,128)(2,1)S(1)}, bf16[2,256,256]{2,1,0:T(8,128)(2,1)S(1)}, bf16[2,256,256]{2,1,0:T(8,128)(2,1)S(1)}) custom-call(s32[32]{0:T(128)S(1)} %copy-done.4, bf16[8,256,256]{2,1,0:T(8,128)(2,1)S(1)} %copy-done), custom_call_target="tpu_custom_call" | custom-call | tf_op jit(solution)/shard_map/select/pallas_call | solution.py:69
  8.2 0.0 copy-done.2
  8.2 0.0 copy-done.3
  8.3 0.1 collective-permute-start.1
  8.4 0.0 collective-permute-done.3.refs_1_
  8.4 0.2 collective-permute-start.7
  8.6 1.8 %collective-permute-start.8 = (bf16[2,256,256]{2,1,0:T(8,128)(2,1)S(1)}, bf16[2,256,256]{2,1,0:T(8,128)(2,1)S(1)}, u32[]{:S(2)}, u32[]{:S(2)}) collective-permute-start(bf16[2,256,256]{2,1,0:T(8,128)(2,1)S(1)} %get-tuple-element.33), channel_id=1, source_target_pairs={{0,2},{1,3},{2,0},{3,1},{4,6},{5,7},{6,4},{7,5},{8,10},{9,11},{10,... | collective-permute-start | bytes 786440 | tf_op jit(solution)/shard_map/ppermute | solution.py:362
  10.4 0.2 collective-permute-start
  10.6 4.2 %collective-permute-done.4.refs_0_ = bf16[192,1024]{1,0:T(8,128)(2,1)S(1)} collective-permute-done((bf16[192,1024]{1,0:T(8,128)(2,1)S(1)}, bf16[192,1024]{1,0:T(8,128)(2,1)S(1)}, u32[]{:S(2)}, u32[]{:S(2)}) %collective-permute-start.4) | collective-permute-done | bytes 393248 | tf_op jit(solution)/shard_map/ppermute | solution.py:362
  14.8 2.0 %collective-permute-start.12 = (bf16[192,1024]{1,0:T(8,128)(2,1)S(1)}, bf16[192,1024]{1,0:T(8,128)(2,1)S(1)}, u32[]{:S(2)}, u32[]{:S(2)}) collective-permute-start(bf16[192,1024]{1,0:T(8,128)(2,1)S(1)} %collective-permute-done.4.refs_0_), channel_id=1, source_target_pairs={{0,4},{4,0},{8,12},{12,8},{1,5},{5,1},{9,13},{13,9},{2,6},{6,2},{1... | collective-permute-start | bytes 1179656 | tf_op jit(solution)/shard_map/ppermute | solution.py:363
  16.8 1.1 %collective-permute-done.1.refs_2_ = bf16[288,256]{1,0:T(8,128)(2,1)S(1)} collective-permute-done((bf16[288,256]{1,0:T(8,128)(2,1)S(1)}, bf16[288,256]{1,0:T(8,128)(2,1)S(1)}, u32[]{:S(2)}, u32[]{:S(2)}) %collective-permute-start.1) | collective-permute-done | bytes 147488 | tf_op jit(solution)/shard_map/ppermute | solution.py:362
  17.9 0.0 collective-permute-start.2
  18.0 0.0 collective-permute-done.refs_1_
  18.0 2.1 %collective-permute-start.5 = (bf16[2,256,256]{2,1,0:T(8,128)(2,1)S(1)}, bf16[2,256,256]{2,1,0:T(8,128)(2,1)S(1)}, u32[]{:S(2)}, u32[]{:S(2)}) collective-permute-start(bf16[2,256,256]{2,1,0:T(8,128)(2,1)S(1)} %get-tuple-element.28), channel_id=1, source_target_pairs={{0,3},{1,2},{2,1},{3,0},{4,7},{5,6},{6,5},{7,4},{8,11},{9,10},{10,... | collective-permute-start | bytes 786440 | tf_op jit(solution)/shard_map/ppermute | solution.py:362
  20.0 0.0 collective-permute-done.2.refs_3_
  20.0 0.6 %fields.1 = f32[4,2,256]{2,1,0:T(2,128)S(1)} custom-call(s32[32]{0:T(128)S(1)} %copy-done.4, bf16[288,256]{1,0:T(8,128)(2,1)S(1)} %message.1.refs_0_, bf16[288,256]{1,0:T(8,128)(2,1)S(1)} %collective-permute-done.refs_1_, bf16[288,256]{1,0:T(8,128)(2,1)S(1)} %collective-permute-done.1.refs_2_, bf16[288,256]{1,0:T(8,128)(2,1)S(1)} %collective-permute-done.2.refs_3_), custom_call_target="tpu_custom_call" | custom-call | tf_op jit(solution)/shard_map/fields/pallas_call | solution.py:119
  20.6 0.7 %collective-permute-start.6 = (f32[4,2,256]{2,1,0:T(2,128)S(1)}, f32[4,2,256]{2,1,0:T(2,128)S(1)}, u32[]{:S(2)}, u32[]{:S(2)}) collective-permute-start(f32[4,2,256]{2,1,0:T(2,128)S(1)} %fields.1), channel_id=1, source_target_pairs={{0,0},{1,5},{2,10},{3,15},{4,4},{5,1},{6,14},{7,11},{8,8},{9,13},{... | collective-permute-start | bytes 24584 | tf_op jit(solution)/shard_map/ppermute | solution.py:364
  21.3 0.0 copy-done.1
  22.0 0.8 %turn.1 = (bf16[256,1024]{1,0:T(8,128)(2,1)S(1)}, f32[8,128]{1,0:T(8,128)S(1)}) custom-call(s32[32]{0:T(128)S(1)} %copy-done.4, s32[1]{0:T(128)S(6)} %copy.8.counts, bf16[288,256]{1,0:T(8,128)(2,1)S(1)} %message.1.refs_0_, bf16[288,256]{1,0:T(8,128)(2,1)S(1)} %collective-permute-done.refs_1_, bf16[288,256]{1,0:T(8,128)(2,1)S(1)} %collective-permute-done.1.refs_2_, ...), custom_call_target="tpu_custom_call" | custom-call | tf_op jit(solution)/shard_map/turn/pallas_call | solution.py:146
  22.8 0.0 collective-permute-done.6.refs_4_.refs_2_
  22.8 0.0 collective-permute-done.7.refs_1_
  22.8 0.8 %collective-permute-done.8.refs_2_ = bf16[2,256,256]{2,1,0:T(8,128)(2,1)S(1)} collective-permute-done((bf16[2,256,256]{2,1,0:T(8,128)(2,1)S(1)}, bf16[2,256,256]{2,1,0:T(8,128)(2,1)S(1)}, u32[]{:S(2)}, u32[]{:S(2)}) %collective-permute-start.8) | collective-permute-done | bytes 262176 | tf_op jit(solution)/shard_map/ppermute | solution.py:362
  23.6 0.8 %first.1 = (bf16[768,512]{1,0:T(8,128)(2,1)S(1)}, f32[256,512]{1,0:T(8,128)S(1)}) custom-call(bf16[2,256,256]{2,1,0:T(8,128)(2,1)S(1)} %get-tuple-element.24.refs_0_, bf16[2,256,256]{2,1,0:T(8,128)(2,1)S(1)} %collective-permute-done.7.refs_1_, bf16[2,256,256]{2,1,0:T(8,128)(2,1)S(1)} %collective-permute-done.8.refs_2_, ...), custom_call_target="tpu_custom_call" | custom-call | flops 1073741824 | bytes 1048576 | tf_op jit(solution)/shard_map/first/pallas_call | solution.py:187
  24.4 4.8 %collective-permute-start.9 = (bf16[128,1024]{1,0:T(8,128)(2,1)S(1)}, bf16[128,1024]{1,0:T(8,128)(2,1)S(1)}, u32[]{:S(2)}, u32[]{:S(2)}) collective-permute-start(bf16[128,1024]{1,0:T(8,128)(2,1)S(1)} %slice.4), channel_id=1, source_target_pairs={{0,2},{1,3},{2,0},{3,1},{4,6},{5,7},{6,4},{7,5},{8,10},{9,11},{10,... | collective-permute-start | bytes 786440 | tf_op jit(solution)/shard_map/ppermute | solution.py:362
  29.2 0.2 collective-permute-start.11
  29.4 0.0 collective-permute-done.5.refs_0_
  29.4 5.1 %green.1.refs_2_.refs_4_ = bf16[1024,512]{1,0:T(8,128)(2,1)S(1)} custom-call(bf16[2,256,256]{2,1,0:T(8,128)(2,1)S(1)} %collective-permute-done.5.refs_0_, bf16[256,1024]{1,0:T(8,128)(2,1)S(1)} %get-tuple-element.29.refs_3_.refs_1_, f32[4,2,256]{2,1,0:T(2,128)S(1)} %collective-permute-done.6.refs_4_.refs_2_, bf16[768,512]{1,0:T(8,128)(2,1)S(1)} %get-tuple-element.34.refs_3_, ...), custom_call_target="tpu_custom_call" | custom-call | tf_op jit(solution)/shard_map/green/pallas_call | solution.py:245
  34.5 0.0 collective-permute-done.12.refs_2_
  34.5 0.4 collective-permute-start.13
  34.9 1.5 %contract.3 = f32[2,8,128]{2,1,0:T(8,128)S(1)} custom-call(bf16[512,1024]{1,0:T(8,128)(2,1)S(1)} %bitcast.6, bf16[512,1024]{1,0:T(8,128)(2,1)S(1)} %collective-permute-done.3.refs_1_, bf16[1024,512]{1,0:T(8,128)(2,1)S(1)} %green.1.refs_2_.refs_4_), custom_call_target="tpu_custom_call" | custom-call | flops 1073741824 | bytes 3145728 | tf_op jit(solution)/shard_map/contract/pallas_call | solution.py:313
  36.4 0.0 collective-permute-done.9.refs_0_
  36.4 0.2 collective-permute-start.10
  36.7 0.0 collective-permute-done.11.refs_1_
  36.7 0.0 collective-permute-done.13.refs_3_
  36.7 1.4 %contract.4 = (f32[2,8,128]{2,1,0:T(8,128)S(1)}, f32[128,512]{1,0:T(8,128)S(1)}, f32[128,512]{1,0:T(8,128)S(1)}) custom-call(bf16[192,1024]{1,0:T(8,128)(2,1)S(1)} %collective-permute-done.4.refs_0_, bf16[192,1024]{1,0:T(8,128)(2,1)S(1)} %collective-permute-done.11.refs_1_, bf16[192,1024]{1,0:T(8,128)(2,1)S(1)} %collective-permute-done.12.refs_2_, ...), custom_call_target="tpu_custom_call" | custom-call | flops 805306368 | bytes 2621440 | tf_op jit(solution)/shard_map/contract/pallas_call | solution.py:313
  38.1 0.0 collective-permute-done.10.refs_1_
  38.1 0.7 %contract.5 = f32[2,8,128]{2,1,0:T(8,128)S(1)} custom-call(bf16[128,1024]{1,0:T(8,128)(2,1)S(1)} %collective-permute-done.9.refs_0_, bf16[128,1024]{1,0:T(8,128)(2,1)S(1)} %collective-permute-done.10.refs_1_, bf16[1024,512]{1,0:T(8,128)(2,1)S(1)} %green.1.refs_2_.refs_4_, f32[128,512]{1,0:T(8,128)S(1)} %get-tuple-element.40.refs_3_, ...), custom_call_target="tpu_custom_call" | custom-call | flops 268435456 | bytes 1572864 | tf_op jit(solution)/shard_map/contract/pallas_call | solution.py:313
  38.8 0.7 %collective-permute-start.14 = (f32[2,8,128]{2,1,0:T(8,128)S(1)}, f32[2,8,128]{2,1,0:T(8,128)S(1)}, u32[]{:S(2)}, u32[]{:S(2)}) collective-permute-start(f32[2,8,128]{2,1,0:T(8,128)S(1)} %contract.3), channel_id=1, source_target_pairs={{0,0},{1,5},{2,10},{3,15},{4,4},{5,1},{6,14},{7,11},{8,8},{9,13},{... | collective-permute-start | bytes 24584 | tf_op jit(solution)/shard_map/ppermute | solution.py:365
  39.5 5.1 %collective-permute-start.16 = (f32[2,8,128]{2,1,0:T(8,128)S(1)}, f32[2,8,128]{2,1,0:T(8,128)S(1)}, u32[]{:S(2)}, u32[]{:S(2)}) collective-permute-start(f32[2,8,128]{2,1,0:T(8,128)S(1)} %contract.5), channel_id=1, source_target_pairs={{0,2},{1,7},{2,8},{3,13},{4,6},{5,3},{6,12},{7,9},{8,10},{9,15},{1... | collective-permute-start | bytes 24584 | tf_op jit(solution)/shard_map/ppermute | solution.py:365
  44.6 0.0 collective-permute-done.14.refs_0_
  44.6 0.0 collective-permute-start.15
  44.6 1.5 %collective-permute-done.16.refs_2_ = f32[2,8,128]{2,1,0:T(8,128)S(1)} collective-permute-done((f32[2,8,128]{2,1,0:T(8,128)S(1)}, f32[2,8,128]{2,1,0:T(8,128)S(1)}, u32[]{:S(2)}, u32[]{:S(2)}) %collective-permute-start.16) | collective-permute-done | bytes 8224 | tf_op jit(solution)/shard_map/ppermute | solution.py:365
  46.1 1.5 %collective-permute-start.17 = (f32[2,8,128]{2,1,0:T(8,128)S(1)}, f32[2,8,128]{2,1,0:T(8,128)S(1)}, u32[]{:S(2)}, u32[]{:S(2)}) collective-permute-start(f32[2,8,128]{2,1,0:T(8,128)S(1)} %collective-permute-done.16.refs_2_), channel_id=1, source_target_pairs={{0,1},{1,0},{2,3},{3,2},{4,5},{5,4},{6,7},{7,6},{8,9},{9,8},{10,11... | collective-permute-start | bytes 24584 | tf_op jit(solution)/shard_map/ppermute | solution.py:362
  47.6 0.0 collective-permute-done.15.refs_1_
  47.6 0.8 %collective-permute-done.17.refs_3_ = f32[2,8,128]{2,1,0:T(8,128)S(1)} collective-permute-done((f32[2,8,128]{2,1,0:T(8,128)S(1)}, f32[2,8,128]{2,1,0:T(8,128)S(1)}, u32[]{:S(2)}, u32[]{:S(2)}) %collective-permute-start.17) | collective-permute-done | bytes 8224 | tf_op jit(solution)/shard_map/ppermute | solution.py:362
  48.5 0.6 %unpack.1 = (f32[2,8]{1,0:T(2,128)}, f32[2,8]{1,0:T(2,128)}) custom-call(f32[8,128]{1,0:T(8,128)S(1)} %get-tuple-element.26.masks, f32[2,8,128]{2,1,0:T(8,128)S(1)} %collective-permute-done.14.refs_0_, f32[2,8,128]{2,1,0:T(8,128)S(1)} %collective-permute-done.15.refs_1_, f32[2,8,128]{2,1,0:T(8,128)S(1)} %collective-permute-done.16.refs_2_, ...), custom_call_target="tpu_custom_call" | custom-call | tf_op jit(solution)/shard_map/unpack/pallas_call | solution.py:345
  (2 shorter events, 0.0 us)
Async XLA Ops:
  0.6 7.7 %collective-permute-start.3 = (bf16[512,1024]{1,0:T(8,128)(2,1)}, bf16[512,1024]{1,0:T(8,128)(2,1)S(1)}, u32[]{:S(2)}, u32[]{:S(2)}) collective-permute-start(bf16[512,1024]{1,0:T(8,128)(2,1)} %bitcast.3), channel_id=1, source_target_pairs={{0,1},{1,0},{2,3},{3,2},{4,5},{5,4},{6,7},{7,6},{8,9},{9,8},{10,11... | collective-permute-start | bytes 3145736 | tf_op jit(solution)/shard_map/ppermute | solution.py:362
  1.1 3.7 %copy-start.4 = (s32[32]{0:T(128)S(1)}, s32[32]{0:T(128)}, u32[]{:S(2)}) copy-start(s32[32]{0:T(128)} %branches.5) | copy-start | bytes 388
  1.2 7.1 %copy-start.2 = (bf16[256,256]{1,0:T(8,128)(2,1)S(1)}, bf16[256,256]{1,0:T(8,128)(2,1)}, u32[]{:S(2)}) copy-start(bf16[256,256]{1,0:T(8,128)(2,1)} %trial) | copy-start | bytes 393220
  1.2 7.1 %copy-start.3 = (f32[8,256]{1,0:T(8,128)S(1)}, f32[8,256]{1,0:T(8,128)}, u32[]{:S(2)}) copy-start(f32[8,256]{1,0:T(8,128)} %field.1) | copy-start | bytes 24580
  2.2 12.6 %collective-permute-start.4 = (bf16[192,1024]{1,0:T(8,128)(2,1)S(1)}, bf16[192,1024]{1,0:T(8,128)(2,1)S(1)}, u32[]{:S(2)}, u32[]{:S(2)}) collective-permute-start(bf16[192,1024]{1,0:T(8,128)(2,1)S(1)} %constant_dynamic-slice_fusion), channel_id=1, source_target_pairs={{0,2},{1,3},{2,0},{3,1},{4,6},{5,7},{6,4},{7,5},{8,10},{9,11},{10,... | collective-permute-start | bytes 1179656 | tf_op jit(solution)/shard_map/ppermute | solution.py:362
  4.8 1.2 %copy-start = (bf16[8,256,256]{2,1,0:T(8,128)(2,1)S(1)}, bf16[8,256,256]{2,1,0:T(8,128)(2,1)}, u32[]{:S(2)}) copy-start(bf16[8,256,256]{2,1,0:T(8,128)(2,1)} %walkers.1) | copy-start | bytes 3145732
  6.0 15.3 %copy-start.1 = (bf16[2,256,1024]{2,1,0:T(8,128)(2,1)S(1)}, bf16[2,256,1024]{2,1,0:T(8,128)(2,1)}, u32[]{:S(2)}) copy-start(bf16[2,256,1024]{2,1,0:T(8,128)(2,1)} %param.8) | copy-start | bytes 3145732
  8.3 9.7 %collective-permute-start.1 = (bf16[288,256]{1,0:T(8,128)(2,1)S(1)}, bf16[288,256]{1,0:T(8,128)(2,1)S(1)}, u32[]{:S(2)}, u32[]{:S(2)}) collective-permute-start(bf16[288,256]{1,0:T(8,128)(2,1)S(1)} %message.1.refs_0_), channel_id=1, source_target_pairs={{0,2},{1,3},{2,0},{3,1},{4,6},{5,7},{6,4},{7,5},{8,10},{9,11},{10,... | collective-permute-start | bytes 442376 | tf_op jit(solution)/shard_map/ppermute | solution.py:362
  8.4 14.4 %collective-permute-start.7 = (bf16[2,256,256]{2,1,0:T(8,128)(2,1)S(1)}, bf16[2,256,256]{2,1,0:T(8,128)(2,1)S(1)}, u32[]{:S(2)}, u32[]{:S(2)}) collective-permute-start(bf16[2,256,256]{2,1,0:T(8,128)(2,1)S(1)} %get-tuple-element.31), channel_id=1, source_target_pairs={{0,1},{1,0},{2,3},{3,2},{4,5},{5,4},{6,7},{7,6},{8,9},{9,8},{10,11... | collective-permute-start | bytes 786440 | tf_op jit(solution)/shard_map/ppermute | solution.py:362
  8.6 15.0 %collective-permute-start.8 = (bf16[2,256,256]{2,1,0:T(8,128)(2,1)S(1)}, bf16[2,256,256]{2,1,0:T(8,128)(2,1)S(1)}, u32[]{:S(2)}, u32[]{:S(2)}) collective-permute-start(bf16[2,256,256]{2,1,0:T(8,128)(2,1)S(1)} %get-tuple-element.33), channel_id=1, source_target_pairs={{0,2},{1,3},{2,0},{3,1},{4,6},{5,7},{6,4},{7,5},{8,10},{9,11},{10,... | collective-permute-start | bytes 786440 | tf_op jit(solution)/shard_map/ppermute | solution.py:362
  10.4 7.6 %collective-permute-start = (bf16[288,256]{1,0:T(8,128)(2,1)S(1)}, bf16[288,256]{1,0:T(8,128)(2,1)S(1)}, u32[]{:S(2)}, u32[]{:S(2)}) collective-permute-start(bf16[288,256]{1,0:T(8,128)(2,1)S(1)} %message.1.refs_0_), channel_id=1, source_target_pairs={{0,1},{1,0},{2,3},{3,2},{4,5},{5,4},{6,7},{7,6},{8,9},{9,8},{10,11... | collective-permute-start | bytes 442376 | tf_op jit(solution)/shard_map/ppermute | solution.py:362
  14.8 19.7 %collective-permute-start.12 = (bf16[192,1024]{1,0:T(8,128)(2,1)S(1)}, bf16[192,1024]{1,0:T(8,128)(2,1)S(1)}, u32[]{:S(2)}, u32[]{:S(2)}) collective-permute-start(bf16[192,1024]{1,0:T(8,128)(2,1)S(1)} %collective-permute-done.4.refs_0_), channel_id=1, source_target_pairs={{0,4},{4,0},{8,12},{12,8},{1,5},{5,1},{9,13},{13,9},{2,6},{6,2},{1... | collective-permute-start | bytes 1179656 | tf_op jit(solution)/shard_map/ppermute | solution.py:363
  17.9 2.1 %collective-permute-start.2 = (bf16[288,256]{1,0:T(8,128)(2,1)S(1)}, bf16[288,256]{1,0:T(8,128)(2,1)S(1)}, u32[]{:S(2)}, u32[]{:S(2)}) collective-permute-start(bf16[288,256]{1,0:T(8,128)(2,1)S(1)} %collective-permute-done.1.refs_2_), channel_id=1, source_target_pairs={{0,1},{1,0},{2,3},{3,2},{4,5},{5,4},{6,7},{7,6},{8,9},{9,8},{10,11... | collective-permute-start | bytes 442376 | tf_op jit(solution)/shard_map/ppermute | solution.py:362
  18.0 11.4 %collective-permute-start.5 = (bf16[2,256,256]{2,1,0:T(8,128)(2,1)S(1)}, bf16[2,256,256]{2,1,0:T(8,128)(2,1)S(1)}, u32[]{:S(2)}, u32[]{:S(2)}) collective-permute-start(bf16[2,256,256]{2,1,0:T(8,128)(2,1)S(1)} %get-tuple-element.28), channel_id=1, source_target_pairs={{0,3},{1,2},{2,1},{3,0},{4,7},{5,6},{6,5},{7,4},{8,11},{9,10},{10,... | collective-permute-start | bytes 786440 | tf_op jit(solution)/shard_map/ppermute | solution.py:362
  20.6 2.2 %collective-permute-start.6 = (f32[4,2,256]{2,1,0:T(2,128)S(1)}, f32[4,2,256]{2,1,0:T(2,128)S(1)}, u32[]{:S(2)}, u32[]{:S(2)}) collective-permute-start(f32[4,2,256]{2,1,0:T(2,128)S(1)} %fields.1), channel_id=1, source_target_pairs={{0,0},{1,5},{2,10},{3,15},{4,4},{5,1},{6,14},{7,11},{8,8},{9,13},{... | collective-permute-start | bytes 24584 | tf_op jit(solution)/shard_map/ppermute | solution.py:364
  24.4 12.1 %collective-permute-start.9 = (bf16[128,1024]{1,0:T(8,128)(2,1)S(1)}, bf16[128,1024]{1,0:T(8,128)(2,1)S(1)}, u32[]{:S(2)}, u32[]{:S(2)}) collective-permute-start(bf16[128,1024]{1,0:T(8,128)(2,1)S(1)} %slice.4), channel_id=1, source_target_pairs={{0,2},{1,3},{2,0},{3,1},{4,6},{5,7},{6,4},{7,5},{8,10},{9,11},{10,... | collective-permute-start | bytes 786440 | tf_op jit(solution)/shard_map/ppermute | solution.py:362
  29.2 7.5 %collective-permute-start.11 = (bf16[192,1024]{1,0:T(8,128)(2,1)S(1)}, bf16[192,1024]{1,0:T(8,128)(2,1)S(1)}, u32[]{:S(2)}, u32[]{:S(2)}) collective-permute-start(bf16[192,1024]{1,0:T(8,128)(2,1)S(1)} %collective-permute-done.4.refs_0_), channel_id=1, source_target_pairs={{0,1},{1,0},{2,3},{3,2},{4,5},{5,4},{6,7},{7,6},{8,9},{9,8},{10,11... | collective-permute-start | bytes 1179656 | tf_op jit(solution)/shard_map/ppermute | solution.py:362
  34.5 2.2 %collective-permute-start.13 = (bf16[192,1024]{1,0:T(8,128)(2,1)S(1)}, bf16[192,1024]{1,0:T(8,128)(2,1)S(1)}, u32[]{:S(2)}, u32[]{:S(2)}) collective-permute-start(bf16[192,1024]{1,0:T(8,128)(2,1)S(1)} %collective-permute-done.12.refs_2_), channel_id=1, source_target_pairs={{0,1},{1,0},{2,3},{3,2},{4,5},{5,4},{6,7},{7,6},{8,9},{9,8},{10,11... | collective-permute-start | bytes 1179656 | tf_op jit(solution)/shard_map/ppermute | solution.py:362
  36.4 1.6 %collective-permute-start.10 = (bf16[128,1024]{1,0:T(8,128)(2,1)S(1)}, bf16[128,1024]{1,0:T(8,128)(2,1)S(1)}, u32[]{:S(2)}, u32[]{:S(2)}) collective-permute-start(bf16[128,1024]{1,0:T(8,128)(2,1)S(1)} %collective-permute-done.9.refs_0_), channel_id=1, source_target_pairs={{0,1},{1,0},{2,3},{3,2},{4,5},{5,4},{6,7},{7,6},{8,9},{9,8},{10,11... | collective-permute-start | bytes 786440 | tf_op jit(solution)/shard_map/ppermute | solution.py:362
  38.8 5.7 %collective-permute-start.14 = (f32[2,8,128]{2,1,0:T(8,128)S(1)}, f32[2,8,128]{2,1,0:T(8,128)S(1)}, u32[]{:S(2)}, u32[]{:S(2)}) collective-permute-start(f32[2,8,128]{2,1,0:T(8,128)S(1)} %contract.3), channel_id=1, source_target_pairs={{0,0},{1,5},{2,10},{3,15},{4,4},{5,1},{6,14},{7,11},{8,8},{9,13},{... | collective-permute-start | bytes 24584 | tf_op jit(solution)/shard_map/ppermute | solution.py:365
  39.5 6.6 %collective-permute-start.16 = (f32[2,8,128]{2,1,0:T(8,128)S(1)}, f32[2,8,128]{2,1,0:T(8,128)S(1)}, u32[]{:S(2)}, u32[]{:S(2)}) collective-permute-start(f32[2,8,128]{2,1,0:T(8,128)S(1)} %contract.5), channel_id=1, source_target_pairs={{0,2},{1,7},{2,8},{3,13},{4,6},{5,3},{6,12},{7,9},{8,10},{9,15},{1... | collective-permute-start | bytes 24584 | tf_op jit(solution)/shard_map/ppermute | solution.py:365
  44.6 3.1 %collective-permute-start.15 = (f32[2,8,128]{2,1,0:T(8,128)S(1)}, f32[2,8,128]{2,1,0:T(8,128)S(1)}, u32[]{:S(2)}, u32[]{:S(2)}) collective-permute-start(f32[2,8,128]{2,1,0:T(8,128)S(1)} %collective-permute-done.14.refs_0_), channel_id=1, source_target_pairs={{0,1},{1,0},{2,3},{3,2},{4,5},{5,4},{6,7},{7,6},{8,9},{9,8},{10,11... | collective-permute-start | bytes 24584 | tf_op jit(solution)/shard_map/ppermute | solution.py:362
  46.1 2.4 %collective-permute-start.17 = (f32[2,8,128]{2,1,0:T(8,128)S(1)}, f32[2,8,128]{2,1,0:T(8,128)S(1)}, u32[]{:S(2)}, u32[]{:S(2)}) collective-permute-start(f32[2,8,128]{2,1,0:T(8,128)S(1)} %collective-permute-done.16.refs_2_), channel_id=1, source_target_pairs={{0,1},{1,0},{2,3},{3,2},{4,5},{5,4},{6,7},{7,6},{8,9},{9,8},{10,11... | collective-permute-start | bytes 24584 | tf_op jit(solution)/shard_map/ppermute | solution.py:362
